TPU v7x, 32 devices: a whole 2x2x4 slice. The times are simulated.
32 devices in a mesh: groups: 2 (over x), seq: 16 (over z, y, core).
Axes of the slice: x: 2, y: 2, z: 4, core: 2. Of those that a mesh axis runs over, the one named last changes fastest.
Arguments:
- query_seq: bfloat16 [8192, 6144], P(('groups', 'seq')), parts along dimension 0, may hold values from -15 to 15
- key_seq: bfloat16 [8192, 6144], P(('groups', 'seq')), parts along dimension 0, may hold values from -15 to 15
- value_seq: bfloat16 [8192, 6144], P(('groups', 'seq')), parts along dimension 0, may hold values from -288 to 288
- conv_kernel: bfloat16 [3, 4, 6144], replicated, may hold values from -3 to 3
- feature_map: bfloat16 [128, 128], replicated, may hold values from -1.5 to 1.5
- norm_gain: float32 [6144], replicated, may hold values from 0.25 to 1.75
Outputs:
- attended: bfloat16 [8192, 6144], P(('groups', 'seq')), parts along dimension 0
There are 2 independent parts, one for each index of `groups`. A program takes and returns all parts, laid end to end along the dimension named above; an argument that names none is the same for every part. Nothing has to cross between parts.
All inputs are finite; a program needn't handle non-finite values.
Results may differ from a plain program's by a relative error of at most 0.012.
The roundings to bfloat16 on the way count: a program that leaves them out, or rounds other values in their place, can miss the bound.
Values may be sent and summed in bfloat16 or wider, within the bound.
No kernel may reach another device: no remote copies, remote signals or barrier semaphores. Data moves between devices by JAX's collectives and lax.ppermute only.
A program may use at most 128 MiB of HBM per device.

v0:
```python
import jax
import jax.numpy as jnp
from jax import lax
from jax.sharding import PartitionSpec as P

SPAN = 256


def from_behind(block, axis, distance):
    devices = range(lax.axis_size(axis))
    route = [(i - distance, i) for i in devices if i - distance in devices]
    return lax.ppermute(block, axis, route)


def short_conv(seq_rows, rim_rows, kernel):
    tap_count = kernel.shape[0]
    length = seq_rows.shape[0]
    padded = jnp.concatenate([rim_rows, seq_rows], axis=0)
    summed = jnp.zeros(seq_rows.shape, jnp.float32)
    for offset in range(tap_count):
        window = padded[tap_count - 1 - offset : tap_count - 1 - offset + length]
        summed = summed + kernel[offset].astype(jnp.float32) * window.astype(jnp.float32)
    return summed.astype(jnp.bfloat16)


def feature_rows(conv_rows, feature_map):
    head_dim = feature_map.shape[0]
    flattened = conv_rows.reshape(-1, head_dim)
    projected = jnp.dot(flattened, feature_map, preferred_element_type=jnp.float32)
    return (jax.nn.elu(projected) + 1.0).astype(jnp.bfloat16)


def block_states(key_feat, value_heads):
    block_terms = jnp.einsum(
        "cjhd,cjhe->chde", key_feat, value_heads, preferred_element_type=jnp.float32
    )
    running = jnp.cumsum(block_terms, axis=0)
    local_prefix = jnp.concatenate([jnp.zeros_like(block_terms), running[:-1]], axis=0)
    return (local_prefix, running[-1])


def on_device(query_seq, key_seq, value_seq, conv_kernel, feature_map, norm_gain):
    tok_count = query_seq.shape[0]
    model_width = query_seq.shape[1]
    head_dim = feature_map.shape[0]
    head_count = model_width // head_dim
    tap_count = conv_kernel.shape[1]
    rim_start = tok_count - (tap_count - 1)
    query_rim, key_rim, value_rim = from_behind(
        (query_seq[rim_start:], key_seq[rim_start:], value_seq[rim_start:]), "seq", 1
    )
    query_conv = short_conv(query_seq, query_rim, conv_kernel[0])
    key_conv = short_conv(key_seq, key_rim, conv_kernel[1])
    value_conv = short_conv(value_seq, value_rim, conv_kernel[2])
    block_count = tok_count // SPAN
    query_feat = feature_rows(query_conv, feature_map).reshape(
        block_count, SPAN, head_count, head_dim
    )
    key_feat = feature_rows(key_conv, feature_map).reshape(block_count, SPAN, head_count, head_dim)
    value_heads = value_conv.reshape(block_count, SPAN, head_count, head_dim)
    local_prefix, device_total = block_states(key_feat, value_heads)
    stacked = device_total.reshape(1, head_count * head_dim, head_dim)
    shares = lax.all_to_all(stacked, "seq", split_axis=1, concat_axis=0, tiled=True)
    running = jnp.cumsum(shares, axis=0)
    before = jnp.concatenate([jnp.zeros_like(shares[:1]), running[:-1]], axis=0)
    gathered = lax.all_to_all(before, "seq", split_axis=0, concat_axis=1, tiled=True)
    earlier = gathered.reshape(head_count, head_dim, head_dim)
    prefix_bf = (earlier[None] + local_prefix).astype(jnp.bfloat16)
    scores = jnp.einsum("cihd,cjhd->chij", query_feat, key_feat, preferred_element_type=jnp.float32)
    causal = lax.broadcasted_iota(jnp.int32, (SPAN, SPAN), 0) >= lax.broadcasted_iota(
        jnp.int32, (SPAN, SPAN), 1
    )
    weights = jnp.where(causal, scores, 0.0).astype(jnp.bfloat16)
    mixed_rows = jnp.einsum(
        "chij,cjhd->cihd", weights, value_heads, preferred_element_type=jnp.float32
    )
    mixed_rows = mixed_rows + jnp.einsum(
        "cihd,chde->cihe", query_feat, prefix_bf, preferred_element_type=jnp.float32
    )
    inverse_rms = lax.rsqrt(jnp.mean(mixed_rows * mixed_rows, axis=-1, keepdims=True) + 1e-06)
    normed = (mixed_rows * inverse_rms).reshape(tok_count, model_width) * norm_gain
    return normed.astype(jnp.bfloat16)


def solution(mesh):
    return jax.shard_map(
        on_device,
        mesh=mesh,
        in_specs=(
            P(("groups", "seq"), None),
            P(("groups", "seq"), None),
            P(("groups", "seq"), None),
            P(),
            P(),
            P(),
        ),
        out_specs=P(("groups", "seq"), None),
        check_vma=False,
    )
```

profile of v0, /device:TPU:16, one launch (start us, length us, event | category | flops | bytes accessed | tf_op | source)
XLA Modules:
  0.0 212.9 jit_solution(609619368015761294)
XLA Ops:
  0.0 0.0 copy-start
  0.0 0.9 slice.104
  0.9 1.9 collective-permute-start
  2.9 0.9 slice.120
  3.8 3.5 %collective-permute-start.2 = (bf16[3,6144]{1,0:T(4,128)(2,1)S(1)}, bf16[3,6144]{1,0:T(4,128)(2,1)S(1)}, u32[]{:S(2)}, u32[]{:S(2)}) collective-permute-start(bf16[3,6144]{1,0:T(4,128)(2,1)S(1)} %slice.120), channel_id=1, source_target_pairs={{0,1},{1,2},{2,3},{3,4},{4,5},{5,6},{6,7},{7,8},{8,9},{9,10},{10,1... | collective-permute-start | bytes 110600 | tf_op jit(solution)/shard_map/ppermute | solution.py:12
  7.3 1.4 slice_convert_fusion.7
  8.7 1.4 collective-permute-done.2
  10.1 7.4 %add_convert_fusion = bf16[256,6144]{1,0:T(8,128)(2,1)S(1)} fusion(bf16[256,6144]{1,0:T(8,128)(2,1)} %param.7, bf16[3,6144]{1,0:T(4,128)(2,1)S(1)} %collective-permute-done.2, f32[6144]{0:T(1024)S(1)} %bitcast.60, f32[6144]{0:T(1024)S(1)} %bitcast.61, f32[6144]{0:T(1024)S(1)} %bitcast.58, f32[6144]{0:T(1024)S(1)} %bitcast.59), kind=kLoop, calls=%fused_computation.17 | loop fusion | flops 33030144 | bytes 6426624 | tf_op jit(solution)/shard_map/convert_element_type | solution.py:23
  17.5 2.9 %reshape.179 = bf16[12288,128]{1,0:T(8,128)(2,1)} reshape(bf16[256,6144]{1,0:T(8,128)(2,1)S(1)} %add_convert_fusion) | data formatting | bytes 6291456 | tf_op jit(solution)/shard_map/reshape | solution.py:28
  20.4 0.0 copy-done
  20.4 6.4 %fusion.6 = bf16[12288,128]{1,0:T(8,128)(2,1)} fusion(bf16[12288,128]{1,0:T(8,128)(2,1)} %reshape.179, bf16[128,128]{1,0:T(8,128)(2,1)S(1)} %copy-done), kind=kOutput, calls=%fused_computation.11 | convolution fusion | flops 410517504 | bytes 6324224 | tf_op jit(solution)/shard_map/dot_general | solution.py:29
  26.7 3.9 %copy.21 = bf16[256,48,128]{0,2,1:T(8,128)(2,1)S(1)} copy(bf16[256,48,128]{2,1,0:T(8,128)(2,1)} %bitcast.47) | data formatting | bytes 6291456 | tf_op jit(solution)/shard_map/reshape.31
  30.6 0.0 copy-start.2
  30.6 0.0 collective-permute-done
  30.6 7.7 %fusion.21 = bf16[32,48,8,128]{3,2,1,0:T(8,128)(2,1)S(1)} fusion(bf16[256,6144]{1,0:T(8,128)(2,1)} %param.8, bf16[3,6144]{1,0:T(4,128)(2,1)S(1)} %collective-permute-done, f32[6144]{0:T(1024)S(1)} %bitcast.54, f32[6144]{0:T(1024)S(1)} %bitcast.55, f32[6144]{0:T(1024)S(1)} %bitcast.56, f32[6144]{0:T(1024)S(1)} %bitcast.57), kind=kLoop, calls=%fused_computation.40 | loop fusion | flops 33030144 | bytes 6426624
  38.4 0.0 copy-start.4
  38.4 1.0 fusion.19
  39.4 0.0 copy-done.2
  39.4 75.2 %all_to_all.21 = f32[1,6144,128]{2,0,1:T(1,128)S(1)} all-to-all(f32[1,6144,128]{2,0,1:T(1,128)S(1)} %bitcast.46), channel_id=1, replica_groups=mesh['groups'=2,'seq'=16] {'seq'}, dimensions={1} | all-to-all | bytes 6291456 | tf_op jit(solution)/shard_map/all_to_all | solution.py:63
  114.6 0.0 copy-done.4
  114.6 0.2 fusion.31
  114.8 0.1 slice.139
  114.9 1.3 concatenate.15
  116.3 4.9 %all-to-all-start.1 = ((bf16[16,384,128]{2,1,0:T(8,128)(2,1)}), bf16[16,384,128]{2,1,0:T(8,128)(2,1)}, u32[]{:S(2)}, u32[]{:S(2)}) async-start(bf16[16,384,128]{2,1,0:T(8,128)(2,1)} %concatenate.15), calls=%async_computation.1 | async-start | bytes 3145728 | tf_op jit(solution)/shard_map/all_to_all | solution.py:66
  121.2 0.9 slice.112
  122.1 2.2 %collective-permute-start.1 = (bf16[3,6144]{1,0:T(4,128)(2,1)S(1)}, bf16[3,6144]{1,0:T(4,128)(2,1)S(1)}, u32[]{:S(2)}, u32[]{:S(2)}) collective-permute-start(bf16[3,6144]{1,0:T(4,128)(2,1)S(1)} %slice.112), channel_id=1, source_target_pairs={{0,1},{1,2},{2,3},{3,4},{4,5},{5,6},{6,7},{7,8},{8,9},{9,10},{10,1... | collective-permute-start | bytes 110600 | tf_op jit(solution)/shard_map/ppermute | solution.py:12
  124.4 33.7 %collective-permute-done.1 = bf16[3,6144]{1,0:T(4,128)(2,1)S(1)} collective-permute-done((bf16[3,6144]{1,0:T(4,128)(2,1)S(1)}, bf16[3,6144]{1,0:T(4,128)(2,1)S(1)}, u32[]{:S(2)}, u32[]{:S(2)}) %collective-permute-start.1) | collective-permute-done | bytes 36896 | tf_op jit(solution)/shard_map/ppermute | solution.py:12
  158.1 7.3 %add_convert_fusion.1 = bf16[256,6144]{1,0:T(8,128)(2,1)S(1)} fusion(bf16[256,6144]{1,0:T(8,128)(2,1)} %param.6, bf16[3,6144]{1,0:T(4,128)(2,1)S(1)} %collective-permute-done.1, f32[6144]{0:T(1024)S(1)} %bitcast.51, f32[6144]{0:T(1024)S(1)} %bitcast.52, f32[6144]{0:T(1024)S(1)} %bitcast.53, f32[6144]{0:T(1024)S(1)} %bitcast.50), kind=kLoop, calls=%fused_computation.18 | loop fusion | flops 33030144 | bytes 6426624 | tf_op jit(solution)/shard_map/convert_element_type | solution.py:23
  165.4 2.9 %reshape.177 = bf16[12288,128]{1,0:T(8,128)(2,1)} reshape(bf16[256,6144]{1,0:T(8,128)(2,1)S(1)} %add_convert_fusion.1) | data formatting | bytes 6291456 | tf_op jit(solution)/shard_map/reshape | solution.py:28
  168.3 6.4 %fusion.3 = bf16[12288,128]{1,0:T(8,128)(2,1)} fusion(bf16[12288,128]{1,0:T(8,128)(2,1)} %reshape.177, bf16[128,128]{1,0:T(8,128)(2,1)S(1)} %copy-done), kind=kOutput, calls=%fused_computation.8 | convolution fusion | flops 410517504 | bytes 6324224 | tf_op jit(solution)/shard_map/dot_general | solution.py:29
  174.7 0.0 copy-start.3
  174.7 0.0 all-to-all-done.1
  174.7 6.2 %fusion.24 = f32[48,128,256]{2,1,0:T(8,128)} fusion(bf16[48,128,128]{2,1,0:T(8,128)(2,1)} %bitcast.17, bf16[256,48,128]{2,1,0:T(8,128)(2,1)} %bitcast.48), kind=kOutput, calls=%fused_computation.43 | convolution fusion | flops 402653184 | bytes 11010048 | tf_op jit(solution)/shard_map/cihd,chde->cihe/dot_general | solution.py:77
  180.9 0.0 copy-done.3
  180.9 11.1 %fusion.7 = (f32[256,48]{0,1:T(8,128)S(1)}, f32[48,128,256]{2,1,0:T(8,128)}) fusion(f32[48,128,256]{2,1,0:T(8,128)} %fusion.24, pred[256,256]{1,0:T(8,128)(4,1)S(1)} %iota_compare_fusion, bf16[256,48,128]{0,2,1:T(8,128)(2,1)S(1)} %copy-done.3, bf16[256,48,128]{2,1,0:T(8,128)(2,1)} %bitcast.49, bf16[32,48,8,128]{3,2,1,0:T(8,128)(2,1)} %copy-done.4), kind=kOutput, calls=%fused_computation.14 | convolution fusion | flops 1621610496 | bytes 22134784 | tf_op jit(solution)/shard_map/chij,cjhd->cihd/dot_general | solution.py:74
  192.0 9.3 %bitcast_multiply_fusion = f32[1,256,48,128]{1,3,2,0:T(8,128)} fusion(f32[256,48]{0,1:T(8,128)S(1)} %add_rsqrt_fusion, f32[48,128,256]{2,1,0:T(8,128)} %get-tuple-element.18, f32[48,128,256]{2,1,0:T(8,128)} %fusion.24), kind=kLoop, calls=%fused_computation.12 | loop fusion | flops 3145728 | bytes 18923520 | tf_op jit(solution)/shard_map/mul | solution.py:81
  201.3 0.0 copy-start.5
  201.3 0.0 copy-start.1
  201.3 6.6 %copy.26 = f32[256,6144]{1,0:T(8,128)} copy(f32[256,6144]{0,1:T(8,128)} %bitcast.44) | data formatting | bytes 12582912 | tf_op jit(solution)/shard_map/reshape | solution.py:81
  207.9 0.0 copy-done.5
  207.9 5.0 %multiply_convert_fusion = bf16[256,6144]{1,0:T(8,128)(2,1)} fusion(f32[256,6144]{1,0:T(8,128)} %copy.26, f32[6144]{0:T(1024)S(1)} %copy-done.5), kind=kLoop, calls=%fused_computation.15 | loop fusion | flops 3145728 | bytes 9461760 | tf_op jit(solution)/shard_map/convert_element_type | solution.py:82
  212.9 0.0 copy-done.1
  (2 shorter events, 0.0 us)
Async XLA Ops:
  0.0 20.4 %copy-start = (bf16[128,128]{1,0:T(8,128)(2,1)S(1)}, bf16[128,128]{1,0:T(8,128)(2,1)}, u32[]{:S(2)}) copy-start(bf16[128,128]{1,0:T(8,128)(2,1)} %param.10) | copy-start | bytes 98308
  0.9 29.7 %collective-permute-start = (bf16[3,6144]{1,0:T(4,128)(2,1)S(1)}, bf16[3,6144]{1,0:T(4,128)(2,1)S(1)}, u32[]{:S(2)}, u32[]{:S(2)}) collective-permute-start(bf16[3,6144]{1,0:T(4,128)(2,1)S(1)} %slice.104), channel_id=1, source_target_pairs={{0,1},{1,2},{2,3},{3,4},{4,5},{5,6},{6,7},{7,8},{8,9},{9,10},{10,1... | collective-permute-start | bytes 110600 | tf_op jit(solution)/shard_map/ppermute | solution.py:12
  3.8 6.3 %collective-permute-start.2 = (bf16[3,6144]{1,0:T(4,128)(2,1)S(1)}, bf16[3,6144]{1,0:T(4,128)(2,1)S(1)}, u32[]{:S(2)}, u32[]{:S(2)}) collective-permute-start(bf16[3,6144]{1,0:T(4,128)(2,1)S(1)} %slice.120), channel_id=1, source_target_pairs={{0,1},{1,2},{2,3},{3,4},{4,5},{5,6},{6,7},{7,8},{8,9},{9,10},{10,1... | collective-permute-start | bytes 110600 | tf_op jit(solution)/shard_map/ppermute | solution.py:12
  30.6 8.8 %copy-start.2 = (bf16[256,48,128]{0,2,1:T(8,128)(2,1)}, bf16[256,48,128]{0,2,1:T(8,128)(2,1)S(1)}, u32[]{:S(2)}) copy-start(bf16[256,48,128]{0,2,1:T(8,128)(2,1)S(1)} %copy.21) | copy-start | bytes 9437188
  38.4 76.2 %copy-start.4 = (bf16[32,48,8,128]{3,2,1,0:T(8,128)(2,1)}, bf16[32,48,8,128]{3,2,1,0:T(8,128)(2,1)S(1)}, u32[]{:S(2)}) copy-start(bf16[32,48,8,128]{3,2,1,0:T(8,128)(2,1)S(1)} %fusion.21) | copy-start | bytes 9437188
  116.3 58.4 %all-to-all-start.1 = ((bf16[16,384,128]{2,1,0:T(8,128)(2,1)}), bf16[16,384,128]{2,1,0:T(8,128)(2,1)}, u32[]{:S(2)}, u32[]{:S(2)}) async-start(bf16[16,384,128]{2,1,0:T(8,128)(2,1)} %concatenate.15), calls=%async_computation.1 | async-start | bytes 3145728 | tf_op jit(solution)/shard_map/all_to_all | solution.py:66
  122.1 36.0 %collective-permute-start.1 = (bf16[3,6144]{1,0:T(4,128)(2,1)S(1)}, bf16[3,6144]{1,0:T(4,128)(2,1)S(1)}, u32[]{:S(2)}, u32[]{:S(2)}) collective-permute-start(bf16[3,6144]{1,0:T(4,128)(2,1)S(1)} %slice.112), channel_id=1, source_target_pairs={{0,1},{1,2},{2,3},{3,4},{4,5},{5,6},{6,7},{7,8},{8,9},{9,10},{10,1... | collective-permute-start | bytes 110600 | tf_op jit(solution)/shard_map/ppermute | solution.py:12
  174.7 6.2 %copy-start.3 = (bf16[256,48,128]{0,2,1:T(8,128)(2,1)S(1)}, bf16[256,48,128]{0,2,1:T(8,128)(2,1)}, u32[]{:S(2)}) copy-start(bf16[256,48,128]{0,2,1:T(8,128)(2,1)} %copy-done.2) | copy-start | bytes 9437188
  201.3 6.6 %copy-start.5 = (f32[6144]{0:T(1024)S(1)}, f32[6144]{0:T(1024)}, u32[]{:S(2)}) copy-start(f32[6144]{0:T(1024)} %param.11) | copy-start | bytes 73732
  201.3 11.6 %copy-start.1 = (bf16[128,128]{1,0:T(8,128)(2,1)S(1)}, bf16[128,128]{1,0:T(8,128)(2,1)}, u32[]{:S(2)}) copy-start(bf16[128,128]{1,0:T(8,128)(2,1)} %param.10) | copy-start | bytes 98308
where the time goes:
time: 214 us; the launch traced here: 213 us
  blocking collectives  75.2 us (35%)
  other arithmetic  38.3 us (18%)
  waiting for transfers between devices  35.1 us (16%)
  matrix products  31.1 us (15%)
  local copies, waits for them, and re-layouts  20.5 us (10%)
  starting transfers between devices  12.6 us (6%)
    all_to_all x1, blocking collectives, on_device(): lax.all_to_all(stacked, 'seq', split_axis=1, concat_axis=0, tiled=True)  75.2 us
    ppermute x3, waiting for transfers between devices, from_behind(): return lax.ppermute(block, axis, route)  35.1 us
    convert_element_type x2, other arithmetic, short_conv(): return summed.astype(jnp.bfloat16)  14.7 us
    dot_general x2, matrix products, feature_rows(): jnp.dot(flattened, feature_map, preferred_element_type=jnp.float32)  12.7 us
    dot_general x1, matrix products, on_device(): jnp.einsum('chij,cjhd->cihd', weights, value_heads, preferred_element_typ...  11.1 us
    mul x1, other arithmetic, on_device(): mixed_rows * inverse_rms  9.28 us
    unnamed x1, other arithmetic  7.72 us
    ppermute x3, starting transfers between devices, from_behind(): return lax.ppermute(block, axis, route)  7.69 us
  transfers between devices with their start and end apart: 4, of which 2 were waited for; matrix products, arithmetic and copies ran while one was open for 19% of the time, Pallas kernels for 0%

commit v1 on v0

v1 whole, which is shorter than its diff:
```python
import functools

import jax
import jax.numpy as jnp
from jax import lax
from jax.experimental import pallas as pl
from jax.experimental.pallas import tpu as pltpu
from jax.sharding import PartitionSpec as P

SPAN = 256
GROUPS = 1
RIM = 16
TILE = 8
VMEM_BYTES = 40 * 1024 * 1024


def pack_kernel(tap_count, query_ref, key_ref, value_ref, rim_ref):
    taps = tap_count - 1
    row = lax.broadcasted_iota(jnp.int32, (TILE, query_ref.shape[1]), 0)
    key_tail = key_ref[...].astype(jnp.float32)[-TILE:]
    value_tail = value_ref[...].astype(jnp.float32)[-TILE:]
    query_tail = query_ref[...].astype(jnp.float32)[-TILE:]
    key_rows = pltpu.roll(key_tail, taps, 0)
    value_rows = pltpu.roll(value_tail, 2 * taps, 0)
    first = jnp.where(row < taps, key_rows, value_rows)
    rim_ref[...] = jnp.concatenate([first, query_tail], axis=0).astype(jnp.bfloat16)


def pack_rims(query_seq, key_seq, value_seq, tap_count):
    tok_count, width = query_seq.shape
    tail = pl.BlockSpec((RIM, width), lambda i: (tok_count // RIM - 1, 0))
    return pl.pallas_call(
        functools.partial(pack_kernel, tap_count),
        grid=(1,),
        in_specs=[tail] * 3,
        out_specs=pl.BlockSpec((RIM, width), lambda i: (0, 0)),
        out_shape=jax.ShapeDtypeStruct((RIM, width), jnp.bfloat16),
        name="pack_rims",
    )(query_seq, key_seq, value_seq)


def convolved(rows, taps, rim=None, rim_end=0):
    total = taps[0:1] * rows
    row = lax.broadcasted_iota(jnp.int32, (TILE, rows.shape[1]), 0)
    for offset in range(1, taps.shape[0]):
        moved = pltpu.roll(rows, offset, 0)
        before = 0.0 if rim is None else pltpu.roll(rim, (offset - rim_end) % TILE, 0)
        first = jnp.where(row < offset, before, moved[:TILE])
        moved = jnp.concatenate([first, moved[TILE:]], axis=0)
        total = total + taps[offset : offset + 1] * moved
    return total.astype(jnp.bfloat16)


def features(conv_rows, feature_map):
    projected = jnp.dot(conv_rows, feature_map, preferred_element_type=jnp.float32)
    return jnp.where(projected > 0, projected + 1.0, jnp.exp(projected)).astype(jnp.bfloat16)


def query_kernel(query_ref, taps_ref, map_ref, feat_ref):
    head_dim = map_ref.shape[0]
    for start in range(0, query_ref.shape[1], head_dim):
        cols = slice(start, start + head_dim)
        conv = convolved(query_ref[:, cols].astype(jnp.float32), taps_ref[0, :, cols].astype(jnp.float32))
        feat_ref[:, cols] = features(conv, map_ref[...])


def query_features(query_seq, conv_kernel, feature_map, step):
    tok_count, width = query_seq.shape
    tap_count = conv_kernel.shape[1]
    block = pl.BlockSpec((tok_count, step), lambda i: (0, i))
    return pl.pallas_call(
        query_kernel,
        grid=(width // step,),
        in_specs=[
            block,
            pl.BlockSpec((1, tap_count, step), lambda i: (0, 0, i)),
            pl.BlockSpec(feature_map.shape, lambda i: (0, 0)),
        ],
        out_specs=block,
        out_shape=jax.ShapeDtypeStruct(query_seq.shape, jnp.bfloat16),
        compiler_params=pltpu.CompilerParams(vmem_limit_bytes=VMEM_BYTES),
        cost_estimate=pl.CostEstimate(
            flops=2 * query_seq.size * feature_map.shape[0],
            bytes_accessed=4 * query_seq.size,
            transcendentals=query_seq.size,
        ),
        name="query_features",
    )(query_seq, conv_kernel, feature_map)


def state_kernel(places, key_ref, value_ref, rim_ref, taps_ref, map_ref, feat_ref, conv_ref, state_ref):
    head_dim = map_ref.shape[0]
    back = taps_ref.shape[1] - 1
    for head in range(key_ref.shape[1] // head_dim):
        cols = slice(head * head_dim, (head + 1) * head_dim)
        rim = rim_ref[:, cols].astype(jnp.float32)[:TILE]
        rim = jnp.where(places[0] > 0, rim, 0.0)
        taps = taps_ref[:, :, cols].astype(jnp.float32)
        key_conv = convolved(key_ref[:, cols].astype(jnp.float32), taps[1], rim, back)
        key_feat = features(key_conv, map_ref[...])
        feat_ref[:, cols] = key_feat
        value_conv = convolved(value_ref[:, cols].astype(jnp.float32), taps[2], rim, 2 * back)
        conv_ref[:, cols] = value_conv
        state = lax.dot_general(
            key_feat, value_conv, (((0,), (0,)), ((), ())), preferred_element_type=jnp.float32
        )
        state_ref[head * head_dim : (head + 1) * head_dim] = state.astype(state_ref.dtype)


def key_states(places, key_seq, value_seq, rims, conv_kernel, feature_map, group, first, state_type):
    tok_count, width = key_seq.shape
    tap_count = conv_kernel.shape[1]
    head_dim = feature_map.shape[0]
    step = width // (4 * GROUPS)

    def natural(i, places):
        return places[1 + first + i] * GROUPS + group

    block = pl.BlockSpec((tok_count, step), lambda i, places: (0, natural(i, places)))
    local = pl.BlockSpec((tok_count, step), lambda i, places: (0, i))
    return pl.pallas_call(
        state_kernel,
        grid_spec=pltpu.PrefetchScalarGridSpec(
            num_scalar_prefetch=1,
            grid=(2,),
            in_specs=[
                block,
                block,
                pl.BlockSpec((RIM, step), lambda i, places: (0, natural(i, places))),
                pl.BlockSpec((3, tap_count, step), lambda i, places: (0, 0, natural(i, places))),
                pl.BlockSpec(feature_map.shape, lambda i, places: (0, 0)),
            ],
            out_specs=[local, local, pl.BlockSpec((step, head_dim), lambda i, places: (i, 0))],
        ),
        out_shape=[
            jax.ShapeDtypeStruct((tok_count, 2 * step), jnp.bfloat16),
            jax.ShapeDtypeStruct((tok_count, 2 * step), jnp.bfloat16),
            jax.ShapeDtypeStruct((2 * step, head_dim), state_type),
        ],
        compiler_params=pltpu.CompilerParams(vmem_limit_bytes=VMEM_BYTES),
        cost_estimate=pl.CostEstimate(
            flops=8 * tok_count * step * head_dim,
            bytes_accessed=16 * tok_count * step,
            transcendentals=2 * tok_count * step,
        ),
        name="key_states",
    )(places, key_seq, value_seq, rims, conv_kernel, feature_map)


def within_kernel(
    places, query_ref, feat_ref, rim_ref, taps_ref, map_ref, key_ref, value_ref, fixed_ref, mixed_ref
):
    head_dim = map_ref.shape[0]
    tok_count = feat_ref.shape[0]
    half = tok_count // 2
    causal = lax.broadcasted_iota(jnp.int32, (half, half), 0) >= lax.broadcasted_iota(
        jnp.int32, (half, half), 1
    )
    for start in range(0, feat_ref.shape[1], head_dim):
        cols = slice(start, start + head_dim)
        rim = rim_ref[:, cols].astype(jnp.float32)[TILE:]
        rim = jnp.where(places[0] > 0, rim, 0.0)
        first = convolved(
            query_ref[:, cols].astype(jnp.float32), taps_ref[0, :, cols].astype(jnp.float32), rim, TILE
        )
        first = features(first, map_ref[...])
        feat = jnp.concatenate([first, feat_ref[RIM:, cols]], axis=0)
        fixed_ref[:, cols] = feat
        key, value = key_ref[:, cols], value_ref[:, cols]
        for at in (0, half):
            scores = lax.dot_general(
                feat[at : at + half],
                key[: at + half],
                (((1,), (1,)), ((), ())),
                preferred_element_type=jnp.float32,
            )
            masked = jnp.where(causal, scores[:, at:], 0.0).astype(jnp.bfloat16)
            if at:
                masked = jnp.concatenate([scores[:, :at].astype(jnp.bfloat16), masked], axis=1)
            mixed_ref[at : at + half, cols] = jnp.dot(
                masked, value[: at + half], preferred_element_type=jnp.float32
            )


def within_block(places, query_seq, query_feat, rims, conv_kernel, feature_map, key_feat, value_conv, group, first):
    tok_count, width = query_seq.shape
    tap_count = conv_kernel.shape[1]
    head_dim = feature_map.shape[0]
    step = width // (4 * GROUPS)

    def natural(i, places):
        return places[1 + first + i] * GROUPS + group

    local = pl.BlockSpec((tok_count, step), lambda i, places: (0, i))
    return pl.pallas_call(
        within_kernel,
        grid_spec=pltpu.PrefetchScalarGridSpec(
            num_scalar_prefetch=1,
            grid=(2,),
            in_specs=[
                pl.BlockSpec((RIM, step), lambda i, places: (0, natural(i, places))),
                pl.BlockSpec((tok_count, step), lambda i, places: (0, natural(i, places))),
                pl.BlockSpec((RIM, step), lambda i, places: (0, natural(i, places))),
                pl.BlockSpec((1, tap_count, step), lambda i, places: (0, 0, natural(i, places))),
                pl.BlockSpec(feature_map.shape, lambda i, places: (0, 0)),
                local,
                local,
            ],
            out_specs=[local, local],
        ),
        out_shape=[
            jax.ShapeDtypeStruct((tok_count, 2 * step), jnp.bfloat16),
            jax.ShapeDtypeStruct((tok_count, 2 * step), jnp.float32),
        ],
        compiler_params=pltpu.CompilerParams(vmem_limit_bytes=VMEM_BYTES),
        cost_estimate=pl.CostEstimate(
            flops=8 * tok_count * tok_count * step,
            bytes_accessed=24 * tok_count * step,
            transcendentals=0,
        ),
        name="within_block",
    )(places, query_seq, query_feat, rims, conv_kernel, feature_map, key_feat, value_conv)


def finish_kernel(places, feat_ref, mixed_ref, prefix_ref, gain_ref, *rest):
    out_ref = rest[-1]
    head_dim = prefix_ref.shape[1]
    for start in range(0, feat_ref.shape[1], head_dim):
        cols = slice(start, start + head_dim)
        mixed = mixed_ref[:, cols] + jnp.dot(
            feat_ref[:, cols], prefix_ref[cols], preferred_element_type=jnp.float32
        )
        inverse_rms = lax.rsqrt(jnp.mean(mixed * mixed, axis=-1, keepdims=True) + 1e-06)
        out_ref[:, cols] = (mixed * inverse_rms * gain_ref[:, cols]).astype(jnp.bfloat16)


def finish(places, fixed_feat, mixed, prefix, norm_gain, before, group, first, position):
    tok_count = mixed.shape[0]
    width = norm_gain.shape[1]
    step = width // (4 * GROUPS)
    head_dim = prefix.shape[1]

    def natural(i, places):
        return places[1 + position] * GROUPS + group

    local = pl.BlockSpec((tok_count, step), lambda i, places: (0, position - first))
    in_specs = [
        local,
        local,
        pl.BlockSpec((step, head_dim), lambda i, places: (0, 0)),
        pl.BlockSpec((1, step), lambda i, places: (0, natural(i, places))),
    ]
    operands = [places, fixed_feat, mixed, prefix, norm_gain]
    aliases = {}
    if before is not None:
        in_specs.append(pl.BlockSpec(memory_space=pl.ANY))
        operands.append(before)
        aliases = {5: 0}
    return pl.pallas_call(
        finish_kernel,
        grid_spec=pltpu.PrefetchScalarGridSpec(
            num_scalar_prefetch=1,
            grid=(1,),
            in_specs=in_specs,
            out_specs=pl.BlockSpec((tok_count, step), lambda i, places: (0, natural(i, places))),
        ),
        out_shape=jax.ShapeDtypeStruct((tok_count, width), jnp.bfloat16),
        input_output_aliases=aliases,
        compiler_params=pltpu.CompilerParams(vmem_limit_bytes=VMEM_BYTES),
        cost_estimate=pl.CostEstimate(
            flops=2 * tok_count * step * head_dim,
            bytes_accessed=8 * tok_count * step,
            transcendentals=tok_count * step // head_dim,
        ),
        name="finish",
    )(*operands)


def swapped(block, axis, distance):
    return lax.ppermute(block, axis, [(i, i ^ distance) for i in range(lax.axis_size(axis))])


def rotated(block, axis, distance):
    count = lax.axis_size(axis)
    return lax.ppermute(block, axis, [(i, (i + distance) % count) for i in range(count)])


def on_device(query_seq, key_seq, value_seq, conv_kernel, feature_map, norm_gain):
    tok_count, width = query_seq.shape
    tap_count = conv_kernel.shape[1]
    head_dim = feature_map.shape[0]
    step = width // (4 * GROUPS)
    assert tok_count == SPAN and step % head_dim == 0
    device_count = lax.axis_size("seq")
    device = lax.axis_index("seq")
    core, pair = device % 2, device // 2 % 2
    places = jnp.stack(
        [
            device,
            2 * (1 - core) + 1 - pair,
            2 * (1 - core) + pair,
            2 * core + 1 - pair,
            2 * core + pair,
        ]
    ).astype(jnp.int32)
    gain = norm_gain.reshape(1, width)
    f32, bf16 = jnp.float32, jnp.bfloat16

    rims = rotated(pack_rims(query_seq, key_seq, value_seq, tap_count), "seq", 1)
    query_feat = query_features(query_seq, conv_kernel, feature_map, step)

    out = None
    for group in range(GROUPS):
        states = functools.partial(
            key_states, places, key_seq, value_seq, rims, conv_kernel, feature_map, group
        )
        key_a, value_a, state_a = states(0, bf16)
        from_core = swapped(state_a, "seq", 1).astype(f32)
        key_b, value_b, state_b = states(2, f32)
        chip = state_b + from_core
        from_pair = swapped(chip[:step].astype(bf16), "seq", 2).astype(f32)
        total = chip[step:] + from_pair
        earlier = jnp.zeros_like(total)
        running = total
        distance = 4
        while distance < device_count:
            arrived = rotated(running.astype(bf16), "seq", distance).astype(f32)
            arrived = jnp.where(device >= distance, arrived, 0.0)
            earlier = earlier + arrived
            running = running + arrived
            distance *= 2
        own = earlier + jnp.where(pair == 1, from_pair, 0.0)
        others = earlier + jnp.where(pair == 0, chip[step:], 0.0)
        back = swapped(others.astype(bf16), "seq", 2).astype(f32)
        prefix_3 = (own + jnp.where(core == 1, from_core[step:], 0.0)).astype(bf16)
        give_3 = (own + jnp.where(core == 0, state_b[step:], 0.0)).astype(bf16)
        prefix_1 = swapped(give_3, "seq", 1)
        prefix_2 = (back + jnp.where(core == 1, from_core[:step], 0.0)).astype(bf16)
        give_2 = (back + jnp.where(core == 0, state_b[:step], 0.0)).astype(bf16)
        prefix_0 = swapped(give_2, "seq", 1)
        within = functools.partial(
            within_block, places, query_seq, query_feat, rims, conv_kernel, feature_map
        )
        feat_a, mixed_a = within(key_a, value_a, group, 0)
        feat_b, mixed_b = within(key_b, value_b, group, 2)
        for position, prefix in ((3, prefix_3), (1, prefix_1), (2, prefix_2), (0, prefix_0)):
            feat, mixed = (feat_a, mixed_a) if position < 2 else (feat_b, mixed_b)
            first = 0 if position < 2 else 2
            out = finish(places, feat, mixed, prefix, gain, out, group, first, position)
    return out


def solution(mesh):
    return jax.shard_map(
        on_device,
        mesh=mesh,
        in_specs=(
            P(("groups", "seq"), None),
            P(("groups", "seq"), None),
            P(("groups", "seq"), None),
            P(),
            P(),
            P(),
        ),
        out_specs=P(("groups", "seq"), None),
        check_vma=False,
    )
```

time: 214 us -> 118 us (0.55)
  the two profiles are of different devices: /device:TPU:16 before, /device:TPU:0 now
where the time goes in v1:
time: 118 us
  waiting for transfers between devices  59 us (50%)
  Pallas kernels  44.8 us (38%)
  local copies, waits for them, and re-layouts  7.29 us (6%)
  other arithmetic  4.47 us (4%)
  starting transfers between devices  2.1 us (2%)
    ppermute x3, waiting for transfers between devices, rotated(): lax.ppermute(block, axis, [(i, (i + distance) % count) for i in range(cou...  37.9 us
    ppermute x5, waiting for transfers between devices, swapped(): lax.ppermute(block, axis, [(i, i ^ distance) for i in range(lax.axis_size...  21.1 us
    pallas_call x2, Pallas kernels, within_block(): pl.pallas_call(within_kernel, grid_spec=pltpu.PrefetchScalarGridSpec(num_...  18.4 us
    pallas_call x2, Pallas kernels, key_states(): pl.pallas_call(state_kernel, grid_spec=pltpu.PrefetchScalarGridSpec(num_s...  11.1 us
    pallas_call x4, Pallas kernels, finish(): pl.pallas_call(finish_kernel, grid_spec=pltpu.PrefetchScalarGridSpec(num_...  8.49 us
    unnamed x44, local copies, waits for them, and re-layouts  7.16 us
    pallas_call x1, Pallas kernels, query_features(): pl.pallas_call(query_kernel, grid=(width // step,), in_specs=[block, pl.B...  4.79 us
  transfers between devices with their start and end apart: 8, of which 5 were waited for; matrix products, arithmetic and copies ran while one was open for 1% of the time, Pallas kernels for 30%

profile of v1, /device:TPU:0, one launch (start us, length us, event | category | flops | bytes accessed | tf_op | source)
XLA Modules:
  0.0 117.9 jit_solution(11166881761179041494)
XLA Ops:
  0.0 2.0 %pack_rims.1 = bf16[16,6144]{1,0:T(8,128)(2,1)} custom-call(bf16[256,6144]{1,0:T(8,128)(2,1)} %query_ref.7, bf16[256,6144]{1,0:T(8,128)(2,1)} %key_ref.5, bf16[256,6144]{1,0:T(8,128)(2,1)} %value_ref.5), custom_call_target="tpu_custom_call" | custom-call | tf_op jit(solution)/shard_map/pack_rims/pallas_call | solution.py:32
  2.0 0.5 collective-permute-start
  2.4 0.1 stack.23.places
  2.5 8.5 %collective-permute-done.rim_ref = bf16[16,6144]{1,0:T(8,128)(2,1)S(1)} collective-permute-done((bf16[16,6144]{1,0:T(8,128)(2,1)}, bf16[16,6144]{1,0:T(8,128)(2,1)S(1)}, u32[]{:S(2)}, u32[]{:S(2)}) %collective-permute-start) | collective-permute-done | bytes 196640 | tf_op jit(solution)/shard_map/ppermute | solution.py:285
  11.0 0.0 copy-start.2
  11.0 1.9 %copy-done.2 = bf16[256,6144]{1,0:T(8,128)(2,1)S(1)} copy-done((bf16[256,6144]{1,0:T(8,128)(2,1)S(1)}, bf16[256,6144]{1,0:T(8,128)(2,1)}, u32[]{:S(2)}) %copy-start.2) | copy-done | bytes 3145752
  12.9 5.5 %key_states.2 = (bf16[256,3072]{1,0:T(8,128)(2,1)S(1)}, bf16[256,3072]{1,0:T(8,128)(2,1)S(1)}, bf16[3072,128]{1,0:T(8,128)(2,1)S(1)}) custom-call(s32[5]{0:T(128)S(1)} %stack.23.places, bf16[256,6144]{1,0:T(8,128)(2,1)S(1)} %copy-done.1, bf16[256,6144]{1,0:T(8,128)(2,1)S(1)} %copy-done.2, bf16[16,6144]{1,0:T(8,128)(2,1)S(1)} %collective-permute-done.rim_ref, ...), custom_call_target="tpu_custom_call" | custom-call | flops 402653184 | bytes 6291456 | tf_op jit(solution)/shard_map/key_states/pallas_call | solution.py:121
  18.5 0.0 copy-start.6
  18.5 1.1 copy-done.6
  19.6 1.2 copy-done.8
  20.8 0.0 collective-permute-start.1
  20.8 5.5 %key_states.3 = (bf16[256,3072]{1,0:T(8,128)(2,1)S(1)}, bf16[256,3072]{1,0:T(8,128)(2,1)S(1)}, f32[3072,128]{1,0:T(8,128)S(1)}) custom-call(s32[5]{0:T(128)S(1)} %stack.23.places, bf16[256,6144]{1,0:T(8,128)(2,1)S(1)} %copy-done.1, bf16[256,6144]{1,0:T(8,128)(2,1)S(1)} %copy-done.2, bf16[16,6144]{1,0:T(8,128)(2,1)S(1)} %collective-permute-done.rim_ref, ...), custom_call_target="tpu_custom_call" | custom-call | flops 402653184 | bytes 6291456 | tf_op jit(solution)/shard_map/key_states/pallas_call | solution.py:121
  26.3 1.2 copy-done.12
  27.5 0.0 collective-permute-done.1
  27.5 0.1 convert_add_fusion.3
  27.6 1.1 copy-done.3
  28.7 0.4 copy-done.10
  29.1 0.3 copy-done.19
  29.4 0.1 collective-permute-start.2
  29.5 11.5 %collective-permute-done.2 = bf16[1536,128]{1,0:T(8,128)(2,1)S(1)} collective-permute-done((bf16[1536,128]{1,0:T(8,128)(2,1)S(1)}, bf16[1536,128]{1,0:T(8,128)(2,1)S(1)}, u32[]{:S(2)}, u32[]{:S(2)}) %collective-permute-start.2) | collective-permute-done | bytes 393248 | tf_op jit(solution)/shard_map/ppermute | solution.py:280
  41.0 0.1 fusion.5
  41.1 0.5 collective-permute-start.3
  41.5 12.3 %collective-permute-done.3 = bf16[1536,128]{1,0:T(8,128)(2,1)S(1)} collective-permute-done((bf16[1536,128]{1,0:T(8,128)(2,1)S(1)}, bf16[1536,128]{1,0:T(8,128)(2,1)S(1)}, u32[]{:S(2)}, u32[]{:S(2)}) %collective-permute-start.3) | collective-permute-done | bytes 393248 | tf_op jit(solution)/shard_map/ppermute | solution.py:285
  53.9 0.2 add_convert_fusion.2
  54.0 0.1 collective-permute-start.4
  54.1 17.1 %collective-permute-done.4 = bf16[1536,128]{1,0:T(8,128)(2,1)S(1)} collective-permute-done((bf16[1536,128]{1,0:T(8,128)(2,1)S(1)}, bf16[1536,128]{1,0:T(8,128)(2,1)S(1)}, u32[]{:S(2)}, u32[]{:S(2)}) %collective-permute-start.4) | collective-permute-done | bytes 393248 | tf_op jit(solution)/shard_map/ppermute | solution.py:285
  71.3 1.0 add_convert_fusion.1
  72.3 0.0 copy-done.17
  72.3 0.5 collective-permute-start.5
  72.8 1.3 %convert_element_type.37 = f32[3072,128]{1,0:T(8,128)S(1)} convert(bf16[3072,128]{1,0:T(8,128)(2,1)} %copy-done.19) | non-fusion elementwise | flops 393216 | bytes 2359296 | tf_op jit(solution)/shard_map/convert_element_type | solution.py:318
  74.1 9.5 %collective-permute-done.5 = bf16[1536,128]{1,0:T(8,128)(2,1)} collective-permute-done((bf16[1536,128]{1,0:T(8,128)(2,1)}, bf16[1536,128]{1,0:T(8,128)(2,1)}, u32[]{:S(2)}, u32[]{:S(2)}) %collective-permute-start.5) | collective-permute-done | bytes 393248 | tf_op jit(solution)/shard_map/ppermute | solution.py:280
  83.6 0.0 copy-done.21
  83.6 0.0 copy-start
  83.6 1.8 %add_convert_fusion = (bf16[1536,128]{1,0:T(8,128)(2,1)S(1)}, bf16[1536,128]{1,0:T(8,128)(2,1)S(1)}, bf16[1536,128]{1,0:T(8,128)(2,1)S(1)}, bf16[1536,128]{1,0:T(8,128)(2,1)S(1)}) fusion(f32[3072,128]{1,0:T(8,128)S(1)} %copy-done.4, pred[]{:T(512)S(6)} %eq.18, bf16[1536,128]{1,0:T(8,128)(2,1)} %copy-done.16, pred[]{:T(512)S(6)} %eq.20, ...), kind=kLoop, calls=%fused_computation.12 | loop fusion | flops 4128768 | bytes 6291461 | tf_op jit(solution)/shard_map/convert_element_type | solution.py:336
  85.4 0.1 collective-permute-start.7
  85.5 0.0 copy-start.7
  85.5 0.5 collective-permute-start.6
  86.0 0.0 copy-done
  86.0 4.8 %query_features.1.feat_ref = bf16[256,6144]{1,0:T(8,128)(2,1)S(1)} custom-call(bf16[256,6144]{1,0:T(8,128)(2,1)S(1)} %copy-done, bf16[3,4,6144]{2,1,0:T(4,128)(2,1)S(1)} %copy-done.5, bf16[128,128]{1,0:T(8,128)(2,1)S(1)} %copy-done.14), custom_call_target="tpu_custom_call" | custom-call | flops 402653184 | bytes 6291456 | tf_op jit(solution)/shard_map/query_features/pallas_call | solution.py:71
  90.9 9.2 %within_block.2 = (bf16[256,3072]{1,0:T(8,128)(2,1)S(1)}, f32[256,3072]{1,0:T(8,128)S(1)}) custom-call(s32[5]{0:T(128)S(1)} %stack.23.places, bf16[256,6144]{1,0:T(8,128)(2,1)S(1)} %copy-done, bf16[256,6144]{1,0:T(8,128)(2,1)S(1)} %query_features.1.feat_ref, bf16[16,6144]{1,0:T(8,128)(2,1)S(1)} %collective-permute-done.rim_ref, ...), custom_call_target="tpu_custom_call" | custom-call | flops 805306368 | bytes 9437184 | tf_op jit(solution)/shard_map/within_block/pallas_call | solution.py:195
  100.1 0.0 copy-start.15
  100.1 9.2 %within_block.3 = (bf16[256,3072]{1,0:T(8,128)(2,1)S(1)}, f32[256,3072]{1,0:T(8,128)S(1)}) custom-call(s32[5]{0:T(128)S(1)} %stack.23.places, bf16[256,6144]{1,0:T(8,128)(2,1)S(1)} %copy-done, bf16[256,6144]{1,0:T(8,128)(2,1)S(1)} %query_features.1.feat_ref, bf16[16,6144]{1,0:T(8,128)(2,1)S(1)} %collective-permute-done.rim_ref, ...), custom_call_target="tpu_custom_call" | custom-call | flops 805306368 | bytes 9437184 | tf_op jit(solution)/shard_map/within_block/pallas_call | solution.py:195
  109.4 2.1 %finish.4.rest_0_ = bf16[256,6144]{1,0:T(8,128)(2,1)} custom-call(s32[5]{0:T(128)S(1)} %stack.23.places, bf16[256,3072]{1,0:T(8,128)(2,1)S(1)} %get-tuple-element.23.feat_ref, f32[256,3072]{1,0:T(8,128)S(1)} %get-tuple-element.24.mixed_ref, bf16[1536,128]{1,0:T(8,128)(2,1)S(1)} %get-tuple-element.30.prefix_ref, f32[1,6144]{1,0:T(1,128)S(1)} %bitcast.6), custom_call_target="tpu_custom_call" | custom-call | flops 100663296 | bytes 3145728 | tf_op jit(solution)/shard_map/finish/pallas_call | solution.py:259
  111.5 0.0 collective-permute-done.7.prefix_ref
  111.5 2.1 %finish.5.rest_0_ = bf16[256,6144]{1,0:T(8,128)(2,1)} custom-call(s32[5]{0:T(128)S(1)} %stack.23.places, bf16[256,3072]{1,0:T(8,128)(2,1)S(1)} %get-tuple-element.17.feat_ref, f32[256,3072]{1,0:T(8,128)S(1)} %get-tuple-element.18.mixed_ref, bf16[1536,128]{1,0:T(8,128)(2,1)S(1)} %collective-permute-done.7.prefix_ref, ...), custom_call_target="tpu_custom_call", output_to_operand_aliasing={{}: (5, {})} | custom-call | flops 100663296 | bytes 3145728 | tf_op jit(solution)/shard_map/finish/pallas_call | solution.py:259
  113.6 2.1 %finish.6.rest_0_ = bf16[256,6144]{1,0:T(8,128)(2,1)} custom-call(s32[5]{0:T(128)S(1)} %stack.23.places, bf16[256,3072]{1,0:T(8,128)(2,1)S(1)} %get-tuple-element.23.feat_ref, f32[256,3072]{1,0:T(8,128)S(1)} %get-tuple-element.24.mixed_ref, bf16[1536,128]{1,0:T(8,128)(2,1)S(1)} %get-tuple-element.29.prefix_ref, ...), custom_call_target="tpu_custom_call", output_to_operand_aliasing={{}: (5, {})} | custom-call | flops 100663296 | bytes 3145728 | tf_op jit(solution)/shard_map/finish/pallas_call | solution.py:259
  115.8 0.0 collective-permute-done.6.prefix_ref
  115.8 2.1 %finish.7 = bf16[256,6144]{1,0:T(8,128)(2,1)} custom-call(s32[5]{0:T(128)S(1)} %stack.23.places, bf16[256,3072]{1,0:T(8,128)(2,1)S(1)} %get-tuple-element.17.feat_ref, f32[256,3072]{1,0:T(8,128)S(1)} %get-tuple-element.18.mixed_ref, bf16[1536,128]{1,0:T(8,128)(2,1)S(1)} %collective-permute-done.6.prefix_ref, ...), custom_call_target="tpu_custom_call", output_to_operand_aliasing={{}: (5, {})} | custom-call | flops 100663296 | bytes 3145728 | tf_op jit(solution)/shard_map/finish/pallas_call | solution.py:259
  (30 shorter events, 0.1 us)
Async XLA Ops:
  0.0 11.0 %copy-start.5 = (bf16[3,4,6144]{2,1,0:T(4,128)(2,1)S(1)}, bf16[3,4,6144]{2,1,0:T(4,128)(2,1)}, u32[]{:S(2)}) copy-start(bf16[3,4,6144]{2,1,0:T(4,128)(2,1)} %taps_ref.9) | copy-start | bytes 442372
  0.0 11.0 %copy-start.14 = (bf16[128,128]{1,0:T(8,128)(2,1)S(1)}, bf16[128,128]{1,0:T(8,128)(2,1)}, u32[]{:S(2)}) copy-start(bf16[128,128]{1,0:T(8,128)(2,1)} %map_ref.9) | copy-start | bytes 98308
  0.0 11.0 %copy-start.1 = (bf16[256,6144]{1,0:T(8,128)(2,1)S(1)}, bf16[256,6144]{1,0:T(8,128)(2,1)}, u32[]{:S(2)}) copy-start(bf16[256,6144]{1,0:T(8,128)(2,1)} %key_ref.5) | copy-start | bytes 9437188
  2.0 9.0 %collective-permute-start = (bf16[16,6144]{1,0:T(8,128)(2,1)}, bf16[16,6144]{1,0:T(8,128)(2,1)S(1)}, u32[]{:S(2)}, u32[]{:S(2)}) collective-permute-start(bf16[16,6144]{1,0:T(8,128)(2,1)} %pack_rims.1), channel_id=1, source_target_pairs={{0,1},{1,2},{2,3},{3,4},{4,5},{5,6},{6,7},{7,8},{8,9},{9,10},{10,1... | collective-permute-start | bytes 589832 | tf_op jit(solution)/shard_map/ppermute | solution.py:285
  11.0 1.9 %copy-start.2 = (bf16[256,6144]{1,0:T(8,128)(2,1)S(1)}, bf16[256,6144]{1,0:T(8,128)(2,1)}, u32[]{:S(2)}) copy-start(bf16[256,6144]{1,0:T(8,128)(2,1)} %value_ref.5) | copy-start | bytes 9437188
  18.5 1.1 copy-start.6
  19.6 1.2 copy-start.8
  20.8 6.7 %collective-permute-start.1 = (bf16[3072,128]{1,0:T(8,128)(2,1)S(1)}, bf16[3072,128]{1,0:T(8,128)(2,1)S(1)}, u32[]{:S(2)}, u32[]{:S(2)}) collective-permute-start(bf16[3072,128]{1,0:T(8,128)(2,1)S(1)} %get-tuple-element.20), channel_id=1, source_target_pairs={{0,1},{1,0},{2,3},{3,2},{4,5},{5,4},{6,7},{7,6},{8,9},{9,8},{10,11... | collective-permute-start | bytes 2359304 | tf_op jit(solution)/shard_map/ppermute | solution.py:280
  26.3 1.2 %copy-start.12 = (bf16[256,3072]{1,0:T(8,128)(2,1)}, bf16[256,3072]{1,0:T(8,128)(2,1)S(1)}, u32[]{:S(2)}) copy-start(bf16[256,3072]{1,0:T(8,128)(2,1)S(1)} %get-tuple-element.22.value_ref) | copy-start | bytes 4718596
  27.5 1.2 %copy-start.3 = (f32[3072,128]{1,0:T(8,128)}, f32[3072,128]{1,0:T(8,128)S(1)}, u32[]{:S(2)}) copy-start(f32[3072,128]{1,0:T(8,128)S(1)} %get-tuple-element.19) | copy-start | bytes 4718596
  27.5 1.6 %copy-start.10 = (bf16[256,3072]{1,0:T(8,128)(2,1)}, bf16[256,3072]{1,0:T(8,128)(2,1)S(1)}, u32[]{:S(2)}) copy-start(bf16[256,3072]{1,0:T(8,128)(2,1)S(1)} %get-tuple-element.21.key_ref) | copy-start | bytes 4718596
  27.5 1.9 %copy-start.19 = (bf16[3072,128]{1,0:T(8,128)(2,1)}, bf16[3072,128]{1,0:T(8,128)(2,1)S(1)}, u32[]{:S(2)}) copy-start(bf16[3072,128]{1,0:T(8,128)(2,1)S(1)} %collective-permute-done.1) | copy-start | bytes 2359300
  29.4 11.6 %collective-permute-start.2 = (bf16[1536,128]{1,0:T(8,128)(2,1)S(1)}, bf16[1536,128]{1,0:T(8,128)(2,1)S(1)}, u32[]{:S(2)}, u32[]{:S(2)}) collective-permute-start(bf16[1536,128]{1,0:T(8,128)(2,1)S(1)} %slice.47), channel_id=1, source_target_pairs={{0,2},{1,3},{2,0},{3,1},{4,6},{5,7},{6,4},{7,5},{8,10},{9,11},{10,... | collective-permute-start | bytes 1179656 | tf_op jit(solution)/shard_map/ppermute | solution.py:280
  41.0 13.0 %copy-start.16 = (bf16[1536,128]{1,0:T(8,128)(2,1)}, bf16[1536,128]{1,0:T(8,128)(2,1)S(1)}, u32[]{:S(2)}) copy-start(bf16[1536,128]{1,0:T(8,128)(2,1)S(1)} %collective-permute-done.2) | copy-start | bytes 1179652
  41.1 12.8 %collective-permute-start.3 = (bf16[1536,128]{1,0:T(8,128)(2,1)S(1)}, bf16[1536,128]{1,0:T(8,128)(2,1)S(1)}, u32[]{:S(2)}, u32[]{:S(2)}) collective-permute-start(bf16[1536,128]{1,0:T(8,128)(2,1)S(1)} %fusion.5), channel_id=1, source_target_pairs={{0,4},{1,5},{2,6},{3,7},{4,8},{5,9},{6,10},{7,11},{8,12},{9,13},{1... | collective-permute-start | bytes 1179656 | tf_op jit(solution)/shard_map/ppermute | solution.py:285
  53.9 18.4 %copy-start.17 = (bf16[1536,128]{1,0:T(8,128)(2,1)}, bf16[1536,128]{1,0:T(8,128)(2,1)S(1)}, u32[]{:S(2)}) copy-start(bf16[1536,128]{1,0:T(8,128)(2,1)S(1)} %collective-permute-done.3) | copy-start | bytes 1179652
  54.0 17.2 %collective-permute-start.4 = (bf16[1536,128]{1,0:T(8,128)(2,1)S(1)}, bf16[1536,128]{1,0:T(8,128)(2,1)S(1)}, u32[]{:S(2)}, u32[]{:S(2)}) collective-permute-start(bf16[1536,128]{1,0:T(8,128)(2,1)S(1)} %add_convert_fusion.2), channel_id=1, source_target_pairs={{0,8},{1,9},{2,10},{3,11},{4,12},{5,13},{6,14},{7,15},{8,0},{9,1},... | collective-permute-start | bytes 1179656 | tf_op jit(solution)/shard_map/ppermute | solution.py:285
  71.3 1.5 %copy-start.20 = (bf16[1536,128]{1,0:T(8,128)(2,1)}, bf16[1536,128]{1,0:T(8,128)(2,1)S(1)}, u32[]{:S(2)}) copy-start(bf16[1536,128]{1,0:T(8,128)(2,1)S(1)} %collective-permute-done.4) | copy-start | bytes 1179652
  72.3 11.4 %copy-start.4 = (f32[3072,128]{1,0:T(8,128)S(1)}, f32[3072,128]{1,0:T(8,128)}, u32[]{:S(2)}) copy-start(f32[3072,128]{1,0:T(8,128)} %copy-done.3) | copy-start | bytes 4718596
  72.3 11.4 %collective-permute-start.5 = (bf16[1536,128]{1,0:T(8,128)(2,1)}, bf16[1536,128]{1,0:T(8,128)(2,1)}, u32[]{:S(2)}, u32[]{:S(2)}) collective-permute-start(bf16[1536,128]{1,0:T(8,128)(2,1)} %add_convert_fusion.1), channel_id=1, source_target_pairs={{0,2},{1,3},{2,0},{3,1},{4,6},{5,7},{6,4},{7,5},{8,10},{9,11},{10,... | collective-permute-start | bytes 1179656 | tf_op jit(solution)/shard_map/ppermute | solution.py:280
  72.8 10.9 %copy-start.18 = (bf16[1536,128]{1,0:T(8,128)(2,1)S(1)}, bf16[1536,128]{1,0:T(8,128)(2,1)}, u32[]{:S(2)}) copy-start(bf16[1536,128]{1,0:T(8,128)(2,1)} %copy-done.17) | copy-start | bytes 1179652
  72.8 10.9 %copy-start.21 = (bf16[1536,128]{1,0:T(8,128)(2,1)S(1)}, bf16[1536,128]{1,0:T(8,128)(2,1)}, u32[]{:S(2)}) copy-start(bf16[1536,128]{1,0:T(8,128)(2,1)} %copy-done.20) | copy-start | bytes 1179652
  83.6 2.4 %copy-start = (bf16[256,6144]{1,0:T(8,128)(2,1)S(1)}, bf16[256,6144]{1,0:T(8,128)(2,1)}, u32[]{:S(2)}) copy-start(bf16[256,6144]{1,0:T(8,128)(2,1)} %query_ref.7) | copy-start | bytes 9437188
  85.4 26.1 %collective-permute-start.7 = (bf16[1536,128]{1,0:T(8,128)(2,1)S(1)}, bf16[1536,128]{1,0:T(8,128)(2,1)S(1)}, u32[]{:S(2)}, u32[]{:S(2)}) collective-permute-start(bf16[1536,128]{1,0:T(8,128)(2,1)S(1)} %get-tuple-element.27), channel_id=1, source_target_pairs={{0,1},{1,0},{2,3},{3,2},{4,5},{5,4},{6,7},{7,6},{8,9},{9,8},{10,11... | collective-permute-start | bytes 1179656 | tf_op jit(solution)/shard_map/ppermute | solution.py:280
  85.5 5.3 %copy-start.7 = (bf16[256,3072]{1,0:T(8,128)(2,1)S(1)}, bf16[256,3072]{1,0:T(8,128)(2,1)}, u32[]{:S(2)}) copy-start(bf16[256,3072]{1,0:T(8,128)(2,1)} %copy-done.6) | copy-start | bytes 4718596
  85.5 5.3 %copy-start.9 = (bf16[256,3072]{1,0:T(8,128)(2,1)S(1)}, bf16[256,3072]{1,0:T(8,128)(2,1)}, u32[]{:S(2)}) copy-start(bf16[256,3072]{1,0:T(8,128)(2,1)} %copy-done.8) | copy-start | bytes 4718596
  85.5 30.2 %collective-permute-start.6 = (bf16[1536,128]{1,0:T(8,128)(2,1)S(1)}, bf16[1536,128]{1,0:T(8,128)(2,1)S(1)}, u32[]{:S(2)}, u32[]{:S(2)}) collective-permute-start(bf16[1536,128]{1,0:T(8,128)(2,1)S(1)} %get-tuple-element.28), channel_id=1, source_target_pairs={{0,1},{1,0},{2,3},{3,2},{4,5},{5,4},{6,7},{7,6},{8,9},{9,8},{10,11... | collective-permute-start | bytes 1179656 | tf_op jit(solution)/shard_map/ppermute | solution.py:280
  90.8 9.2 %copy-start.11 = (bf16[256,3072]{1,0:T(8,128)(2,1)S(1)}, bf16[256,3072]{1,0:T(8,128)(2,1)}, u32[]{:S(2)}) copy-start(bf16[256,3072]{1,0:T(8,128)(2,1)} %copy-done.10) | copy-start | bytes 4718596
  90.9 9.2 %copy-start.13 = (bf16[256,3072]{1,0:T(8,128)(2,1)S(1)}, bf16[256,3072]{1,0:T(8,128)(2,1)}, u32[]{:S(2)}) copy-start(bf16[256,3072]{1,0:T(8,128)(2,1)} %copy-done.12) | copy-start | bytes 4718596
  100.1 9.3 %copy-start.15 = (f32[6144]{0:T(1024)S(1)}, f32[6144]{0:T(1024)}, u32[]{:S(2)}) copy-start(f32[6144]{0:T(1024)} %param.11) | copy-start | bytes 73732

commit v2 on v1

--- a/solution.py
+++ b/solution.py
@@ -11,7 +11,11 @@
 GROUPS = 1
 RIM = 16
 TILE = 8
-VMEM_BYTES = 40 * 1024 * 1024
+VMEM_BYTES = 16 * 1024 * 1024
+
+
+def in_hbm(array):
+    return pltpu.with_memory_space_constraint(array, pltpu.HBM)
 
 
 def pack_kernel(tap_count, query_ref, key_ref, value_ref, rim_ref):
@@ -36,7 +40,7 @@
         out_specs=pl.BlockSpec((RIM, width), lambda i: (0, 0)),
         out_shape=jax.ShapeDtypeStruct((RIM, width), jnp.bfloat16),
         name="pack_rims",
-    )(query_seq, key_seq, value_seq)
+    )(in_hbm(query_seq), in_hbm(key_seq), in_hbm(value_seq))
 
 
 def convolved(rows, taps, rim=None, rim_end=0):
@@ -51,16 +55,31 @@
     return total.astype(jnp.bfloat16)
 
 
+def convolved_by(scratch, rows, taps, rim=None, rim_end=0):
+    length = rows.shape[0]
+    if rim is None:
+        scratch[:TILE] = jnp.zeros((TILE, rows.shape[1]), jnp.float32)
+    else:
+        scratch[:TILE] = pltpu.roll(rim, (-rim_end) % TILE, 0)
+    scratch[TILE : TILE + length] = rows
+    total = taps[0:1] * rows
+    for offset in range(1, taps.shape[0]):
+        total = total + taps[offset : offset + 1] * scratch[TILE - offset : TILE - offset + length]
+    return total.astype(jnp.bfloat16)
+
+
 def features(conv_rows, feature_map):
     projected = jnp.dot(conv_rows, feature_map, preferred_element_type=jnp.float32)
     return jnp.where(projected > 0, projected + 1.0, jnp.exp(projected)).astype(jnp.bfloat16)
 
 
-def query_kernel(query_ref, taps_ref, map_ref, feat_ref):
+def query_kernel(query_ref, taps_ref, map_ref, feat_ref, scratch):
     head_dim = map_ref.shape[0]
     for start in range(0, query_ref.shape[1], head_dim):
         cols = slice(start, start + head_dim)
-        conv = convolved(query_ref[:, cols].astype(jnp.float32), taps_ref[0, :, cols].astype(jnp.float32))
+        conv = convolved_by(
+            scratch.at[start // head_dim], query_ref[:, cols].astype(jnp.float32), taps_ref[0, :, cols].astype(jnp.float32)
+        )
         feat_ref[:, cols] = features(conv, map_ref[...])
 
 
@@ -77,6 +96,7 @@
             pl.BlockSpec(feature_map.shape, lambda i: (0, 0)),
         ],
         out_specs=block,
+        scratch_shapes=[pltpu.VMEM((step // feature_map.shape[0], TILE + tok_count, feature_map.shape[0]), jnp.float32)],
         out_shape=jax.ShapeDtypeStruct(query_seq.shape, jnp.bfloat16),
         compiler_params=pltpu.CompilerParams(vmem_limit_bytes=VMEM_BYTES),
         cost_estimate=pl.CostEstimate(
@@ -85,10 +105,10 @@
             transcendentals=query_seq.size,
         ),
         name="query_features",
-    )(query_seq, conv_kernel, feature_map)
-
-
-def state_kernel(places, key_ref, value_ref, rim_ref, taps_ref, map_ref, feat_ref, conv_ref, state_ref):
+    )(in_hbm(query_seq), conv_kernel, feature_map)
+
+
+def state_kernel(places, key_ref, value_ref, rim_ref, taps_ref, map_ref, feat_ref, conv_ref, state_ref, scratch):
     head_dim = map_ref.shape[0]
     back = taps_ref.shape[1] - 1
     for head in range(key_ref.shape[1] // head_dim):
@@ -96,10 +116,10 @@
         rim = rim_ref[:, cols].astype(jnp.float32)[:TILE]
         rim = jnp.where(places[0] > 0, rim, 0.0)
         taps = taps_ref[:, :, cols].astype(jnp.float32)
-        key_conv = convolved(key_ref[:, cols].astype(jnp.float32), taps[1], rim, back)
+        key_conv = convolved_by(scratch.at[0, head], key_ref[:, cols].astype(jnp.float32), taps[1], rim, back)
         key_feat = features(key_conv, map_ref[...])
         feat_ref[:, cols] = key_feat
-        value_conv = convolved(value_ref[:, cols].astype(jnp.float32), taps[2], rim, 2 * back)
+        value_conv = convolved_by(scratch.at[1, head], value_ref[:, cols].astype(jnp.float32), taps[2], rim, 2 * back)
         conv_ref[:, cols] = value_conv
         state = lax.dot_general(
             key_feat, value_conv, (((0,), (0,)), ((), ())), preferred_element_type=jnp.float32
@@ -131,6 +151,7 @@
                 pl.BlockSpec(feature_map.shape, lambda i, places: (0, 0)),
             ],
             out_specs=[local, local, pl.BlockSpec((step, head_dim), lambda i, places: (i, 0))],
+            scratch_shapes=[pltpu.VMEM((2, step // head_dim, TILE + tok_count, head_dim), jnp.float32)],
         ),
         out_shape=[
             jax.ShapeDtypeStruct((tok_count, 2 * step), jnp.bfloat16),
@@ -144,7 +165,7 @@
             transcendentals=2 * tok_count * step,
         ),
         name="key_states",
-    )(places, key_seq, value_seq, rims, conv_kernel, feature_map)
+    )(places, in_hbm(key_seq), in_hbm(value_seq), rims, conv_kernel, feature_map)
 
 
 def within_kernel(
@@ -152,9 +173,8 @@
 ):
     head_dim = map_ref.shape[0]
     tok_count = feat_ref.shape[0]
-    half = tok_count // 2
-    causal = lax.broadcasted_iota(jnp.int32, (half, half), 0) >= lax.broadcasted_iota(
-        jnp.int32, (half, half), 1
+    causal = lax.broadcasted_iota(jnp.int32, (tok_count, tok_count), 0) >= lax.broadcasted_iota(
+        jnp.int32, (tok_count, tok_count), 1
     )
     for start in range(0, feat_ref.shape[1], head_dim):
         cols = slice(start, start + head_dim)
@@ -166,20 +186,11 @@
         first = features(first, map_ref[...])
         feat = jnp.concatenate([first, feat_ref[RIM:, cols]], axis=0)
         fixed_ref[:, cols] = feat
-        key, value = key_ref[:, cols], value_ref[:, cols]
-        for at in (0, half):
-            scores = lax.dot_general(
-                feat[at : at + half],
-                key[: at + half],
-                (((1,), (1,)), ((), ())),
-                preferred_element_type=jnp.float32,
-            )
-            masked = jnp.where(causal, scores[:, at:], 0.0).astype(jnp.bfloat16)
-            if at:
-                masked = jnp.concatenate([scores[:, :at].astype(jnp.bfloat16), masked], axis=1)
-            mixed_ref[at : at + half, cols] = jnp.dot(
-                masked, value[: at + half], preferred_element_type=jnp.float32
-            )
+        scores = lax.dot_general(
+            feat, key_ref[:, cols], (((1,), (1,)), ((), ())), preferred_element_type=jnp.float32
+        )
+        weights = jnp.where(causal, scores, 0.0).astype(jnp.bfloat16)
+        mixed_ref[:, cols] = jnp.dot(weights, value_ref[:, cols], preferred_element_type=jnp.float32)
 
 
 def within_block(places, query_seq, query_feat, rims, conv_kernel, feature_map, key_feat, value_conv, group, first):
@@ -219,7 +230,7 @@
             transcendentals=0,
         ),
         name="within_block",
-    )(places, query_seq, query_feat, rims, conv_kernel, feature_map, key_feat, value_conv)
+    )(places, in_hbm(query_seq), query_feat, rims, conv_kernel, feature_map, key_feat, value_conv)
 
 
 def finish_kernel(places, feat_ref, mixed_ref, prefix_ref, gain_ref, *rest):
@@ -276,13 +287,17 @@
     )(*operands)
 
 
-def swapped(block, axis, distance):
-    return lax.ppermute(block, axis, [(i, i ^ distance) for i in range(lax.axis_size(axis))])
-
-
-def rotated(block, axis, distance):
-    count = lax.axis_size(axis)
-    return lax.ppermute(block, axis, [(i, (i + distance) % count) for i in range(count)])
+def swapped(block, distance):
+    return lax.ppermute(block, "seq", [(i, i ^ distance) for i in range(lax.axis_size("seq"))])
+
+
+def rotated(block):
+    count = lax.axis_size("seq")
+    return lax.ppermute(block, "seq", [(i, (i + 1) % count) for i in range(count)])
+
+
+def tied(*arrays):
+    return lax.optimization_barrier(arrays)
 
 
 def on_device(query_seq, key_seq, value_seq, conv_kernel, feature_map, norm_gain):
@@ -290,10 +305,10 @@
     tap_count = conv_kernel.shape[1]
     head_dim = feature_map.shape[0]
     step = width // (4 * GROUPS)
-    assert tok_count == SPAN and step % head_dim == 0
     device_count = lax.axis_size("seq")
+    assert tok_count == SPAN and step % head_dim == 0 and device_count & (device_count - 1) == 0
     device = lax.axis_index("seq")
-    core, pair = device % 2, device // 2 % 2
+    core, pair = device & 1, (device >> 1) & 1
     places = jnp.stack(
         [
             device,
@@ -306,48 +321,65 @@
     gain = norm_gain.reshape(1, width)
     f32, bf16 = jnp.float32, jnp.bfloat16
 
-    rims = rotated(pack_rims(query_seq, key_seq, value_seq, tap_count), "seq", 1)
+    packed, query_seq = tied(pack_rims(query_seq, key_seq, value_seq, tap_count), query_seq)
+    rims = rotated(packed)
     query_feat = query_features(query_seq, conv_kernel, feature_map, step)
-
+    rims, query_feat = tied(rims, query_feat)
+
+    def within(key_feat, value_conv, first):
+        return within_block(
+            places, query_seq, query_feat, rims, conv_kernel, feature_map, key_feat, value_conv, 0, first
+        )
+
+    states = functools.partial(key_states, places, key_seq, value_seq, rims, conv_kernel, feature_map, 0)
+    key_a, value_a, state_a = states(0, bf16)
+    from_core = swapped(state_a, 1)
+    key_b, value_b, state_b = states(2, f32)
+    from_core, key_b, value_b, state_b = tied(from_core, key_b, value_b, state_b)
+    from_core = from_core.astype(f32)
+    chip = state_b + from_core
+    give, key_a, value_a = tied(chip[:step].astype(bf16), key_a, value_a)
+    from_pair = swapped(give, 2)
+    feat_a, mixed_a = within(key_a, value_a, 0)
+    from_pair, feat_a, mixed_a = tied(from_pair, feat_a, mixed_a)
+    from_pair = from_pair.astype(f32)
+    running = chip[step:] + from_pair
+    earlier = jnp.zeros_like(running)
+    distance = 4
+    while distance < device_count:
+        upper = (device & distance) != 0
+        give = running.astype(bf16)
+        if distance == 4:
+            give, key_b, value_b = tied(give, key_b, value_b)
+            arrived = swapped(give, distance)
+            feat_b, mixed_b = within(key_b, value_b, 2)
+            arrived, feat_b, mixed_b = tied(arrived, feat_b, mixed_b)
+        else:
+            half = step // 2
+            odd = (device & (distance // 2)) != 0
+            mine = swapped(jnp.where(odd, give[half:], give[:half]), distance)
+            other = swapped(mine, distance // 2)
+            arrived = jnp.concatenate([jnp.where(odd, other, mine), jnp.where(odd, mine, other)], axis=0)
+        arrived = arrived.astype(f32)
+        earlier = earlier + jnp.where(upper, arrived, 0.0)
+        running = running + arrived
+        distance *= 2
+    own = earlier + jnp.where(pair == 1, from_pair, 0.0)
+    others = earlier + jnp.where(pair == 0, chip[step:], 0.0)
+    back = swapped(others.astype(bf16), 2).astype(f32)
+    prefix_3 = (own + jnp.where(core == 1, from_core[step:], 0.0)).astype(bf16)
+    give_3 = (own + jnp.where(core == 0, state_b[step:], 0.0)).astype(bf16)
+    prefix_1 = swapped(give_3, 1)
     out = None
-    for group in range(GROUPS):
-        states = functools.partial(
-            key_states, places, key_seq, value_seq, rims, conv_kernel, feature_map, group
-        )
-        key_a, value_a, state_a = states(0, bf16)
-        from_core = swapped(state_a, "seq", 1).astype(f32)
-        key_b, value_b, state_b = states(2, f32)
-        chip = state_b + from_core
-        from_pair = swapped(chip[:step].astype(bf16), "seq", 2).astype(f32)
-        total = chip[step:] + from_pair
-        earlier = jnp.zeros_like(total)
-        running = total
-        distance = 4
-        while distance < device_count:
-            arrived = rotated(running.astype(bf16), "seq", distance).astype(f32)
-            arrived = jnp.where(device >= distance, arrived, 0.0)
-            earlier = earlier + arrived
-            running = running + arrived
-            distance *= 2
-        own = earlier + jnp.where(pair == 1, from_pair, 0.0)
-        others = earlier + jnp.where(pair == 0, chip[step:], 0.0)
-        back = swapped(others.astype(bf16), "seq", 2).astype(f32)
-        prefix_3 = (own + jnp.where(core == 1, from_core[step:], 0.0)).astype(bf16)
-        give_3 = (own + jnp.where(core == 0, state_b[step:], 0.0)).astype(bf16)
-        prefix_1 = swapped(give_3, "seq", 1)
-        prefix_2 = (back + jnp.where(core == 1, from_core[:step], 0.0)).astype(bf16)
-        give_2 = (back + jnp.where(core == 0, state_b[:step], 0.0)).astype(bf16)
-        prefix_0 = swapped(give_2, "seq", 1)
-        within = functools.partial(
-            within_block, places, query_seq, query_feat, rims, conv_kernel, feature_map
-        )
-        feat_a, mixed_a = within(key_a, value_a, group, 0)
-        feat_b, mixed_b = within(key_b, value_b, group, 2)
-        for position, prefix in ((3, prefix_3), (1, prefix_1), (2, prefix_2), (0, prefix_0)):
-            feat, mixed = (feat_a, mixed_a) if position < 2 else (feat_b, mixed_b)
-            first = 0 if position < 2 else 2
-            out = finish(places, feat, mixed, prefix, gain, out, group, first, position)
-    return out
+    out = finish(places, feat_b, mixed_b, prefix_3, gain, out, 0, 2, 3)
+    out = finish(places, feat_a, mixed_a, prefix_1, gain, out, 0, 0, 1)
+    back, out = tied(back, out)
+    prefix_2 = (back + jnp.where(core == 1, from_core[:step], 0.0)).astype(bf16)
+    give_2 = (back + jnp.where(core == 0, state_b[:step], 0.0)).astype(bf16)
+    prefix_0 = swapped(give_2, 1)
+    out = finish(places, feat_b, mixed_b, prefix_2, gain, out, 0, 2, 2)
+    prefix_0, out = tied(prefix_0, out)
+    return finish(places, feat_a, mixed_a, prefix_0, gain, out, 0, 0, 0)
 
 
 def solution(mesh):

time: 118 us -> 88.7 us (0.75)
  waiting for transfers between devices: 59 us -> 25.7 us
  local copies, waits for them, and re-layouts: 7.29 us -> 11.9 us
  Pallas kernels: 44.8 us -> 41.4 us
  starting transfers between devices: 2.1 us -> 4.83 us
    ppermute x8 -> x9, waiting for transfers between devices: 59 us -> 25.7 us  [the longest x8 22.3 us: swapped(): lax.ppermute(block, 'seq', [(i, i ^ distance) for i in range(lax.axis_siz...]
    unnamed x44 -> x50, local copies, waits for them, and re-layouts: 7.16 us -> 11.8 us
    pallas_call x2, Pallas kernels: 18.4 us -> 14.3 us  [within_block(): pl.pallas_call(within_kernel, grid_spec=pltpu.PrefetchScalarGridSpec(num_...]
    ppermute x8 -> x9, starting transfers between devices: 2.1 us -> 4.83 us  [the longest x8 4.38 us: swapped(): lax.ppermute(block, 'seq', [(i, i ^ distance) for i in range(lax.axis_siz...]
    convert_element_type x5 -> x6, other arithmetic: 4.34 us -> 4.05 us  [the longest x2 2.1 us: on_device(): give = running.astype(bf16)]
  transfers between devices with their start and end apart: 8 -> 9, of which waited for: 5 -> 5; matrix products, arithmetic and copies ran while one was open for 1% -> 0% of each run, Pallas kernels for 30% -> 33%
where the time goes in v2:
time: 88.7 us; the launch traced here: 88.3 us
  Pallas kernels  41.4 us (47%)
  waiting for transfers between devices  25.7 us (29%)
  local copies, waits for them, and re-layouts  11.9 us (13%)
  starting transfers between devices  4.83 us (5%)
  other arithmetic  4.24 us (5%)
    ppermute x8, waiting for transfers between devices, swapped(): lax.ppermute(block, 'seq', [(i, i ^ distance) for i in range(lax.axis_siz...  22.3 us
    pallas_call x2, Pallas kernels, within_block(): pl.pallas_call(within_kernel, grid_spec=pltpu.PrefetchScalarGridSpec(num_...  14.3 us
    unnamed x50, local copies, waits for them, and re-layouts  11.8 us
    pallas_call x2, Pallas kernels, key_states(): pl.pallas_call(state_kernel, grid_spec=pltpu.PrefetchScalarGridSpec(num_s...  11.6 us
    pallas_call x4, Pallas kernels, finish(): pl.pallas_call(finish_kernel, grid_spec=pltpu.PrefetchScalarGridSpec(num_...  8.5 us
    pallas_call x1, Pallas kernels, query_features(): pl.pallas_call(query_kernel, grid=(width // step,), in_specs=[block, pl.B...  5.04 us
    ppermute x8, starting transfers between devices, swapped(): lax.ppermute(block, 'seq', [(i, i ^ distance) for i in range(lax.axis_siz...  4.38 us
    ppermute x1, waiting for transfers between devices, rotated(): lax.ppermute(block, 'seq', [(i, (i + 1) % count) for i in range(count)])  3.42 us
  transfers between devices with their start and end apart: 9, of which 5 were waited for; matrix products, arithmetic and copies ran while one was open for 0% of the time, Pallas kernels for 33%

profile of v2, /device:TPU:0, one launch (start us, length us, event | category | flops | bytes accessed | tf_op | source)
XLA Modules:
  0.0 88.3 jit_solution(6255587103290930015)
XLA Ops:
  0.0 1.9 %pack_rims.1 = bf16[16,6144]{1,0:T(8,128)(2,1)} custom-call(bf16[256,6144]{1,0:T(8,128)(2,1)} %query_ref.4, bf16[256,6144]{1,0:T(8,128)(2,1)} %key_ref.5, bf16[256,6144]{1,0:T(8,128)(2,1)} %value_ref.5), custom_call_target="tpu_custom_call" | custom-call | tf_op jit(solution)/shard_map/pack_rims/pallas_call | solution.py:36
  1.9 0.5 collective-permute-start
  2.3 0.1 stack.23.places
  2.4 5.0 %query_features.1.feat_ref = bf16[256,6144]{1,0:T(8,128)(2,1)S(1)} custom-call(bf16[256,6144]{1,0:T(8,128)(2,1)} %query_ref.4, bf16[3,4,6144]{2,1,0:T(4,128)(2,1)S(1)} %copy-done.10, bf16[128,128]{1,0:T(8,128)(2,1)S(1)} %copy-done.15), custom_call_target="tpu_custom_call" | custom-call | flops 402653184 | bytes 6291456 | tf_op jit(solution)/shard_map/query_features/pallas_call | solution.py:90
  7.5 3.4 %collective-permute-done.rim_ref = bf16[16,6144]{1,0:T(8,128)(2,1)S(1)} collective-permute-done((bf16[16,6144]{1,0:T(8,128)(2,1)}, bf16[16,6144]{1,0:T(8,128)(2,1)S(1)}, u32[]{:S(2)}, u32[]{:S(2)}) %collective-permute-start) | collective-permute-done | bytes 196640 | tf_op jit(solution)/shard_map/ppermute | solution.py:296
  10.9 5.8 %key_states.2 = (bf16[256,3072]{1,0:T(8,128)(2,1)S(1)}, bf16[256,3072]{1,0:T(8,128)(2,1)S(1)}, bf16[3072,128]{1,0:T(8,128)(2,1)S(1)}) custom-call(s32[5]{0:T(128)S(1)} %stack.23.places, bf16[256,6144]{1,0:T(8,128)(2,1)} %key_ref.5, bf16[256,6144]{1,0:T(8,128)(2,1)} %value_ref.5, bf16[16,6144]{1,0:T(8,128)(2,1)S(1)} %collective-permute-done.rim_ref, ...), custom_call_target="tpu_custom_call" | custom-call | flops 402653184 | bytes 6291456 | tf_op jit(solution)/shard_map/key_states/pallas_call | solution.py:141
  16.7 0.1 collective-permute-start.1
  16.8 5.8 %key_states.3 = (bf16[256,3072]{1,0:T(8,128)(2,1)S(1)}, bf16[256,3072]{1,0:T(8,128)(2,1)S(1)}, f32[3072,128]{1,0:T(8,128)S(1)}) custom-call(s32[5]{0:T(128)S(1)} %stack.23.places, bf16[256,6144]{1,0:T(8,128)(2,1)} %key_ref.5, bf16[256,6144]{1,0:T(8,128)(2,1)} %value_ref.5, bf16[16,6144]{1,0:T(8,128)(2,1)S(1)} %collective-permute-done.rim_ref, ...), custom_call_target="tpu_custom_call" | custom-call | flops 402653184 | bytes 6291456 | tf_op jit(solution)/shard_map/key_states/pallas_call | solution.py:141
  22.6 0.0 copy-start.11
  22.6 1.1 %copy-done.11 = bf16[256,3072]{1,0:T(8,128)(2,1)} copy-done((bf16[256,3072]{1,0:T(8,128)(2,1)}, bf16[256,3072]{1,0:T(8,128)(2,1)S(1)}, u32[]{:S(2)}) %copy-start.11) | copy-done | bytes 1572888
  23.8 0.1 convert_add_fusion.2
  23.9 1.1 %copy-done.8 = f32[3072,128]{1,0:T(8,128)} copy-done((f32[3072,128]{1,0:T(8,128)}, f32[3072,128]{1,0:T(8,128)S(1)}, u32[]{:S(2)}) %copy-start.8) | copy-done | bytes 1572888
  25.0 0.5 copy-done.13
  25.4 0.3 copy-done.23
  25.7 0.8 collective-permute-start.2
  26.5 7.1 %within_block.2 = (bf16[256,3072]{1,0:T(8,128)(2,1)S(1)}, f32[256,3072]{1,0:T(8,128)S(1)}) custom-call(s32[5]{0:T(128)S(1)} %stack.23.places, bf16[256,6144]{1,0:T(8,128)(2,1)} %query_ref.4, bf16[256,6144]{1,0:T(8,128)(2,1)S(1)} %query_features.1.feat_ref, bf16[16,6144]{1,0:T(8,128)(2,1)S(1)} %collective-permute-done.rim_ref, ...), custom_call_target="tpu_custom_call" | custom-call | flops 805306368 | bytes 9437184 | tf_op jit(solution)/shard_map/within_block/pallas_call | solution.py:206
  33.6 1.6 %copy-done.2 = f32[256,3072]{1,0:T(8,128)} copy-done((f32[256,3072]{1,0:T(8,128)}, f32[256,3072]{1,0:T(8,128)S(1)}, u32[]{:S(2)}) %copy-start.2) | copy-done | bytes 3145752
  35.2 1.1 %copy-done.4 = bf16[256,3072]{1,0:T(8,128)(2,1)} copy-done((bf16[256,3072]{1,0:T(8,128)(2,1)}, bf16[256,3072]{1,0:T(8,128)(2,1)S(1)}, u32[]{:S(2)}) %copy-start.4) | copy-done | bytes 1572888
  36.4 0.9 %collective-permute-done.2 = bf16[1536,128]{1,0:T(8,128)(2,1)S(1)} collective-permute-done((bf16[1536,128]{1,0:T(8,128)(2,1)S(1)}, bf16[1536,128]{1,0:T(8,128)(2,1)S(1)}, u32[]{:S(2)}, u32[]{:S(2)}) %collective-permute-start.2) | collective-permute-done | bytes 393248 | tf_op jit(solution)/shard_map/ppermute | solution.py:291
  37.3 0.9 %fusion.7 = bf16[1536,128]{1,0:T(8,128)(2,1)} fusion(bf16[1536,128]{1,0:T(8,128)(2,1)S(1)} %collective-permute-done.2, f32[3072,128]{1,0:T(8,128)S(1)} %convert_add_fusion.2), kind=kLoop, calls=%fused_computation.17 | loop fusion | flops 589824 | bytes 1572864 | tf_op jit(solution)/shard_map/convert_element_type | solution.py:351
  38.2 0.6 collective-permute-start.3
  38.9 1.4 %copy-done.12 = bf16[256,3072]{1,0:T(8,128)(2,1)S(1)} copy-done((bf16[256,3072]{1,0:T(8,128)(2,1)S(1)}, bf16[256,3072]{1,0:T(8,128)(2,1)}, u32[]{:S(2)}) %copy-start.12) | copy-done | bytes 1572888
  40.3 1.4 %copy-done.14 = bf16[256,3072]{1,0:T(8,128)(2,1)S(1)} copy-done((bf16[256,3072]{1,0:T(8,128)(2,1)S(1)}, bf16[256,3072]{1,0:T(8,128)(2,1)}, u32[]{:S(2)}) %copy-start.14) | copy-done | bytes 1572888
  41.7 7.3 %within_block.3 = (bf16[256,3072]{1,0:T(8,128)(2,1)S(1)}, f32[256,3072]{1,0:T(8,128)S(1)}) custom-call(s32[5]{0:T(128)S(1)} %stack.23.places, bf16[256,6144]{1,0:T(8,128)(2,1)} %query_ref.4, bf16[256,6144]{1,0:T(8,128)(2,1)S(1)} %query_features.1.feat_ref, bf16[16,6144]{1,0:T(8,128)(2,1)S(1)} %collective-permute-done.rim_ref, ...), custom_call_target="tpu_custom_call" | custom-call | flops 805306368 | bytes 9437184 | tf_op jit(solution)/shard_map/within_block/pallas_call | solution.py:206
  49.0 0.0 copy-start
  49.0 1.7 %copy-done = f32[256,3072]{1,0:T(8,128)} copy-done((f32[256,3072]{1,0:T(8,128)}, f32[256,3072]{1,0:T(8,128)S(1)}, u32[]{:S(2)}) %copy-start) | copy-done | bytes 3145752
  50.6 1.2 %copy-done.6 = bf16[256,3072]{1,0:T(8,128)(2,1)} copy-done((bf16[256,3072]{1,0:T(8,128)(2,1)}, bf16[256,3072]{1,0:T(8,128)(2,1)S(1)}, u32[]{:S(2)}) %copy-start.6) | copy-done | bytes 1572888
  51.9 0.0 collective-permute-done.3
  51.9 1.2 %fusion.2 = bf16[1536,128]{1,0:T(8,128)(2,1)S(1)} fusion(bf16[1536,128]{1,0:T(8,128)(2,1)} %collective-permute-done.3, bf16[1536,128]{1,0:T(8,128)(2,1)S(1)} %copy-done.21, f32[3072,128]{1,0:T(8,128)S(1)} %copy-done.18), kind=kLoop, calls=%fused_computation.6 | loop fusion | flops 983040 | bytes 1966080 | tf_op jit(solution)/shard_map/convert_element_type | solution.py:351
  53.1 2.3 %collective-permute-start.4 = (bf16[768,128]{1,0:T(8,128)(2,1)S(1)}, bf16[768,128]{1,0:T(8,128)(2,1)S(1)}, u32[]{:S(2)}, u32[]{:S(2)}) collective-permute-start(bf16[768,128]{1,0:T(8,128)(2,1)S(1)} %slice_select_fusion.2), channel_id=1, source_target_pairs={{0,8},{1,9},{2,10},{3,11},{4,12},{5,13},{6,14},{7,15},{8,0},{9,1},... | collective-permute-start | bytes 589832 | tf_op jit(solution)/shard_map/ppermute | solution.py:291
  55.4 9.1 %collective-permute-done.4 = bf16[768,128]{1,0:T(8,128)(2,1)S(1)} collective-permute-done((bf16[768,128]{1,0:T(8,128)(2,1)S(1)}, bf16[768,128]{1,0:T(8,128)(2,1)S(1)}, u32[]{:S(2)}, u32[]{:S(2)}) %collective-permute-start.4) | collective-permute-done | bytes 196640 | tf_op jit(solution)/shard_map/ppermute | solution.py:291
  64.6 0.0 collective-permute-start.5
  64.6 0.1 convert_element_type.37
  64.7 5.8 %collective-permute-done.5 = bf16[768,128]{1,0:T(8,128)(2,1)S(1)} collective-permute-done((bf16[768,128]{1,0:T(8,128)(2,1)S(1)}, bf16[768,128]{1,0:T(8,128)(2,1)S(1)}, u32[]{:S(2)}, u32[]{:S(2)}) %collective-permute-start.5) | collective-permute-done | bytes 196640 | tf_op jit(solution)/shard_map/ppermute | solution.py:291
  70.6 0.0 copy-start.1
  70.6 1.6 %fusion.6 = (bf16[1536,128]{1,0:T(8,128)(2,1)S(1)}, bf16[1536,128]{1,0:T(8,128)(2,1)S(1)}, bf16[1536,128]{1,0:T(8,128)(2,1)S(1)}) fusion(f32[3072,128]{1,0:T(8,128)S(1)} %convert_element_type.37, pred[]{:T(512)S(6)} %eq.17, bf16[1536,128]{1,0:T(8,128)(2,1)S(1)} %copy-done.22, pred[]{:T(512)S(6)} %eq.15, pred[]{:T(512)S(6)} %ne.8, ...), kind=kLoop, calls=%fused_computation.12 | loop fusion | flops 3932160 | bytes 4718598 | tf_op jit(solution)/shard_map/convert_element_type | solution.py:370
  72.2 0.5 collective-permute-start.6
  72.7 0.3 copy-done.7
  73.1 2.1 %finish.4.rest_0_ = bf16[256,6144]{1,0:T(8,128)(2,1)} custom-call(s32[5]{0:T(128)S(1)} %stack.23.places, bf16[256,3072]{1,0:T(8,128)(2,1)S(1)} %copy-done.7, f32[256,3072]{1,0:T(8,128)S(1)} %copy-done.1, bf16[1536,128]{1,0:T(8,128)(2,1)S(1)} %get-tuple-element.73.prefix_ref, f32[1,6144]{1,0:T(1,128)S(1)} %bitcast.6), custom_call_target="tpu_custom_call" | custom-call | flops 100663296 | bytes 3145728 | tf_op jit(solution)/shard_map/finish/pallas_call | solution.py:270
  75.2 6.4 %collective-permute-done.6 = bf16[1536,128]{1,0:T(8,128)(2,1)S(1)} collective-permute-done((bf16[1536,128]{1,0:T(8,128)(2,1)S(1)}, bf16[1536,128]{1,0:T(8,128)(2,1)S(1)}, u32[]{:S(2)}, u32[]{:S(2)}) %collective-permute-start.6) | collective-permute-done | bytes 393248 | tf_op jit(solution)/shard_map/ppermute | solution.py:291
  81.6 0.1 convert_element_type.44
  81.6 0.0 collective-permute-done.7.prefix_ref
  81.7 2.2 %finish.5.rest_0_ = bf16[256,6144]{1,0:T(8,128)(2,1)} custom-call(s32[5]{0:T(128)S(1)} %stack.23.places, bf16[256,3072]{1,0:T(8,128)(2,1)S(1)} %copy-done.5, f32[256,3072]{1,0:T(8,128)S(1)} %copy-done.3, bf16[1536,128]{1,0:T(8,128)(2,1)S(1)} %collective-permute-done.7.prefix_ref, f32[1,6144]{1,0:T(1,128)S(1)} %bitcast.7, ...), custom_call_target="tpu_custom_call", output_to_operand_aliasing={{}: (5, {})} | custom-call | flops 100663296 | bytes 3145728 | tf_op jit(solution)/shard_map/finish/pallas_call | solution.py:270
  83.8 0.2 fusion.4
  84.0 0.1 collective-permute-start.8
  84.0 2.1 %finish.6.rest_0_ = bf16[256,6144]{1,0:T(8,128)(2,1)} custom-call(s32[5]{0:T(128)S(1)} %stack.23.places, bf16[256,3072]{1,0:T(8,128)(2,1)S(1)} %copy-done.7, f32[256,3072]{1,0:T(8,128)S(1)} %copy-done.1, bf16[1536,128]{1,0:T(8,128)(2,1)S(1)} %get-tuple-element.75.prefix_ref, f32[1,6144]{1,0:T(1,128)S(1)} %bitcast.8, ...), custom_call_target="tpu_custom_call", output_to_operand_aliasing={{}: (5, {})} | custom-call | flops 100663296 | bytes 3145728 | tf_op jit(solution)/shard_map/finish/pallas_call | solution.py:270
  86.2 0.0 collective-permute-done.8.prefix_ref
  86.2 2.1 %finish.7 = bf16[256,6144]{1,0:T(8,128)(2,1)} custom-call(s32[5]{0:T(128)S(1)} %stack.23.places, bf16[256,3072]{1,0:T(8,128)(2,1)S(1)} %copy-done.5, f32[256,3072]{1,0:T(8,128)S(1)} %copy-done.3, bf16[1536,128]{1,0:T(8,128)(2,1)S(1)} %collective-permute-done.8.prefix_ref, f32[1,6144]{1,0:T(1,128)S(1)} %bitcast.9, ...), custom_call_target="tpu_custom_call", output_to_operand_aliasing={{}: (5, {})} | custom-call | flops 100663296 | bytes 3145728 | tf_op jit(solution)/shard_map/finish/pallas_call | solution.py:270
  (41 shorter events, 0.2 us)
Async XLA Ops:
  0.0 2.4 %copy-start.15 = (bf16[128,128]{1,0:T(8,128)(2,1)S(1)}, bf16[128,128]{1,0:T(8,128)(2,1)}, u32[]{:S(2)}) copy-start(bf16[128,128]{1,0:T(8,128)(2,1)} %map_ref.9) | copy-start | bytes 98308
  0.0 2.4 %copy-start.10 = (bf16[3,4,6144]{2,1,0:T(4,128)(2,1)S(1)}, bf16[3,4,6144]{2,1,0:T(4,128)(2,1)}, u32[]{:S(2)}) copy-start(bf16[3,4,6144]{2,1,0:T(4,128)(2,1)} %taps_ref.9) | copy-start | bytes 442372
  1.9 9.0 %collective-permute-start = (bf16[16,6144]{1,0:T(8,128)(2,1)}, bf16[16,6144]{1,0:T(8,128)(2,1)S(1)}, u32[]{:S(2)}, u32[]{:S(2)}) collective-permute-start(bf16[16,6144]{1,0:T(8,128)(2,1)} %pack_rims.1), channel_id=1, source_target_pairs={{0,1},{1,2},{2,3},{3,4},{4,5},{5,6},{6,7},{7,8},{8,9},{9,10},{10,1... | collective-permute-start | bytes 589832 | tf_op jit(solution)/shard_map/ppermute | solution.py:296
  16.7 7.0 %collective-permute-start.1 = (bf16[3072,128]{1,0:T(8,128)(2,1)S(1)}, bf16[3072,128]{1,0:T(8,128)(2,1)S(1)}, u32[]{:S(2)}, u32[]{:S(2)}) collective-permute-start(bf16[3072,128]{1,0:T(8,128)(2,1)S(1)} %get-tuple-element.42), channel_id=1, source_target_pairs={{0,1},{1,0},{2,3},{3,2},{4,5},{5,4},{6,7},{7,6},{8,9},{9,8},{10,11... | collective-permute-start | bytes 2359304 | tf_op jit(solution)/shard_map/ppermute | solution.py:291
  22.6 1.1 %copy-start.11 = (bf16[256,3072]{1,0:T(8,128)(2,1)}, bf16[256,3072]{1,0:T(8,128)(2,1)S(1)}, u32[]{:S(2)}) copy-start(bf16[256,3072]{1,0:T(8,128)(2,1)S(1)} %get-tuple-element.62.key_ref) | copy-start | bytes 4718596
  23.7 1.2 %copy-start.8 = (f32[3072,128]{1,0:T(8,128)}, f32[3072,128]{1,0:T(8,128)S(1)}, u32[]{:S(2)}) copy-start(f32[3072,128]{1,0:T(8,128)S(1)} %get-tuple-element.46) | copy-start | bytes 4718596
  23.7 1.7 %copy-start.13 = (bf16[256,3072]{1,0:T(8,128)(2,1)}, bf16[256,3072]{1,0:T(8,128)(2,1)S(1)}, u32[]{:S(2)}) copy-start(bf16[256,3072]{1,0:T(8,128)(2,1)S(1)} %get-tuple-element.63.value_ref) | copy-start | bytes 4718596
  23.7 2.0 %copy-start.23 = (bf16[3072,128]{1,0:T(8,128)(2,1)}, bf16[3072,128]{1,0:T(8,128)(2,1)S(1)}, u32[]{:S(2)}) copy-start(bf16[3072,128]{1,0:T(8,128)(2,1)S(1)} %collective-permute-done.1) | copy-start | bytes 2359300
  25.7 11.6 %copy-start.17 = (f32[3072,128]{1,0:T(8,128)}, f32[3072,128]{1,0:T(8,128)S(1)}, u32[]{:S(2)}) copy-start(f32[3072,128]{1,0:T(8,128)S(1)} %convert_add_fusion.2) | copy-start | bytes 4718596
  25.7 11.6 %collective-permute-start.2 = (bf16[1536,128]{1,0:T(8,128)(2,1)S(1)}, bf16[1536,128]{1,0:T(8,128)(2,1)S(1)}, u32[]{:S(2)}, u32[]{:S(2)}) collective-permute-start(bf16[1536,128]{1,0:T(8,128)(2,1)S(1)} %slice.61), channel_id=1, source_target_pairs={{0,2},{1,3},{2,0},{3,1},{4,6},{5,7},{6,4},{7,5},{8,10},{9,11},{10,... | collective-permute-start | bytes 1179656 | tf_op jit(solution)/shard_map/ppermute | solution.py:291
  33.6 1.6 %copy-start.2 = (f32[256,3072]{1,0:T(8,128)}, f32[256,3072]{1,0:T(8,128)S(1)}, u32[]{:S(2)}) copy-start(f32[256,3072]{1,0:T(8,128)S(1)} %get-tuple-element.57.mixed_ref) | copy-start | bytes 9437188
  35.2 1.1 %copy-start.4 = (bf16[256,3072]{1,0:T(8,128)(2,1)}, bf16[256,3072]{1,0:T(8,128)(2,1)S(1)}, u32[]{:S(2)}) copy-start(bf16[256,3072]{1,0:T(8,128)(2,1)S(1)} %get-tuple-element.56.feat_ref) | copy-start | bytes 4718596
  37.3 0.9 %copy-start.20 = (bf16[1536,128]{1,0:T(8,128)(2,1)}, bf16[1536,128]{1,0:T(8,128)(2,1)S(1)}, u32[]{:S(2)}) copy-start(bf16[1536,128]{1,0:T(8,128)(2,1)S(1)} %collective-permute-done.2) | copy-start | bytes 1179652
  38.2 13.6 %collective-permute-start.3 = (bf16[1536,128]{1,0:T(8,128)(2,1)}, bf16[1536,128]{1,0:T(8,128)(2,1)}, u32[]{:S(2)}, u32[]{:S(2)}) collective-permute-start(bf16[1536,128]{1,0:T(8,128)(2,1)} %fusion.7), channel_id=1, source_target_pairs={{0,4},{1,5},{2,6},{3,7},{4,0},{5,1},{6,2},{7,3},{8,12},{9,13},{10,... | collective-permute-start | bytes 1179656 | tf_op jit(solution)/shard_map/ppermute | solution.py:291
  38.9 1.4 %copy-start.12 = (bf16[256,3072]{1,0:T(8,128)(2,1)S(1)}, bf16[256,3072]{1,0:T(8,128)(2,1)}, u32[]{:S(2)}) copy-start(bf16[256,3072]{1,0:T(8,128)(2,1)} %copy-done.11) | copy-start | bytes 4718596
  40.3 1.4 %copy-start.14 = (bf16[256,3072]{1,0:T(8,128)(2,1)S(1)}, bf16[256,3072]{1,0:T(8,128)(2,1)}, u32[]{:S(2)}) copy-start(bf16[256,3072]{1,0:T(8,128)(2,1)} %copy-done.13) | copy-start | bytes 4718596
  41.7 10.2 %copy-start.18 = (f32[3072,128]{1,0:T(8,128)S(1)}, f32[3072,128]{1,0:T(8,128)}, u32[]{:S(2)}) copy-start(f32[3072,128]{1,0:T(8,128)} %copy-done.17) | copy-start | bytes 4718596
  41.7 10.2 %copy-start.21 = (bf16[1536,128]{1,0:T(8,128)(2,1)S(1)}, bf16[1536,128]{1,0:T(8,128)(2,1)}, u32[]{:S(2)}) copy-start(bf16[1536,128]{1,0:T(8,128)(2,1)} %copy-done.20) | copy-start | bytes 1179652
  49.0 1.7 %copy-start = (f32[256,3072]{1,0:T(8,128)}, f32[256,3072]{1,0:T(8,128)S(1)}, u32[]{:S(2)}) copy-start(f32[256,3072]{1,0:T(8,128)S(1)} %get-tuple-element.68.mixed_ref) | copy-start | bytes 9437188
  50.6 1.2 %copy-start.6 = (bf16[256,3072]{1,0:T(8,128)(2,1)}, bf16[256,3072]{1,0:T(8,128)(2,1)S(1)}, u32[]{:S(2)}) copy-start(bf16[256,3072]{1,0:T(8,128)(2,1)S(1)} %get-tuple-element.67.feat_ref) | copy-start | bytes 4718596
  51.9 12.7 %copy-start.24 = (bf16[3072,128]{1,0:T(8,128)(2,1)S(1)}, bf16[3072,128]{1,0:T(8,128)(2,1)}, u32[]{:S(2)}) copy-start(bf16[3072,128]{1,0:T(8,128)(2,1)} %copy-done.23) | copy-start | bytes 2359300
  53.1 17.5 %copy-start.19 = (f32[3072,128]{1,0:T(8,128)S(1)}, f32[3072,128]{1,0:T(8,128)}, u32[]{:S(2)}) copy-start(f32[3072,128]{1,0:T(8,128)} %copy-done.17) | copy-start | bytes 4718596
  53.1 11.4 %collective-permute-start.4 = (bf16[768,128]{1,0:T(8,128)(2,1)S(1)}, bf16[768,128]{1,0:T(8,128)(2,1)S(1)}, u32[]{:S(2)}, u32[]{:S(2)}) collective-permute-start(bf16[768,128]{1,0:T(8,128)(2,1)S(1)} %slice_select_fusion.2), channel_id=1, source_target_pairs={{0,8},{1,9},{2,10},{3,11},{4,12},{5,13},{6,14},{7,15},{8,0},{9,1},... | collective-permute-start | bytes 589832 | tf_op jit(solution)/shard_map/ppermute | solution.py:291
  64.6 6.0 %collective-permute-start.5 = (bf16[768,128]{1,0:T(8,128)(2,1)S(1)}, bf16[768,128]{1,0:T(8,128)(2,1)S(1)}, u32[]{:S(2)}, u32[]{:S(2)}) collective-permute-start(bf16[768,128]{1,0:T(8,128)(2,1)S(1)} %collective-permute-done.4), channel_id=1, source_target_pairs={{0,4},{1,5},{2,6},{3,7},{4,0},{5,1},{6,2},{7,3},{8,12},{9,13},{10,... | collective-permute-start | bytes 589832 | tf_op jit(solution)/shard_map/ppermute | solution.py:291
  64.6 6.0 %copy-start.9 = (f32[3072,128]{1,0:T(8,128)S(1)}, f32[3072,128]{1,0:T(8,128)}, u32[]{:S(2)}) copy-start(f32[3072,128]{1,0:T(8,128)} %copy-done.8) | copy-start | bytes 4718596
  64.6 6.0 %copy-start.22 = (bf16[1536,128]{1,0:T(8,128)(2,1)S(1)}, bf16[1536,128]{1,0:T(8,128)(2,1)}, u32[]{:S(2)}) copy-start(bf16[1536,128]{1,0:T(8,128)(2,1)} %copy-done.20) | copy-start | bytes 1179652
  70.5 2.2 %copy-start.16 = (f32[6144]{0:T(1024)S(1)}, f32[6144]{0:T(1024)}, u32[]{:S(2)}) copy-start(f32[6144]{0:T(1024)} %param.11) | copy-start | bytes 73732
  70.6 2.1 %copy-start.1 = (f32[256,3072]{1,0:T(8,128)S(1)}, f32[256,3072]{1,0:T(8,128)}, u32[]{:S(2)}) copy-start(f32[256,3072]{1,0:T(8,128)} %copy-done) | copy-start | bytes 9437188
  70.6 2.5 %copy-start.7 = (bf16[256,3072]{1,0:T(8,128)(2,1)S(1)}, bf16[256,3072]{1,0:T(8,128)(2,1)}, u32[]{:S(2)}) copy-start(bf16[256,3072]{1,0:T(8,128)(2,1)} %copy-done.6) | copy-start | bytes 4718596
  72.2 9.3 %collective-permute-start.6 = (bf16[1536,128]{1,0:T(8,128)(2,1)S(1)}, bf16[1536,128]{1,0:T(8,128)(2,1)S(1)}, u32[]{:S(2)}, u32[]{:S(2)}) collective-permute-start(bf16[1536,128]{1,0:T(8,128)(2,1)S(1)} %get-tuple-element.77), channel_id=1, source_target_pairs={{0,2},{1,3},{2,0},{3,1},{4,6},{5,7},{6,4},{7,5},{8,10},{9,11},{10,... | collective-permute-start | bytes 1179656 | tf_op jit(solution)/shard_map/ppermute | solution.py:291
  72.7 8.9 %collective-permute-start.7 = (bf16[1536,128]{1,0:T(8,128)(2,1)S(1)}, bf16[1536,128]{1,0:T(8,128)(2,1)S(1)}, u32[]{:S(2)}, u32[]{:S(2)}) collective-permute-start(bf16[1536,128]{1,0:T(8,128)(2,1)S(1)} %get-tuple-element.74), channel_id=1, source_target_pairs={{0,1},{1,0},{2,3},{3,2},{4,5},{5,4},{6,7},{7,6},{8,9},{9,8},{10,11... | collective-permute-start | bytes 1179656 | tf_op jit(solution)/shard_map/ppermute | solution.py:291
  73.1 8.6 %copy-start.3 = (f32[256,3072]{1,0:T(8,128)S(1)}, f32[256,3072]{1,0:T(8,128)}, u32[]{:S(2)}) copy-start(f32[256,3072]{1,0:T(8,128)} %copy-done.2) | copy-start | bytes 9437188
  73.1 8.6 %copy-start.5 = (bf16[256,3072]{1,0:T(8,128)(2,1)S(1)}, bf16[256,3072]{1,0:T(8,128)(2,1)}, u32[]{:S(2)}) copy-start(bf16[256,3072]{1,0:T(8,128)(2,1)} %copy-done.4) | copy-start | bytes 4718596
  84.0 2.2 %collective-permute-start.8 = (bf16[1536,128]{1,0:T(8,128)(2,1)S(1)}, bf16[1536,128]{1,0:T(8,128)(2,1)S(1)}, u32[]{:S(2)}, u32[]{:S(2)}) collective-permute-start(bf16[1536,128]{1,0:T(8,128)(2,1)S(1)} %get-tuple-element.76), channel_id=1, source_target_pairs={{0,1},{1,0},{2,3},{3,2},{4,5},{5,4},{6,7},{7,6},{8,9},{9,8},{10,11... | collective-permute-start | bytes 1179656 | tf_op jit(solution)/shard_map/ppermute | solution.py:291

commit v3 on v0

v3 whole, which is shorter than its diff:
```python
import functools

import jax
import jax.numpy as jnp
from jax import lax
from jax.experimental import pallas as pl
from jax.experimental.pallas import tpu as pltpu
from jax.sharding import PartitionSpec as P

SPAN = 256
GROUPS = 2
BLOCK_HEADS = 6
RIM = 16
TILE = 8
VMEM_BYTES = 16 * 1024 * 1024
f32, bf16 = jnp.float32, jnp.bfloat16
IN_VMEM = pl.BlockSpec(memory_space=pltpu.VMEM)
IN_PLACE = pl.BlockSpec(memory_space=pl.ANY)
LIGHT = pl.CostEstimate(flops=1024, bytes_accessed=1024, transcendentals=0)


def in_hbm(array):
    return pltpu.with_memory_space_constraint(array, pltpu.HBM)


def kernel_call(body, name, in_specs, out_specs, out_shape, scratch=(), aliases=None):
    return pl.pallas_call(
        body,
        in_specs=in_specs,
        out_specs=out_specs,
        out_shape=out_shape,
        scratch_shapes=list(scratch),
        input_output_aliases=aliases or {},
        compiler_params=pltpu.CompilerParams(vmem_limit_bytes=VMEM_BYTES),
        cost_estimate=LIGHT,
        name=name,
    )


def shape(dims, kind):
    return jax.ShapeDtypeStruct(dims, kind)


def quarter_start(quarter, width):
    device = lax.axis_index("seq")
    core = (device & 1) ^ int(quarter < 2)
    pair = ((device >> 1) & 1) ^ int(quarter % 2 == 0)
    return (2 * core + pair) * (width // 4)


def columns(start, size):
    return pl.ds(pl.multiple_of(start, 128), size)


def block_heads(heads):
    return max(n for n in range(1, BLOCK_HEADS + 1) if heads % n == 0)


def pack_kernel(tap_count, query_ref, key_ref, value_ref, rim_ref, tails, sems):
    taps = tap_count - 1
    rows = pl.ds(query_ref.shape[0] - RIM, RIM)
    copies = [
        pltpu.make_async_copy(ref.at[rows], tails.at[i], sems.at[i])
        for i, ref in enumerate((key_ref, value_ref, query_ref))
    ]
    for copy in copies:
        copy.start()
    for copy in copies:
        copy.wait()
    key_tail, value_tail, query_tail = (tails[i].astype(f32)[-TILE:] for i in range(3))
    row = lax.broadcasted_iota(jnp.int32, key_tail.shape, 0)
    first = jnp.where(row < taps, pltpu.roll(key_tail, taps, 0), pltpu.roll(value_tail, 2 * taps, 0))
    rim_ref[...] = jnp.concatenate([first, query_tail], axis=0).astype(bf16)


def pack_rims(query_seq, key_seq, value_seq, tap_count):
    width = query_seq.shape[1]
    return kernel_call(
        functools.partial(pack_kernel, tap_count),
        "pack_rims",
        [IN_PLACE] * 3,
        IN_VMEM,
        shape((RIM, width), bf16),
        [pltpu.VMEM((3, RIM, width), bf16), pltpu.SemaphoreType.DMA((3,))],
    )(in_hbm(query_seq), in_hbm(key_seq), in_hbm(value_seq))


def convolved(scratch, rows, taps, rim=None, rim_end=0):
    length = rows.shape[0]
    if rim is None:
        scratch[:TILE] = jnp.zeros((TILE, rows.shape[1]), f32)
    else:
        scratch[:TILE] = pltpu.roll(rim, (-rim_end) % TILE, 0)
    scratch[TILE : TILE + length] = rows
    total = taps[0:1] * rows
    for offset in range(1, taps.shape[0]):
        total = total + taps[offset : offset + 1] * scratch[TILE - offset : TILE - offset + length]
    return total.astype(bf16)


def features(conv_rows, feature_map):
    projected = jnp.dot(conv_rows, feature_map, preferred_element_type=f32)
    return jnp.where(projected > 0, projected + 1.0, jnp.exp(projected)).astype(bf16)


def state_of(key_feat, value_conv):
    return lax.dot_general(
        key_feat, value_conv, (((0,), (0,)), ((), ())), preferred_element_type=f32
    )


def rim_rows(rim_ref, cols, start):
    rim = rim_ref[:, cols].astype(f32)[start : start + TILE]
    return jnp.where(lax.axis_index("seq") > 0, rim, 0.0)


def head_states(key, value, taps_ref, map_ref, rim_ref, natural, local, feat_ref, conv_ref, state_ref, scratch):
    head_dim = map_ref.shape[0]
    back = taps_ref.shape[1] - 1
    rim = None if rim_ref is None else rim_rows(rim_ref, natural, 0)
    key_conv = convolved(scratch.at[0], key.astype(f32), taps_ref[1, :, natural].astype(f32), rim, back)
    key_feat = features(key_conv, map_ref[...])
    feat_ref[:, local] = key_feat
    value_conv = convolved(scratch.at[1], value.astype(f32), taps_ref[2, :, natural].astype(f32), rim, 2 * back)
    conv_ref[:, local] = value_conv
    if rim is None:
        row = lax.broadcasted_iota(jnp.int32, (RIM, head_dim), 0)
        later = jnp.where(row < back, 0.0, key_feat[:RIM].astype(f32)).astype(bf16)
        key_feat = jnp.concatenate([later, key_feat[RIM:]], axis=0)
    state_ref[local] = state_of(key_feat, value_conv).astype(state_ref.dtype)


def near_states_kernel(
    key_ref, value_ref, taps_ref, map_ref,
    feat_ref, conv_ref, state_ref, key_first, value_first, key_other, value_other, key_rows, value_rows, scratch, sems,
):
    head_dim = map_ref.shape[0]
    width = key_ref.shape[1]
    quarter = width // 4
    heads = quarter // head_dim
    size = block_heads(heads) * head_dim
    count = quarter // size

    def copies(i, quarter_of, key_to, value_to):
        cols = columns(quarter_start(quarter_of + i // count, width) + i % count * size, size)
        local = pl.ds(i * size, size)
        slot = 2 * (quarter_of // 2)
        return (
            pltpu.make_async_copy(key_ref.at[:, cols], key_to.at[:, local], sems.at[slot, i]),
            pltpu.make_async_copy(value_ref.at[:, cols], value_to.at[:, local], sems.at[slot + 1, i]),
        )

    near = [copies(i, 2, key_rows, value_rows) for i in range(2 * count)]
    other = [copies(i, 0, key_other, value_other) for i in range(2 * count)]
    for pair in near + other:
        for copy in pair:
            copy.start()
    for i in range(2 * count):
        for copy in near[i]:
            copy.wait()
        natural = quarter_start(2 + i // count, width) + i % count * size
        for head in range(size // head_dim):
            start = i * size + head * head_dim
            local = slice(start, start + head_dim)
            head_states(
                key_rows[:, local], value_rows[:, local], taps_ref, map_ref, None,
                columns(natural + head * head_dim, head_dim), local,
                feat_ref, conv_ref, state_ref, scratch.at[head],
            )
    key_first[...] = key_rows[:RIM]
    value_first[...] = value_rows[:RIM]
    for pair in other:
        for copy in pair:
            copy.wait()


def near_states(key_seq, value_seq, conv_kernel, feature_map):
    tok_count, width = key_seq.shape
    head_dim = feature_map.shape[0]
    half = width // 2
    size = block_heads(half // 2 // head_dim)
    count = half // (size * head_dim)
    rows = shape((tok_count, half), bf16)
    return kernel_call(
        near_states_kernel,
        "near_states",
        [IN_PLACE, IN_PLACE, IN_VMEM, IN_VMEM],
        [IN_VMEM] * 7,
        [rows, rows, shape((half, head_dim), f32), shape((RIM, half), bf16), shape((RIM, half), bf16), rows, rows],
        [
            pltpu.VMEM((tok_count, half), bf16),
            pltpu.VMEM((tok_count, half), bf16),
            pltpu.VMEM((size, 2, TILE + tok_count, head_dim), f32),
            pltpu.SemaphoreType.DMA((4, count)),
        ],
    )(in_hbm(key_seq), in_hbm(value_seq), conv_kernel, feature_map)


def other_states_kernel(key_ref, value_ref, taps_ref, map_ref, rim_ref, feat_ref, conv_ref, state_ref, scratch):
    head_dim = map_ref.shape[0]
    half = key_ref.shape[1]
    for head in range(half // head_dim):
        local = slice(head * head_dim, (head + 1) * head_dim)
        natural = quarter_start(local.start // (half // 2), 2 * half) + local.start % (half // 2)
        head_states(
            key_ref[:, local], value_ref[:, local], taps_ref, map_ref, rim_ref,
            columns(natural, head_dim), local, feat_ref, conv_ref, state_ref, scratch.at[head % scratch.shape[0]],
        )


def other_states(key_rows, value_rows, conv_kernel, feature_map, rims):
    tok_count, half = key_rows.shape
    head_dim = feature_map.shape[0]
    rows = shape((tok_count, half), bf16)
    return kernel_call(
        other_states_kernel,
        "other_states",
        [IN_VMEM] * 5,
        [IN_VMEM] * 3,
        [rows, rows, shape((half, head_dim), bf16)],
        [pltpu.VMEM((BLOCK_HEADS, 2, TILE + tok_count, head_dim), f32)],
    )(key_rows, value_rows, conv_kernel, feature_map, rims)


def first_rows_kernel(
    key_ref, value_ref, taps_ref, map_ref, rim_ref, state_ref, feat_ref, conv_ref, sum_ref, scratch
):
    head_dim = map_ref.shape[0]
    half = key_ref.shape[1]
    back = taps_ref.shape[1] - 1
    row = lax.broadcasted_iota(jnp.int32, (RIM, head_dim), 0)
    size = block_heads(half // 2 // head_dim) * head_dim
    for start in range(0, half, size):
        local = slice(start, start + size)
        natural = columns(quarter_start(2 + start // (half // 2), 2 * half) + start % (half // 2), size)
        rim = rim_rows(rim_ref, natural, 0)
        conv = convolved(scratch.at[0], key_ref[:, local].astype(f32), taps_ref[1, :, natural].astype(f32), rim, back)
        value_conv = convolved(
            scratch.at[1], value_ref[:, local].astype(f32), taps_ref[2, :, natural].astype(f32), rim, 2 * back
        )
        conv_ref[:, local] = value_conv
        parts = [slice(at, at + head_dim) for at in range(0, size, head_dim)]
        feats = [features(conv[:, part], map_ref[...]) for part in parts]
        feat_ref[:, local] = jnp.concatenate(feats, axis=1)
        firsts = [jnp.where(row < back, feat.astype(f32), 0.0).astype(bf16) for feat in feats]
        for part, first in zip(parts, firsts):
            at = slice(start + part.start, start + part.stop)
            sum_ref[at] = state_ref[at] + state_of(first, value_conv[:, part])


def first_rows(key_first, value_first, conv_kernel, feature_map, rims, state):
    half = key_first.shape[1]
    head_dim = feature_map.shape[0]
    size = block_heads(half // 2 // head_dim) * head_dim
    rows = shape((RIM, half), bf16)
    return kernel_call(
        first_rows_kernel,
        "first_rows",
        [IN_VMEM] * 6,
        [IN_VMEM] * 3,
        [rows, rows, shape(state.shape, f32)],
        [pltpu.VMEM((2, TILE + RIM, size), f32)],
    )(key_first, value_first, conv_kernel, feature_map, rims, state)


def within_kernel(quarter, query_ref, taps_ref, map_ref, rim_ref, key_ref, value_ref, *rest):
    (*firsts, feat_ref, mixed_ref, scratch) = rest
    head_dim = map_ref.shape[0]
    tok_count, width = query_ref.shape
    causal = lax.broadcasted_iota(jnp.int32, (tok_count, tok_count), 0) >= lax.broadcasted_iota(
        jnp.int32, (tok_count, tok_count), 1
    )
    for head in range(width // 4 // head_dim):
        natural = columns(quarter_start(quarter, width) + head * head_dim, head_dim)
        local = slice(head * head_dim, (head + 1) * head_dim)
        at = quarter % 2 * (width // 4) + head * head_dim
        at = slice(at, at + head_dim)
        key, value = key_ref[:, at], value_ref[:, at]
        if firsts:
            key = jnp.concatenate([firsts[0][:, at], key[RIM:]], axis=0)
            value = jnp.concatenate([firsts[1][:, at], value[RIM:]], axis=0)
        rim = rim_rows(rim_ref, natural, TILE)
        taps = taps_ref[0, :, natural].astype(f32)
        conv = convolved(scratch.at[head % scratch.shape[0]], query_ref[:, natural].astype(f32), taps, rim, TILE)
        feat = features(conv, map_ref[...])
        feat_ref[:, local] = feat
        scores = lax.dot_general(feat, key, (((1,), (1,)), ((), ())), preferred_element_type=f32)
        weights = jnp.where(causal, scores, 0.0).astype(bf16)
        mixed_ref[:, local] = jnp.dot(weights, value, preferred_element_type=f32)


def within_block(quarter, query_seq, conv_kernel, feature_map, rims, key_feat, value_conv, firsts):
    tok_count, width = query_seq.shape
    head_dim = feature_map.shape[0]
    operands = (query_seq, conv_kernel, feature_map, rims, key_feat, value_conv, *firsts)
    return kernel_call(
        functools.partial(within_kernel, quarter),
        "within_block",
        [IN_VMEM] * len(operands),
        [IN_VMEM] * 2,
        [shape((tok_count, width // 4), bf16), shape((tok_count, width // 4), f32)],
        [pltpu.VMEM((BLOCK_HEADS, TILE + tok_count, head_dim), f32)],
    )(*operands)


def finish_kernel(pieces, gain_ref, *rest):
    count = len(pieces)
    feats, mixes, prefixes = rest[:count], rest[count : 2 * count], rest[2 * count : 3 * count]
    out_ref, rows, sems = rest[-3:]
    head_dim = prefixes[0].shape[1]
    width = out_ref.shape[1]
    copies = []
    for i, (quarter, group) in enumerate(pieces):
        size = prefixes[i].shape[0]
        natural = quarter_start(quarter, width) + group * size
        for start in range(0, size, head_dim):
            cols = slice(group * size + start, group * size + start + head_dim)
            mixed = mixes[i][:, cols] + jnp.dot(
                feats[i][:, cols], prefixes[i][start : start + head_dim], preferred_element_type=f32
            )
            inverse_rms = lax.rsqrt(jnp.mean(mixed * mixed, axis=-1, keepdims=True) + 1e-06)
            gain = gain_ref[:, columns(natural + start, head_dim)]
            rows[i, :, start : start + head_dim] = (mixed * inverse_rms * gain).astype(bf16)
        copies.append(pltpu.make_async_copy(rows.at[i], out_ref.at[:, columns(natural, size)], sems.at[i]))
        copies[-1].start()
    for copy in copies:
        copy.wait()


def finish(pieces, mixed, prefixes, norm_gain, before):
    width = norm_gain.shape[1]
    count = len(pieces)
    tok_count = mixed[pieces[0][0]][0].shape[0]
    operands = [norm_gain, *(mixed[q][0] for q, _ in pieces), *(mixed[q][1] for q, _ in pieces), *prefixes]
    in_specs = [IN_VMEM] * len(operands)
    aliases = {}
    if before is not None:
        aliases = {len(operands): 0}
        operands.append(in_hbm(before))
        in_specs.append(IN_PLACE)
    return kernel_call(
        functools.partial(finish_kernel, pieces),
        "finish",
        in_specs,
        IN_PLACE,
        pltpu.HBM((tok_count, width), bf16),
        [pltpu.VMEM((count, tok_count, prefixes[0].shape[0]), bf16), pltpu.SemaphoreType.DMA((count,))],
        aliases,
    )(*operands)


def swapped(block, distance):
    return lax.ppermute(block, "seq", [(i, i ^ distance) for i in range(lax.axis_size("seq"))])


def rotated(block):
    count = lax.axis_size("seq")
    return lax.ppermute(block, "seq", [(i, (i + 1) % count) for i in range(count)])


def tied(*arrays):
    return lax.optimization_barrier(arrays)


def mapped(name, function, outputs, *arrays):
    def body(*refs):
        values = [ref[...] for ref in refs[: len(arrays)]]
        for ref, value in zip(refs[len(arrays) :], function(lax.axis_index("seq"), *values)):
            ref[...] = value.astype(ref.dtype)

    columns = arrays[0].shape[1]
    return kernel_call(
        body,
        name,
        [IN_VMEM] * len(arrays),
        [IN_VMEM] * len(outputs),
        [shape((rows, columns), kind) for rows, kind in outputs],
    )(*arrays)


def on_device(query_seq, key_seq, value_seq, conv_kernel, feature_map, norm_gain):
    tok_count, width = query_seq.shape
    tap_count = conv_kernel.shape[1]
    head_dim = feature_map.shape[0]
    device_count = lax.axis_size("seq")
    assert tok_count == SPAN and width % (4 * GROUPS * head_dim) == 0
    assert device_count >= 4 and device_count & (device_count - 1) == 0
    groups = range(GROUPS)
    rows = width // (4 * GROUPS)
    gain = norm_gain.reshape(1, width)

    def of_core(device):
        return (device & 1) != 0

    def of_pair(device):
        return (device & 2) != 0

    packed, key_seq, value_seq = tied(
        pack_rims(query_seq, key_seq, value_seq, tap_count), key_seq, value_seq
    )
    rims = rotated(packed)
    near = near_states(key_seq, value_seq, conv_kernel, feature_map)
    rims, *near = tied(rims, *near)
    feat_b, conv_b, state_b, key_first, value_first, key_other, value_other = near
    feat_a, conv_a, state_a = other_states(key_other, value_other, conv_kernel, feature_map, rims)
    state_a, key_first = tied(state_a, key_first)
    from_core = swapped(state_a, 1)
    feat_first, conv_first, state_b = first_rows(
        key_first, value_first, conv_kernel, feature_map, rims, state_b
    )
    from_core, state_b = tied(from_core, state_b)

    mixed = {}
    fill = [2, 3, 0, 1]
    turn = [rims]

    def beside(*gives):
        if fill:
            q = fill.pop(0)
            *gives, turn[0] = tied(*gives, turn[0])
            operands = (feat_b, conv_b, (feat_first, conv_first)) if q >= 2 else (feat_a, conv_a, ())
            mixed[q] = within_block(q, query_seq, conv_kernel, feature_map, turn[0], *operands)
        return gives

    def after(arrived):
        names = list(mixed)
        arrived, turn[0], *done = tied(arrived, turn[0], *(mixed[q][0] for q in names))
        for q, feat in zip(names, done):
            mixed[q] = (feat, mixed[q][1])
        return arrived

    def chip_sums(device, state, arrived):
        for g in groups:
            here = slice(g * rows, (g + 1) * rows)
            yield state[here] + arrived[here].astype(f32)
        for g in groups:
            here = slice((GROUPS + g) * rows, (GROUPS + g + 1) * rows)
            yield state[here] + arrived[here].astype(f32)

    sums = mapped(
        "chip_sums", chip_sums, [(rows, bf16)] * GROUPS + [(rows, f32)] * GROUPS, state_b, from_core
    )
    gives, chip = beside(*sums[:GROUPS]), sums[GROUPS:]
    arriving = [swapped(give, 2) for give in gives]
    running, earlier, from_pair = [None] * GROUPS, [None] * GROUPS, [None] * GROUPS

    def pair_sums(device, own, arrived):
        total = own + arrived.astype(f32)
        return total, total

    def plane_sums(distance, device, total, before, *arrived):
        upper = (device & distance) != 0
        if len(arrived) == 2:
            odd = (device & (distance // 2)) != 0
            mine, other = arrived
            arrived = (jnp.concatenate([jnp.where(odd, other, mine), jnp.where(odd, mine, other)], axis=0),)
        arrived = arrived[0].astype(f32)
        before = before + jnp.where(upper, arrived, 0.0)
        total = total + arrived
        give = total.astype(bf16)
        return total, before, jnp.where(upper, give[rows // 2 :], give[: rows // 2])

    distance = 4
    for g in groups:
        from_pair[g] = after(arriving[g])
        running[g], give = mapped("pair_sums", pair_sums, [(rows, f32), (rows, bf16)], chip[g], from_pair[g])
        earlier[g] = jnp.zeros((rows, head_dim), f32)
        if distance < device_count:
            (give,) = beside(give)
            arriving[g] = (swapped(give, distance),)
    while distance < device_count:
        for g in groups:
            arrived = [after(part) for part in arriving[g]]
            running[g], earlier[g], give = mapped(
                "plane_sums",
                functools.partial(plane_sums, distance),
                [(rows, f32), (rows, f32), (rows // 2, bf16)],
                running[g],
                earlier[g],
                *arrived,
            )
            if 2 * distance < device_count:
                (give,) = beside(give)
                arriving[g] = swapped(give, 2 * distance)
        if 2 * distance < device_count:
            mine = [after(arriving[g]) for g in groups]
            arriving = [(half, swapped(half, distance)) for half in mine]
        distance *= 2
    while fill:
        beside()

    def own_prefixes(g, device, before, own, paired, cored, state):
        own_part = before + jnp.where(of_pair(device), paired.astype(f32), 0.0)
        others = before + jnp.where(of_pair(device), 0.0, own)
        here = slice((GROUPS + g) * rows, (GROUPS + g + 1) * rows)
        return (
            others,
            own_part + jnp.where(of_core(device), cored[here].astype(f32), 0.0),
            own_part + jnp.where(of_core(device), 0.0, state[here]),
        )

    def paired_prefixes(g, device, arrived, cored, state):
        arrived = arrived.astype(f32)
        here = slice(g * rows, (g + 1) * rows)
        return (
            arrived + jnp.where(of_core(device), cored[here].astype(f32), 0.0),
            arrived + jnp.where(of_core(device), 0.0, state[here]),
        )

    back, prefix_own, prefix_core = [], [], []
    for g in groups:
        others, own, cored = mapped(
            "own_prefixes",
            functools.partial(own_prefixes, g),
            [(rows, bf16)] * 3,
            earlier[g],
            chip[g],
            from_pair[g],
            from_core,
            state_b,
        )
        back.append(others)
        prefix_own.append(own)
        prefix_core.append(cored)
    *back, gain = tied(*back, gain)
    back = [swapped(give, 2) for give in back]
    prefix_core = [swapped(give, 1) for give in prefix_core]
    pieces = [(q, g) for g in groups for q in (3, 1)]
    prefixes = [(prefix_own if q == 3 else prefix_core)[g] for q, g in pieces]
    out = finish(pieces, mixed, prefixes, gain, None)
    for g in groups:
        arrived, out = tied(back[g], out)
        prefix_2, prefix_0 = mapped(
            "paired_prefixes",
            functools.partial(paired_prefixes, g),
            [(rows, bf16)] * 2,
            arrived,
            from_core,
            state_b,
        )
        prefix_0, prefix_2 = tied(prefix_0, prefix_2)
        prefix_0 = swapped(prefix_0, 1)
        out = finish([(2, g)], mixed, [prefix_2], gain, out)
        prefix_0, out = tied(prefix_0, out)
        out = finish([(0, g)], mixed, [prefix_0], gain, out)
    return out


def solution(mesh):
    return jax.shard_map(
        on_device,
        mesh=mesh,
        in_specs=(
            P(("groups", "seq"), None),
            P(("groups", "seq"), None),
            P(("groups", "seq"), None),
            P(),
            P(),
            P(),
        ),
        out_specs=P(("groups", "seq"), None),
        check_vma=False,
    )
```

time: 214 us -> 67.1 us (0.31)
  the two profiles are of different devices: /device:TPU:16 before, /device:TPU:0 now
where the time goes in v3:
time: 67.1 us; the launch traced here: 67 us
  Pallas kernels  31.3 us (47%)
  waiting for transfers between devices  21.9 us (33%)
  starting transfers between devices  13.4 us (20%)
    ppermute x15, waiting for transfers between devices, swapped(): lax.ppermute(block, 'seq', [(i, i ^ distance) for i in range(lax.axis_siz...  18.7 us
    ppermute x15, starting transfers between devices, swapped(): lax.ppermute(block, 'seq', [(i, i ^ distance) for i in range(lax.axis_siz...  12.9 us
    pallas_call x4, Pallas kernels, within_block(): kernel_call(functools.partial(within_kernel, quarter), 'within_block', [I...  10.9 us
    pallas_call x5, Pallas kernels, finish(): kernel_call(functools.partial(finish_kernel, pieces), 'finish', in_specs,...  6.67 us
    pallas_call x1, Pallas kernels, near_states(): kernel_call(near_states_kernel, 'near_states', [IN_PLACE, IN_PLACE, IN_VM...  5.16 us
    pallas_call x1, Pallas kernels, other_states(): kernel_call(other_states_kernel, 'other_states', [IN_VMEM] * 5, [IN_VMEM]...  3.55 us
    ppermute x1, waiting for transfers between devices, rotated(): lax.ppermute(block, 'seq', [(i, (i + 1) % count) for i in range(count)])  3.18 us
    pallas_call x11, Pallas kernels, mapped(): kernel_call(body, name, [IN_VMEM] * len(arrays), [IN_VMEM] * len(outputs)...  2.68 us
  transfers between devices with their start and end apart: 16, of which 9 were waited for; matrix products, arithmetic and copies ran while one was open for 0% of the time, Pallas kernels for 36%

profile of v3, /device:TPU:0, one launch (start us, length us, event | category | flops | bytes accessed | tf_op | source)
XLA Modules:
  0.0 67.0 jit_solution(9327304838940749296)
XLA Ops:
  0.0 1.2 %pack_rims.1 = bf16[16,6144]{1,0:T(8,128)(2,1)S(1)} custom-call(bf16[256,6144]{1,0:T(8,128)(2,1)} %query_ref.9, bf16[256,6144]{1,0:T(8,128)(2,1)} %key_ref.2, bf16[256,6144]{1,0:T(8,128)(2,1)} %value_ref.2), custom_call_target="tpu_custom_call" | custom-call | flops 1024 | bytes 1024 | tf_op jit(solution)/shard_map/pack_rims/pallas_call | solution.py:78
  1.2 0.5 collective-permute-start
  1.7 5.2 %near_states.1 = (bf16[256,3072]{1,0:T(8,128)(2,1)S(1)}, bf16[256,3072]{1,0:T(8,128)(2,1)S(1)}, f32[3072,128]{1,0:T(8,128)S(1)}, bf16[16,3072]{1,0:T(8,128)(2,1)...) custom-call(bf16[256,6144]{1,0:T(8,128)(2,1)} %key_ref.2, ...), custom_call_target="tpu_custom_call" | custom-call | flops 1024 | bytes 1024 | tf_op jit(solution)/shard_map/near_states/pallas_call | solution.py:184
  6.9 3.2 %collective-permute-done.rim_ref = bf16[16,6144]{1,0:T(8,128)(2,1)S(1)} collective-permute-done((bf16[16,6144]{1,0:T(8,128)(2,1)S(1)}, bf16[16,6144]{1,0:T(8,128)(2,1)S(1)}, u32[]{:S(2)}, u32[]{:S(2)}) %collective-permute-start) | collective-permute-done | bytes 196640 | tf_op jit(solution)/shard_map/ppermute | solution.py:358
  10.1 3.6 %other_states.1 = (bf16[256,3072]{1,0:T(8,128)(2,1)S(1)}, bf16[256,3072]{1,0:T(8,128)(2,1)S(1)}, bf16[3072,128]{1,0:T(8,128)(2,1)S(1)}) custom-call(bf16[256,3072]{1,0:T(8,128)(2,1)S(1)} %get-tuple-element.148.key_ref, bf16[256,3072]{1,0:T(8,128)(2,1)S(1)} %get-tuple-element.149.value_ref, bf16[3,4,6144]{2,1,0:T(4,128)(2,1)S(1)} %copy-done.1, ...), custom_call_target="tpu_custom_call" | custom-call | flops 1024 | bytes 1024 | tf_op jit(solution)/shard_map/other_states/pallas_call | solution.py:215
  13.6 0.1 collective-permute-start.1
  13.7 1.1 %first_rows.1 = (bf16[16,3072]{1,0:T(8,128)(2,1)S(1)}, bf16[16,3072]{1,0:T(8,128)(2,1)S(1)}, f32[3072,128]{1,0:T(8,128)S(1)}) custom-call(bf16[16,3072]{1,0:T(8,128)(2,1)S(1)} %get-tuple-element.154.key_ref, bf16[16,3072]{1,0:T(8,128)(2,1)S(1)} %get-tuple-element.155.value_ref, bf16[3,4,6144]{2,1,0:T(4,128)(2,1)S(1)} %copy-done.1, ...), custom_call_target="tpu_custom_call" | custom-call | flops 1024 | bytes 1024 | tf_op jit(solution)/shard_map/first_rows/pallas_call | solution.py:256
  14.9 1.1 %collective-permute-done.1.refs_1_.refs_3_ = bf16[3072,128]{1,0:T(8,128)(2,1)S(1)} collective-permute-done((bf16[3072,128]{1,0:T(8,128)(2,1)S(1)}, bf16[3072,128]{1,0:T(8,128)(2,1)S(1)}, u32[]{:S(2)}, u32[]{:S(2)}) %collective-permute-start.1) | collective-permute-done | bytes 786464 | tf_op jit(solution)/shard_map/ppermute | solution.py:353
  16.0 0.1 chip_sums.1
  16.1 0.7 %collective-permute-start.2 = (bf16[768,128]{1,0:T(8,128)(2,1)S(1)}, bf16[768,128]{1,0:T(8,128)(2,1)S(1)}, u32[]{:S(2)}, u32[]{:S(2)}) collective-permute-start(bf16[768,128]{1,0:T(8,128)(2,1)S(1)} %get-tuple-element.163), channel_id=1, source_target_pairs={{0,2},{1,3},{2,0},{3,1},{4,6},{5,7},{6,4},{7,5},{8,10},{9,11},{10,... | collective-permute-start | bytes 589832 | tf_op jit(solution)/shard_map/ppermute | solution.py:353
  16.8 1.4 %collective-permute-start.4 = (bf16[768,128]{1,0:T(8,128)(2,1)S(1)}, bf16[768,128]{1,0:T(8,128)(2,1)S(1)}, u32[]{:S(2)}, u32[]{:S(2)}) collective-permute-start(bf16[768,128]{1,0:T(8,128)(2,1)S(1)} %get-tuple-element.176), channel_id=1, source_target_pairs={{0,2},{1,3},{2,0},{3,1},{4,6},{5,7},{6,4},{7,5},{8,10},{9,11},{10,... | collective-permute-start | bytes 589832 | tf_op jit(solution)/shard_map/ppermute | solution.py:353
  18.2 2.7 %within_block.4 = (bf16[256,1536]{1,0:T(8,128)(2,1)S(1)}, f32[256,1536]{1,0:T(8,128)S(1)}) custom-call(bf16[256,6144]{1,0:T(8,128)(2,1)S(1)} %copy-done, bf16[3,4,6144]{2,1,0:T(4,128)(2,1)S(1)} %copy-done.1, bf16[128,128]{1,0:T(8,128)(2,1)S(1)} %copy-done.2, bf16[16,6144]{1,0:T(8,128)(2,1)S(1)} %collective-permute-done.rim_ref, ...), custom_call_target="tpu_custom_call" | custom-call | flops 1024 | bytes 1024 | tf_op jit(solution)/shard_map/within_block/pallas_call | solution.py:296
  20.9 3.0 %collective-permute-done.2.refs_1_.refs_2_ = bf16[768,128]{1,0:T(8,128)(2,1)S(1)} collective-permute-done((bf16[768,128]{1,0:T(8,128)(2,1)S(1)}, bf16[768,128]{1,0:T(8,128)(2,1)S(1)}, u32[]{:S(2)}, u32[]{:S(2)}) %collective-permute-start.2) | collective-permute-done | bytes 196640 | tf_op jit(solution)/shard_map/ppermute | solution.py:353
  24.0 0.7 %collective-permute-start.3 = (bf16[768,128]{1,0:T(8,128)(2,1)S(1)}, bf16[768,128]{1,0:T(8,128)(2,1)S(1)}, u32[]{:S(2)}, u32[]{:S(2)}) collective-permute-start(bf16[768,128]{1,0:T(8,128)(2,1)S(1)} %get-tuple-element.174), channel_id=1, source_target_pairs={{0,4},{1,5},{2,6},{3,7},{4,0},{5,1},{6,2},{7,3},{8,12},{9,13},{10,... | collective-permute-start | bytes 589832 | tf_op jit(solution)/shard_map/ppermute | solution.py:353
  24.7 2.8 %within_block.5 = (bf16[256,1536]{1,0:T(8,128)(2,1)S(1)}, f32[256,1536]{1,0:T(8,128)S(1)}) custom-call(bf16[256,6144]{1,0:T(8,128)(2,1)S(1)} %copy-done, bf16[3,4,6144]{2,1,0:T(4,128)(2,1)S(1)} %copy-done.1, bf16[128,128]{1,0:T(8,128)(2,1)S(1)} %copy-done.2, bf16[16,6144]{1,0:T(8,128)(2,1)S(1)} %collective-permute-done.rim_ref, ...), custom_call_target="tpu_custom_call" | custom-call | flops 1024 | bytes 1024 | tf_op jit(solution)/shard_map/within_block/pallas_call | solution.py:296
  27.6 0.1 pair_sums.3
  27.6 1.4 %collective-permute-start.6 = (bf16[768,128]{1,0:T(8,128)(2,1)S(1)}, bf16[768,128]{1,0:T(8,128)(2,1)S(1)}, u32[]{:S(2)}, u32[]{:S(2)}) collective-permute-start(bf16[768,128]{1,0:T(8,128)(2,1)S(1)} %get-tuple-element.195), channel_id=1, source_target_pairs={{0,4},{1,5},{2,6},{3,7},{4,0},{5,1},{6,2},{7,3},{8,12},{9,13},{10,... | collective-permute-start | bytes 589832 | tf_op jit(solution)/shard_map/ppermute | solution.py:353
  29.1 2.7 %within_block.6 = (bf16[256,1536]{1,0:T(8,128)(2,1)S(1)}, f32[256,1536]{1,0:T(8,128)S(1)}) custom-call(bf16[256,6144]{1,0:T(8,128)(2,1)S(1)} %copy-done, bf16[3,4,6144]{2,1,0:T(4,128)(2,1)S(1)} %copy-done.1, bf16[128,128]{1,0:T(8,128)(2,1)S(1)} %copy-done.2, bf16[16,6144]{1,0:T(8,128)(2,1)S(1)} %collective-permute-done.rim_ref, ...), custom_call_target="tpu_custom_call" | custom-call | flops 1024 | bytes 1024 | tf_op jit(solution)/shard_map/within_block/pallas_call | solution.py:296
  31.8 0.1 plane_sums.4
  31.9 2.0 %collective-permute-start.5 = (bf16[384,128]{1,0:T(8,128)(2,1)S(1)}, bf16[384,128]{1,0:T(8,128)(2,1)S(1)}, u32[]{:S(2)}, u32[]{:S(2)}) collective-permute-start(bf16[384,128]{1,0:T(8,128)(2,1)S(1)} %get-tuple-element.194), channel_id=1, source_target_pairs={{0,8},{1,9},{2,10},{3,11},{4,12},{5,13},{6,14},{7,15},{8,0},{9,1},... | collective-permute-start | bytes 294920 | tf_op jit(solution)/shard_map/ppermute | solution.py:353
  33.9 2.7 %within_block.7 = (bf16[256,1536]{1,0:T(8,128)(2,1)S(1)}, f32[256,1536]{1,0:T(8,128)S(1)}) custom-call(bf16[256,6144]{1,0:T(8,128)(2,1)S(1)} %copy-done, bf16[3,4,6144]{2,1,0:T(4,128)(2,1)S(1)} %copy-done.1, bf16[128,128]{1,0:T(8,128)(2,1)S(1)} %copy-done.2, bf16[16,6144]{1,0:T(8,128)(2,1)S(1)} %collective-permute-done.rim_ref, ...), custom_call_target="tpu_custom_call" | custom-call | flops 1024 | bytes 1024 | tf_op jit(solution)/shard_map/within_block/pallas_call | solution.py:296
  36.6 0.1 plane_sums.5
  36.7 1.1 %collective-permute-start.7 = (bf16[384,128]{1,0:T(8,128)(2,1)S(1)}, bf16[384,128]{1,0:T(8,128)(2,1)S(1)}, u32[]{:S(2)}, u32[]{:S(2)}) collective-permute-start(bf16[384,128]{1,0:T(8,128)(2,1)S(1)} %get-tuple-element.208), channel_id=1, source_target_pairs={{0,8},{1,9},{2,10},{3,11},{4,12},{5,13},{6,14},{7,15},{8,0},{9,1},... | collective-permute-start | bytes 294920 | tf_op jit(solution)/shard_map/ppermute | solution.py:353
  37.8 0.8 %collective-permute-done.5.refs_2_ = bf16[384,128]{1,0:T(8,128)(2,1)S(1)} collective-permute-done((bf16[384,128]{1,0:T(8,128)(2,1)S(1)}, bf16[384,128]{1,0:T(8,128)(2,1)S(1)}, u32[]{:S(2)}, u32[]{:S(2)}) %collective-permute-start.5) | collective-permute-done | bytes 98336 | tf_op jit(solution)/shard_map/ppermute | solution.py:353
  38.6 1.8 %collective-permute-start.8 = (bf16[384,128]{1,0:T(8,128)(2,1)S(1)}, bf16[384,128]{1,0:T(8,128)(2,1)S(1)}, u32[]{:S(2)}, u32[]{:S(2)}) collective-permute-start(bf16[384,128]{1,0:T(8,128)(2,1)S(1)} %collective-permute-done.5.refs_2_), channel_id=1, source_target_pairs={{0,4},{1,5},{2,6},{3,7},{4,0},{5,1},{6,2},{7,3},{8,12},{9,13},{10,... | collective-permute-start | bytes 294920 | tf_op jit(solution)/shard_map/ppermute | solution.py:353
  40.4 3.0 %collective-permute-done.7.refs_2_ = bf16[384,128]{1,0:T(8,128)(2,1)S(1)} collective-permute-done((bf16[384,128]{1,0:T(8,128)(2,1)S(1)}, bf16[384,128]{1,0:T(8,128)(2,1)S(1)}, u32[]{:S(2)}, u32[]{:S(2)}) %collective-permute-start.7) | collective-permute-done | bytes 98336 | tf_op jit(solution)/shard_map/ppermute | solution.py:353
  43.4 0.3 collective-permute-start.9
  43.8 0.8 %plane_sums.6 = (f32[768,128]{1,0:T(8,128)}, f32[768,128]{1,0:T(8,128)S(1)}, bf16[384,128]{1,0:T(8,128)(2,1)}) custom-call(f32[768,128]{1,0:T(8,128)S(1)} %get-tuple-element.190.refs_0_, f32[768,128]{1,0:T(8,128)S(1)} %get-tuple-element.191.refs_1_, bf16[384,128]{1,0:T(8,128)(2,1)S(1)} %collective-permute-done.5.refs_2_, ...), custom_call_target="tpu_custom_call" | custom-call | flops 1024 | bytes 1024 | tf_op jit(solution)/shard_map/plane_sums/pallas_call | solution.py:372
  44.6 0.2 own_prefixes.2
  44.8 3.3 %collective-permute-done.9.refs_3_ = bf16[384,128]{1,0:T(8,128)(2,1)S(1)} collective-permute-done((bf16[384,128]{1,0:T(8,128)(2,1)S(1)}, bf16[384,128]{1,0:T(8,128)(2,1)S(1)}, u32[]{:S(2)}, u32[]{:S(2)}) %collective-permute-start.9) | collective-permute-done | bytes 98336 | tf_op jit(solution)/shard_map/ppermute | solution.py:353
  48.1 0.8 %plane_sums.7 = (f32[768,128]{1,0:T(8,128)}, f32[768,128]{1,0:T(8,128)S(1)}, bf16[384,128]{1,0:T(8,128)(2,1)}) custom-call(f32[768,128]{1,0:T(8,128)S(1)} %get-tuple-element.225.refs_0_, f32[768,128]{1,0:T(8,128)S(1)} %get-tuple-element.226.refs_1_, bf16[384,128]{1,0:T(8,128)(2,1)S(1)} %collective-permute-done.7.refs_2_, ...), custom_call_target="tpu_custom_call" | custom-call | flops 1024 | bytes 1024 | tf_op jit(solution)/shard_map/plane_sums/pallas_call | solution.py:372
  48.9 0.2 own_prefixes.3
  49.1 0.1 collective-permute-start.13
  49.2 0.5 collective-permute-start.12
  49.7 1.3 %collective-permute-start.11 = (bf16[768,128]{1,0:T(8,128)(2,1)S(1)}, bf16[768,128]{1,0:T(8,128)(2,1)S(1)}, u32[]{:S(2)}, u32[]{:S(2)}) collective-permute-start(bf16[768,128]{1,0:T(8,128)(2,1)S(1)} %get-tuple-element.244), channel_id=1, source_target_pairs={{0,2},{1,3},{2,0},{3,1},{4,6},{5,7},{6,4},{7,5},{8,10},{9,11},{10,... | collective-permute-start | bytes 589832 | tf_op jit(solution)/shard_map/ppermute | solution.py:353
  51.0 1.9 %finish.5.rest_3_ = bf16[256,6144]{1,0:T(8,128)(2,1)} custom-call(f32[1,6144]{1,0:T(1,128)S(1)} %bitcast.1, bf16[256,1536]{1,0:T(8,128)(2,1)S(1)} %get-tuple-element.245.rest_0_.rest_2_, bf16[256,1536]{1,0:T(8,128)(2,1)S(1)} %get-tuple-element.246.rest_1_.rest_3_, bf16[256,1536]{1,0:T(8,128)(2,1)S(1)} %get-tuple-element.245.rest_0_.rest_2_, ...), custom_call_target="tpu_custom_call" | custom-call | flops 1024 | bytes 1024 | tf_op jit(solution)/shard_map/finish/pallas_call | solution.py:341
  52.9 3.7 %collective-permute-done.11.refs_0_ = bf16[768,128]{1,0:T(8,128)(2,1)S(1)} collective-permute-done((bf16[768,128]{1,0:T(8,128)(2,1)S(1)}, bf16[768,128]{1,0:T(8,128)(2,1)S(1)}, u32[]{:S(2)}, u32[]{:S(2)}) %collective-permute-start.11) | collective-permute-done | bytes 196640 | tf_op jit(solution)/shard_map/ppermute | solution.py:353
  56.5 0.1 paired_prefixes.2
  56.6 0.1 collective-permute-start.14
  56.7 1.4 %collective-permute-start.10 = (bf16[768,128]{1,0:T(8,128)(2,1)S(1)}, bf16[768,128]{1,0:T(8,128)(2,1)S(1)}, u32[]{:S(2)}, u32[]{:S(2)}) collective-permute-start(bf16[768,128]{1,0:T(8,128)(2,1)S(1)} %get-tuple-element.243), channel_id=1, source_target_pairs={{0,2},{1,3},{2,0},{3,1},{4,6},{5,7},{6,4},{7,5},{8,10},{9,11},{10,... | collective-permute-start | bytes 589832 | tf_op jit(solution)/shard_map/ppermute | solution.py:353
  58.1 1.2 %finish.6.rest_3_ = bf16[256,6144]{1,0:T(8,128)(2,1)} custom-call(f32[1,6144]{1,0:T(1,128)S(1)} %bitcast.2, bf16[256,1536]{1,0:T(8,128)(2,1)S(1)} %get-tuple-element.257.rest_0_, f32[256,1536]{1,0:T(8,128)S(1)} %get-tuple-element.258.rest_1_, bf16[768,128]{1,0:T(8,128)(2,1)S(1)} %get-tuple-element.259.rest_2_, ...), custom_call_target="tpu_custom_call", output_to_operand_aliasing={{}: (4, {})} | custom-call | flops 1024 | bytes 1024 | tf_op jit(solution)/shard_map/finish/pallas_call | solution.py:341
  59.3 1.2 %finish.7.rest_3_ = bf16[256,6144]{1,0:T(8,128)(2,1)} custom-call(f32[1,6144]{1,0:T(1,128)S(1)} %bitcast.3, bf16[256,1536]{1,0:T(8,128)(2,1)S(1)} %get-tuple-element.241.rest_0_, f32[256,1536]{1,0:T(8,128)S(1)} %get-tuple-element.242.rest_1_, bf16[768,128]{1,0:T(8,128)(2,1)S(1)} %collective-permute-done.14.rest_2_, ...), custom_call_target="tpu_custom_call", output_to_operand_aliasing={{}: (4, {})} | custom-call | flops 1024 | bytes 1024 | tf_op jit(solution)/shard_map/finish/pallas_call | solution.py:341
  60.5 3.5 %collective-permute-done.10.refs_0_ = bf16[768,128]{1,0:T(8,128)(2,1)S(1)} collective-permute-done((bf16[768,128]{1,0:T(8,128)(2,1)S(1)}, bf16[768,128]{1,0:T(8,128)(2,1)S(1)}, u32[]{:S(2)}, u32[]{:S(2)}) %collective-permute-start.10) | collective-permute-done | bytes 196640 | tf_op jit(solution)/shard_map/ppermute | solution.py:353
  64.0 0.1 paired_prefixes.3
  64.1 0.1 collective-permute-start.15
  64.2 1.2 %finish.8.rest_3_ = bf16[256,6144]{1,0:T(8,128)(2,1)} custom-call(f32[1,6144]{1,0:T(1,128)S(1)} %bitcast.4, bf16[256,1536]{1,0:T(8,128)(2,1)S(1)} %get-tuple-element.257.rest_0_, f32[256,1536]{1,0:T(8,128)S(1)} %get-tuple-element.258.rest_1_, bf16[768,128]{1,0:T(8,128)(2,1)S(1)} %get-tuple-element.267.rest_2_, ...), custom_call_target="tpu_custom_call", output_to_operand_aliasing={{}: (4, {})} | custom-call | flops 1024 | bytes 1024 | tf_op jit(solution)/shard_map/finish/pallas_call | solution.py:341
  65.4 0.2 collective-permute-done.15.rest_2_
  65.6 1.2 %finish.9 = bf16[256,6144]{1,0:T(8,128)(2,1)} custom-call(f32[1,6144]{1,0:T(1,128)S(1)} %bitcast.5, bf16[256,1536]{1,0:T(8,128)(2,1)S(1)} %get-tuple-element.241.rest_0_, f32[256,1536]{1,0:T(8,128)S(1)} %get-tuple-element.242.rest_1_, bf16[768,128]{1,0:T(8,128)(2,1)S(1)} %collective-permute-done.15.rest_2_, ...), custom_call_target="tpu_custom_call", output_to_operand_aliasing={{}: (4, {})} | custom-call | flops 1024 | bytes 1024 | tf_op jit(solution)/shard_map/finish/pallas_call | solution.py:341
  (17 shorter events, 0.1 us)
Async XLA Ops:
  0.0 1.7 %copy-start.2 = (bf16[128,128]{1,0:T(8,128)(2,1)S(1)}, bf16[128,128]{1,0:T(8,128)(2,1)}, u32[]{:S(2)}) copy-start(bf16[128,128]{1,0:T(8,128)(2,1)} %map_ref.13) | copy-start | bytes 98308
  0.0 1.7 %copy-start.1 = (bf16[3,4,6144]{2,1,0:T(4,128)(2,1)S(1)}, bf16[3,4,6144]{2,1,0:T(4,128)(2,1)}, u32[]{:S(2)}) copy-start(bf16[3,4,6144]{2,1,0:T(4,128)(2,1)} %taps_ref.13) | copy-start | bytes 442372
  1.2 8.9 %collective-permute-start = (bf16[16,6144]{1,0:T(8,128)(2,1)S(1)}, bf16[16,6144]{1,0:T(8,128)(2,1)S(1)}, u32[]{:S(2)}, u32[]{:S(2)}) collective-permute-start(bf16[16,6144]{1,0:T(8,128)(2,1)S(1)} %pack_rims.1), channel_id=1, source_target_pairs={{0,1},{1,2},{2,3},{3,4},{4,5},{5,6},{6,7},{7,8},{8,9},{9,10},{10,1... | collective-permute-start | bytes 589832 | tf_op jit(solution)/shard_map/ppermute | solution.py:358
  13.6 2.4 %collective-permute-start.1 = (bf16[3072,128]{1,0:T(8,128)(2,1)S(1)}, bf16[3072,128]{1,0:T(8,128)(2,1)S(1)}, u32[]{:S(2)}, u32[]{:S(2)}) collective-permute-start(bf16[3072,128]{1,0:T(8,128)(2,1)S(1)} %get-tuple-element.153), channel_id=1, source_target_pairs={{0,1},{1,0},{2,3},{3,2},{4,5},{5,4},{6,7},{7,6},{8,9},{9,8},{10,11... | collective-permute-start | bytes 2359304 | tf_op jit(solution)/shard_map/ppermute | solution.py:353
  13.7 4.5 %copy-start = (bf16[256,6144]{1,0:T(8,128)(2,1)S(1)}, bf16[256,6144]{1,0:T(8,128)(2,1)}, u32[]{:S(2)}) copy-start(bf16[256,6144]{1,0:T(8,128)(2,1)} %query_ref.9) | copy-start | bytes 9437188
  16.1 7.8 %collective-permute-start.2 = (bf16[768,128]{1,0:T(8,128)(2,1)S(1)}, bf16[768,128]{1,0:T(8,128)(2,1)S(1)}, u32[]{:S(2)}, u32[]{:S(2)}) collective-permute-start(bf16[768,128]{1,0:T(8,128)(2,1)S(1)} %get-tuple-element.163), channel_id=1, source_target_pairs={{0,2},{1,3},{2,0},{3,1},{4,6},{5,7},{6,4},{7,5},{8,10},{9,11},{10,... | collective-permute-start | bytes 589832 | tf_op jit(solution)/shard_map/ppermute | solution.py:353
  16.8 10.8 %collective-permute-start.4 = (bf16[768,128]{1,0:T(8,128)(2,1)S(1)}, bf16[768,128]{1,0:T(8,128)(2,1)S(1)}, u32[]{:S(2)}, u32[]{:S(2)}) collective-permute-start(bf16[768,128]{1,0:T(8,128)(2,1)S(1)} %get-tuple-element.176), channel_id=1, source_target_pairs={{0,2},{1,3},{2,0},{3,1},{4,6},{5,7},{6,4},{7,5},{8,10},{9,11},{10,... | collective-permute-start | bytes 589832 | tf_op jit(solution)/shard_map/ppermute | solution.py:353
  24.0 7.8 %collective-permute-start.3 = (bf16[768,128]{1,0:T(8,128)(2,1)S(1)}, bf16[768,128]{1,0:T(8,128)(2,1)S(1)}, u32[]{:S(2)}, u32[]{:S(2)}) collective-permute-start(bf16[768,128]{1,0:T(8,128)(2,1)S(1)} %get-tuple-element.174), channel_id=1, source_target_pairs={{0,4},{1,5},{2,6},{3,7},{4,0},{5,1},{6,2},{7,3},{8,12},{9,13},{10,... | collective-permute-start | bytes 589832 | tf_op jit(solution)/shard_map/ppermute | solution.py:353
  27.6 8.9 %collective-permute-start.6 = (bf16[768,128]{1,0:T(8,128)(2,1)S(1)}, bf16[768,128]{1,0:T(8,128)(2,1)S(1)}, u32[]{:S(2)}, u32[]{:S(2)}) collective-permute-start(bf16[768,128]{1,0:T(8,128)(2,1)S(1)} %get-tuple-element.195), channel_id=1, source_target_pairs={{0,4},{1,5},{2,6},{3,7},{4,0},{5,1},{6,2},{7,3},{8,12},{9,13},{10,... | collective-permute-start | bytes 589832 | tf_op jit(solution)/shard_map/ppermute | solution.py:353
  31.9 6.6 %collective-permute-start.5 = (bf16[384,128]{1,0:T(8,128)(2,1)S(1)}, bf16[384,128]{1,0:T(8,128)(2,1)S(1)}, u32[]{:S(2)}, u32[]{:S(2)}) collective-permute-start(bf16[384,128]{1,0:T(8,128)(2,1)S(1)} %get-tuple-element.194), channel_id=1, source_target_pairs={{0,8},{1,9},{2,10},{3,11},{4,12},{5,13},{6,14},{7,15},{8,0},{9,1},... | collective-permute-start | bytes 294920 | tf_op jit(solution)/shard_map/ppermute | solution.py:353
  36.7 6.7 %collective-permute-start.7 = (bf16[384,128]{1,0:T(8,128)(2,1)S(1)}, bf16[384,128]{1,0:T(8,128)(2,1)S(1)}, u32[]{:S(2)}, u32[]{:S(2)}) collective-permute-start(bf16[384,128]{1,0:T(8,128)(2,1)S(1)} %get-tuple-element.208), channel_id=1, source_target_pairs={{0,8},{1,9},{2,10},{3,11},{4,12},{5,13},{6,14},{7,15},{8,0},{9,1},... | collective-permute-start | bytes 294920 | tf_op jit(solution)/shard_map/ppermute | solution.py:353
  38.6 5.2 %collective-permute-start.8 = (bf16[384,128]{1,0:T(8,128)(2,1)S(1)}, bf16[384,128]{1,0:T(8,128)(2,1)S(1)}, u32[]{:S(2)}, u32[]{:S(2)}) collective-permute-start(bf16[384,128]{1,0:T(8,128)(2,1)S(1)} %collective-permute-done.5.refs_2_), channel_id=1, source_target_pairs={{0,4},{1,5},{2,6},{3,7},{4,0},{5,1},{6,2},{7,3},{8,12},{9,13},{10,... | collective-permute-start | bytes 294920 | tf_op jit(solution)/shard_map/ppermute | solution.py:353
  43.4 4.6 %collective-permute-start.9 = (bf16[384,128]{1,0:T(8,128)(2,1)S(1)}, bf16[384,128]{1,0:T(8,128)(2,1)S(1)}, u32[]{:S(2)}, u32[]{:S(2)}) collective-permute-start(bf16[384,128]{1,0:T(8,128)(2,1)S(1)} %collective-permute-done.7.refs_2_), channel_id=1, source_target_pairs={{0,4},{1,5},{2,6},{3,7},{4,0},{5,1},{6,2},{7,3},{8,12},{9,13},{10,... | collective-permute-start | bytes 294920 | tf_op jit(solution)/shard_map/ppermute | solution.py:353
  48.9 2.1 %copy-start.3 = (f32[6144]{0:T(1024)S(1)}, f32[6144]{0:T(1024)}, u32[]{:S(2)}) copy-start(f32[6144]{0:T(1024)} %param.11) | copy-start | bytes 73732
  49.1 1.9 %collective-permute-start.13 = (bf16[768,128]{1,0:T(8,128)(2,1)S(1)}, bf16[768,128]{1,0:T(8,128)(2,1)S(1)}, u32[]{:S(2)}, u32[]{:S(2)}) collective-permute-start(bf16[768,128]{1,0:T(8,128)(2,1)S(1)} %get-tuple-element.252), channel_id=1, source_target_pairs={{0,1},{1,0},{2,3},{3,2},{4,5},{5,4},{6,7},{7,6},{8,9},{9,8},{10,11... | collective-permute-start | bytes 589832 | tf_op jit(solution)/shard_map/ppermute | solution.py:353
  49.2 1.8 %collective-permute-start.12 = (bf16[768,128]{1,0:T(8,128)(2,1)S(1)}, bf16[768,128]{1,0:T(8,128)(2,1)S(1)}, u32[]{:S(2)}, u32[]{:S(2)}) collective-permute-start(bf16[768,128]{1,0:T(8,128)(2,1)S(1)} %get-tuple-element.250), channel_id=1, source_target_pairs={{0,1},{1,0},{2,3},{3,2},{4,5},{5,4},{6,7},{7,6},{8,9},{9,8},{10,11... | collective-permute-start | bytes 589832 | tf_op jit(solution)/shard_map/ppermute | solution.py:353
  49.7 6.9 %collective-permute-start.11 = (bf16[768,128]{1,0:T(8,128)(2,1)S(1)}, bf16[768,128]{1,0:T(8,128)(2,1)S(1)}, u32[]{:S(2)}, u32[]{:S(2)}) collective-permute-start(bf16[768,128]{1,0:T(8,128)(2,1)S(1)} %get-tuple-element.244), channel_id=1, source_target_pairs={{0,2},{1,3},{2,0},{3,1},{4,6},{5,7},{6,4},{7,5},{8,10},{9,11},{10,... | collective-permute-start | bytes 589832 | tf_op jit(solution)/shard_map/ppermute | solution.py:353
  56.6 2.7 %collective-permute-start.14 = (bf16[768,128]{1,0:T(8,128)(2,1)S(1)}, bf16[768,128]{1,0:T(8,128)(2,1)S(1)}, u32[]{:S(2)}, u32[]{:S(2)}) collective-permute-start(bf16[768,128]{1,0:T(8,128)(2,1)S(1)} %get-tuple-element.256), channel_id=1, source_target_pairs={{0,1},{1,0},{2,3},{3,2},{4,5},{5,4},{6,7},{7,6},{8,9},{9,8},{10,11... | collective-permute-start | bytes 589832 | tf_op jit(solution)/shard_map/ppermute | solution.py:353
  56.7 7.3 %collective-permute-start.10 = (bf16[768,128]{1,0:T(8,128)(2,1)S(1)}, bf16[768,128]{1,0:T(8,128)(2,1)S(1)}, u32[]{:S(2)}, u32[]{:S(2)}) collective-permute-start(bf16[768,128]{1,0:T(8,128)(2,1)S(1)} %get-tuple-element.243), channel_id=1, source_target_pairs={{0,2},{1,3},{2,0},{3,1},{4,6},{5,7},{6,4},{7,5},{8,10},{9,11},{10,... | collective-permute-start | bytes 589832 | tf_op jit(solution)/shard_map/ppermute | solution.py:353
  64.1 1.5 %collective-permute-start.15 = (bf16[768,128]{1,0:T(8,128)(2,1)S(1)}, bf16[768,128]{1,0:T(8,128)(2,1)S(1)}, u32[]{:S(2)}, u32[]{:S(2)}) collective-permute-start(bf16[768,128]{1,0:T(8,128)(2,1)S(1)} %get-tuple-element.266), channel_id=1, source_target_pairs={{0,1},{1,0},{2,3},{3,2},{4,5},{5,4},{6,7},{7,6},{8,9},{9,8},{10,11... | collective-permute-start | bytes 589832 | tf_op jit(solution)/shard_map/ppermute | solution.py:353

commit v4 on v3

v4 whole, which is shorter than its diff:
```python
import functools

import jax
import jax.numpy as jnp
from jax import lax
from jax.experimental import pallas as pl
from jax.experimental.pallas import tpu as pltpu
from jax.sharding import PartitionSpec as P

SPAN = 256
GROUPS = 2
BLOCK_HEADS = 6
RIM = 16
TILE = 8
VMEM_BYTES = 12 * 1024 * 1024
f32, bf16 = jnp.float32, jnp.bfloat16
IN_VMEM = pl.BlockSpec(memory_space=pltpu.VMEM)
IN_PLACE = pl.BlockSpec(memory_space=pl.ANY)
LIGHT = pl.CostEstimate(flops=1024, bytes_accessed=1024, transcendentals=0)


def in_hbm(array):
    return pltpu.with_memory_space_constraint(array, pltpu.HBM)


class Turn:
    last = ()


def kernel_call(body, name, in_specs, out_specs, out_shape, scratch=(), aliases=None):
    count = len(in_specs)

    def call(*operands):
        before = Turn.last

        def ordered(*refs):
            body(*refs[:count], *refs[count + len(before) :])

        results = pl.pallas_call(
            ordered,
            in_specs=[*in_specs, *[IN_PLACE] * len(before)],
            out_specs=out_specs,
            out_shape=out_shape,
            scratch_shapes=list(scratch),
            input_output_aliases=aliases or {},
            compiler_params=pltpu.CompilerParams(vmem_limit_bytes=VMEM_BYTES),
            cost_estimate=LIGHT,
            name=name,
        )(*operands, *before)
        Turn.last = (results[-1] if isinstance(results, (list, tuple)) else results,)
        return results

    return call


def shape(dims, kind):
    return jax.ShapeDtypeStruct(dims, kind)


def quarter_start(quarter, width):
    device = lax.axis_index("seq")
    core = (device & 1) ^ int(quarter < 2)
    pair = ((device >> 1) & 1) ^ int(quarter % 2 == 0)
    return (2 * core + pair) * (width // 4)


def columns(start, size):
    return pl.ds(pl.multiple_of(start, 128), size)


def block_heads(heads):
    return max(n for n in range(1, BLOCK_HEADS + 1) if heads % n == 0)


def pack_kernel(tap_count, query_ref, key_ref, value_ref, rim_ref, tails, sems):
    taps = tap_count - 1
    rows = pl.ds(query_ref.shape[0] - RIM, RIM)
    copies = [
        pltpu.make_async_copy(ref.at[rows], tails.at[i], sems.at[i])
        for i, ref in enumerate((key_ref, value_ref, query_ref))
    ]
    for copy in copies:
        copy.start()
    for copy in copies:
        copy.wait()
    key_tail, value_tail, query_tail = (tails[i].astype(f32)[-TILE:] for i in range(3))
    row = lax.broadcasted_iota(jnp.int32, key_tail.shape, 0)
    first = jnp.where(row < taps, pltpu.roll(key_tail, taps, 0), pltpu.roll(value_tail, 2 * taps, 0))
    rim_ref[...] = jnp.concatenate([first, query_tail], axis=0).astype(bf16)


def pack_rims(query_seq, key_seq, value_seq, tap_count):
    width = query_seq.shape[1]
    return kernel_call(
        functools.partial(pack_kernel, tap_count),
        "pack_rims",
        [IN_PLACE] * 3,
        IN_VMEM,
        shape((RIM, width), bf16),
        [pltpu.VMEM((3, RIM, width), bf16), pltpu.SemaphoreType.DMA((3,))],
    )(in_hbm(query_seq), in_hbm(key_seq), in_hbm(value_seq))


def convolved(scratch, rows, taps, rim=None, rim_end=0):
    length = rows.shape[0]
    if rim is None:
        scratch[:TILE] = jnp.zeros((TILE, rows.shape[1]), f32)
    else:
        scratch[:TILE] = pltpu.roll(rim, (-rim_end) % TILE, 0)
    scratch[TILE : TILE + length] = rows
    total = taps[0:1] * rows
    for offset in range(1, taps.shape[0]):
        total = total + taps[offset : offset + 1] * scratch[TILE - offset : TILE - offset + length]
    return total.astype(bf16)


def features(conv_rows, feature_map):
    projected = jnp.dot(conv_rows, feature_map, preferred_element_type=f32)
    return jnp.where(projected > 0, projected + 1.0, jnp.exp(projected)).astype(bf16)


def state_of(key_feat, value_conv):
    return lax.dot_general(
        key_feat, value_conv, (((0,), (0,)), ((), ())), preferred_element_type=f32
    )


def rim_rows(rim_ref, cols, start):
    rim = rim_ref[:, cols].astype(f32)[start : start + TILE]
    return jnp.where(lax.axis_index("seq") > 0, rim, 0.0)


def near_states_kernel(
    group, key_ref, value_ref, taps_ref, map_ref, feat_ref, conv_ref, state_ref, key_first, value_first, scratch
):
    head_dim = map_ref.shape[0]
    width = key_ref.shape[1]
    size = width // (4 * GROUPS)
    back = taps_ref.shape[1] - 1
    row = lax.broadcasted_iota(jnp.int32, (RIM, head_dim), 0)
    for quarter in range(4):
        for start in range(0, size, head_dim):
            natural = columns(quarter_start(quarter, width) + group * size + start, head_dim)
            at = quarter * size + start
            local = slice(at, at + head_dim)
            buffers = scratch.at[at // head_dim % scratch.shape[0]]
            key, value = key_ref[:, natural], value_ref[:, natural]
            key_first[:, local] = key[:RIM]
            value_first[:, local] = value[:RIM]
            key_conv = convolved(buffers.at[0], key.astype(f32), taps_ref[1, :, natural].astype(f32))
            key_feat = features(key_conv, map_ref[...])
            feat_ref[:, local] = key_feat
            value_conv = convolved(buffers.at[1], value.astype(f32), taps_ref[2, :, natural].astype(f32))
            conv_ref[:, local] = value_conv
            later = jnp.where(row < back, 0.0, key_feat[:RIM].astype(f32)).astype(bf16)
            key_feat = jnp.concatenate([later, key_feat[RIM:]], axis=0)
            state_ref[local] = state_of(key_feat, value_conv)


def near_states(group, key_seq, value_seq, conv_kernel, feature_map):
    tok_count, width = key_seq.shape
    head_dim = feature_map.shape[0]
    size = width // GROUPS
    rows, firsts = shape((tok_count, size), bf16), shape((RIM, size), bf16)
    return kernel_call(
        functools.partial(near_states_kernel, group),
        "near_states",
        [IN_VMEM] * 4,
        [IN_VMEM] * 5,
        [rows, rows, shape((size, head_dim), f32), firsts, firsts],
        [pltpu.VMEM((BLOCK_HEADS, 2, TILE + tok_count, head_dim), f32)],
    )(key_seq, value_seq, conv_kernel, feature_map)


def first_rows_kernel(
    group, quarters, key_ref, value_ref, taps_ref, map_ref, rim_ref, state_ref,
    feat_ref, conv_ref, sum_ref, scratch,
):
    head_dim = map_ref.shape[0]
    width = taps_ref.shape[2]
    back = taps_ref.shape[1] - 1
    row = lax.broadcasted_iota(jnp.int32, (RIM, head_dim), 0)
    size = width // (4 * GROUPS)
    for i, quarter in enumerate(quarters):
        there = slice(quarter * size, (quarter + 1) * size)
        natural = columns(quarter_start(quarter, width) + group * size, size)
        rim = rim_rows(rim_ref, natural, 0)
        conv = convolved(
            scratch.at[i, 0], key_ref[:, there].astype(f32), taps_ref[1, :, natural].astype(f32), rim, back
        )
        value_conv = convolved(
            scratch.at[i, 1], value_ref[:, there].astype(f32), taps_ref[2, :, natural].astype(f32), rim, 2 * back
        )
        conv_ref[:, i * size : (i + 1) * size] = value_conv
        parts = [slice(at, at + head_dim) for at in range(0, size, head_dim)]
        feats = [features(conv[:, part], map_ref[...]) for part in parts]
        feat_ref[:, i * size : (i + 1) * size] = jnp.concatenate(feats, axis=1)
        firsts = [jnp.where(row < back, feat.astype(f32), 0.0).astype(bf16) for feat in feats]
        for part, first in zip(parts, firsts):
            state = state_ref[there.start + part.start : there.start + part.stop]
            state = state + state_of(first, value_conv[:, part])
            sum_ref[i * size + part.start : i * size + part.stop] = state.astype(sum_ref.dtype)


def first_rows(group, quarters, state_type, key_first, value_first, conv_kernel, feature_map, rims, state):
    width = conv_kernel.shape[2]
    head_dim = feature_map.shape[0]
    size = width // (4 * GROUPS)
    rows = shape((RIM, len(quarters) * size), bf16)
    return kernel_call(
        functools.partial(first_rows_kernel, group, quarters),
        "first_rows",
        [IN_VMEM] * 6,
        [IN_VMEM] * 3,
        [rows, rows, shape((len(quarters) * size, head_dim), state_type)],
        [pltpu.VMEM((len(quarters), 2, TILE + RIM, size), f32)],
    )(key_first, value_first, conv_kernel, feature_map, rims, state)


def within_kernel(
    quarter, group, query_ref, taps_ref, map_ref, rim_ref, key_ref, value_ref, key_first, value_first,
    feat_ref, mixed_ref, scratch,
):
    head_dim = map_ref.shape[0]
    tok_count, width = query_ref.shape
    size = width // (4 * GROUPS)
    causal = lax.broadcasted_iota(jnp.int32, (tok_count, tok_count), 0) >= lax.broadcasted_iota(
        jnp.int32, (tok_count, tok_count), 1
    )
    for start in range(0, size, head_dim):
        natural = columns(quarter_start(quarter, width) + group * size + start, head_dim)
        local = slice(start, start + head_dim)
        at = slice(quarter * size + start, quarter * size + start + head_dim)
        first = slice(quarter % 2 * size + start, quarter % 2 * size + start + head_dim)
        key = jnp.concatenate([key_first[:, first], key_ref[RIM:, at]], axis=0)
        value = jnp.concatenate([value_first[:, first], value_ref[RIM:, at]], axis=0)
        rim = rim_rows(rim_ref, natural, TILE)
        taps = taps_ref[0, :, natural].astype(f32)
        buffer = scratch.at[start // head_dim % scratch.shape[0]]
        conv = convolved(buffer, query_ref[:, natural].astype(f32), taps, rim, TILE)
        feat = features(conv, map_ref[...])
        feat_ref[:, local] = feat
        scores = lax.dot_general(feat, key, (((1,), (1,)), ((), ())), preferred_element_type=f32)
        weights = jnp.where(causal, scores, 0.0).astype(bf16)
        mixed_ref[:, local] = jnp.dot(weights, value, preferred_element_type=f32)


def within_block(quarter, group, query_seq, conv_kernel, feature_map, rims, feat, conv, firsts):
    tok_count, width = query_seq.shape
    head_dim = feature_map.shape[0]
    size = width // (4 * GROUPS)
    operands = (query_seq, conv_kernel, feature_map, rims, feat, conv, *firsts)
    return kernel_call(
        functools.partial(within_kernel, quarter, group),
        "within_block",
        [IN_VMEM] * len(operands),
        [IN_VMEM] * 2,
        [shape((tok_count, size), bf16), shape((tok_count, size), f32)],
        [pltpu.VMEM((BLOCK_HEADS, TILE + tok_count, head_dim), f32)],
    )(*operands)


def finish_kernel(pieces, gain_ref, *rest):
    count = sum(len(part) for part in pieces)
    prefixes, rest = rest[: len(pieces)], rest[len(pieces) :]
    feats, mixes = rest[:count], rest[count : 2 * count]
    out_ref, token_ref, rows, sems = rest[-4:]
    token_ref[...] = jnp.zeros(token_ref.shape, f32)
    head_dim = prefixes[0].shape[1]
    tok_count, size = feats[0].shape
    copies = []
    for prefix_ref, part in zip(prefixes, pieces):
        for at, (quarter, group) in enumerate(part):
            i = len(copies)
            natural = quarter_start(quarter, out_ref.shape[1]) + group * size
            for start in range(0, size, head_dim):
                cols = slice(start, start + head_dim)
                prefix = prefix_ref[at * size + start : at * size + start + head_dim]
                mixed = mixes[i][:, cols] + jnp.dot(feats[i][:, cols], prefix, preferred_element_type=f32)
                inverse_rms = lax.rsqrt(jnp.mean(mixed * mixed, axis=-1, keepdims=True) + 1e-06)
                gain = gain_ref[:, columns(natural + start, head_dim)]
                rows[i, :, cols] = (mixed * inverse_rms * gain).astype(bf16)
            copies.append(pltpu.make_async_copy(rows.at[i], out_ref.at[:, columns(natural, size)], sems.at[i]))
            copies[-1].start()
    for copy in copies:
        copy.wait()


def finish(pieces, mixed, prefixes, norm_gain, before):
    width = norm_gain.shape[1]
    every = [piece for part in pieces for piece in part]
    count = len(every)
    tok_count, size = mixed[every[0]][0].shape
    operands = [norm_gain, *prefixes, *(mixed[p][0] for p in every), *(mixed[p][1] for p in every)]
    in_specs = [IN_VMEM] * len(operands)
    aliases = {}
    if before is not None:
        aliases = {len(operands): 0}
        operands.append(in_hbm(before))
        in_specs.append(IN_PLACE)
    return kernel_call(
        functools.partial(finish_kernel, pieces),
        "finish",
        in_specs,
        [IN_PLACE, IN_VMEM],
        [pltpu.HBM((tok_count, width), bf16), shape((TILE, 128), f32)],
        [pltpu.VMEM((count, tok_count, size), bf16), pltpu.SemaphoreType.DMA((count,))],
        aliases,
    )(*operands)[0]


def swapped(block, distance):
    return lax.ppermute(block, "seq", [(i, i ^ distance) for i in range(lax.axis_size("seq"))])


def rotated(block):
    count = lax.axis_size("seq")
    return lax.ppermute(block, "seq", [(i, (i + 1) % count) for i in range(count)])


def mapped(name, function, outputs, *arrays):
    def body(*refs):
        values = [ref[...] for ref in refs[: len(arrays)]]
        for ref, value in zip(refs[len(arrays) :], function(lax.axis_index("seq"), *values)):
            ref[...] = value.astype(ref.dtype)

    columns = arrays[0].shape[1]
    return kernel_call(
        body,
        name,
        [IN_VMEM] * len(arrays),
        [IN_VMEM] * len(outputs),
        [shape((rows, columns), kind) for rows, kind in outputs],
    )(*arrays)


def on_device(query_seq, key_seq, value_seq, conv_kernel, feature_map, norm_gain):
    tok_count, width = query_seq.shape
    tap_count = conv_kernel.shape[1]
    head_dim = feature_map.shape[0]
    device_count = lax.axis_size("seq")
    assert tok_count == SPAN and width % (4 * GROUPS * head_dim) == 0
    assert device_count >= 8 and device_count & (device_count - 1) == 0
    groups = range(GROUPS)
    rows = width // (4 * GROUPS)
    gain = norm_gain.reshape(1, width)

    def of_core(device):
        return (device & 1) != 0

    def of_pair(device):
        return (device & 2) != 0

    Turn.last = ()
    rims = rotated(pack_rims(query_seq, key_seq, value_seq, tap_count))
    near = [near_states(g, key_seq, value_seq, conv_kernel, feature_map) for g in groups]
    firsts, from_core = [], []
    for g in groups:
        *first, state_a = first_rows(
            g, (0, 1), bf16, *near[g][3:], conv_kernel, feature_map, rims, near[g][2]
        )
        firsts.append([first])
        from_core.append(swapped(state_a, 1))
    for g in groups:
        firsts[g].append(
            first_rows(g, (2, 3), f32, *near[g][3:], conv_kernel, feature_map, rims, near[g][2])
        )
    state_b = [first[1][2] for first in firsts]

    mixed = {}
    fill = [(q, g) for q in (3, 2, 1, 0) for g in groups]
    total = len(fill)

    def score(share):
        while fill and total - len(fill) < round(share * total):
            q, g = fill.pop(0)
            mixed[q, g] = within_block(
                q, g, query_seq, conv_kernel, feature_map, rims, *near[g][:2], firsts[g][q // 2][:2]
            )

    def chip_sums(device, state, arrived):
        return (
            state[:rows] + arrived[:rows].astype(f32),
            state[rows:] + arrived[rows:].astype(f32),
        )

    def pair_sums(device, own, arrived):
        total = own + arrived.astype(f32)
        return total, total

    def plane_sums(distance, device, total, *arrived):
        before, arrived = (0.0, arrived) if distance == 4 else (arrived[0], arrived[1:])
        upper = (device & distance) != 0
        if len(arrived) == 2:
            odd = (device & (distance // 2)) != 0
            mine, other = arrived
            arrived = (jnp.concatenate([jnp.where(odd, other, mine), jnp.where(odd, mine, other)], axis=0),)
        arrived = arrived[0].astype(f32)
        before = before + jnp.where(upper, arrived, 0.0)
        total = total + arrived
        give = total.astype(bf16)
        return total, before, jnp.where(upper, give[rows // 2 :], give[: rows // 2])

    def own_prefixes(distance, device, own, paired, cored, state, *step):
        before = plane_sums(distance, device, *step)[1] if step else jnp.zeros((rows, head_dim), f32)
        own_part = before + jnp.where(of_pair(device), paired.astype(f32), 0.0)
        others = before + jnp.where(of_pair(device), 0.0, own)
        return (
            others,
            own_part + jnp.where(of_core(device), cored[rows:].astype(f32), 0.0),
            own_part + jnp.where(of_core(device), 0.0, state[rows:]),
        )

    def paired_prefixes(device, arrived, cored, state, own):
        arrived = arrived.astype(f32)
        give = arrived + jnp.where(of_core(device), 0.0, state[:rows])
        return (
            arrived + jnp.where(of_core(device), cored[:rows].astype(f32), 0.0),
            jnp.concatenate([give.astype(bf16), own], axis=0),
        )

    chip, arriving = [None] * GROUPS, [None] * GROUPS
    for g in groups:
        give, chip[g] = mapped(
            "chip_sums", chip_sums, [(rows, bf16), (rows, f32)], state_b[g], from_core[g]
        )
        arriving[g] = swapped(give, 2)
    running, earlier, from_pair = [None] * GROUPS, [None] * GROUPS, [None] * GROUPS
    distance = 4
    score(0.375)
    for g in groups:
        from_pair[g] = arriving[g]
        if distance < device_count:
            running[g], give = mapped("pair_sums", pair_sums, [(rows, f32), (rows, bf16)], chip[g], from_pair[g])
            arriving[g] = (swapped(give, distance),)
            if g == 0:
                score(0.625)
    while 2 * distance < device_count:
        for g in groups:
            before = [] if distance == 4 else [earlier[g]]
            running[g], earlier[g], give = mapped(
                "plane_sums",
                functools.partial(plane_sums, distance),
                [(rows, f32), (rows, f32), (rows // 2, bf16)],
                running[g],
                *before,
                *arriving[g],
            )
            arriving[g] = swapped(give, 2 * distance)
            if g == 0:
                score(0.875)
        arriving = [(mine, swapped(mine, distance)) for mine in arriving]
        distance *= 2
    score(1)

    back, own_give = [None] * GROUPS, [None] * GROUPS
    out = None
    for g in groups:
        step = ()
        if distance < device_count:
            step = (running[g], *([] if distance == 4 else [earlier[g]]), *arriving[g])
        others, own, own_give[g] = mapped(
            "own_prefixes",
            functools.partial(own_prefixes, distance),
            [(rows, bf16)] * 3,
            chip[g],
            from_pair[g],
            from_core[g],
            state_b[g],
            *step,
        )
        back[g] = swapped(others, 2)
        out = finish([[(3, g)]], mixed, [own], gain, out)
    from_other = [None] * GROUPS
    for g in groups:
        prefix_2, give = mapped(
            "paired_prefixes",
            paired_prefixes,
            [(rows, bf16), (2 * rows, bf16)],
            back[g],
            from_core[g],
            state_b[g],
            own_give[g],
        )
        from_other[g] = swapped(give, 1)
        if g == 0:
            out = finish([[(2, g)]], mixed, [prefix_2], gain, out)
        else:
            pieces = [[(2, g)], [(0, g - 1), (1, g - 1)]]
            out = finish(pieces, mixed, [prefix_2, from_other[g - 1]], gain, out)
    return finish([[(0, g), (1, g)]], mixed, [from_other[g]], gain, out)


def solution(mesh):
    return jax.shard_map(
        on_device,
        mesh=mesh,
        in_specs=(
            P(("groups", "seq"), None),
            P(("groups", "seq"), None),
            P(("groups", "seq"), None),
            P(),
            P(),
            P(),
        ),
        out_specs=P(("groups", "seq"), None),
        check_vma=False,
    )
```

time: 67.1 us -> 57.1 us (0.85)
  waiting for transfers between devices: 21.9 us -> 6.45 us
  starting transfers between devices: 13.4 us -> 17.5 us
  local copies, waits for them, and re-layouts: 0.04 us -> 1.29 us
    ppermute x15 -> x14, waiting for transfers between devices: 18.7 us -> 6.45 us  [swapped(): lax.ppermute(block, 'seq', [(i, i ^ distance) for i in range(lax.axis_siz...]
    ppermute x15 -> x14, starting transfers between devices: 12.9 us -> 17 us  [swapped(): lax.ppermute(block, 'seq', [(i, i ^ distance) for i in range(lax.axis_siz...]
    ppermute x1, waiting for transfers between devices: 3.18 us -> 0.01 us  [rotated(): lax.ppermute(block, 'seq', [(i, (i + 1) % count) for i in range(count)])]
    unnamed x8 -> x12, local copies, waits for them, and re-layouts: 0.02 us -> 1.29 us
    pallas_call x24 -> x30, Pallas kernels: 31.3 us -> 31.3 us  [call(): pl.pallas_call(ordered, in_specs=[*in_specs, *[IN_PLACE] * len(before)],...]
  transfers between devices with their start and end apart: 16 -> 15, of which waited for: 9 -> 5; matrix products, arithmetic and copies ran while one was open for 0% -> 0% of each run, Pallas kernels for 36% -> 48%
where the time goes in v4:
time: 57.1 us; the launch traced here: 57 us
  Pallas kernels  31.3 us (55%)
  starting transfers between devices  17.5 us (31%)
  waiting for transfers between devices  6.45 us (11%)
  local copies, waits for them, and re-layouts  1.29 us (2%)
    pallas_call x30, Pallas kernels, call(): pl.pallas_call(ordered, in_specs=[*in_specs, *[IN_PLACE] * len(before)],...  31.3 us
    ppermute x14, starting transfers between devices, swapped(): lax.ppermute(block, 'seq', [(i, i ^ distance) for i in range(lax.axis_siz...  17 us
    ppermute x14, waiting for transfers between devices, swapped(): lax.ppermute(block, 'seq', [(i, i ^ distance) for i in range(lax.axis_siz...  6.45 us
    unnamed x12, local copies, waits for them, and re-layouts  1.29 us
  transfers between devices with their start and end apart: 15, of which 5 were waited for; matrix products, arithmetic and copies ran while one was open for 0% of the time, Pallas kernels for 48%

profile of v4, /device:TPU:0, one launch (start us, length us, event | category | flops | bytes accessed | tf_op | source)
XLA Modules:
  0.0 57.0 jit_solution(12573964695362872800)
XLA Ops:
  0.0 1.3 %pack_rims.1.refs_4_ = bf16[16,6144]{1,0:T(8,128)(2,1)S(1)} custom-call(bf16[256,6144]{1,0:T(8,128)(2,1)} %refs_0_.21, bf16[256,6144]{1,0:T(8,128)(2,1)} %refs_0_.13, bf16[256,6144]{1,0:T(8,128)(2,1)} %refs_1_.13), custom_call_target="tpu_custom_call" | custom-call | flops 1024 | bytes 1024 | tf_op jit(solution)/shard_map/pack_rims/pallas_call | solution.py:39
  1.3 0.5 collective-permute-start
  1.9 0.3 copy-done.2
  2.2 1.0 %copy-done.3 = bf16[256,6144]{1,0:T(8,128)(2,1)S(1)} copy-done((bf16[256,6144]{1,0:T(8,128)(2,1)S(1)}, bf16[256,6144]{1,0:T(8,128)(2,1)}, u32[]{:S(2)}) %copy-start.3) | copy-done | bytes 3145752
  3.1 3.6 %near_states.2 = (bf16[256,3072]{1,0:T(8,128)(2,1)S(1)}, bf16[256,3072]{1,0:T(8,128)(2,1)S(1)}, f32[3072,128]{1,0:T(8,128)S(1)}, bf16[16,3072]{1,0:T(8,128)(2,1)S(1)}, bf16[16,3072]{1,0:T(8,128)(2,1)S(1)}) custom-call(bf16[256,6144]{1,0:T(8,128)(2,1)S(1)} %copy-done.2, bf16[256,6144]{1,0:T(8,128)(2,1)S(1)} %copy-done.3, bf16[3,4,6144]{2,1,0:T(4,128)(2,1)S(1)} %copy-done.1, ...), custom_call_target="tpu_custom_call" | custom-call | flops 1024 | bytes 1024 | tf_op jit(solution)/shard_map/near_states/pallas_call | solution.py:39
  6.7 3.6 %near_states.3 = (bf16[256,3072]{1,0:T(8,128)(2,1)S(1)}, bf16[256,3072]{1,0:T(8,128)(2,1)S(1)}, f32[3072,128]{1,0:T(8,128)S(1)}, bf16[16,3072]{1,0:T(8,128)(2,1)S(1)}, bf16[16,3072]{1,0:T(8,128)(2,1)S(1)}) custom-call(bf16[256,6144]{1,0:T(8,128)(2,1)S(1)} %copy-done.2, bf16[256,6144]{1,0:T(8,128)(2,1)S(1)} %copy-done.3, bf16[3,4,6144]{2,1,0:T(4,128)(2,1)S(1)} %copy-done.1, ...), custom_call_target="tpu_custom_call" | custom-call | flops 1024 | bytes 1024 | tf_op jit(solution)/shard_map/near_states/pallas_call | solution.py:39
  10.4 0.7 %first_rows.4 = (bf16[16,1536]{1,0:T(8,128)(2,1)S(1)}, bf16[16,1536]{1,0:T(8,128)(2,1)S(1)}, bf16[1536,128]{1,0:T(8,128)(2,1)S(1)}) custom-call(bf16[16,3072]{1,0:T(8,128)(2,1)S(1)} %get-tuple-element.80.refs_0_, bf16[16,3072]{1,0:T(8,128)(2,1)S(1)} %get-tuple-element.76.refs_4_.refs_1_, bf16[3,4,6144]{2,1,0:T(4,128)(2,1)S(1)} %copy-done.1, ...), custom_call_target="tpu_custom_call" | custom-call | flops 1024 | bytes 1024 | tf_op jit(solution)/shard_map/first_rows/pallas_call | solution.py:39
  11.0 1.4 %collective-permute-start.2 = (bf16[1536,128]{1,0:T(8,128)(2,1)S(1)}, bf16[1536,128]{1,0:T(8,128)(2,1)S(1)}, u32[]{:S(2)}, u32[]{:S(2)}) collective-permute-start(bf16[1536,128]{1,0:T(8,128)(2,1)S(1)} %get-tuple-element.82.refs_6_), channel_id=1, source_target_pairs={{0,1},{1,0},{2,3},{3,2},{4,5},{5,4},{6,7},{7,6},{8,9},{9,8},{10,11... | collective-permute-start | bytes 1179656 | tf_op jit(solution)/shard_map/ppermute | solution.py:313
  12.5 0.6 %first_rows.5 = (bf16[16,1536]{1,0:T(8,128)(2,1)S(1)}, bf16[16,1536]{1,0:T(8,128)(2,1)S(1)}, bf16[1536,128]{1,0:T(8,128)(2,1)S(1)}) custom-call(bf16[16,3072]{1,0:T(8,128)(2,1)S(1)} %get-tuple-element.77.refs_0_, bf16[16,3072]{1,0:T(8,128)(2,1)S(1)} %get-tuple-element.78.refs_6_.refs_1_, bf16[3,4,6144]{2,1,0:T(4,128)(2,1)S(1)} %copy-done.1, ...), custom_call_target="tpu_custom_call" | custom-call | flops 1024 | bytes 1024 | tf_op jit(solution)/shard_map/first_rows/pallas_call | solution.py:39
  13.1 0.1 collective-permute-start.1
  13.2 0.7 %first_rows.6 = (bf16[16,1536]{1,0:T(8,128)(2,1)S(1)}, bf16[16,1536]{1,0:T(8,128)(2,1)S(1)}, f32[1536,128]{1,0:T(8,128)S(1)}) custom-call(bf16[16,3072]{1,0:T(8,128)(2,1)S(1)} %get-tuple-element.80.refs_0_, bf16[16,3072]{1,0:T(8,128)(2,1)S(1)} %get-tuple-element.76.refs_4_.refs_1_, bf16[3,4,6144]{2,1,0:T(4,128)(2,1)S(1)} %copy-done.1, ...), custom_call_target="tpu_custom_call" | custom-call | flops 1024 | bytes 1024 | tf_op jit(solution)/shard_map/first_rows/pallas_call | solution.py:39
  13.9 0.7 %first_rows.7 = (bf16[16,1536]{1,0:T(8,128)(2,1)S(1)}, bf16[16,1536]{1,0:T(8,128)(2,1)S(1)}, f32[1536,128]{1,0:T(8,128)S(1)}) custom-call(bf16[16,3072]{1,0:T(8,128)(2,1)S(1)} %get-tuple-element.77.refs_0_, bf16[16,3072]{1,0:T(8,128)(2,1)S(1)} %get-tuple-element.78.refs_6_.refs_1_, bf16[3,4,6144]{2,1,0:T(4,128)(2,1)S(1)} %copy-done.1, ...), custom_call_target="tpu_custom_call" | custom-call | flops 1024 | bytes 1024 | tf_op jit(solution)/shard_map/first_rows/pallas_call | solution.py:39
  14.6 2.2 %collective-permute-start.4 = (bf16[768,128]{1,0:T(8,128)(2,1)S(1)}, bf16[768,128]{1,0:T(8,128)(2,1)S(1)}, u32[]{:S(2)}, u32[]{:S(2)}) collective-permute-start(bf16[768,128]{1,0:T(8,128)(2,1)S(1)} %get-tuple-element.97), channel_id=1, source_target_pairs={{0,2},{1,3},{2,0},{3,1},{4,6},{5,7},{6,4},{7,5},{8,10},{9,11},{10,... | collective-permute-start | bytes 589832 | tf_op jit(solution)/shard_map/ppermute | solution.py:313
  16.9 0.1 collective-permute-start.3
  17.0 1.5 %within_block.8 = (bf16[256,768]{1,0:T(8,128)(2,1)S(1)}, f32[256,768]{1,0:T(8,128)S(1)}) custom-call(bf16[256,6144]{1,0:T(8,128)(2,1)S(1)} %copy-done, bf16[3,4,6144]{2,1,0:T(4,128)(2,1)S(1)} %copy-done.1, bf16[128,128]{1,0:T(8,128)(2,1)S(1)} %copy-done.4, bf16[16,6144]{1,0:T(8,128)(2,1)S(1)} %collective-permute-done.refs_4_.refs_3_, ...), custom_call_target="tpu_custom_call" | custom-call | flops 1024 | bytes 1024 | tf_op jit(solution)/shard_map/within_block/pallas_call | solution.py:39
  18.4 1.5 %within_block.9 = (bf16[256,768]{1,0:T(8,128)(2,1)S(1)}, f32[256,768]{1,0:T(8,128)S(1)}) custom-call(bf16[256,6144]{1,0:T(8,128)(2,1)S(1)} %copy-done, bf16[3,4,6144]{2,1,0:T(4,128)(2,1)S(1)} %copy-done.1, bf16[128,128]{1,0:T(8,128)(2,1)S(1)} %copy-done.4, bf16[16,6144]{1,0:T(8,128)(2,1)S(1)} %collective-permute-done.refs_4_.refs_3_, ...), custom_call_target="tpu_custom_call" | custom-call | flops 1024 | bytes 1024 | tf_op jit(solution)/shard_map/within_block/pallas_call | solution.py:39
  19.9 1.5 %within_block.10 = (bf16[256,768]{1,0:T(8,128)(2,1)S(1)}, f32[256,768]{1,0:T(8,128)S(1)}) custom-call(bf16[256,6144]{1,0:T(8,128)(2,1)S(1)} %copy-done, bf16[3,4,6144]{2,1,0:T(4,128)(2,1)S(1)} %copy-done.1, bf16[128,128]{1,0:T(8,128)(2,1)S(1)} %copy-done.4, bf16[16,6144]{1,0:T(8,128)(2,1)S(1)} %collective-permute-done.refs_4_.refs_3_, ...), custom_call_target="tpu_custom_call" | custom-call | flops 1024 | bytes 1024 | tf_op jit(solution)/shard_map/within_block/pallas_call | solution.py:39
  21.3 1.1 %collective-permute-done.4.refs_1_ = bf16[768,128]{1,0:T(8,128)(2,1)S(1)} collective-permute-done((bf16[768,128]{1,0:T(8,128)(2,1)S(1)}, bf16[768,128]{1,0:T(8,128)(2,1)S(1)}, u32[]{:S(2)}, u32[]{:S(2)}) %collective-permute-start.4) | collective-permute-done | bytes 196640 | tf_op jit(solution)/shard_map/ppermute | solution.py:313
  22.5 2.2 %collective-permute-start.6 = (bf16[768,128]{1,0:T(8,128)(2,1)S(1)}, bf16[768,128]{1,0:T(8,128)(2,1)S(1)}, u32[]{:S(2)}, u32[]{:S(2)}) collective-permute-start(bf16[768,128]{1,0:T(8,128)(2,1)S(1)} %get-tuple-element.103.refs_8_), channel_id=1, source_target_pairs={{0,4},{1,5},{2,6},{3,7},{4,0},{5,1},{6,2},{7,3},{8,12},{9,13},{10,... | collective-permute-start | bytes 589832 | tf_op jit(solution)/shard_map/ppermute | solution.py:313
  24.7 1.6 %within_block.11 = (bf16[256,768]{1,0:T(8,128)(2,1)S(1)}, f32[256,768]{1,0:T(8,128)S(1)}) custom-call(bf16[256,6144]{1,0:T(8,128)(2,1)S(1)} %copy-done, bf16[3,4,6144]{2,1,0:T(4,128)(2,1)S(1)} %copy-done.1, bf16[128,128]{1,0:T(8,128)(2,1)S(1)} %copy-done.4, bf16[16,6144]{1,0:T(8,128)(2,1)S(1)} %collective-permute-done.refs_4_.refs_3_, ...), custom_call_target="tpu_custom_call" | custom-call | flops 1024 | bytes 1024 | tf_op jit(solution)/shard_map/within_block/pallas_call | solution.py:39
  26.4 1.5 %within_block.12 = (bf16[256,768]{1,0:T(8,128)(2,1)S(1)}, f32[256,768]{1,0:T(8,128)S(1)}) custom-call(bf16[256,6144]{1,0:T(8,128)(2,1)S(1)} %copy-done, bf16[3,4,6144]{2,1,0:T(4,128)(2,1)S(1)} %copy-done.1, bf16[128,128]{1,0:T(8,128)(2,1)S(1)} %copy-done.4, bf16[16,6144]{1,0:T(8,128)(2,1)S(1)} %collective-permute-done.refs_4_.refs_3_, ...), custom_call_target="tpu_custom_call" | custom-call | flops 1024 | bytes 1024 | tf_op jit(solution)/shard_map/within_block/pallas_call | solution.py:39
  27.9 0.1 collective-permute-start.5
  28.0 0.6 collective-permute-done.6.refs_1_
  28.6 0.1 plane_sums.2
  28.7 3.1 %collective-permute-start.9 = (bf16[384,128]{1,0:T(8,128)(2,1)S(1)}, bf16[384,128]{1,0:T(8,128)(2,1)S(1)}, u32[]{:S(2)}, u32[]{:S(2)}) collective-permute-start(bf16[384,128]{1,0:T(8,128)(2,1)S(1)} %get-tuple-element.111.refs_8_), channel_id=1, source_target_pairs={{0,8},{1,9},{2,10},{3,11},{4,12},{5,13},{6,14},{7,15},{8,0},{9,1},... | collective-permute-start | bytes 294920 | tf_op jit(solution)/shard_map/ppermute | solution.py:313
  31.8 1.5 %within_block.13 = (bf16[256,768]{1,0:T(8,128)(2,1)S(1)}, f32[256,768]{1,0:T(8,128)S(1)}) custom-call(bf16[256,6144]{1,0:T(8,128)(2,1)S(1)} %copy-done, bf16[3,4,6144]{2,1,0:T(4,128)(2,1)S(1)} %copy-done.1, bf16[128,128]{1,0:T(8,128)(2,1)S(1)} %copy-done.4, bf16[16,6144]{1,0:T(8,128)(2,1)S(1)} %collective-permute-done.refs_4_.refs_3_, ...), custom_call_target="tpu_custom_call" | custom-call | flops 1024 | bytes 1024 | tf_op jit(solution)/shard_map/within_block/pallas_call | solution.py:39
  33.3 1.5 %within_block.14 = (bf16[256,768]{1,0:T(8,128)(2,1)S(1)}, f32[256,768]{1,0:T(8,128)S(1)}) custom-call(bf16[256,6144]{1,0:T(8,128)(2,1)S(1)} %copy-done, bf16[3,4,6144]{2,1,0:T(4,128)(2,1)S(1)} %copy-done.1, bf16[128,128]{1,0:T(8,128)(2,1)S(1)} %copy-done.4, bf16[16,6144]{1,0:T(8,128)(2,1)S(1)} %collective-permute-done.refs_4_.refs_3_, ...), custom_call_target="tpu_custom_call" | custom-call | flops 1024 | bytes 1024 | tf_op jit(solution)/shard_map/within_block/pallas_call | solution.py:39
  34.8 0.1 plane_sums.3
  34.9 2.0 %collective-permute-start.7 = (bf16[384,128]{1,0:T(8,128)(2,1)S(1)}, bf16[384,128]{1,0:T(8,128)(2,1)S(1)}, u32[]{:S(2)}, u32[]{:S(2)}) collective-permute-start(bf16[384,128]{1,0:T(8,128)(2,1)S(1)} %get-tuple-element.116.refs_8_), channel_id=1, source_target_pairs={{0,8},{1,9},{2,10},{3,11},{4,12},{5,13},{6,14},{7,15},{8,0},{9,1},... | collective-permute-start | bytes 294920 | tf_op jit(solution)/shard_map/ppermute | solution.py:313
  36.9 1.6 %collective-permute-start.10 = (bf16[384,128]{1,0:T(8,128)(2,1)S(1)}, bf16[384,128]{1,0:T(8,128)(2,1)S(1)}, u32[]{:S(2)}, u32[]{:S(2)}) collective-permute-start(bf16[384,128]{1,0:T(8,128)(2,1)S(1)} %collective-permute-done.9.refs_6_), channel_id=1, source_target_pairs={{0,4},{1,5},{2,6},{3,7},{4,0},{5,1},{6,2},{7,3},{8,12},{9,13},{10,... | collective-permute-start | bytes 294920 | tf_op jit(solution)/shard_map/ppermute | solution.py:313
  38.4 2.1 %collective-permute-done.7.refs_6_ = bf16[384,128]{1,0:T(8,128)(2,1)S(1)} collective-permute-done((bf16[384,128]{1,0:T(8,128)(2,1)S(1)}, bf16[384,128]{1,0:T(8,128)(2,1)S(1)}, u32[]{:S(2)}, u32[]{:S(2)}) %collective-permute-start.7) | collective-permute-done | bytes 98336 | tf_op jit(solution)/shard_map/ppermute | solution.py:313
  40.5 1.9 %collective-permute-start.8 = (bf16[384,128]{1,0:T(8,128)(2,1)S(1)}, bf16[384,128]{1,0:T(8,128)(2,1)S(1)}, u32[]{:S(2)}, u32[]{:S(2)}) collective-permute-start(bf16[384,128]{1,0:T(8,128)(2,1)S(1)} %collective-permute-done.7.refs_6_), channel_id=1, source_target_pairs={{0,4},{1,5},{2,6},{3,7},{4,0},{5,1},{6,2},{7,3},{8,12},{9,13},{10,... | collective-permute-start | bytes 294920 | tf_op jit(solution)/shard_map/ppermute | solution.py:313
  42.4 1.5 %within_block.15 = (bf16[256,768]{1,0:T(8,128)(2,1)S(1)}, f32[256,768]{1,0:T(8,128)S(1)}) custom-call(bf16[256,6144]{1,0:T(8,128)(2,1)S(1)} %copy-done, bf16[3,4,6144]{2,1,0:T(4,128)(2,1)S(1)} %copy-done.1, bf16[128,128]{1,0:T(8,128)(2,1)S(1)} %copy-done.4, bf16[16,6144]{1,0:T(8,128)(2,1)S(1)} %collective-permute-done.refs_4_.refs_3_, ...), custom_call_target="tpu_custom_call" | custom-call | flops 1024 | bytes 1024 | tf_op jit(solution)/shard_map/within_block/pallas_call | solution.py:39
  43.8 0.2 own_prefixes.2
  44.1 1.7 %collective-permute-start.12 = (bf16[768,128]{1,0:T(8,128)(2,1)S(1)}, bf16[768,128]{1,0:T(8,128)(2,1)S(1)}, u32[]{:S(2)}, u32[]{:S(2)}) collective-permute-start(bf16[768,128]{1,0:T(8,128)(2,1)S(1)} %get-tuple-element.126), channel_id=1, source_target_pairs={{0,2},{1,3},{2,0},{3,1},{4,6},{5,7},{6,4},{7,5},{8,10},{9,11},{10,... | collective-permute-start | bytes 589832 | tf_op jit(solution)/shard_map/ppermute | solution.py:313
  45.8 1.2 %finish.5 = (bf16[256,6144]{1,0:T(8,128)(2,1)}, f32[8,128]{1,0:T(8,128)S(1)}) custom-call(f32[1,6144]{1,0:T(1,128)S(1)} %bitcast.1, bf16[768,128]{1,0:T(8,128)(2,1)S(1)} %get-tuple-element.120.refs_1_, bf16[256,768]{1,0:T(8,128)(2,1)S(1)} %get-tuple-element.121.refs_2_, f32[256,768]{1,0:T(8,128)S(1)} %get-tuple-element.100.refs_8_.refs_3_, ...), custom_call_target="tpu_custom_call" | custom-call | flops 1024 | bytes 1024 | tf_op jit(solution)/shard_map/finish/pallas_call | solution.py:39
  47.0 0.2 own_prefixes.3
  47.2 0.5 collective-permute-start.11
  47.7 1.2 %finish.6 = (bf16[256,6144]{1,0:T(8,128)(2,1)}, f32[8,128]{1,0:T(8,128)S(1)}) custom-call(f32[1,6144]{1,0:T(1,128)S(1)} %bitcast.2, bf16[768,128]{1,0:T(8,128)(2,1)S(1)} %get-tuple-element.127.refs_1_, bf16[256,768]{1,0:T(8,128)(2,1)S(1)} %get-tuple-element.128.refs_2_, ...), custom_call_target="tpu_custom_call", output_to_operand_aliasing={{0}: (4, {})} | custom-call | flops 1024 | bytes 1024 | tf_op jit(solution)/shard_map/finish/pallas_call | solution.py:39
  48.9 1.6 %collective-permute-done.12.refs_0_ = bf16[768,128]{1,0:T(8,128)(2,1)S(1)} collective-permute-done((bf16[768,128]{1,0:T(8,128)(2,1)S(1)}, bf16[768,128]{1,0:T(8,128)(2,1)S(1)}, u32[]{:S(2)}, u32[]{:S(2)}) %collective-permute-start.12) | collective-permute-done | bytes 196640 | tf_op jit(solution)/shard_map/ppermute | solution.py:313
  50.5 0.1 paired_prefixes.2
  50.6 0.1 collective-permute-start.14
  50.6 1.2 %finish.7 = (bf16[256,6144]{1,0:T(8,128)(2,1)}, f32[8,128]{1,0:T(8,128)S(1)}) custom-call(f32[1,6144]{1,0:T(1,128)S(1)} %bitcast.3, bf16[768,128]{1,0:T(8,128)(2,1)S(1)} %get-tuple-element.131.refs_1_, bf16[256,768]{1,0:T(8,128)(2,1)S(1)} %get-tuple-element.132.refs_2_, ...), custom_call_target="tpu_custom_call", output_to_operand_aliasing={{0}: (4, {})} | custom-call | flops 1024 | bytes 1024 | tf_op jit(solution)/shard_map/finish/pallas_call | solution.py:39
  51.9 1.1 %collective-permute-done.11.refs_0_ = bf16[768,128]{1,0:T(8,128)(2,1)S(1)} collective-permute-done((bf16[768,128]{1,0:T(8,128)(2,1)S(1)}, bf16[768,128]{1,0:T(8,128)(2,1)S(1)}, u32[]{:S(2)}, u32[]{:S(2)}) %collective-permute-start.11) | collective-permute-done | bytes 196640 | tf_op jit(solution)/shard_map/ppermute | solution.py:313
  52.9 0.1 paired_prefixes.3
  53.0 0.1 collective-permute-start.13
  53.1 1.6 %finish.8 = (bf16[256,6144]{1,0:T(8,128)(2,1)}, f32[8,128]{1,0:T(8,128)S(1)}) custom-call(f32[1,6144]{1,0:T(1,128)S(1)} %bitcast.4, bf16[768,128]{1,0:T(8,128)(2,1)S(1)} %get-tuple-element.139.refs_1_, bf16[1536,128]{1,0:T(8,128)(2,1)S(1)} %collective-permute-done.14.refs_2_, ...), custom_call_target="tpu_custom_call", output_to_operand_aliasing={{0}: (9, {})} | custom-call | flops 1024 | bytes 1024 | tf_op jit(solution)/shard_map/finish/pallas_call | solution.py:39
  54.8 2.0 %finish.9 = (bf16[256,6144]{1,0:T(8,128)(2,1)}, f32[8,128]{1,0:T(8,128)}) custom-call(f32[1,6144]{1,0:T(1,128)S(1)} %bitcast.5, bf16[1536,128]{1,0:T(8,128)(2,1)S(1)} %collective-permute-done.13.refs_1_, bf16[256,768]{1,0:T(8,128)(2,1)S(1)} %get-tuple-element.137.refs_2_, ...), custom_call_target="tpu_custom_call", output_to_operand_aliasing={{0}: (6, {})} | custom-call | flops 1024 | bytes 1024 | tf_op jit(solution)/shard_map/finish/pallas_call | solution.py:39
  (24 shorter events, 0.3 us)
Async XLA Ops:
  0.0 2.2 %copy-start.2 = (bf16[256,6144]{1,0:T(8,128)(2,1)S(1)}, bf16[256,6144]{1,0:T(8,128)(2,1)}, u32[]{:S(2)}) copy-start(bf16[256,6144]{1,0:T(8,128)(2,1)} %refs_0_.13) | copy-start | bytes 9437188
  0.0 3.1 %copy-start.3 = (bf16[256,6144]{1,0:T(8,128)(2,1)S(1)}, bf16[256,6144]{1,0:T(8,128)(2,1)}, u32[]{:S(2)}) copy-start(bf16[256,6144]{1,0:T(8,128)(2,1)} %refs_1_.13) | copy-start | bytes 9437188
  0.0 3.1 %copy-start.1 = (bf16[3,4,6144]{2,1,0:T(4,128)(2,1)S(1)}, bf16[3,4,6144]{2,1,0:T(4,128)(2,1)}, u32[]{:S(2)}) copy-start(bf16[3,4,6144]{2,1,0:T(4,128)(2,1)} %refs_1_.21) | copy-start | bytes 442372
  0.0 3.1 %copy-start.4 = (bf16[128,128]{1,0:T(8,128)(2,1)S(1)}, bf16[128,128]{1,0:T(8,128)(2,1)}, u32[]{:S(2)}) copy-start(bf16[128,128]{1,0:T(8,128)(2,1)} %refs_2_.29) | copy-start | bytes 98308
  1.3 9.0 %collective-permute-start = (bf16[16,6144]{1,0:T(8,128)(2,1)S(1)}, bf16[16,6144]{1,0:T(8,128)(2,1)S(1)}, u32[]{:S(2)}, u32[]{:S(2)}) collective-permute-start(bf16[16,6144]{1,0:T(8,128)(2,1)S(1)} %pack_rims.1.refs_4_), channel_id=1, source_target_pairs={{0,1},{1,2},{2,3},{3,4},{4,5},{5,6},{6,7},{7,8},{8,9},{9,10},{10,1... | collective-permute-start | bytes 589832 | tf_op jit(solution)/shard_map/ppermute | solution.py:318
  11.0 3.5 %collective-permute-start.2 = (bf16[1536,128]{1,0:T(8,128)(2,1)S(1)}, bf16[1536,128]{1,0:T(8,128)(2,1)S(1)}, u32[]{:S(2)}, u32[]{:S(2)}) collective-permute-start(bf16[1536,128]{1,0:T(8,128)(2,1)S(1)} %get-tuple-element.82.refs_6_), channel_id=1, source_target_pairs={{0,1},{1,0},{2,3},{3,2},{4,5},{5,4},{6,7},{7,6},{8,9},{9,8},{10,11... | collective-permute-start | bytes 1179656 | tf_op jit(solution)/shard_map/ppermute | solution.py:313
  13.1 3.7 %collective-permute-start.1 = (bf16[1536,128]{1,0:T(8,128)(2,1)S(1)}, bf16[1536,128]{1,0:T(8,128)(2,1)S(1)}, u32[]{:S(2)}, u32[]{:S(2)}) collective-permute-start(bf16[1536,128]{1,0:T(8,128)(2,1)S(1)} %get-tuple-element.83.refs_6_), channel_id=1, source_target_pairs={{0,1},{1,0},{2,3},{3,2},{4,5},{5,4},{6,7},{7,6},{8,9},{9,8},{10,11... | collective-permute-start | bytes 1179656 | tf_op jit(solution)/shard_map/ppermute | solution.py:313
  13.9 3.1 %copy-start = (bf16[256,6144]{1,0:T(8,128)(2,1)S(1)}, bf16[256,6144]{1,0:T(8,128)(2,1)}, u32[]{:S(2)}) copy-start(bf16[256,6144]{1,0:T(8,128)(2,1)} %refs_0_.21) | copy-start | bytes 9437188
  14.6 7.8 %collective-permute-start.4 = (bf16[768,128]{1,0:T(8,128)(2,1)S(1)}, bf16[768,128]{1,0:T(8,128)(2,1)S(1)}, u32[]{:S(2)}, u32[]{:S(2)}) collective-permute-start(bf16[768,128]{1,0:T(8,128)(2,1)S(1)} %get-tuple-element.97), channel_id=1, source_target_pairs={{0,2},{1,3},{2,0},{3,1},{4,6},{5,7},{6,4},{7,5},{8,10},{9,11},{10,... | collective-permute-start | bytes 589832 | tf_op jit(solution)/shard_map/ppermute | solution.py:313
  16.9 11.0 %collective-permute-start.3 = (bf16[768,128]{1,0:T(8,128)(2,1)S(1)}, bf16[768,128]{1,0:T(8,128)(2,1)S(1)}, u32[]{:S(2)}, u32[]{:S(2)}) collective-permute-start(bf16[768,128]{1,0:T(8,128)(2,1)S(1)} %get-tuple-element.88), channel_id=1, source_target_pairs={{0,2},{1,3},{2,0},{3,1},{4,6},{5,7},{6,4},{7,5},{8,10},{9,11},{10,... | collective-permute-start | bytes 589832 | tf_op jit(solution)/shard_map/ppermute | solution.py:313
  22.5 6.0 %collective-permute-start.6 = (bf16[768,128]{1,0:T(8,128)(2,1)S(1)}, bf16[768,128]{1,0:T(8,128)(2,1)S(1)}, u32[]{:S(2)}, u32[]{:S(2)}) collective-permute-start(bf16[768,128]{1,0:T(8,128)(2,1)S(1)} %get-tuple-element.103.refs_8_), channel_id=1, source_target_pairs={{0,4},{1,5},{2,6},{3,7},{4,0},{5,1},{6,2},{7,3},{8,12},{9,13},{10,... | collective-permute-start | bytes 589832 | tf_op jit(solution)/shard_map/ppermute | solution.py:313
  27.9 6.8 %collective-permute-start.5 = (bf16[768,128]{1,0:T(8,128)(2,1)S(1)}, bf16[768,128]{1,0:T(8,128)(2,1)S(1)}, u32[]{:S(2)}, u32[]{:S(2)}) collective-permute-start(bf16[768,128]{1,0:T(8,128)(2,1)S(1)} %get-tuple-element.107.refs_2_), channel_id=1, source_target_pairs={{0,4},{1,5},{2,6},{3,7},{4,0},{5,1},{6,2},{7,3},{8,12},{9,13},{10,... | collective-permute-start | bytes 589832 | tf_op jit(solution)/shard_map/ppermute | solution.py:313
  28.7 8.2 %collective-permute-start.9 = (bf16[384,128]{1,0:T(8,128)(2,1)S(1)}, bf16[384,128]{1,0:T(8,128)(2,1)S(1)}, u32[]{:S(2)}, u32[]{:S(2)}) collective-permute-start(bf16[384,128]{1,0:T(8,128)(2,1)S(1)} %get-tuple-element.111.refs_8_), channel_id=1, source_target_pairs={{0,8},{1,9},{2,10},{3,11},{4,12},{5,13},{6,14},{7,15},{8,0},{9,1},... | collective-permute-start | bytes 294920 | tf_op jit(solution)/shard_map/ppermute | solution.py:313
  34.9 5.6 %collective-permute-start.7 = (bf16[384,128]{1,0:T(8,128)(2,1)S(1)}, bf16[384,128]{1,0:T(8,128)(2,1)S(1)}, u32[]{:S(2)}, u32[]{:S(2)}) collective-permute-start(bf16[384,128]{1,0:T(8,128)(2,1)S(1)} %get-tuple-element.116.refs_8_), channel_id=1, source_target_pairs={{0,8},{1,9},{2,10},{3,11},{4,12},{5,13},{6,14},{7,15},{8,0},{9,1},... | collective-permute-start | bytes 294920 | tf_op jit(solution)/shard_map/ppermute | solution.py:313
  36.9 7.0 %collective-permute-start.10 = (bf16[384,128]{1,0:T(8,128)(2,1)S(1)}, bf16[384,128]{1,0:T(8,128)(2,1)S(1)}, u32[]{:S(2)}, u32[]{:S(2)}) collective-permute-start(bf16[384,128]{1,0:T(8,128)(2,1)S(1)} %collective-permute-done.9.refs_6_), channel_id=1, source_target_pairs={{0,4},{1,5},{2,6},{3,7},{4,0},{5,1},{6,2},{7,3},{8,12},{9,13},{10,... | collective-permute-start | bytes 294920 | tf_op jit(solution)/shard_map/ppermute | solution.py:313
  40.5 6.5 %collective-permute-start.8 = (bf16[384,128]{1,0:T(8,128)(2,1)S(1)}, bf16[384,128]{1,0:T(8,128)(2,1)S(1)}, u32[]{:S(2)}, u32[]{:S(2)}) collective-permute-start(bf16[384,128]{1,0:T(8,128)(2,1)S(1)} %collective-permute-done.7.refs_6_), channel_id=1, source_target_pairs={{0,4},{1,5},{2,6},{3,7},{4,0},{5,1},{6,2},{7,3},{8,12},{9,13},{10,... | collective-permute-start | bytes 294920 | tf_op jit(solution)/shard_map/ppermute | solution.py:313
  43.8 1.9 %copy-start.5 = (f32[6144]{0:T(1024)S(1)}, f32[6144]{0:T(1024)}, u32[]{:S(2)}) copy-start(f32[6144]{0:T(1024)} %param.11) | copy-start | bytes 73732
  44.1 6.4 %collective-permute-start.12 = (bf16[768,128]{1,0:T(8,128)(2,1)S(1)}, bf16[768,128]{1,0:T(8,128)(2,1)S(1)}, u32[]{:S(2)}, u32[]{:S(2)}) collective-permute-start(bf16[768,128]{1,0:T(8,128)(2,1)S(1)} %get-tuple-element.126), channel_id=1, source_target_pairs={{0,2},{1,3},{2,0},{3,1},{4,6},{5,7},{6,4},{7,5},{8,10},{9,11},{10,... | collective-permute-start | bytes 589832 | tf_op jit(solution)/shard_map/ppermute | solution.py:313
  47.2 5.7 %collective-permute-start.11 = (bf16[768,128]{1,0:T(8,128)(2,1)S(1)}, bf16[768,128]{1,0:T(8,128)(2,1)S(1)}, u32[]{:S(2)}, u32[]{:S(2)}) collective-permute-start(bf16[768,128]{1,0:T(8,128)(2,1)S(1)} %get-tuple-element.124), channel_id=1, source_target_pairs={{0,2},{1,3},{2,0},{3,1},{4,6},{5,7},{6,4},{7,5},{8,10},{9,11},{10,... | collective-permute-start | bytes 589832 | tf_op jit(solution)/shard_map/ppermute | solution.py:313
  50.6 2.6 %collective-permute-start.14 = (bf16[1536,128]{1,0:T(8,128)(2,1)S(1)}, bf16[1536,128]{1,0:T(8,128)(2,1)S(1)}, u32[]{:S(2)}, u32[]{:S(2)}) collective-permute-start(bf16[1536,128]{1,0:T(8,128)(2,1)S(1)} %get-tuple-element.134.refs_5_), channel_id=1, source_target_pairs={{0,1},{1,0},{2,3},{3,2},{4,5},{5,4},{6,7},{7,6},{8,9},{9,8},{10,11... | collective-permute-start | bytes 1179656 | tf_op jit(solution)/shard_map/ppermute | solution.py:313
  53.0 1.8 %collective-permute-start.13 = (bf16[1536,128]{1,0:T(8,128)(2,1)S(1)}, bf16[1536,128]{1,0:T(8,128)(2,1)S(1)}, u32[]{:S(2)}, u32[]{:S(2)}) collective-permute-start(bf16[1536,128]{1,0:T(8,128)(2,1)S(1)} %get-tuple-element.136.refs_10_), channel_id=1, source_target_pairs={{0,1},{1,0},{2,3},{3,2},{4,5},{5,4},{6,7},{7,6},{8,9},{9,8},{10,11... | collective-permute-start | bytes 1179656 | tf_op jit(solution)/shard_map/ppermute | solution.py:313

commit v5 on v4

--- a/solution.py
+++ b/solution.py
@@ -72,9 +72,10 @@
     return max(n for n in range(1, BLOCK_HEADS + 1) if heads % n == 0)
 
 
-def pack_kernel(tap_count, query_ref, key_ref, value_ref, rim_ref, tails, sems):
-    taps = tap_count - 1
-    rows = pl.ds(query_ref.shape[0] - RIM, RIM)
+def pack_kernel(tap_count, head_dim, query_ref, key_ref, value_ref, rim_ref, tails, sems):
+    back = tap_count - 1
+    tok_count, width = query_ref.shape
+    rows = pl.ds(tok_count - RIM, RIM)
     copies = [
         pltpu.make_async_copy(ref.at[rows], tails.at[i], sems.at[i])
         for i, ref in enumerate((key_ref, value_ref, query_ref))
@@ -84,21 +85,52 @@
     for copy in copies:
         copy.wait()
     key_tail, value_tail, query_tail = (tails[i].astype(f32)[-TILE:] for i in range(3))
-    row = lax.broadcasted_iota(jnp.int32, key_tail.shape, 0)
-    first = jnp.where(row < taps, pltpu.roll(key_tail, taps, 0), pltpu.roll(value_tail, 2 * taps, 0))
-    rim_ref[...] = jnp.concatenate([first, query_tail], axis=0).astype(bf16)
-
-
-def pack_rims(query_seq, key_seq, value_seq, tap_count):
+
+    def paired(first, second):
+        row = lax.broadcasted_iota(jnp.int32, first.shape, 0)
+        return jnp.where(row < back, pltpu.roll(first, back, 0), pltpu.roll(second, 2 * back, 0))
+
+    halves = []
+    for start in (0, width // 2):
+        tiles = [paired(key_tail[:, start : start + width // 2], value_tail[:, start : start + width // 2])]
+        for at in range(start, start + width // 2, 2 * head_dim):
+            heads = query_tail[:, at : at + 2 * head_dim]
+            tiles.append(paired(heads[:, :head_dim], heads[:, head_dim:]))
+        halves.append(jnp.concatenate(tiles, axis=1))
+    rim_ref[...] = jnp.concatenate(halves, axis=0).astype(bf16)
+
+
+def pack_rims(query_seq, key_seq, value_seq, tap_count, head_dim):
     width = query_seq.shape[1]
     return kernel_call(
-        functools.partial(pack_kernel, tap_count),
+        functools.partial(pack_kernel, tap_count, head_dim),
         "pack_rims",
         [IN_PLACE] * 3,
         IN_VMEM,
-        shape((RIM, width), bf16),
+        shape((RIM, 3 * width // 4), bf16),
         [pltpu.VMEM((3, RIM, width), bf16), pltpu.SemaphoreType.DMA((3,))],
     )(in_hbm(query_seq), in_hbm(key_seq), in_hbm(value_seq))
+
+
+def rim_tile(core_rim, chip_rim, quarter, start, size):
+    device = lax.axis_index("seq")
+    upper = ((device & 1) ^ int(quarter < 2)) != 0
+    cols = columns(start, size)
+    from_core, from_chip = (ref[:, cols].astype(f32) for ref in (core_rim, chip_rim))
+    rim = jnp.where((device & 1) != 0, from_core, jnp.where(device > 0, from_chip, 0.0))
+    return jnp.where(upper, rim[TILE:], rim[:TILE])
+
+
+def state_rim(core_rim, chip_rim, quarter, width, start, size):
+    pair = ((lax.axis_index("seq") >> 1) & 1) ^ int(quarter % 2 == 0)
+    return rim_tile(core_rim, chip_rim, quarter, pair * (width // 4) + start, size)
+
+
+def query_rim(core_rim, chip_rim, quarter, width, start, head_dim):
+    pair = ((lax.axis_index("seq") >> 1) & 1) ^ int(quarter % 2 == 0)
+    head = start // head_dim
+    at = width // 2 + pair * (width // 8) + head // 2 * head_dim
+    return rim_tile(core_rim, chip_rim, quarter, at, head_dim), head % 2 + 1
 
 
 def convolved(scratch, rows, taps, rim=None, rim_end=0):
@@ -123,11 +155,6 @@
     return lax.dot_general(
         key_feat, value_conv, (((0,), (0,)), ((), ())), preferred_element_type=f32
     )
-
-
-def rim_rows(rim_ref, cols, start):
-    rim = rim_ref[:, cols].astype(f32)[start : start + TILE]
-    return jnp.where(lax.axis_index("seq") > 0, rim, 0.0)
 
 
 def near_states_kernel(
@@ -172,8 +199,51 @@
     )(key_seq, value_seq, conv_kernel, feature_map)
 
 
+def whole_states_kernel(
+    group, key_ref, value_ref, taps_ref, map_ref, core_rim, chip_rim,
+    feat_ref, conv_ref, other_ref, other_next, state_ref, scratch,
+):
+    head_dim = map_ref.shape[0]
+    width = key_ref.shape[1]
+    size = width // (4 * GROUPS)
+    back = taps_ref.shape[1] - 1
+    for quarter in range(4):
+        for start in range(0, size, head_dim):
+            natural = columns(quarter_start(quarter, width) + group * size + start, head_dim)
+            at = quarter * size + start
+            local = slice(at, at + head_dim)
+            buffers = scratch.at[at // head_dim % scratch.shape[0]]
+            taps = taps_ref[:, :, natural].astype(f32)
+            rim = state_rim(core_rim, chip_rim, quarter, width, group * size + start, head_dim)
+            key_conv = convolved(buffers.at[0], key_ref[:, natural].astype(f32), taps[1], rim, back)
+            key_feat = features(key_conv, map_ref[...])
+            feat_ref[:, local] = key_feat
+            value_conv = convolved(buffers.at[1], value_ref[:, natural].astype(f32), taps[2], rim, 2 * back)
+            conv_ref[:, local] = value_conv
+            state = state_of(key_feat, value_conv)
+            if quarter < 2:
+                (other_ref, other_next)[quarter][start : start + head_dim] = state.astype(bf16)
+            else:
+                state_ref[at - 2 * size : at - 2 * size + head_dim] = state
+
+
+def whole_states(group, key_seq, value_seq, conv_kernel, feature_map, rims):
+    tok_count, width = key_seq.shape
+    head_dim = feature_map.shape[0]
+    size = width // GROUPS
+    rows, other = shape((tok_count, size), bf16), shape((size // 4, head_dim), bf16)
+    return kernel_call(
+        functools.partial(whole_states_kernel, group),
+        "whole_states",
+        [IN_VMEM] * 6,
+        [IN_VMEM] * 5,
+        [rows, rows, other, other, shape((size // 2, head_dim), f32)],
+        [pltpu.VMEM((BLOCK_HEADS, 2, TILE + tok_count, head_dim), f32)],
+    )(key_seq, value_seq, conv_kernel, feature_map, *rims)
+
+
 def first_rows_kernel(
-    group, quarters, key_ref, value_ref, taps_ref, map_ref, rim_ref, state_ref,
+    group, quarters, key_ref, value_ref, taps_ref, map_ref, core_rim, chip_rim, state_ref,
     feat_ref, conv_ref, sum_ref, scratch,
 ):
     head_dim = map_ref.shape[0]
@@ -184,7 +254,7 @@
     for i, quarter in enumerate(quarters):
         there = slice(quarter * size, (quarter + 1) * size)
         natural = columns(quarter_start(quarter, width) + group * size, size)
-        rim = rim_rows(rim_ref, natural, 0)
+        rim = state_rim(core_rim, chip_rim, quarter, width, group * size, size)
         conv = convolved(
             scratch.at[i, 0], key_ref[:, there].astype(f32), taps_ref[1, :, natural].astype(f32), rim, back
         )
@@ -210,17 +280,17 @@
     return kernel_call(
         functools.partial(first_rows_kernel, group, quarters),
         "first_rows",
-        [IN_VMEM] * 6,
+        [IN_VMEM] * 7,
         [IN_VMEM] * 3,
         [rows, rows, shape((len(quarters) * size, head_dim), state_type)],
         [pltpu.VMEM((len(quarters), 2, TILE + RIM, size), f32)],
-    )(key_first, value_first, conv_kernel, feature_map, rims, state)
+    )(key_first, value_first, conv_kernel, feature_map, *rims, state)
 
 
 def within_kernel(
-    quarter, group, query_ref, taps_ref, map_ref, rim_ref, key_ref, value_ref, key_first, value_first,
-    feat_ref, mixed_ref, scratch,
+    quarter, group, query_ref, taps_ref, map_ref, core_rim, chip_rim, key_ref, value_ref, *rest
 ):
+    (*firsts, feat_ref, mixed_ref, scratch) = rest
     head_dim = map_ref.shape[0]
     tok_count, width = query_ref.shape
     size = width // (4 * GROUPS)
@@ -231,13 +301,16 @@
         natural = columns(quarter_start(quarter, width) + group * size + start, head_dim)
         local = slice(start, start + head_dim)
         at = slice(quarter * size + start, quarter * size + start + head_dim)
-        first = slice(quarter % 2 * size + start, quarter % 2 * size + start + head_dim)
-        key = jnp.concatenate([key_first[:, first], key_ref[RIM:, at]], axis=0)
-        value = jnp.concatenate([value_first[:, first], value_ref[RIM:, at]], axis=0)
-        rim = rim_rows(rim_ref, natural, TILE)
+        first = quarter % 2 * size * int(quarter >= 2) + start
+        first = slice(first, first + head_dim)
+        key, value = key_ref[:, at], value_ref[:, at]
+        if firsts:
+            key = jnp.concatenate([firsts[0][:, first], key[RIM:]], axis=0)
+            value = jnp.concatenate([firsts[1][:, first], value[RIM:]], axis=0)
+        rim, end = query_rim(core_rim, chip_rim, quarter, width, group * size + start, head_dim)
         taps = taps_ref[0, :, natural].astype(f32)
         buffer = scratch.at[start // head_dim % scratch.shape[0]]
-        conv = convolved(buffer, query_ref[:, natural].astype(f32), taps, rim, TILE)
+        conv = convolved(buffer, query_ref[:, natural].astype(f32), taps, rim, end * (taps_ref.shape[1] - 1))
         feat = features(conv, map_ref[...])
         feat_ref[:, local] = feat
         scores = lax.dot_general(feat, key, (((1,), (1,)), ((), ())), preferred_element_type=f32)
@@ -249,7 +322,7 @@
     tok_count, width = query_seq.shape
     head_dim = feature_map.shape[0]
     size = width // (4 * GROUPS)
-    operands = (query_seq, conv_kernel, feature_map, rims, feat, conv, *firsts)
+    operands = (query_seq, conv_kernel, feature_map, *rims, feat, conv, *firsts)
     return kernel_call(
         functools.partial(within_kernel, quarter, group),
         "within_block",
@@ -260,12 +333,13 @@
     )(*operands)
 
 
-def finish_kernel(pieces, gain_ref, *rest):
+def finish_kernel(pieces, before, gain_ref, *rest):
     count = sum(len(part) for part in pieces)
     prefixes, rest = rest[: len(pieces)], rest[len(pieces) :]
     feats, mixes = rest[:count], rest[count : 2 * count]
-    out_ref, token_ref, rows, sems = rest[-4:]
-    token_ref[...] = jnp.zeros(token_ref.shape, f32)
+    out_ref, *token, rows, sems = rest[2 * count + before :]
+    for ref in token:
+        ref[...] = jnp.zeros(ref.shape, f32)
     head_dim = prefixes[0].shape[1]
     tok_count, size = feats[0].shape
     copies = []
@@ -286,7 +360,7 @@
         copy.wait()
 
 
-def finish(pieces, mixed, prefixes, norm_gain, before):
+def finish(pieces, mixed, prefixes, norm_gain, before, last=False):
     width = norm_gain.shape[1]
     every = [piece for part in pieces for piece in part]
     count = len(every)
@@ -299,11 +373,11 @@
         operands.append(in_hbm(before))
         in_specs.append(IN_PLACE)
     return kernel_call(
-        functools.partial(finish_kernel, pieces),
+        functools.partial(finish_kernel, pieces, len(aliases)),
         "finish",
         in_specs,
-        [IN_PLACE, IN_VMEM],
-        [pltpu.HBM((tok_count, width), bf16), shape((TILE, 128), f32)],
+        [IN_PLACE, IN_VMEM][: 1 if last else 2],
+        [pltpu.HBM((tok_count, width), bf16), shape((TILE, 128), f32)][: 1 if last else 2],
         [pltpu.VMEM((count, tok_count, size), bf16), pltpu.SemaphoreType.DMA((count,))],
         aliases,
     )(*operands)[0]
@@ -313,9 +387,12 @@
     return lax.ppermute(block, "seq", [(i, i ^ distance) for i in range(lax.axis_size("seq"))])
 
 
-def rotated(block):
+def passed_on(block):
     count = lax.axis_size("seq")
-    return lax.ppermute(block, "seq", [(i, (i + 1) % count) for i in range(count)])
+    route = {i: i + 1 for i in range(1, count - 2, 2)}
+    route |= {i: i - 1 for i in range(4, count - 3, 2)}
+    route |= {0: 1, 2: 0, count - 2: count - 1, count - 1: count - 3}
+    return lax.ppermute(block, "seq", sorted(route.items()))
 
 
 def mapped(name, function, outputs, *arrays):
@@ -352,21 +429,8 @@
         return (device & 2) != 0
 
     Turn.last = ()
-    rims = rotated(pack_rims(query_seq, key_seq, value_seq, tap_count))
-    near = [near_states(g, key_seq, value_seq, conv_kernel, feature_map) for g in groups]
-    firsts, from_core = [], []
-    for g in groups:
-        *first, state_a = first_rows(
-            g, (0, 1), bf16, *near[g][3:], conv_kernel, feature_map, rims, near[g][2]
-        )
-        firsts.append([first])
-        from_core.append(swapped(state_a, 1))
-    for g in groups:
-        firsts[g].append(
-            first_rows(g, (2, 3), f32, *near[g][3:], conv_kernel, feature_map, rims, near[g][2])
-        )
-    state_b = [first[1][2] for first in firsts]
-
+    packed = pack_rims(query_seq, key_seq, value_seq, tap_count, head_dim)
+    rims = (swapped(packed, 1), passed_on(packed))
     mixed = {}
     fill = [(q, g) for q in (3, 2, 1, 0) for g in groups]
     total = len(fill)
@@ -374,15 +438,13 @@
     def score(share):
         while fill and total - len(fill) < round(share * total):
             q, g = fill.pop(0)
-            mixed[q, g] = within_block(
-                q, g, query_seq, conv_kernel, feature_map, rims, *near[g][:2], firsts[g][q // 2][:2]
-            )
-
-    def chip_sums(device, state, arrived):
-        return (
-            state[:rows] + arrived[:rows].astype(f32),
-            state[rows:] + arrived[rows:].astype(f32),
-        )
+            first = ()
+            if firsts[g]:
+                first = [part[q] for part in firsts[g][0]] if q < 2 else firsts[g][1]
+            mixed[q, g] = within_block(q, g, query_seq, conv_kernel, feature_map, rims, *near[g], first)
+
+    def chip_sums(device, state, paired, own):
+        return state[:rows] + paired.astype(f32), state[rows:] + own.astype(f32)
 
     def pair_sums(device, own, arrived):
         total = own + arrived.astype(f32)
@@ -407,7 +469,7 @@
         others = before + jnp.where(of_pair(device), 0.0, own)
         return (
             others,
-            own_part + jnp.where(of_core(device), cored[rows:].astype(f32), 0.0),
+            own_part + jnp.where(of_core(device), cored.astype(f32), 0.0),
             own_part + jnp.where(of_core(device), 0.0, state[rows:]),
         )
 
@@ -415,26 +477,48 @@
         arrived = arrived.astype(f32)
         give = arrived + jnp.where(of_core(device), 0.0, state[:rows])
         return (
-            arrived + jnp.where(of_core(device), cored[:rows].astype(f32), 0.0),
+            arrived + jnp.where(of_core(device), cored.astype(f32), 0.0),
             jnp.concatenate([give.astype(bf16), own], axis=0),
         )
 
-    chip, arriving = [None] * GROUPS, [None] * GROUPS
-    for g in groups:
-        give, chip[g] = mapped(
-            "chip_sums", chip_sums, [(rows, bf16), (rows, f32)], state_b[g], from_core[g]
-        )
-        arriving[g] = swapped(give, 2)
+    near, firsts, state_b, from_core, chip, arriving = [], [], [], [], [], []
     running, earlier, from_pair = [None] * GROUPS, [None] * GROUPS, [None] * GROUPS
     distance = 4
-    score(0.375)
-    for g in groups:
+
+    def pair_step(g):
         from_pair[g] = arriving[g]
         if distance < device_count:
             running[g], give = mapped("pair_sums", pair_sums, [(rows, f32), (rows, bf16)], chip[g], from_pair[g])
             arriving[g] = (swapped(give, distance),)
-            if g == 0:
-                score(0.625)
+
+    for g in groups:
+        if g == 0:
+            *kept, partial, key_first, value_first = near_states(g, key_seq, value_seq, conv_kernel, feature_map)
+            others, first_a = [], [[], []]
+            for q in (0, 1):
+                *first, other = first_rows(
+                    g, (q,), bf16, key_first, value_first, conv_kernel, feature_map, rims, partial
+                )
+                others.append(swapped(other, 1))
+                first_a[0].append(first[0])
+                first_a[1].append(first[1])
+            *first_b, state = first_rows(
+                g, (2, 3), f32, key_first, value_first, conv_kernel, feature_map, rims, partial
+            )
+            firsts.append((first_a, first_b))
+        else:
+            *kept, other, other_next, state = whole_states(g, key_seq, value_seq, conv_kernel, feature_map, rims)
+            others = [swapped(other, 1), swapped(other_next, 1)]
+            firsts.append(None)
+            pair_step(g - 1)
+        near.append(kept)
+        state_b.append(state)
+        from_core.append(others)
+        give, own = mapped("chip_sums", chip_sums, [(rows, bf16), (rows, f32)], state, *others)
+        chip.append(own)
+        arriving.append(swapped(give, 2))
+    score(0.375)
+    pair_step(GROUPS - 1)
     while 2 * distance < device_count:
         for g in groups:
             before = [] if distance == 4 else [earlier[g]]
@@ -448,13 +532,16 @@
             )
             arriving[g] = swapped(give, 2 * distance)
             if g == 0:
-                score(0.875)
-        arriving = [(mine, swapped(mine, distance)) for mine in arriving]
+                score(0.5)
+        for g in groups:
+            (mine,) = mapped("halves", lambda device, half: (half,), [(rows // 2, bf16)], arriving[g])
+            arriving[g] = (mine, swapped(mine, distance))
+            if g == 0:
+                score(0.75)
         distance *= 2
-    score(1)
 
     back, own_give = [None] * GROUPS, [None] * GROUPS
-    out = None
+    owns = []
     for g in groups:
         step = ()
         if distance < device_count:
@@ -465,12 +552,14 @@
             [(rows, bf16)] * 3,
             chip[g],
             from_pair[g],
-            from_core[g],
+            from_core[g][1],
             state_b[g],
             *step,
         )
         back[g] = swapped(others, 2)
-        out = finish([[(3, g)]], mixed, [own], gain, out)
+        owns.append(own)
+        score(0.75 + (1 - 0.75) * (g + 1) / GROUPS)
+    out = finish([[(3, g)] for g in groups], mixed, owns, gain, None)
     from_other = [None] * GROUPS
     for g in groups:
         prefix_2, give = mapped(
@@ -478,7 +567,7 @@
             paired_prefixes,
             [(rows, bf16), (2 * rows, bf16)],
             back[g],
-            from_core[g],
+            from_core[g][0],
             state_b[g],
             own_give[g],
         )
@@ -488,7 +577,7 @@
         else:
             pieces = [[(2, g)], [(0, g - 1), (1, g - 1)]]
             out = finish(pieces, mixed, [prefix_2, from_other[g - 1]], gain, out)
-    return finish([[(0, g), (1, g)]], mixed, [from_other[g]], gain, out)
+    return finish([[(0, g), (1, g)]], mixed, [from_other[g]], gain, out, last=True)
 
 
 def solution(mesh):

time: 57.1 us -> 55.3 us (0.968)
  Pallas kernels: 31.3 us -> 28.7 us
  local copies, waits for them, and re-layouts: 1.29 us -> 0.02 us
  starting transfers between devices: 17.5 us -> 18.6 us
  waiting for transfers between devices: 6.45 us -> 7.37 us
    pallas_call x30, Pallas kernels: 31.3 us -> 28.7 us  [call(): pl.pallas_call(ordered, in_specs=[*in_specs, *[IN_PLACE] * len(before)],...]
    unnamed x12, local copies, waits for them, and re-layouts: 1.29 us -> 0.02 us
    ppermute x14 -> x17, starting transfers between devices: 17 us -> 18.1 us  [swapped(): lax.ppermute(block, 'seq', [(i, i ^ distance) for i in range(lax.axis_siz...]
    ppermute x14 -> x17, waiting for transfers between devices: 6.45 us -> 7.37 us  [swapped(): lax.ppermute(block, 'seq', [(i, i ^ distance) for i in range(lax.axis_siz...]
  transfers between devices with their start and end apart: 15 -> 18, of which waited for: 5 -> 7; matrix products, arithmetic and copies ran while one was open for 0% -> 0% of each run, Pallas kernels for 48% -> 46%
where the time goes in v5:
time: 55.3 us; the launch traced here: 55.2 us
  Pallas kernels  28.7 us (52%)
  starting transfers between devices  18.6 us (34%)
  waiting for transfers between devices  7.37 us (13%)
    pallas_call x30, Pallas kernels, call(): pl.pallas_call(ordered, in_specs=[*in_specs, *[IN_PLACE] * len(before)],...  28.7 us
    ppermute x17, starting transfers between devices, swapped(): lax.ppermute(block, 'seq', [(i, i ^ distance) for i in range(lax.axis_siz...  18.1 us
    ppermute x17, waiting for transfers between devices, swapped(): lax.ppermute(block, 'seq', [(i, i ^ distance) for i in range(lax.axis_siz...  7.37 us
  transfers between devices with their start and end apart: 18, of which 7 were waited for; matrix products, arithmetic and copies ran while one was open for 0% of the time, Pallas kernels for 46%

profile of v5, /device:TPU:0, one launch (start us, length us, event | category | flops | bytes accessed | tf_op | source)
XLA Modules:
  0.0 55.2 jit_solution(5817909819017301177)
XLA Ops:
  0.0 1.3 %pack_rims.1.refs_4_ = bf16[16,4608]{1,0:T(8,128)(2,1)S(1)} custom-call(bf16[256,6144]{1,0:T(8,128)(2,1)} %refs_0_.21, bf16[256,6144]{1,0:T(8,128)(2,1)} %refs_0_.13, bf16[256,6144]{1,0:T(8,128)(2,1)} %refs_1_.13), custom_call_target="tpu_custom_call" | custom-call | flops 1024 | bytes 1024 | tf_op jit(solution)/shard_map/pack_rims/pallas_call | solution.py:39
  1.4 0.5 collective-permute-start.1
  1.9 2.6 %collective-permute-start = (bf16[16,4608]{1,0:T(8,128)(2,1)S(1)}, bf16[16,4608]{1,0:T(8,128)(2,1)S(1)}, u32[]{:S(2)}, u32[]{:S(2)}) collective-permute-start(bf16[16,4608]{1,0:T(8,128)(2,1)S(1)} %pack_rims.1.refs_4_), channel_id=1, source_target_pairs={{0,1},{1,0},{2,3},{3,2},{4,5},{5,4},{6,7},{7,6},{8,9},{9,8},{10,11... | collective-permute-start | bytes 442376 | tf_op jit(solution)/shard_map/ppermute | solution.py:387
  4.5 3.6 %near_states.1 = (bf16[256,3072]{1,0:T(8,128)(2,1)S(1)}, bf16[256,3072]{1,0:T(8,128)(2,1)S(1)}, f32[3072,128]{1,0:T(8,128)S(1)}, bf16[16,3072]{1,0:T(8,128)(2,1)S(1)}, bf16[16,3072]{1,0:T(8,128)(2,1)S(1)}) custom-call(bf16[256,6144]{1,0:T(8,128)(2,1)S(1)} %copy-done.1, bf16[256,6144]{1,0:T(8,128)(2,1)S(1)} %copy-done.2, bf16[3,4,6144]{2,1,0:T(4,128)(2,1)S(1)} %copy-done.3, ...), custom_call_target="tpu_custom_call" | custom-call | flops 1024 | bytes 1024 | tf_op jit(solution)/shard_map/near_states/pallas_call | solution.py:39
  8.2 0.4 first_rows.3
  8.6 0.1 collective-permute-start.2
  8.7 0.4 first_rows.4
  9.1 0.6 %collective-permute-start.3 = (bf16[768,128]{1,0:T(8,128)(2,1)S(1)}, bf16[768,128]{1,0:T(8,128)(2,1)S(1)}, u32[]{:S(2)}, u32[]{:S(2)}) collective-permute-start(bf16[768,128]{1,0:T(8,128)(2,1)S(1)} %get-tuple-element.74.refs_7_), channel_id=1, source_target_pairs={{0,1},{1,0},{2,3},{3,2},{4,5},{5,4},{6,7},{7,6},{8,9},{9,8},{10,11... | collective-permute-start | bytes 589832 | tf_op jit(solution)/shard_map/ppermute | solution.py:387
  9.6 0.7 %first_rows.5 = (bf16[16,1536]{1,0:T(8,128)(2,1)S(1)}, bf16[16,1536]{1,0:T(8,128)(2,1)S(1)}, f32[1536,128]{1,0:T(8,128)S(1)}) custom-call(bf16[16,3072]{1,0:T(8,128)(2,1)S(1)} %get-tuple-element.70.refs_0_, bf16[16,3072]{1,0:T(8,128)(2,1)S(1)} %get-tuple-element.71.refs_1_.refs_7_, bf16[3,4,6144]{2,1,0:T(4,128)(2,1)S(1)} %copy-done.3, ...), custom_call_target="tpu_custom_call" | custom-call | flops 1024 | bytes 1024 | tf_op jit(solution)/shard_map/first_rows/pallas_call | solution.py:39
  10.3 0.4 collective-permute-done.3.refs_2_
  10.8 2.5 %collective-permute-start.6 = (bf16[768,128]{1,0:T(8,128)(2,1)S(1)}, bf16[768,128]{1,0:T(8,128)(2,1)S(1)}, u32[]{:S(2)}, u32[]{:S(2)}) collective-permute-start(bf16[768,128]{1,0:T(8,128)(2,1)S(1)} %get-tuple-element.80), channel_id=1, source_target_pairs={{0,2},{1,3},{2,0},{3,1},{4,6},{5,7},{6,4},{7,5},{8,10},{9,11},{10,... | collective-permute-start | bytes 589832 | tf_op jit(solution)/shard_map/ppermute | solution.py:387
  13.2 3.6 %whole_states.1 = (bf16[256,3072]{1,0:T(8,128)(2,1)S(1)}, bf16[256,3072]{1,0:T(8,128)(2,1)S(1)}, bf16[768,128]{1,0:T(8,128)(2,1)S(1)}, bf16[768,128]{1,0:T(8,128)(2,1)S(1)}, f32[1536,128]{1,0:T(8,128)S(1)}) custom-call(bf16[256,6144]{1,0:T(8,128)(2,1)S(1)} %copy-done.1, bf16[256,6144]{1,0:T(8,128)(2,1)S(1)} %copy-done.2, bf16[3,4,6144]{2,1,0:T(4,128)(2,1)S(1)} %copy-done.3, ...), custom_call_target="tpu_custom_call" | custom-call | flops 1024 | bytes 1024 | tf_op jit(solution)/shard_map/whole_states/pallas_call | solution.py:39
  16.8 0.1 collective-permute-start.4
  17.0 0.4 collective-permute-start.5
  17.4 1.2 %collective-permute-done.6.refs_1_ = bf16[768,128]{1,0:T(8,128)(2,1)S(1)} collective-permute-done((bf16[768,128]{1,0:T(8,128)(2,1)S(1)}, bf16[768,128]{1,0:T(8,128)(2,1)S(1)}, u32[]{:S(2)}, u32[]{:S(2)}) %collective-permute-start.6) | collective-permute-done | bytes 196640 | tf_op jit(solution)/shard_map/ppermute | solution.py:387
  18.8 1.8 %collective-permute-start.7 = (bf16[768,128]{1,0:T(8,128)(2,1)S(1)}, bf16[768,128]{1,0:T(8,128)(2,1)S(1)}, u32[]{:S(2)}, u32[]{:S(2)}) collective-permute-start(bf16[768,128]{1,0:T(8,128)(2,1)S(1)} %get-tuple-element.83), channel_id=1, source_target_pairs={{0,2},{1,3},{2,0},{3,1},{4,6},{5,7},{6,4},{7,5},{8,10},{9,11},{10,... | collective-permute-start | bytes 589832 | tf_op jit(solution)/shard_map/ppermute | solution.py:387
  20.6 1.6 %collective-permute-start.9 = (bf16[768,128]{1,0:T(8,128)(2,1)S(1)}, bf16[768,128]{1,0:T(8,128)(2,1)S(1)}, u32[]{:S(2)}, u32[]{:S(2)}) collective-permute-start(bf16[768,128]{1,0:T(8,128)(2,1)S(1)} %get-tuple-element.81.refs_3_), channel_id=1, source_target_pairs={{0,4},{1,5},{2,6},{3,7},{4,0},{5,1},{6,2},{7,3},{8,12},{9,13},{10,... | collective-permute-start | bytes 589832 | tf_op jit(solution)/shard_map/ppermute | solution.py:387
  22.2 1.5 %within_block.8 = (bf16[256,768]{1,0:T(8,128)(2,1)S(1)}, f32[256,768]{1,0:T(8,128)S(1)}) custom-call(bf16[256,6144]{1,0:T(8,128)(2,1)S(1)} %copy-done, bf16[3,4,6144]{2,1,0:T(4,128)(2,1)S(1)} %copy-done.3, bf16[128,128]{1,0:T(8,128)(2,1)S(1)} %copy-done.4, bf16[16,4608]{1,0:T(8,128)(2,1)S(1)} %collective-permute-done.refs_4_.refs_3_, ...), custom_call_target="tpu_custom_call" | custom-call | flops 1024 | bytes 1024 | tf_op jit(solution)/shard_map/within_block/pallas_call | solution.py:39
  23.7 1.5 %within_block.9 = (bf16[256,768]{1,0:T(8,128)(2,1)S(1)}, f32[256,768]{1,0:T(8,128)S(1)}) custom-call(bf16[256,6144]{1,0:T(8,128)(2,1)S(1)} %copy-done, bf16[3,4,6144]{2,1,0:T(4,128)(2,1)S(1)} %copy-done.3, bf16[128,128]{1,0:T(8,128)(2,1)S(1)} %copy-done.4, bf16[16,4608]{1,0:T(8,128)(2,1)S(1)} %collective-permute-done.refs_4_.refs_3_, ...), custom_call_target="tpu_custom_call" | custom-call | flops 1024 | bytes 1024 | tf_op jit(solution)/shard_map/within_block/pallas_call | solution.py:39
  25.1 1.5 %within_block.10 = (bf16[256,768]{1,0:T(8,128)(2,1)S(1)}, f32[256,768]{1,0:T(8,128)S(1)}) custom-call(bf16[256,6144]{1,0:T(8,128)(2,1)S(1)} %copy-done, bf16[3,4,6144]{2,1,0:T(4,128)(2,1)S(1)} %copy-done.3, bf16[128,128]{1,0:T(8,128)(2,1)S(1)} %copy-done.4, bf16[16,4608]{1,0:T(8,128)(2,1)S(1)} %collective-permute-done.refs_4_.refs_3_, ...), custom_call_target="tpu_custom_call" | custom-call | flops 1024 | bytes 1024 | tf_op jit(solution)/shard_map/within_block/pallas_call | solution.py:39
  26.7 0.8 %collective-permute-start.8 = (bf16[768,128]{1,0:T(8,128)(2,1)S(1)}, bf16[768,128]{1,0:T(8,128)(2,1)S(1)}, u32[]{:S(2)}, u32[]{:S(2)}) collective-permute-start(bf16[768,128]{1,0:T(8,128)(2,1)S(1)} %get-tuple-element.94.refs_2_), channel_id=1, source_target_pairs={{0,4},{1,5},{2,6},{3,7},{4,0},{5,1},{6,2},{7,3},{8,12},{9,13},{10,... | collective-permute-start | bytes 589832 | tf_op jit(solution)/shard_map/ppermute | solution.py:387
  27.5 0.1 plane_sums.2
  27.6 2.3 %collective-permute-start.11 = (bf16[384,128]{1,0:T(8,128)(2,1)S(1)}, bf16[384,128]{1,0:T(8,128)(2,1)S(1)}, u32[]{:S(2)}, u32[]{:S(2)}) collective-permute-start(bf16[384,128]{1,0:T(8,128)(2,1)S(1)} %get-tuple-element.96.refs_7_), channel_id=1, source_target_pairs={{0,8},{1,9},{2,10},{3,11},{4,12},{5,13},{6,14},{7,15},{8,0},{9,1},... | collective-permute-start | bytes 294920 | tf_op jit(solution)/shard_map/ppermute | solution.py:387
  30.0 1.6 %within_block.11 = (bf16[256,768]{1,0:T(8,128)(2,1)S(1)}, f32[256,768]{1,0:T(8,128)S(1)}) custom-call(bf16[256,6144]{1,0:T(8,128)(2,1)S(1)} %copy-done, bf16[3,4,6144]{2,1,0:T(4,128)(2,1)S(1)} %copy-done.3, bf16[128,128]{1,0:T(8,128)(2,1)S(1)} %copy-done.4, bf16[16,4608]{1,0:T(8,128)(2,1)S(1)} %collective-permute-done.refs_4_.refs_3_, ...), custom_call_target="tpu_custom_call" | custom-call | flops 1024 | bytes 1024 | tf_op jit(solution)/shard_map/within_block/pallas_call | solution.py:39
  31.6 3.0 %collective-permute-done.8.refs_1_ = bf16[768,128]{1,0:T(8,128)(2,1)S(1)} collective-permute-done((bf16[768,128]{1,0:T(8,128)(2,1)S(1)}, bf16[768,128]{1,0:T(8,128)(2,1)S(1)}, u32[]{:S(2)}, u32[]{:S(2)}) %collective-permute-start.8) | collective-permute-done | bytes 196640 | tf_op jit(solution)/shard_map/ppermute | solution.py:387
  34.7 0.1 plane_sums.3
  34.8 1.1 %collective-permute-start.10 = (bf16[384,128]{1,0:T(8,128)(2,1)S(1)}, bf16[384,128]{1,0:T(8,128)(2,1)S(1)}, u32[]{:S(2)}, u32[]{:S(2)}) collective-permute-start(bf16[384,128]{1,0:T(8,128)(2,1)S(1)} %get-tuple-element.100.refs_1_), channel_id=1, source_target_pairs={{0,8},{1,9},{2,10},{3,11},{4,12},{5,13},{6,14},{7,15},{8,0},{9,1},... | collective-permute-start | bytes 294920 | tf_op jit(solution)/shard_map/ppermute | solution.py:387
  35.8 2.1 %collective-permute-start.13 = (bf16[384,128]{1,0:T(8,128)(2,1)S(1)}, bf16[384,128]{1,0:T(8,128)(2,1)S(1)}, u32[]{:S(2)}, u32[]{:S(2)}) collective-permute-start(bf16[384,128]{1,0:T(8,128)(2,1)S(1)} %halves.2.refs_9_.refs_6_), channel_id=1, source_target_pairs={{0,4},{1,5},{2,6},{3,7},{4,0},{5,1},{6,2},{7,3},{8,12},{9,13},{10,... | collective-permute-start | bytes 294920 | tf_op jit(solution)/shard_map/ppermute | solution.py:387
  37.9 1.5 %within_block.12 = (bf16[256,768]{1,0:T(8,128)(2,1)S(1)}, f32[256,768]{1,0:T(8,128)S(1)}) custom-call(bf16[256,6144]{1,0:T(8,128)(2,1)S(1)} %copy-done, bf16[3,4,6144]{2,1,0:T(4,128)(2,1)S(1)} %copy-done.3, bf16[128,128]{1,0:T(8,128)(2,1)S(1)} %copy-done.4, bf16[16,4608]{1,0:T(8,128)(2,1)S(1)} %collective-permute-done.refs_4_.refs_3_, ...), custom_call_target="tpu_custom_call" | custom-call | flops 1024 | bytes 1024 | tf_op jit(solution)/shard_map/within_block/pallas_call | solution.py:39
  39.4 1.5 %within_block.13 = (bf16[256,768]{1,0:T(8,128)(2,1)S(1)}, f32[256,768]{1,0:T(8,128)S(1)}) custom-call(bf16[256,6144]{1,0:T(8,128)(2,1)S(1)} %copy-done, bf16[3,4,6144]{2,1,0:T(4,128)(2,1)S(1)} %copy-done.3, bf16[128,128]{1,0:T(8,128)(2,1)S(1)} %copy-done.4, bf16[16,4608]{1,0:T(8,128)(2,1)S(1)} %collective-permute-done.refs_4_.refs_3_, ...), custom_call_target="tpu_custom_call" | custom-call | flops 1024 | bytes 1024 | tf_op jit(solution)/shard_map/within_block/pallas_call | solution.py:39
  40.9 0.2 collective-permute-done.10.refs_0_
  41.1 0.1 collective-permute-start.12
  41.1 0.9 %collective-permute-done.13.refs_7_ = bf16[384,128]{1,0:T(8,128)(2,1)S(1)} collective-permute-done((bf16[384,128]{1,0:T(8,128)(2,1)S(1)}, bf16[384,128]{1,0:T(8,128)(2,1)S(1)}, u32[]{:S(2)}, u32[]{:S(2)}) %collective-permute-start.13) | collective-permute-done | bytes 98336 | tf_op jit(solution)/shard_map/ppermute | solution.py:387
  42.1 0.2 own_prefixes.2
  42.3 1.0 %collective-permute-start.15 = (bf16[768,128]{1,0:T(8,128)(2,1)S(1)}, bf16[768,128]{1,0:T(8,128)(2,1)S(1)}, u32[]{:S(2)}, u32[]{:S(2)}) collective-permute-start(bf16[768,128]{1,0:T(8,128)(2,1)S(1)} %get-tuple-element.113), channel_id=1, source_target_pairs={{0,2},{1,3},{2,0},{3,1},{4,6},{5,7},{6,4},{7,5},{8,10},{9,11},{10,... | collective-permute-start | bytes 589832 | tf_op jit(solution)/shard_map/ppermute | solution.py:387
  43.2 1.5 %within_block.14 = (bf16[256,768]{1,0:T(8,128)(2,1)S(1)}, f32[256,768]{1,0:T(8,128)S(1)}) custom-call(bf16[256,6144]{1,0:T(8,128)(2,1)S(1)} %copy-done, bf16[3,4,6144]{2,1,0:T(4,128)(2,1)S(1)} %copy-done.3, bf16[128,128]{1,0:T(8,128)(2,1)S(1)} %copy-done.4, bf16[16,4608]{1,0:T(8,128)(2,1)S(1)} %collective-permute-done.refs_4_.refs_3_, ...), custom_call_target="tpu_custom_call" | custom-call | flops 1024 | bytes 1024 | tf_op jit(solution)/shard_map/within_block/pallas_call | solution.py:39
  44.7 1.0 %collective-permute-done.12.refs_7_ = bf16[384,128]{1,0:T(8,128)(2,1)S(1)} collective-permute-done((bf16[384,128]{1,0:T(8,128)(2,1)S(1)}, bf16[384,128]{1,0:T(8,128)(2,1)S(1)}, u32[]{:S(2)}, u32[]{:S(2)}) %collective-permute-start.12) | collective-permute-done | bytes 98336 | tf_op jit(solution)/shard_map/ppermute | solution.py:387
  45.7 0.2 own_prefixes.3
  46.0 0.9 %collective-permute-start.14 = (bf16[768,128]{1,0:T(8,128)(2,1)S(1)}, bf16[768,128]{1,0:T(8,128)(2,1)S(1)}, u32[]{:S(2)}, u32[]{:S(2)}) collective-permute-start(bf16[768,128]{1,0:T(8,128)(2,1)S(1)} %get-tuple-element.111), channel_id=1, source_target_pairs={{0,2},{1,3},{2,0},{3,1},{4,6},{5,7},{6,4},{7,5},{8,10},{9,11},{10,... | collective-permute-start | bytes 589832 | tf_op jit(solution)/shard_map/ppermute | solution.py:387
  46.9 1.5 %within_block.15 = (bf16[256,768]{1,0:T(8,128)(2,1)S(1)}, f32[256,768]{1,0:T(8,128)S(1)}) custom-call(bf16[256,6144]{1,0:T(8,128)(2,1)S(1)} %copy-done, bf16[3,4,6144]{2,1,0:T(4,128)(2,1)S(1)} %copy-done.3, bf16[128,128]{1,0:T(8,128)(2,1)S(1)} %copy-done.4, bf16[16,4608]{1,0:T(8,128)(2,1)S(1)} %collective-permute-done.refs_4_.refs_3_, ...), custom_call_target="tpu_custom_call" | custom-call | flops 1024 | bytes 1024 | tf_op jit(solution)/shard_map/within_block/pallas_call | solution.py:39
  48.4 1.4 %finish.4 = (bf16[256,6144]{1,0:T(8,128)(2,1)}, f32[8,128]{1,0:T(8,128)S(1)}) custom-call(f32[1,6144]{1,0:T(1,128)S(1)} %bitcast.1, bf16[768,128]{1,0:T(8,128)(2,1)S(1)} %get-tuple-element.114.refs_1_, bf16[768,128]{1,0:T(8,128)(2,1)S(1)} %get-tuple-element.115.refs_2_, bf16[256,768]{1,0:T(8,128)(2,1)S(1)} %get-tuple-element.116.refs_3_, ...), custom_call_target="tpu_custom_call" | custom-call | flops 1024 | bytes 1024 | tf_op jit(solution)/shard_map/finish/pallas_call | solution.py:39
  49.8 0.1 paired_prefixes.2
  50.0 1.2 %finish.5 = (bf16[256,6144]{1,0:T(8,128)(2,1)}, f32[8,128]{1,0:T(8,128)S(1)}) custom-call(f32[1,6144]{1,0:T(1,128)S(1)} %bitcast.2, bf16[768,128]{1,0:T(8,128)(2,1)S(1)} %get-tuple-element.120.refs_1_, bf16[256,768]{1,0:T(8,128)(2,1)S(1)} %get-tuple-element.121.refs_2_, ...), custom_call_target="tpu_custom_call", output_to_operand_aliasing={{0}: (4, {})} | custom-call | flops 1024 | bytes 1024 | tf_op jit(solution)/shard_map/finish/pallas_call | solution.py:39
  51.2 0.5 collective-permute-done.14.refs_0_
  51.7 0.1 paired_prefixes.3
  51.8 0.1 collective-permute-start.16
  51.9 1.6 %finish.6 = (bf16[256,6144]{1,0:T(8,128)(2,1)}, f32[8,128]{1,0:T(8,128)S(1)}) custom-call(f32[1,6144]{1,0:T(1,128)S(1)} %bitcast.3, bf16[768,128]{1,0:T(8,128)(2,1)S(1)} %get-tuple-element.128.refs_1_, bf16[1536,128]{1,0:T(8,128)(2,1)S(1)} %collective-permute-done.17.refs_2_, ...), custom_call_target="tpu_custom_call", output_to_operand_aliasing={{0}: (9, {})} | custom-call | flops 1024 | bytes 1024 | tf_op jit(solution)/shard_map/finish/pallas_call | solution.py:39
  53.6 1.4 %finish.7 = bf16[256,6144]{1,0:T(8,128)(2,1)} custom-call(f32[1,6144]{1,0:T(1,128)S(1)} %bitcast.4, bf16[1536,128]{1,0:T(8,128)(2,1)S(1)} %collective-permute-done.16.refs_1_, bf16[256,768]{1,0:T(8,128)(2,1)S(1)} %get-tuple-element.126.refs_2_, bf16[256,768]{1,0:T(8,128)(2,1)S(1)} %get-tuple-element.127.refs_3_, ...), custom_call_target="tpu_custom_call", output_to_operand_aliasing={{}: (6, {})} | custom-call | flops 1024 | bytes 1024 | tf_op jit(solution)/shard_map/finish/pallas_call | solution.py:39
  (30 shorter events, 0.4 us)
Async XLA Ops:
  0.0 4.5 %copy-start.2 = (bf16[256,6144]{1,0:T(8,128)(2,1)S(1)}, bf16[256,6144]{1,0:T(8,128)(2,1)}, u32[]{:S(2)}) copy-start(bf16[256,6144]{1,0:T(8,128)(2,1)} %refs_1_.13) | copy-start | bytes 9437188
  0.0 4.5 %copy-start.1 = (bf16[256,6144]{1,0:T(8,128)(2,1)S(1)}, bf16[256,6144]{1,0:T(8,128)(2,1)}, u32[]{:S(2)}) copy-start(bf16[256,6144]{1,0:T(8,128)(2,1)} %refs_0_.13) | copy-start | bytes 9437188
  0.0 4.5 %copy-start.4 = (bf16[128,128]{1,0:T(8,128)(2,1)S(1)}, bf16[128,128]{1,0:T(8,128)(2,1)}, u32[]{:S(2)}) copy-start(bf16[128,128]{1,0:T(8,128)(2,1)} %refs_2_.27) | copy-start | bytes 98308
  0.0 4.5 %copy-start.3 = (bf16[3,4,6144]{2,1,0:T(4,128)(2,1)S(1)}, bf16[3,4,6144]{2,1,0:T(4,128)(2,1)}, u32[]{:S(2)}) copy-start(bf16[3,4,6144]{2,1,0:T(4,128)(2,1)} %refs_1_.21) | copy-start | bytes 442372
  1.4 6.8 %collective-permute-start.1 = (bf16[16,4608]{1,0:T(8,128)(2,1)S(1)}, bf16[16,4608]{1,0:T(8,128)(2,1)S(1)}, u32[]{:S(2)}, u32[]{:S(2)}) collective-permute-start(bf16[16,4608]{1,0:T(8,128)(2,1)S(1)} %pack_rims.1.refs_4_), channel_id=1, source_target_pairs={{0,1},{1,2},{2,0},{3,4},{4,3},{5,6},{6,5},{7,8},{8,7},{9,10},{10,9... | collective-permute-start | bytes 442376 | tf_op jit(solution)/shard_map/ppermute | solution.py:395
  1.9 6.3 %collective-permute-start = (bf16[16,4608]{1,0:T(8,128)(2,1)S(1)}, bf16[16,4608]{1,0:T(8,128)(2,1)S(1)}, u32[]{:S(2)}, u32[]{:S(2)}) collective-permute-start(bf16[16,4608]{1,0:T(8,128)(2,1)S(1)} %pack_rims.1.refs_4_), channel_id=1, source_target_pairs={{0,1},{1,0},{2,3},{3,2},{4,5},{5,4},{6,7},{7,6},{8,9},{9,8},{10,11... | collective-permute-start | bytes 442376 | tf_op jit(solution)/shard_map/ppermute | solution.py:387
  8.6 1.7 %collective-permute-start.2 = (bf16[768,128]{1,0:T(8,128)(2,1)S(1)}, bf16[768,128]{1,0:T(8,128)(2,1)S(1)}, u32[]{:S(2)}, u32[]{:S(2)}) collective-permute-start(bf16[768,128]{1,0:T(8,128)(2,1)S(1)} %get-tuple-element.73.refs_7_), channel_id=1, source_target_pairs={{0,1},{1,0},{2,3},{3,2},{4,5},{5,4},{6,7},{7,6},{8,9},{9,8},{10,11... | collective-permute-start | bytes 589832 | tf_op jit(solution)/shard_map/ppermute | solution.py:387
  9.1 1.6 %collective-permute-start.3 = (bf16[768,128]{1,0:T(8,128)(2,1)S(1)}, bf16[768,128]{1,0:T(8,128)(2,1)S(1)}, u32[]{:S(2)}, u32[]{:S(2)}) collective-permute-start(bf16[768,128]{1,0:T(8,128)(2,1)S(1)} %get-tuple-element.74.refs_7_), channel_id=1, source_target_pairs={{0,1},{1,0},{2,3},{3,2},{4,5},{5,4},{6,7},{7,6},{8,9},{9,8},{10,11... | collective-permute-start | bytes 589832 | tf_op jit(solution)/shard_map/ppermute | solution.py:387
  10.8 7.9 %collective-permute-start.6 = (bf16[768,128]{1,0:T(8,128)(2,1)S(1)}, bf16[768,128]{1,0:T(8,128)(2,1)S(1)}, u32[]{:S(2)}, u32[]{:S(2)}) collective-permute-start(bf16[768,128]{1,0:T(8,128)(2,1)S(1)} %get-tuple-element.80), channel_id=1, source_target_pairs={{0,2},{1,3},{2,0},{3,1},{4,6},{5,7},{6,4},{7,5},{8,10},{9,11},{10,... | collective-permute-start | bytes 589832 | tf_op jit(solution)/shard_map/ppermute | solution.py:387
  13.2 9.0 %copy-start = (bf16[256,6144]{1,0:T(8,128)(2,1)S(1)}, bf16[256,6144]{1,0:T(8,128)(2,1)}, u32[]{:S(2)}) copy-start(bf16[256,6144]{1,0:T(8,128)(2,1)} %refs_0_.21) | copy-start | bytes 9437188
  16.8 1.9 %collective-permute-start.4 = (bf16[768,128]{1,0:T(8,128)(2,1)S(1)}, bf16[768,128]{1,0:T(8,128)(2,1)S(1)}, u32[]{:S(2)}, u32[]{:S(2)}) collective-permute-start(bf16[768,128]{1,0:T(8,128)(2,1)S(1)} %get-tuple-element.78), channel_id=1, source_target_pairs={{0,1},{1,0},{2,3},{3,2},{4,5},{5,4},{6,7},{7,6},{8,9},{9,8},{10,11... | collective-permute-start | bytes 589832 | tf_op jit(solution)/shard_map/ppermute | solution.py:387
  17.0 1.7 %collective-permute-start.5 = (bf16[768,128]{1,0:T(8,128)(2,1)S(1)}, bf16[768,128]{1,0:T(8,128)(2,1)S(1)}, u32[]{:S(2)}, u32[]{:S(2)}) collective-permute-start(bf16[768,128]{1,0:T(8,128)(2,1)S(1)} %get-tuple-element.79), channel_id=1, source_target_pairs={{0,1},{1,0},{2,3},{3,2},{4,5},{5,4},{6,7},{7,6},{8,9},{9,8},{10,11... | collective-permute-start | bytes 589832 | tf_op jit(solution)/shard_map/ppermute | solution.py:387
  18.8 7.8 %collective-permute-start.7 = (bf16[768,128]{1,0:T(8,128)(2,1)S(1)}, bf16[768,128]{1,0:T(8,128)(2,1)S(1)}, u32[]{:S(2)}, u32[]{:S(2)}) collective-permute-start(bf16[768,128]{1,0:T(8,128)(2,1)S(1)} %get-tuple-element.83), channel_id=1, source_target_pairs={{0,2},{1,3},{2,0},{3,1},{4,6},{5,7},{6,4},{7,5},{8,10},{9,11},{10,... | collective-permute-start | bytes 589832 | tf_op jit(solution)/shard_map/ppermute | solution.py:387
  20.6 6.9 %collective-permute-start.9 = (bf16[768,128]{1,0:T(8,128)(2,1)S(1)}, bf16[768,128]{1,0:T(8,128)(2,1)S(1)}, u32[]{:S(2)}, u32[]{:S(2)}) collective-permute-start(bf16[768,128]{1,0:T(8,128)(2,1)S(1)} %get-tuple-element.81.refs_3_), channel_id=1, source_target_pairs={{0,4},{1,5},{2,6},{3,7},{4,0},{5,1},{6,2},{7,3},{8,12},{9,13},{10,... | collective-permute-start | bytes 589832 | tf_op jit(solution)/shard_map/ppermute | solution.py:387
  26.7 8.0 %collective-permute-start.8 = (bf16[768,128]{1,0:T(8,128)(2,1)S(1)}, bf16[768,128]{1,0:T(8,128)(2,1)S(1)}, u32[]{:S(2)}, u32[]{:S(2)}) collective-permute-start(bf16[768,128]{1,0:T(8,128)(2,1)S(1)} %get-tuple-element.94.refs_2_), channel_id=1, source_target_pairs={{0,4},{1,5},{2,6},{3,7},{4,0},{5,1},{6,2},{7,3},{8,12},{9,13},{10,... | collective-permute-start | bytes 589832 | tf_op jit(solution)/shard_map/ppermute | solution.py:387
  27.6 8.2 %collective-permute-start.11 = (bf16[384,128]{1,0:T(8,128)(2,1)S(1)}, bf16[384,128]{1,0:T(8,128)(2,1)S(1)}, u32[]{:S(2)}, u32[]{:S(2)}) collective-permute-start(bf16[384,128]{1,0:T(8,128)(2,1)S(1)} %get-tuple-element.96.refs_7_), channel_id=1, source_target_pairs={{0,8},{1,9},{2,10},{3,11},{4,12},{5,13},{6,14},{7,15},{8,0},{9,1},... | collective-permute-start | bytes 294920 | tf_op jit(solution)/shard_map/ppermute | solution.py:387
  34.8 6.3 %collective-permute-start.10 = (bf16[384,128]{1,0:T(8,128)(2,1)S(1)}, bf16[384,128]{1,0:T(8,128)(2,1)S(1)}, u32[]{:S(2)}, u32[]{:S(2)}) collective-permute-start(bf16[384,128]{1,0:T(8,128)(2,1)S(1)} %get-tuple-element.100.refs_1_), channel_id=1, source_target_pairs={{0,8},{1,9},{2,10},{3,11},{4,12},{5,13},{6,14},{7,15},{8,0},{9,1},... | collective-permute-start | bytes 294920 | tf_op jit(solution)/shard_map/ppermute | solution.py:387
  35.8 6.2 %collective-permute-start.13 = (bf16[384,128]{1,0:T(8,128)(2,1)S(1)}, bf16[384,128]{1,0:T(8,128)(2,1)S(1)}, u32[]{:S(2)}, u32[]{:S(2)}) collective-permute-start(bf16[384,128]{1,0:T(8,128)(2,1)S(1)} %halves.2.refs_9_.refs_6_), channel_id=1, source_target_pairs={{0,4},{1,5},{2,6},{3,7},{4,0},{5,1},{6,2},{7,3},{8,12},{9,13},{10,... | collective-permute-start | bytes 294920 | tf_op jit(solution)/shard_map/ppermute | solution.py:387
  41.1 4.7 %collective-permute-start.12 = (bf16[384,128]{1,0:T(8,128)(2,1)S(1)}, bf16[384,128]{1,0:T(8,128)(2,1)S(1)}, u32[]{:S(2)}, u32[]{:S(2)}) collective-permute-start(bf16[384,128]{1,0:T(8,128)(2,1)S(1)} %halves.3.refs_8_.refs_6_), channel_id=1, source_target_pairs={{0,4},{1,5},{2,6},{3,7},{4,0},{5,1},{6,2},{7,3},{8,12},{9,13},{10,... | collective-permute-start | bytes 294920 | tf_op jit(solution)/shard_map/ppermute | solution.py:387
  42.3 7.5 %collective-permute-start.15 = (bf16[768,128]{1,0:T(8,128)(2,1)S(1)}, bf16[768,128]{1,0:T(8,128)(2,1)S(1)}, u32[]{:S(2)}, u32[]{:S(2)}) collective-permute-start(bf16[768,128]{1,0:T(8,128)(2,1)S(1)} %get-tuple-element.113), channel_id=1, source_target_pairs={{0,2},{1,3},{2,0},{3,1},{4,6},{5,7},{6,4},{7,5},{8,10},{9,11},{10,... | collective-permute-start | bytes 589832 | tf_op jit(solution)/shard_map/ppermute | solution.py:387
  46.0 5.7 %collective-permute-start.14 = (bf16[768,128]{1,0:T(8,128)(2,1)S(1)}, bf16[768,128]{1,0:T(8,128)(2,1)S(1)}, u32[]{:S(2)}, u32[]{:S(2)}) collective-permute-start(bf16[768,128]{1,0:T(8,128)(2,1)S(1)} %get-tuple-element.111), channel_id=1, source_target_pairs={{0,2},{1,3},{2,0},{3,1},{4,6},{5,7},{6,4},{7,5},{8,10},{9,11},{10,... | collective-permute-start | bytes 589832 | tf_op jit(solution)/shard_map/ppermute | solution.py:387
  46.9 1.5 %copy-start.5 = (f32[6144]{0:T(1024)S(1)}, f32[6144]{0:T(1024)}, u32[]{:S(2)}) copy-start(f32[6144]{0:T(1024)} %param.11) | copy-start | bytes 73732
  49.9 2.0 %collective-permute-start.17 = (bf16[1536,128]{1,0:T(8,128)(2,1)S(1)}, bf16[1536,128]{1,0:T(8,128)(2,1)S(1)}, u32[]{:S(2)}, u32[]{:S(2)}) collective-permute-start(bf16[1536,128]{1,0:T(8,128)(2,1)S(1)} %get-tuple-element.123.refs_5_), channel_id=1, source_target_pairs={{0,1},{1,0},{2,3},{3,2},{4,5},{5,4},{6,7},{7,6},{8,9},{9,8},{10,11... | collective-permute-start | bytes 1179656 | tf_op jit(solution)/shard_map/ppermute | solution.py:387
  51.8 1.8 %collective-permute-start.16 = (bf16[1536,128]{1,0:T(8,128)(2,1)S(1)}, bf16[1536,128]{1,0:T(8,128)(2,1)S(1)}, u32[]{:S(2)}, u32[]{:S(2)}) collective-permute-start(bf16[1536,128]{1,0:T(8,128)(2,1)S(1)} %get-tuple-element.125.refs_10_), channel_id=1, source_target_pairs={{0,1},{1,0},{2,3},{3,2},{4,5},{5,4},{6,7},{7,6},{8,9},{9,8},{10,11... | collective-permute-start | bytes 1179656 | tf_op jit(solution)/shard_map/ppermute | solution.py:387

commit v6 on v5

--- a/solution.py
+++ b/solution.py
@@ -200,17 +200,17 @@
 
 
 def whole_states_kernel(
-    group, key_ref, value_ref, taps_ref, map_ref, core_rim, chip_rim,
-    feat_ref, conv_ref, other_ref, other_next, state_ref, scratch,
+    group, quarters, key_ref, value_ref, taps_ref, map_ref, core_rim, chip_rim, feat_ref, conv_ref, *rest
 ):
+    (*states, scratch) = rest
     head_dim = map_ref.shape[0]
     width = key_ref.shape[1]
     size = width // (4 * GROUPS)
     back = taps_ref.shape[1] - 1
-    for quarter in range(4):
+    for i, quarter in enumerate(quarters):
         for start in range(0, size, head_dim):
             natural = columns(quarter_start(quarter, width) + group * size + start, head_dim)
-            at = quarter * size + start
+            at = i * size + start
             local = slice(at, at + head_dim)
             buffers = scratch.at[at // head_dim % scratch.shape[0]]
             taps = taps_ref[:, :, natural].astype(f32)
@@ -220,32 +220,29 @@
             feat_ref[:, local] = key_feat
             value_conv = convolved(buffers.at[1], value_ref[:, natural].astype(f32), taps[2], rim, 2 * back)
             conv_ref[:, local] = value_conv
-            state = state_of(key_feat, value_conv)
-            if quarter < 2:
-                (other_ref, other_next)[quarter][start : start + head_dim] = state.astype(bf16)
-            else:
-                state_ref[at - 2 * size : at - 2 * size + head_dim] = state
-
-
-def whole_states(group, key_seq, value_seq, conv_kernel, feature_map, rims):
+            states[i][start : start + head_dim] = state_of(key_feat, value_conv).astype(states[i].dtype)
+
+
+def whole_states(group, quarters, state_type, key_seq, value_seq, conv_kernel, feature_map, rims):
     tok_count, width = key_seq.shape
     head_dim = feature_map.shape[0]
-    size = width // GROUPS
-    rows, other = shape((tok_count, size), bf16), shape((size // 4, head_dim), bf16)
+    size = width // (4 * GROUPS)
+    rows = shape((tok_count, len(quarters) * size), bf16)
     return kernel_call(
-        functools.partial(whole_states_kernel, group),
+        functools.partial(whole_states_kernel, group, quarters),
         "whole_states",
         [IN_VMEM] * 6,
-        [IN_VMEM] * 5,
-        [rows, rows, other, other, shape((size // 2, head_dim), f32)],
+        [IN_VMEM] * (2 + len(quarters)),
+        [rows, rows, *[shape((size, head_dim), state_type)] * len(quarters)],
         [pltpu.VMEM((BLOCK_HEADS, 2, TILE + tok_count, head_dim), f32)],
     )(key_seq, value_seq, conv_kernel, feature_map, *rims)
 
 
 def first_rows_kernel(
     group, quarters, key_ref, value_ref, taps_ref, map_ref, core_rim, chip_rim, state_ref,
-    feat_ref, conv_ref, sum_ref, scratch,
+    feat_ref, conv_ref, *rest
 ):
+    (*sums, scratch) = rest
     head_dim = map_ref.shape[0]
     width = taps_ref.shape[2]
     back = taps_ref.shape[1] - 1
@@ -269,7 +266,7 @@
         for part, first in zip(parts, firsts):
             state = state_ref[there.start + part.start : there.start + part.stop]
             state = state + state_of(first, value_conv[:, part])
-            sum_ref[i * size + part.start : i * size + part.stop] = state.astype(sum_ref.dtype)
+            sums[i][part] = state.astype(sums[i].dtype)
 
 
 def first_rows(group, quarters, state_type, key_first, value_first, conv_kernel, feature_map, rims, state):
@@ -281,14 +278,14 @@
         functools.partial(first_rows_kernel, group, quarters),
         "first_rows",
         [IN_VMEM] * 7,
-        [IN_VMEM] * 3,
-        [rows, rows, shape((len(quarters) * size, head_dim), state_type)],
+        [IN_VMEM] * (2 + len(quarters)),
+        [rows, rows, *[shape((size, head_dim), state_type)] * len(quarters)],
         [pltpu.VMEM((len(quarters), 2, TILE + RIM, size), f32)],
     )(key_first, value_first, conv_kernel, feature_map, *rims, state)
 
 
 def within_kernel(
-    quarter, group, query_ref, taps_ref, map_ref, core_rim, chip_rim, key_ref, value_ref, *rest
+    quarter, group, base, query_ref, taps_ref, map_ref, core_rim, chip_rim, key_ref, value_ref, *rest
 ):
     (*firsts, feat_ref, mixed_ref, scratch) = rest
     head_dim = map_ref.shape[0]
@@ -297,34 +294,36 @@
     causal = lax.broadcasted_iota(jnp.int32, (tok_count, tok_count), 0) >= lax.broadcasted_iota(
         jnp.int32, (tok_count, tok_count), 1
     )
-    for start in range(0, size, head_dim):
+    starts = range(0, size, head_dim)
+    for start in starts:
         natural = columns(quarter_start(quarter, width) + group * size + start, head_dim)
-        local = slice(start, start + head_dim)
-        at = slice(quarter * size + start, quarter * size + start + head_dim)
+        rim, end = query_rim(core_rim, chip_rim, quarter, width, group * size + start, head_dim)
+        taps = taps_ref[0, :, natural].astype(f32)
+        buffer = scratch.at[start // head_dim % scratch.shape[0]]
+        conv = convolved(buffer, query_ref[:, natural].astype(f32), taps, rim, end * (taps_ref.shape[1] - 1))
+        feat_ref[:, start : start + head_dim] = features(conv, map_ref[...])
+    products = []
+    for start in starts:
+        local, at = slice(start, start + head_dim), slice(base + start, base + start + head_dim)
         first = quarter % 2 * size * int(quarter >= 2) + start
         first = slice(first, first + head_dim)
         key, value = key_ref[:, at], value_ref[:, at]
         if firsts:
             key = jnp.concatenate([firsts[0][:, first], key[RIM:]], axis=0)
             value = jnp.concatenate([firsts[1][:, first], value[RIM:]], axis=0)
-        rim, end = query_rim(core_rim, chip_rim, quarter, width, group * size + start, head_dim)
-        taps = taps_ref[0, :, natural].astype(f32)
-        buffer = scratch.at[start // head_dim % scratch.shape[0]]
-        conv = convolved(buffer, query_ref[:, natural].astype(f32), taps, rim, end * (taps_ref.shape[1] - 1))
-        feat = features(conv, map_ref[...])
-        feat_ref[:, local] = feat
-        scores = lax.dot_general(feat, key, (((1,), (1,)), ((), ())), preferred_element_type=f32)
-        weights = jnp.where(causal, scores, 0.0).astype(bf16)
+        scores = lax.dot_general(feat_ref[:, local], key, (((1,), (1,)), ((), ())), preferred_element_type=f32)
+        products.append((local, jnp.where(causal, scores, 0.0).astype(bf16), value))
+    for local, weights, value in products:
         mixed_ref[:, local] = jnp.dot(weights, value, preferred_element_type=f32)
 
 
-def within_block(quarter, group, query_seq, conv_kernel, feature_map, rims, feat, conv, firsts):
+def within_block(quarter, group, query_seq, conv_kernel, feature_map, rims, feat, conv, base, firsts):
     tok_count, width = query_seq.shape
     head_dim = feature_map.shape[0]
     size = width // (4 * GROUPS)
     operands = (query_seq, conv_kernel, feature_map, *rims, feat, conv, *firsts)
     return kernel_call(
-        functools.partial(within_kernel, quarter, group),
+        functools.partial(within_kernel, quarter, group, base),
         "within_block",
         [IN_VMEM] * len(operands),
         [IN_VMEM] * 2,
@@ -441,10 +440,10 @@
             first = ()
             if firsts[g]:
                 first = [part[q] for part in firsts[g][0]] if q < 2 else firsts[g][1]
-            mixed[q, g] = within_block(q, g, query_seq, conv_kernel, feature_map, rims, *near[g], first)
-
-    def chip_sums(device, state, paired, own):
-        return state[:rows] + paired.astype(f32), state[rows:] + own.astype(f32)
+            mixed[q, g] = within_block(q, g, query_seq, conv_kernel, feature_map, rims, *near[g][q], first)
+
+    def chip_sums(device, paired, own, paired_arrived, own_arrived):
+        return paired + paired_arrived.astype(f32), own + own_arrived.astype(f32)
 
     def pair_sums(device, own, arrived):
         total = own + arrived.astype(f32)
@@ -470,12 +469,12 @@
         return (
             others,
             own_part + jnp.where(of_core(device), cored.astype(f32), 0.0),
-            own_part + jnp.where(of_core(device), 0.0, state[rows:]),
+            own_part + jnp.where(of_core(device), 0.0, state),
         )
 
     def paired_prefixes(device, arrived, cored, state, own):
         arrived = arrived.astype(f32)
-        give = arrived + jnp.where(of_core(device), 0.0, state[:rows])
+        give = arrived + jnp.where(of_core(device), 0.0, state)
         return (
             arrived + jnp.where(of_core(device), cored.astype(f32), 0.0),
             jnp.concatenate([give.astype(bf16), own], axis=0),
@@ -494,6 +493,7 @@
     for g in groups:
         if g == 0:
             *kept, partial, key_first, value_first = near_states(g, key_seq, value_seq, conv_kernel, feature_map)
+            near.append([(*kept, q * rows) for q in range(4)])
             others, first_a = [], [[], []]
             for q in (0, 1):
                 *first, other = first_rows(
@@ -502,19 +502,25 @@
                 others.append(swapped(other, 1))
                 first_a[0].append(first[0])
                 first_a[1].append(first[1])
-            *first_b, state = first_rows(
+            *first_b, paired, single = first_rows(
                 g, (2, 3), f32, key_first, value_first, conv_kernel, feature_map, rims, partial
             )
             firsts.append((first_a, first_b))
         else:
-            *kept, other, other_next, state = whole_states(g, key_seq, value_seq, conv_kernel, feature_map, rims)
+            *kept, other, other_next = whole_states(
+                g, (0, 1), bf16, key_seq, value_seq, conv_kernel, feature_map, rims
+            )
             others = [swapped(other, 1), swapped(other_next, 1)]
+            near.append([(*kept, q * rows) for q in range(2)])
+            *kept, paired, single = whole_states(
+                g, (2, 3), f32, key_seq, value_seq, conv_kernel, feature_map, rims
+            )
+            near[g] += [(*kept, q * rows) for q in range(2)]
             firsts.append(None)
             pair_step(g - 1)
-        near.append(kept)
-        state_b.append(state)
+        state_b.append((paired, single))
         from_core.append(others)
-        give, own = mapped("chip_sums", chip_sums, [(rows, bf16), (rows, f32)], state, *others)
+        give, own = mapped("chip_sums", chip_sums, [(rows, bf16), (rows, f32)], paired, single, *others)
         chip.append(own)
         arriving.append(swapped(give, 2))
     score(0.375)
@@ -553,7 +559,7 @@
             chip[g],
             from_pair[g],
             from_core[g][1],
-            state_b[g],
+            state_b[g][1],
             *step,
         )
         back[g] = swapped(others, 2)
@@ -568,7 +574,7 @@
             [(rows, bf16), (2 * rows, bf16)],
             back[g],
             from_core[g][0],
-            state_b[g],
+            state_b[g][0],
             own_give[g],
         )
         from_other[g] = swapped(give, 1)

time: 55.3 us -> 54.4 us (0.984)
  Pallas kernels: 28.7 us -> 24.3 us
  starting transfers between devices: 18.6 us -> 20.4 us
  waiting for transfers between devices: 7.37 us -> 9.02 us
    pallas_call x30 -> x31, Pallas kernels: 28.7 us -> 24.3 us  [call(): pl.pallas_call(ordered, in_specs=[*in_specs, *[IN_PLACE] * len(before)],...]
    ppermute x17, starting transfers between devices: 18.1 us -> 19.9 us  [swapped(): lax.ppermute(block, 'seq', [(i, i ^ distance) for i in range(lax.axis_siz...]
    ppermute x17, waiting for transfers between devices: 7.37 us -> 9.02 us  [swapped(): lax.ppermute(block, 'seq', [(i, i ^ distance) for i in range(lax.axis_siz...]
  transfers between devices with their start and end apart: 18 -> 18, of which waited for: 7 -> 9; matrix products, arithmetic and copies ran while one was open for 0% -> 0% of each run, Pallas kernels for 46% -> 39%
where the time goes in v6:
time: 54.4 us; the launch traced here: 54.2 us
  Pallas kernels  24.3 us (45%)
  starting transfers between devices  20.4 us (38%)
  waiting for transfers between devices  9.02 us (17%)
    pallas_call x31, Pallas kernels, call(): pl.pallas_call(ordered, in_specs=[*in_specs, *[IN_PLACE] * len(before)],...  24.3 us
    ppermute x17, starting transfers between devices, swapped(): lax.ppermute(block, 'seq', [(i, i ^ distance) for i in range(lax.axis_siz...  19.9 us
    ppermute x17, waiting for transfers between devices, swapped(): lax.ppermute(block, 'seq', [(i, i ^ distance) for i in range(lax.axis_siz...  9.02 us
  transfers between devices with their start and end apart: 18, of which 9 were waited for; matrix products, arithmetic and copies ran while one was open for 0% of the time, Pallas kernels for 39%

profile of v6, /device:TPU:0, one launch (start us, length us, event | category | flops | bytes accessed | tf_op | source)
XLA Modules:
  0.0 54.2 jit_solution(13374053846285430975)
XLA Ops:
  0.0 1.3 %pack_rims.1.refs_4_ = bf16[16,4608]{1,0:T(8,128)(2,1)S(1)} custom-call(bf16[256,6144]{1,0:T(8,128)(2,1)} %refs_0_.23, bf16[256,6144]{1,0:T(8,128)(2,1)} %refs_0_.15, bf16[256,6144]{1,0:T(8,128)(2,1)} %refs_1_.15), custom_call_target="tpu_custom_call" | custom-call | flops 1024 | bytes 1024 | tf_op jit(solution)/shard_map/pack_rims/pallas_call | solution.py:39
  1.4 0.5 collective-permute-start.1
  1.9 2.6 %collective-permute-start = (bf16[16,4608]{1,0:T(8,128)(2,1)S(1)}, bf16[16,4608]{1,0:T(8,128)(2,1)S(1)}, u32[]{:S(2)}, u32[]{:S(2)}) collective-permute-start(bf16[16,4608]{1,0:T(8,128)(2,1)S(1)} %pack_rims.1.refs_4_), channel_id=1, source_target_pairs={{0,1},{1,0},{2,3},{3,2},{4,5},{5,4},{6,7},{7,6},{8,9},{9,8},{10,11... | collective-permute-start | bytes 442376 | tf_op jit(solution)/shard_map/ppermute | solution.py:386
  4.5 3.6 %near_states.1 = (bf16[256,3072]{1,0:T(8,128)(2,1)S(1)}, bf16[256,3072]{1,0:T(8,128)(2,1)S(1)}, f32[3072,128]{1,0:T(8,128)S(1)}, bf16[16,3072]{1,0:T(8,128)(2,1)S(1)}, bf16[16,3072]{1,0:T(8,128)(2,1)S(1)}) custom-call(bf16[256,6144]{1,0:T(8,128)(2,1)S(1)} %copy-done.1, bf16[256,6144]{1,0:T(8,128)(2,1)S(1)} %copy-done.2, bf16[3,4,6144]{2,1,0:T(4,128)(2,1)S(1)} %copy-done.3, ...), custom_call_target="tpu_custom_call" | custom-call | flops 1024 | bytes 1024 | tf_op jit(solution)/shard_map/near_states/pallas_call | solution.py:39
  8.2 0.4 first_rows.3
  8.7 0.4 first_rows.4
  9.1 0.6 %collective-permute-start.3 = (bf16[768,128]{1,0:T(8,128)(2,1)S(1)}, bf16[768,128]{1,0:T(8,128)(2,1)S(1)}, u32[]{:S(2)}, u32[]{:S(2)}) collective-permute-start(bf16[768,128]{1,0:T(8,128)(2,1)S(1)} %get-tuple-element.78.refs_7_), channel_id=1, source_target_pairs={{0,1},{1,0},{2,3},{3,2},{4,5},{5,4},{6,7},{7,6},{8,9},{9,8},{10,11... | collective-permute-start | bytes 589832 | tf_op jit(solution)/shard_map/ppermute | solution.py:386
  9.6 0.7 %first_rows.5 = (bf16[16,1536]{1,0:T(8,128)(2,1)S(1)}, bf16[16,1536]{1,0:T(8,128)(2,1)S(1)}, f32[768,128]{1,0:T(8,128)S(1)}, f32[768,128]{1,0:T(8,128)S(1)}) custom-call(bf16[16,3072]{1,0:T(8,128)(2,1)S(1)} %get-tuple-element.74.refs_0_, bf16[16,3072]{1,0:T(8,128)(2,1)S(1)} %get-tuple-element.75.refs_1_.refs_7_, bf16[3,4,6144]{2,1,0:T(4,128)(2,1)S(1)} %copy-done.3, ...), custom_call_target="tpu_custom_call" | custom-call | flops 1024 | bytes 1024 | tf_op jit(solution)/shard_map/first_rows/pallas_call | solution.py:39
  10.3 0.4 collective-permute-done.3.refs_3_.refs_2_
  10.8 2.5 %collective-permute-start.6 = (bf16[768,128]{1,0:T(8,128)(2,1)S(1)}, bf16[768,128]{1,0:T(8,128)(2,1)S(1)}, u32[]{:S(2)}, u32[]{:S(2)}) collective-permute-start(bf16[768,128]{1,0:T(8,128)(2,1)S(1)} %get-tuple-element.86), channel_id=1, source_target_pairs={{0,2},{1,3},{2,0},{3,1},{4,6},{5,7},{6,4},{7,5},{8,10},{9,11},{10,... | collective-permute-start | bytes 589832 | tf_op jit(solution)/shard_map/ppermute | solution.py:386
  13.2 1.9 %whole_states.2 = (bf16[256,1536]{1,0:T(8,128)(2,1)S(1)}, bf16[256,1536]{1,0:T(8,128)(2,1)S(1)}, bf16[768,128]{1,0:T(8,128)(2,1)S(1)}, bf16[768,128]{1,0:T(8,128)(2,1)S(1)}) custom-call(bf16[256,6144]{1,0:T(8,128)(2,1)S(1)} %copy-done.1, bf16[256,6144]{1,0:T(8,128)(2,1)S(1)} %copy-done.2, bf16[3,4,6144]{2,1,0:T(4,128)(2,1)S(1)} %copy-done.3, ...), custom_call_target="tpu_custom_call" | custom-call | flops 1024 | bytes 1024 | tf_op jit(solution)/shard_map/whole_states/pallas_call | solution.py:39
  15.1 0.1 collective-permute-start.4
  15.3 0.4 collective-permute-start.5
  15.7 1.9 %whole_states.3 = (bf16[256,1536]{1,0:T(8,128)(2,1)S(1)}, bf16[256,1536]{1,0:T(8,128)(2,1)S(1)}, f32[768,128]{1,0:T(8,128)S(1)}, f32[768,128]{1,0:T(8,128)S(1)}) custom-call(bf16[256,6144]{1,0:T(8,128)(2,1)S(1)} %copy-done.1, bf16[256,6144]{1,0:T(8,128)(2,1)S(1)} %copy-done.2, bf16[3,4,6144]{2,1,0:T(4,128)(2,1)S(1)} %copy-done.3, ...), custom_call_target="tpu_custom_call" | custom-call | flops 1024 | bytes 1024 | tf_op jit(solution)/shard_map/whole_states/pallas_call | solution.py:39
  17.6 1.1 %collective-permute-done.6.refs_1_ = bf16[768,128]{1,0:T(8,128)(2,1)S(1)} collective-permute-done((bf16[768,128]{1,0:T(8,128)(2,1)S(1)}, bf16[768,128]{1,0:T(8,128)(2,1)S(1)}, u32[]{:S(2)}, u32[]{:S(2)}) %collective-permute-start.6) | collective-permute-done | bytes 196640 | tf_op jit(solution)/shard_map/ppermute | solution.py:386
  18.8 1.8 %collective-permute-start.7 = (bf16[768,128]{1,0:T(8,128)(2,1)S(1)}, bf16[768,128]{1,0:T(8,128)(2,1)S(1)}, u32[]{:S(2)}, u32[]{:S(2)}) collective-permute-start(bf16[768,128]{1,0:T(8,128)(2,1)S(1)} %get-tuple-element.89), channel_id=1, source_target_pairs={{0,2},{1,3},{2,0},{3,1},{4,6},{5,7},{6,4},{7,5},{8,10},{9,11},{10,... | collective-permute-start | bytes 589832 | tf_op jit(solution)/shard_map/ppermute | solution.py:386
  20.6 1.6 %collective-permute-start.9 = (bf16[768,128]{1,0:T(8,128)(2,1)S(1)}, bf16[768,128]{1,0:T(8,128)(2,1)S(1)}, u32[]{:S(2)}, u32[]{:S(2)}) collective-permute-start(bf16[768,128]{1,0:T(8,128)(2,1)S(1)} %get-tuple-element.87.refs_4_), channel_id=1, source_target_pairs={{0,4},{1,5},{2,6},{3,7},{4,0},{5,1},{6,2},{7,3},{8,12},{9,13},{10,... | collective-permute-start | bytes 589832 | tf_op jit(solution)/shard_map/ppermute | solution.py:386
  22.2 0.9 %within_block.8 = (bf16[256,768]{1,0:T(8,128)(2,1)S(1)}, f32[256,768]{1,0:T(8,128)S(1)}) custom-call(bf16[256,6144]{1,0:T(8,128)(2,1)S(1)} %copy-done, bf16[3,4,6144]{2,1,0:T(4,128)(2,1)S(1)} %copy-done.3, bf16[128,128]{1,0:T(8,128)(2,1)S(1)} %copy-done.4, bf16[16,4608]{1,0:T(8,128)(2,1)S(1)} %collective-permute-done.refs_4_.refs_3_, ...), custom_call_target="tpu_custom_call" | custom-call | flops 1024 | bytes 1024 | tf_op jit(solution)/shard_map/within_block/pallas_call | solution.py:39
  23.1 0.9 %within_block.9 = (bf16[256,768]{1,0:T(8,128)(2,1)S(1)}, f32[256,768]{1,0:T(8,128)S(1)}) custom-call(bf16[256,6144]{1,0:T(8,128)(2,1)S(1)} %copy-done, bf16[3,4,6144]{2,1,0:T(4,128)(2,1)S(1)} %copy-done.3, bf16[128,128]{1,0:T(8,128)(2,1)S(1)} %copy-done.4, bf16[16,4608]{1,0:T(8,128)(2,1)S(1)} %collective-permute-done.refs_4_.refs_3_, ...), custom_call_target="tpu_custom_call" | custom-call | flops 1024 | bytes 1024 | tf_op jit(solution)/shard_map/within_block/pallas_call | solution.py:39
  24.0 0.9 %within_block.10 = (bf16[256,768]{1,0:T(8,128)(2,1)S(1)}, f32[256,768]{1,0:T(8,128)S(1)}) custom-call(bf16[256,6144]{1,0:T(8,128)(2,1)S(1)} %copy-done, bf16[3,4,6144]{2,1,0:T(4,128)(2,1)S(1)} %copy-done.3, bf16[128,128]{1,0:T(8,128)(2,1)S(1)} %copy-done.4, bf16[16,4608]{1,0:T(8,128)(2,1)S(1)} %collective-permute-done.refs_4_.refs_3_, ...), custom_call_target="tpu_custom_call" | custom-call | flops 1024 | bytes 1024 | tf_op jit(solution)/shard_map/within_block/pallas_call | solution.py:39
  24.9 0.5 collective-permute-done.7.refs_1_
  25.5 1.4 %collective-permute-start.8 = (bf16[768,128]{1,0:T(8,128)(2,1)S(1)}, bf16[768,128]{1,0:T(8,128)(2,1)S(1)}, u32[]{:S(2)}, u32[]{:S(2)}) collective-permute-start(bf16[768,128]{1,0:T(8,128)(2,1)S(1)} %get-tuple-element.100.refs_2_), channel_id=1, source_target_pairs={{0,4},{1,5},{2,6},{3,7},{4,0},{5,1},{6,2},{7,3},{8,12},{9,13},{10,... | collective-permute-start | bytes 589832 | tf_op jit(solution)/shard_map/ppermute | solution.py:386
  27.0 0.1 plane_sums.2
  27.1 2.4 %collective-permute-start.11 = (bf16[384,128]{1,0:T(8,128)(2,1)S(1)}, bf16[384,128]{1,0:T(8,128)(2,1)S(1)}, u32[]{:S(2)}, u32[]{:S(2)}) collective-permute-start(bf16[384,128]{1,0:T(8,128)(2,1)S(1)} %get-tuple-element.102.refs_7_), channel_id=1, source_target_pairs={{0,8},{1,9},{2,10},{3,11},{4,12},{5,13},{6,14},{7,15},{8,0},{9,1},... | collective-permute-start | bytes 294920 | tf_op jit(solution)/shard_map/ppermute | solution.py:386
  29.4 0.9 %within_block.11 = (bf16[256,768]{1,0:T(8,128)(2,1)S(1)}, f32[256,768]{1,0:T(8,128)S(1)}) custom-call(bf16[256,6144]{1,0:T(8,128)(2,1)S(1)} %copy-done, bf16[3,4,6144]{2,1,0:T(4,128)(2,1)S(1)} %copy-done.3, bf16[128,128]{1,0:T(8,128)(2,1)S(1)} %copy-done.4, bf16[16,4608]{1,0:T(8,128)(2,1)S(1)} %collective-permute-done.refs_4_.refs_3_, ...), custom_call_target="tpu_custom_call" | custom-call | flops 1024 | bytes 1024 | tf_op jit(solution)/shard_map/within_block/pallas_call | solution.py:39
  30.3 3.1 %collective-permute-done.8.refs_1_ = bf16[768,128]{1,0:T(8,128)(2,1)S(1)} collective-permute-done((bf16[768,128]{1,0:T(8,128)(2,1)S(1)}, bf16[768,128]{1,0:T(8,128)(2,1)S(1)}, u32[]{:S(2)}, u32[]{:S(2)}) %collective-permute-start.8) | collective-permute-done | bytes 196640 | tf_op jit(solution)/shard_map/ppermute | solution.py:386
  33.4 0.1 plane_sums.3
  33.5 1.2 %collective-permute-start.10 = (bf16[384,128]{1,0:T(8,128)(2,1)S(1)}, bf16[384,128]{1,0:T(8,128)(2,1)S(1)}, u32[]{:S(2)}, u32[]{:S(2)}) collective-permute-start(bf16[384,128]{1,0:T(8,128)(2,1)S(1)} %get-tuple-element.106.refs_1_), channel_id=1, source_target_pairs={{0,8},{1,9},{2,10},{3,11},{4,12},{5,13},{6,14},{7,15},{8,0},{9,1},... | collective-permute-start | bytes 294920 | tf_op jit(solution)/shard_map/ppermute | solution.py:386
  34.7 2.2 %collective-permute-start.13 = (bf16[384,128]{1,0:T(8,128)(2,1)S(1)}, bf16[384,128]{1,0:T(8,128)(2,1)S(1)}, u32[]{:S(2)}, u32[]{:S(2)}) collective-permute-start(bf16[384,128]{1,0:T(8,128)(2,1)S(1)} %halves.2.refs_9_.refs_6_), channel_id=1, source_target_pairs={{0,4},{1,5},{2,6},{3,7},{4,0},{5,1},{6,2},{7,3},{8,12},{9,13},{10,... | collective-permute-start | bytes 294920 | tf_op jit(solution)/shard_map/ppermute | solution.py:386
  37.0 1.1 %within_block.12 = (bf16[256,768]{1,0:T(8,128)(2,1)S(1)}, f32[256,768]{1,0:T(8,128)S(1)}) custom-call(bf16[256,6144]{1,0:T(8,128)(2,1)S(1)} %copy-done, bf16[3,4,6144]{2,1,0:T(4,128)(2,1)S(1)} %copy-done.3, bf16[128,128]{1,0:T(8,128)(2,1)S(1)} %copy-done.4, bf16[16,4608]{1,0:T(8,128)(2,1)S(1)} %collective-permute-done.refs_4_.refs_3_, ...), custom_call_target="tpu_custom_call" | custom-call | flops 1024 | bytes 1024 | tf_op jit(solution)/shard_map/within_block/pallas_call | solution.py:39
  38.1 0.9 %within_block.13 = (bf16[256,768]{1,0:T(8,128)(2,1)S(1)}, f32[256,768]{1,0:T(8,128)S(1)}) custom-call(bf16[256,6144]{1,0:T(8,128)(2,1)S(1)} %copy-done, bf16[3,4,6144]{2,1,0:T(4,128)(2,1)S(1)} %copy-done.3, bf16[128,128]{1,0:T(8,128)(2,1)S(1)} %copy-done.4, bf16[16,4608]{1,0:T(8,128)(2,1)S(1)} %collective-permute-done.refs_4_.refs_3_, ...), custom_call_target="tpu_custom_call" | custom-call | flops 1024 | bytes 1024 | tf_op jit(solution)/shard_map/within_block/pallas_call | solution.py:39
  38.9 1.1 %collective-permute-done.10.refs_0_ = bf16[384,128]{1,0:T(8,128)(2,1)S(1)} collective-permute-done((bf16[384,128]{1,0:T(8,128)(2,1)S(1)}, bf16[384,128]{1,0:T(8,128)(2,1)S(1)}, u32[]{:S(2)}, u32[]{:S(2)}) %collective-permute-start.10) | collective-permute-done | bytes 98336 | tf_op jit(solution)/shard_map/ppermute | solution.py:386
  40.2 0.9 %collective-permute-done.13.refs_7_ = bf16[384,128]{1,0:T(8,128)(2,1)S(1)} collective-permute-done((bf16[384,128]{1,0:T(8,128)(2,1)S(1)}, bf16[384,128]{1,0:T(8,128)(2,1)S(1)}, u32[]{:S(2)}, u32[]{:S(2)}) %collective-permute-start.13) | collective-permute-done | bytes 98336 | tf_op jit(solution)/shard_map/ppermute | solution.py:386
  41.1 0.2 own_prefixes.2
  41.3 1.6 %collective-permute-start.15 = (bf16[768,128]{1,0:T(8,128)(2,1)S(1)}, bf16[768,128]{1,0:T(8,128)(2,1)S(1)}, u32[]{:S(2)}, u32[]{:S(2)}) collective-permute-start(bf16[768,128]{1,0:T(8,128)(2,1)S(1)} %get-tuple-element.121), channel_id=1, source_target_pairs={{0,2},{1,3},{2,0},{3,1},{4,6},{5,7},{6,4},{7,5},{8,10},{9,11},{10,... | collective-permute-start | bytes 589832 | tf_op jit(solution)/shard_map/ppermute | solution.py:386
  42.9 0.9 %within_block.14 = (bf16[256,768]{1,0:T(8,128)(2,1)S(1)}, f32[256,768]{1,0:T(8,128)S(1)}) custom-call(bf16[256,6144]{1,0:T(8,128)(2,1)S(1)} %copy-done, bf16[3,4,6144]{2,1,0:T(4,128)(2,1)S(1)} %copy-done.3, bf16[128,128]{1,0:T(8,128)(2,1)S(1)} %copy-done.4, bf16[16,4608]{1,0:T(8,128)(2,1)S(1)} %collective-permute-done.refs_4_.refs_3_, ...), custom_call_target="tpu_custom_call" | custom-call | flops 1024 | bytes 1024 | tf_op jit(solution)/shard_map/within_block/pallas_call | solution.py:39
  43.9 0.9 %collective-permute-done.12.refs_7_ = bf16[384,128]{1,0:T(8,128)(2,1)S(1)} collective-permute-done((bf16[384,128]{1,0:T(8,128)(2,1)S(1)}, bf16[384,128]{1,0:T(8,128)(2,1)S(1)}, u32[]{:S(2)}, u32[]{:S(2)}) %collective-permute-start.12) | collective-permute-done | bytes 98336 | tf_op jit(solution)/shard_map/ppermute | solution.py:386
  44.8 0.2 own_prefixes.3
  45.0 1.1 %collective-permute-start.14 = (bf16[768,128]{1,0:T(8,128)(2,1)S(1)}, bf16[768,128]{1,0:T(8,128)(2,1)S(1)}, u32[]{:S(2)}, u32[]{:S(2)}) collective-permute-start(bf16[768,128]{1,0:T(8,128)(2,1)S(1)} %get-tuple-element.119), channel_id=1, source_target_pairs={{0,2},{1,3},{2,0},{3,1},{4,6},{5,7},{6,4},{7,5},{8,10},{9,11},{10,... | collective-permute-start | bytes 589832 | tf_op jit(solution)/shard_map/ppermute | solution.py:386
  46.1 0.9 %within_block.15 = (bf16[256,768]{1,0:T(8,128)(2,1)S(1)}, f32[256,768]{1,0:T(8,128)S(1)}) custom-call(bf16[256,6144]{1,0:T(8,128)(2,1)S(1)} %copy-done, bf16[3,4,6144]{2,1,0:T(4,128)(2,1)S(1)} %copy-done.3, bf16[128,128]{1,0:T(8,128)(2,1)S(1)} %copy-done.4, bf16[16,4608]{1,0:T(8,128)(2,1)S(1)} %collective-permute-done.refs_4_.refs_3_, ...), custom_call_target="tpu_custom_call" | custom-call | flops 1024 | bytes 1024 | tf_op jit(solution)/shard_map/within_block/pallas_call | solution.py:39
  47.0 1.4 %finish.4 = (bf16[256,6144]{1,0:T(8,128)(2,1)}, f32[8,128]{1,0:T(8,128)S(1)}) custom-call(f32[1,6144]{1,0:T(1,128)S(1)} %bitcast.1, bf16[768,128]{1,0:T(8,128)(2,1)S(1)} %get-tuple-element.122.refs_1_, bf16[768,128]{1,0:T(8,128)(2,1)S(1)} %get-tuple-element.123.refs_2_, bf16[256,768]{1,0:T(8,128)(2,1)S(1)} %get-tuple-element.124.refs_3_, ...), custom_call_target="tpu_custom_call" | custom-call | flops 1024 | bytes 1024 | tf_op jit(solution)/shard_map/finish/pallas_call | solution.py:39
  48.4 0.1 collective-permute-done.15.refs_0_
  48.5 0.1 paired_prefixes.2
  48.7 1.2 %finish.5 = (bf16[256,6144]{1,0:T(8,128)(2,1)}, f32[8,128]{1,0:T(8,128)S(1)}) custom-call(f32[1,6144]{1,0:T(1,128)S(1)} %bitcast.2, bf16[768,128]{1,0:T(8,128)(2,1)S(1)} %get-tuple-element.128.refs_1_, bf16[256,768]{1,0:T(8,128)(2,1)S(1)} %get-tuple-element.129.refs_2_, ...), custom_call_target="tpu_custom_call", output_to_operand_aliasing={{0}: (4, {})} | custom-call | flops 1024 | bytes 1024 | tf_op jit(solution)/shard_map/finish/pallas_call | solution.py:39
  50.0 0.8 %collective-permute-done.14.refs_0_ = bf16[768,128]{1,0:T(8,128)(2,1)S(1)} collective-permute-done((bf16[768,128]{1,0:T(8,128)(2,1)S(1)}, bf16[768,128]{1,0:T(8,128)(2,1)S(1)}, u32[]{:S(2)}, u32[]{:S(2)}) %collective-permute-start.14) | collective-permute-done | bytes 196640 | tf_op jit(solution)/shard_map/ppermute | solution.py:386
  50.7 0.1 paired_prefixes.3
  50.9 1.6 %finish.6 = (bf16[256,6144]{1,0:T(8,128)(2,1)}, f32[8,128]{1,0:T(8,128)S(1)}) custom-call(f32[1,6144]{1,0:T(1,128)S(1)} %bitcast.3, bf16[768,128]{1,0:T(8,128)(2,1)S(1)} %get-tuple-element.136.refs_1_, bf16[1536,128]{1,0:T(8,128)(2,1)S(1)} %collective-permute-done.17.refs_2_, ...), custom_call_target="tpu_custom_call", output_to_operand_aliasing={{0}: (9, {})} | custom-call | flops 1024 | bytes 1024 | tf_op jit(solution)/shard_map/finish/pallas_call | solution.py:39
  52.6 1.4 %finish.7 = bf16[256,6144]{1,0:T(8,128)(2,1)} custom-call(f32[1,6144]{1,0:T(1,128)S(1)} %bitcast.4, bf16[1536,128]{1,0:T(8,128)(2,1)S(1)} %collective-permute-done.16.refs_1_, bf16[256,768]{1,0:T(8,128)(2,1)S(1)} %get-tuple-element.134.refs_2_, bf16[256,768]{1,0:T(8,128)(2,1)S(1)} %get-tuple-element.135.refs_3_, ...), custom_call_target="tpu_custom_call", output_to_operand_aliasing={{}: (6, {})} | custom-call | flops 1024 | bytes 1024 | tf_op jit(solution)/shard_map/finish/pallas_call | solution.py:39
  (31 shorter events, 0.6 us)
Async XLA Ops:
  0.0 4.5 %copy-start.2 = (bf16[256,6144]{1,0:T(8,128)(2,1)S(1)}, bf16[256,6144]{1,0:T(8,128)(2,1)}, u32[]{:S(2)}) copy-start(bf16[256,6144]{1,0:T(8,128)(2,1)} %refs_1_.15) | copy-start | bytes 9437188
  0.0 4.5 %copy-start.1 = (bf16[256,6144]{1,0:T(8,128)(2,1)S(1)}, bf16[256,6144]{1,0:T(8,128)(2,1)}, u32[]{:S(2)}) copy-start(bf16[256,6144]{1,0:T(8,128)(2,1)} %refs_0_.15) | copy-start | bytes 9437188
  0.0 4.5 %copy-start.4 = (bf16[128,128]{1,0:T(8,128)(2,1)S(1)}, bf16[128,128]{1,0:T(8,128)(2,1)}, u32[]{:S(2)}) copy-start(bf16[128,128]{1,0:T(8,128)(2,1)} %refs_2_.29) | copy-start | bytes 98308
  0.0 4.5 %copy-start.3 = (bf16[3,4,6144]{2,1,0:T(4,128)(2,1)S(1)}, bf16[3,4,6144]{2,1,0:T(4,128)(2,1)}, u32[]{:S(2)}) copy-start(bf16[3,4,6144]{2,1,0:T(4,128)(2,1)} %refs_1_.23) | copy-start | bytes 442372
  1.4 6.8 %collective-permute-start.1 = (bf16[16,4608]{1,0:T(8,128)(2,1)S(1)}, bf16[16,4608]{1,0:T(8,128)(2,1)S(1)}, u32[]{:S(2)}, u32[]{:S(2)}) collective-permute-start(bf16[16,4608]{1,0:T(8,128)(2,1)S(1)} %pack_rims.1.refs_4_), channel_id=1, source_target_pairs={{0,1},{1,2},{2,0},{3,4},{4,3},{5,6},{6,5},{7,8},{8,7},{9,10},{10,9... | collective-permute-start | bytes 442376 | tf_op jit(solution)/shard_map/ppermute | solution.py:394
  1.9 6.3 %collective-permute-start = (bf16[16,4608]{1,0:T(8,128)(2,1)S(1)}, bf16[16,4608]{1,0:T(8,128)(2,1)S(1)}, u32[]{:S(2)}, u32[]{:S(2)}) collective-permute-start(bf16[16,4608]{1,0:T(8,128)(2,1)S(1)} %pack_rims.1.refs_4_), channel_id=1, source_target_pairs={{0,1},{1,0},{2,3},{3,2},{4,5},{5,4},{6,7},{7,6},{8,9},{9,8},{10,11... | collective-permute-start | bytes 442376 | tf_op jit(solution)/shard_map/ppermute | solution.py:386
  8.6 1.7 %collective-permute-start.2 = (bf16[768,128]{1,0:T(8,128)(2,1)S(1)}, bf16[768,128]{1,0:T(8,128)(2,1)S(1)}, u32[]{:S(2)}, u32[]{:S(2)}) collective-permute-start(bf16[768,128]{1,0:T(8,128)(2,1)S(1)} %get-tuple-element.77.refs_7_), channel_id=1, source_target_pairs={{0,1},{1,0},{2,3},{3,2},{4,5},{5,4},{6,7},{7,6},{8,9},{9,8},{10,11... | collective-permute-start | bytes 589832 | tf_op jit(solution)/shard_map/ppermute | solution.py:386
  9.1 1.6 %collective-permute-start.3 = (bf16[768,128]{1,0:T(8,128)(2,1)S(1)}, bf16[768,128]{1,0:T(8,128)(2,1)S(1)}, u32[]{:S(2)}, u32[]{:S(2)}) collective-permute-start(bf16[768,128]{1,0:T(8,128)(2,1)S(1)} %get-tuple-element.78.refs_7_), channel_id=1, source_target_pairs={{0,1},{1,0},{2,3},{3,2},{4,5},{5,4},{6,7},{7,6},{8,9},{9,8},{10,11... | collective-permute-start | bytes 589832 | tf_op jit(solution)/shard_map/ppermute | solution.py:386
  10.8 7.9 %collective-permute-start.6 = (bf16[768,128]{1,0:T(8,128)(2,1)S(1)}, bf16[768,128]{1,0:T(8,128)(2,1)S(1)}, u32[]{:S(2)}, u32[]{:S(2)}) collective-permute-start(bf16[768,128]{1,0:T(8,128)(2,1)S(1)} %get-tuple-element.86), channel_id=1, source_target_pairs={{0,2},{1,3},{2,0},{3,1},{4,6},{5,7},{6,4},{7,5},{8,10},{9,11},{10,... | collective-permute-start | bytes 589832 | tf_op jit(solution)/shard_map/ppermute | solution.py:386
  15.1 3.6 %collective-permute-start.4 = (bf16[768,128]{1,0:T(8,128)(2,1)S(1)}, bf16[768,128]{1,0:T(8,128)(2,1)S(1)}, u32[]{:S(2)}, u32[]{:S(2)}) collective-permute-start(bf16[768,128]{1,0:T(8,128)(2,1)S(1)} %get-tuple-element.85), channel_id=1, source_target_pairs={{0,1},{1,0},{2,3},{3,2},{4,5},{5,4},{6,7},{7,6},{8,9},{9,8},{10,11... | collective-permute-start | bytes 589832 | tf_op jit(solution)/shard_map/ppermute | solution.py:386
  15.3 6.9 %copy-start = (bf16[256,6144]{1,0:T(8,128)(2,1)S(1)}, bf16[256,6144]{1,0:T(8,128)(2,1)}, u32[]{:S(2)}) copy-start(bf16[256,6144]{1,0:T(8,128)(2,1)} %refs_0_.23) | copy-start | bytes 9437188
  15.3 3.4 %collective-permute-start.5 = (bf16[768,128]{1,0:T(8,128)(2,1)S(1)}, bf16[768,128]{1,0:T(8,128)(2,1)S(1)}, u32[]{:S(2)}, u32[]{:S(2)}) collective-permute-start(bf16[768,128]{1,0:T(8,128)(2,1)S(1)} %get-tuple-element.82.refs_6_), channel_id=1, source_target_pairs={{0,1},{1,0},{2,3},{3,2},{4,5},{5,4},{6,7},{7,6},{8,9},{9,8},{10,11... | collective-permute-start | bytes 589832 | tf_op jit(solution)/shard_map/ppermute | solution.py:386
  18.8 6.7 %collective-permute-start.7 = (bf16[768,128]{1,0:T(8,128)(2,1)S(1)}, bf16[768,128]{1,0:T(8,128)(2,1)S(1)}, u32[]{:S(2)}, u32[]{:S(2)}) collective-permute-start(bf16[768,128]{1,0:T(8,128)(2,1)S(1)} %get-tuple-element.89), channel_id=1, source_target_pairs={{0,2},{1,3},{2,0},{3,1},{4,6},{5,7},{6,4},{7,5},{8,10},{9,11},{10,... | collective-permute-start | bytes 589832 | tf_op jit(solution)/shard_map/ppermute | solution.py:386
  20.6 6.4 %collective-permute-start.9 = (bf16[768,128]{1,0:T(8,128)(2,1)S(1)}, bf16[768,128]{1,0:T(8,128)(2,1)S(1)}, u32[]{:S(2)}, u32[]{:S(2)}) collective-permute-start(bf16[768,128]{1,0:T(8,128)(2,1)S(1)} %get-tuple-element.87.refs_4_), channel_id=1, source_target_pairs={{0,4},{1,5},{2,6},{3,7},{4,0},{5,1},{6,2},{7,3},{8,12},{9,13},{10,... | collective-permute-start | bytes 589832 | tf_op jit(solution)/shard_map/ppermute | solution.py:386
  25.5 7.9 %collective-permute-start.8 = (bf16[768,128]{1,0:T(8,128)(2,1)S(1)}, bf16[768,128]{1,0:T(8,128)(2,1)S(1)}, u32[]{:S(2)}, u32[]{:S(2)}) collective-permute-start(bf16[768,128]{1,0:T(8,128)(2,1)S(1)} %get-tuple-element.100.refs_2_), channel_id=1, source_target_pairs={{0,4},{1,5},{2,6},{3,7},{4,0},{5,1},{6,2},{7,3},{8,12},{9,13},{10,... | collective-permute-start | bytes 589832 | tf_op jit(solution)/shard_map/ppermute | solution.py:386
  27.1 7.6 %collective-permute-start.11 = (bf16[384,128]{1,0:T(8,128)(2,1)S(1)}, bf16[384,128]{1,0:T(8,128)(2,1)S(1)}, u32[]{:S(2)}, u32[]{:S(2)}) collective-permute-start(bf16[384,128]{1,0:T(8,128)(2,1)S(1)} %get-tuple-element.102.refs_7_), channel_id=1, source_target_pairs={{0,8},{1,9},{2,10},{3,11},{4,12},{5,13},{6,14},{7,15},{8,0},{9,1},... | collective-permute-start | bytes 294920 | tf_op jit(solution)/shard_map/ppermute | solution.py:386
  33.5 6.6 %collective-permute-start.10 = (bf16[384,128]{1,0:T(8,128)(2,1)S(1)}, bf16[384,128]{1,0:T(8,128)(2,1)S(1)}, u32[]{:S(2)}, u32[]{:S(2)}) collective-permute-start(bf16[384,128]{1,0:T(8,128)(2,1)S(1)} %get-tuple-element.106.refs_1_), channel_id=1, source_target_pairs={{0,8},{1,9},{2,10},{3,11},{4,12},{5,13},{6,14},{7,15},{8,0},{9,1},... | collective-permute-start | bytes 294920 | tf_op jit(solution)/shard_map/ppermute | solution.py:386
  34.7 6.4 %collective-permute-start.13 = (bf16[384,128]{1,0:T(8,128)(2,1)S(1)}, bf16[384,128]{1,0:T(8,128)(2,1)S(1)}, u32[]{:S(2)}, u32[]{:S(2)}) collective-permute-start(bf16[384,128]{1,0:T(8,128)(2,1)S(1)} %halves.2.refs_9_.refs_6_), channel_id=1, source_target_pairs={{0,4},{1,5},{2,6},{3,7},{4,0},{5,1},{6,2},{7,3},{8,12},{9,13},{10,... | collective-permute-start | bytes 294920 | tf_op jit(solution)/shard_map/ppermute | solution.py:386
  40.1 4.7 %collective-permute-start.12 = (bf16[384,128]{1,0:T(8,128)(2,1)S(1)}, bf16[384,128]{1,0:T(8,128)(2,1)S(1)}, u32[]{:S(2)}, u32[]{:S(2)}) collective-permute-start(bf16[384,128]{1,0:T(8,128)(2,1)S(1)} %halves.3.refs_8_.refs_6_), channel_id=1, source_target_pairs={{0,4},{1,5},{2,6},{3,7},{4,0},{5,1},{6,2},{7,3},{8,12},{9,13},{10,... | collective-permute-start | bytes 294920 | tf_op jit(solution)/shard_map/ppermute | solution.py:386
  41.3 7.2 %collective-permute-start.15 = (bf16[768,128]{1,0:T(8,128)(2,1)S(1)}, bf16[768,128]{1,0:T(8,128)(2,1)S(1)}, u32[]{:S(2)}, u32[]{:S(2)}) collective-permute-start(bf16[768,128]{1,0:T(8,128)(2,1)S(1)} %get-tuple-element.121), channel_id=1, source_target_pairs={{0,2},{1,3},{2,0},{3,1},{4,6},{5,7},{6,4},{7,5},{8,10},{9,11},{10,... | collective-permute-start | bytes 589832 | tf_op jit(solution)/shard_map/ppermute | solution.py:386
  45.0 2.0 %copy-start.5 = (f32[6144]{0:T(1024)S(1)}, f32[6144]{0:T(1024)}, u32[]{:S(2)}) copy-start(f32[6144]{0:T(1024)} %param.11) | copy-start | bytes 73732
  45.0 5.7 %collective-permute-start.14 = (bf16[768,128]{1,0:T(8,128)(2,1)S(1)}, bf16[768,128]{1,0:T(8,128)(2,1)S(1)}, u32[]{:S(2)}, u32[]{:S(2)}) collective-permute-start(bf16[768,128]{1,0:T(8,128)(2,1)S(1)} %get-tuple-element.119), channel_id=1, source_target_pairs={{0,2},{1,3},{2,0},{3,1},{4,6},{5,7},{6,4},{7,5},{8,10},{9,11},{10,... | collective-permute-start | bytes 589832 | tf_op jit(solution)/shard_map/ppermute | solution.py:386
  48.7 2.3 %collective-permute-start.17 = (bf16[1536,128]{1,0:T(8,128)(2,1)S(1)}, bf16[1536,128]{1,0:T(8,128)(2,1)S(1)}, u32[]{:S(2)}, u32[]{:S(2)}) collective-permute-start(bf16[1536,128]{1,0:T(8,128)(2,1)S(1)} %get-tuple-element.131.refs_5_), channel_id=1, source_target_pairs={{0,1},{1,0},{2,3},{3,2},{4,5},{5,4},{6,7},{7,6},{8,9},{9,8},{10,11... | collective-permute-start | bytes 1179656 | tf_op jit(solution)/shard_map/ppermute | solution.py:386
  50.9 1.8 %collective-permute-start.16 = (bf16[1536,128]{1,0:T(8,128)(2,1)S(1)}, bf16[1536,128]{1,0:T(8,128)(2,1)S(1)}, u32[]{:S(2)}, u32[]{:S(2)}) collective-permute-start(bf16[1536,128]{1,0:T(8,128)(2,1)S(1)} %get-tuple-element.133.refs_10_), channel_id=1, source_target_pairs={{0,1},{1,0},{2,3},{3,2},{4,5},{5,4},{6,7},{7,6},{8,9},{9,8},{10,11... | collective-permute-start | bytes 1179656 | tf_op jit(solution)/shard_map/ppermute | solution.py:386

commit v7 on v6

--- a/solution.py
+++ b/solution.py
@@ -158,7 +158,8 @@
 
 
 def near_states_kernel(
-    group, key_ref, value_ref, taps_ref, map_ref, feat_ref, conv_ref, state_ref, key_first, value_first, scratch
+    group, key_ref, value_ref, taps_ref, map_ref,
+    feat_ref, conv_ref, other_ref, other_next, state_ref, key_first, value_first, scratch,
 ):
     head_dim = map_ref.shape[0]
     width = key_ref.shape[1]
@@ -181,7 +182,11 @@
             conv_ref[:, local] = value_conv
             later = jnp.where(row < back, 0.0, key_feat[:RIM].astype(f32)).astype(bf16)
             key_feat = jnp.concatenate([later, key_feat[RIM:]], axis=0)
-            state_ref[local] = state_of(key_feat, value_conv)
+            state = state_of(key_feat, value_conv)
+            if quarter < 2:
+                (other_ref, other_next)[quarter][start : start + head_dim] = state.astype(bf16)
+            else:
+                state_ref[at - 2 * size : at - 2 * size + head_dim] = state
 
 
 def near_states(group, key_seq, value_seq, conv_kernel, feature_map):
@@ -189,12 +194,13 @@
     head_dim = feature_map.shape[0]
     size = width // GROUPS
     rows, firsts = shape((tok_count, size), bf16), shape((RIM, size), bf16)
+    other = shape((size // 4, head_dim), bf16)
     return kernel_call(
         functools.partial(near_states_kernel, group),
         "near_states",
         [IN_VMEM] * 4,
-        [IN_VMEM] * 5,
-        [rows, rows, shape((size, head_dim), f32), firsts, firsts],
+        [IN_VMEM] * 7,
+        [rows, rows, other, other, shape((size // 2, head_dim), f32), firsts, firsts],
         [pltpu.VMEM((BLOCK_HEADS, 2, TILE + tok_count, head_dim), f32)],
     )(key_seq, value_seq, conv_kernel, feature_map)
 
@@ -239,17 +245,15 @@
 
 
 def first_rows_kernel(
-    group, quarters, key_ref, value_ref, taps_ref, map_ref, core_rim, chip_rim, state_ref,
-    feat_ref, conv_ref, *rest
+    group, quarters, key_ref, value_ref, taps_ref, map_ref, core_rim, chip_rim, *rest
 ):
-    (*sums, scratch) = rest
+    (*state_refs, feat_ref, conv_ref, scratch) = rest
     head_dim = map_ref.shape[0]
     width = taps_ref.shape[2]
     back = taps_ref.shape[1] - 1
-    row = lax.broadcasted_iota(jnp.int32, (RIM, head_dim), 0)
     size = width // (4 * GROUPS)
     for i, quarter in enumerate(quarters):
-        there = slice(quarter * size, (quarter + 1) * size)
+        here, there = slice(i * size, (i + 1) * size), slice(quarter * size, (quarter + 1) * size)
         natural = columns(quarter_start(quarter, width) + group * size, size)
         rim = state_rim(core_rim, chip_rim, quarter, width, group * size, size)
         conv = convolved(
@@ -258,30 +262,44 @@
         value_conv = convolved(
             scratch.at[i, 1], value_ref[:, there].astype(f32), taps_ref[2, :, natural].astype(f32), rim, 2 * back
         )
-        conv_ref[:, i * size : (i + 1) * size] = value_conv
-        parts = [slice(at, at + head_dim) for at in range(0, size, head_dim)]
-        feats = [features(conv[:, part], map_ref[...]) for part in parts]
-        feat_ref[:, i * size : (i + 1) * size] = jnp.concatenate(feats, axis=1)
-        firsts = [jnp.where(row < back, feat.astype(f32), 0.0).astype(bf16) for feat in feats]
-        for part, first in zip(parts, firsts):
-            state = state_ref[there.start + part.start : there.start + part.stop]
-            state = state + state_of(first, value_conv[:, part])
-            sums[i][part] = state.astype(sums[i].dtype)
-
-
-def first_rows(group, quarters, state_type, key_first, value_first, conv_kernel, feature_map, rims, state):
+        feats = [features(conv[:, at : at + head_dim], map_ref[...]) for at in range(0, size, head_dim)]
+        feat = jnp.concatenate(feats, axis=1)
+        feat_ref[:, here], conv_ref[:, here] = feat, value_conv
+        if state_refs:
+            old_ref, *new_refs = state_refs
+            new_refs[i][...] = old_ref[here] + first_states(feat, value_conv, head_dim, back)
+
+
+def first_states(feat, value_conv, head_dim, back):
+    row = lax.broadcasted_iota(jnp.int32, (RIM, head_dim), 0)
+    states = []
+    for at in range(0, feat.shape[1], head_dim):
+        first = jnp.where(row < back, feat[:, at : at + head_dim].astype(f32), 0.0).astype(bf16)
+        states.append(state_of(first, value_conv[:, at : at + head_dim]))
+    return jnp.concatenate(states, axis=0)
+
+
+def first_rows(group, quarters, key_first, value_first, conv_kernel, feature_map, rims, state=None):
     width = conv_kernel.shape[2]
     head_dim = feature_map.shape[0]
     size = width // (4 * GROUPS)
     rows = shape((RIM, len(quarters) * size), bf16)
+    states = [] if state is None else [shape((size, head_dim), f32)] * len(quarters)
+    operands = [key_first, value_first, conv_kernel, feature_map, *rims, *([] if state is None else [state])]
+    body = functools.partial(first_rows_kernel, group, quarters)
+
+    def reordered(*refs):
+        sources, (feat_ref, conv_ref, *sums, scratch) = refs[:6], refs[len(operands) :]
+        body(*sources, *refs[6 : len(operands)], *sums, feat_ref, conv_ref, scratch)
+
     return kernel_call(
-        functools.partial(first_rows_kernel, group, quarters),
+        reordered,
         "first_rows",
-        [IN_VMEM] * 7,
-        [IN_VMEM] * (2 + len(quarters)),
-        [rows, rows, *[shape((size, head_dim), state_type)] * len(quarters)],
+        [IN_VMEM] * len(operands),
+        [IN_VMEM] * (2 + len(states)),
+        [rows, rows, *states],
         [pltpu.VMEM((len(quarters), 2, TILE + RIM, size), f32)],
-    )(key_first, value_first, conv_kernel, feature_map, *rims, state)
+    )(*operands)
 
 
 def within_kernel(
@@ -305,7 +323,7 @@
     products = []
     for start in starts:
         local, at = slice(start, start + head_dim), slice(base + start, base + start + head_dim)
-        first = quarter % 2 * size * int(quarter >= 2) + start
+        first = quarter % 2 * size + start
         first = slice(first, first + head_dim)
         key, value = key_ref[:, at], value_ref[:, at]
         if firsts:
@@ -439,11 +457,15 @@
             q, g = fill.pop(0)
             first = ()
             if firsts[g]:
-                first = [part[q] for part in firsts[g][0]] if q < 2 else firsts[g][1]
+                first = firsts[g][q // 2]
             mixed[q, g] = within_block(q, g, query_seq, conv_kernel, feature_map, rims, *near[g][q], first)
 
-    def chip_sums(device, paired, own, paired_arrived, own_arrived):
-        return paired + paired_arrived.astype(f32), own + own_arrived.astype(f32)
+    def chip_sums(device, paired, own, *arrived):
+        states, firsts = [part.astype(f32) for part in arrived[:2]], arrived[2:]
+        for first in firsts:
+            more = first_states(first[:RIM], first[RIM:], head_dim, tap_count - 1)
+            states = [states[0] + more[:rows], states[1] + more[rows:]]
+        return paired + states[0], own + states[1], *states
 
     def pair_sums(device, own, arrived):
         total = own + arrived.astype(f32)
@@ -492,18 +514,15 @@
 
     for g in groups:
         if g == 0:
-            *kept, partial, key_first, value_first = near_states(g, key_seq, value_seq, conv_kernel, feature_map)
+            *kept, other, other_next, partial, key_first, value_first = near_states(
+                g, key_seq, value_seq, conv_kernel, feature_map
+            )
             near.append([(*kept, q * rows) for q in range(4)])
-            others, first_a = [], [[], []]
-            for q in (0, 1):
-                *first, other = first_rows(
-                    g, (q,), bf16, key_first, value_first, conv_kernel, feature_map, rims, partial
-                )
-                others.append(swapped(other, 1))
-                first_a[0].append(first[0])
-                first_a[1].append(first[1])
+            others = [swapped(other, 1), swapped(other_next, 1)]
+            first_a = first_rows(g, (0, 1), key_first, value_first, conv_kernel, feature_map, rims)
+            others.append(swapped(jnp.concatenate(first_a, axis=0), 1))
             *first_b, paired, single = first_rows(
-                g, (2, 3), f32, key_first, value_first, conv_kernel, feature_map, rims, partial
+                g, (2, 3), key_first, value_first, conv_kernel, feature_map, rims, partial
             )
             firsts.append((first_a, first_b))
         else:
@@ -519,8 +538,10 @@
             firsts.append(None)
             pair_step(g - 1)
         state_b.append((paired, single))
+        give, own, *others = mapped(
+            "chip_sums", chip_sums, [(rows, bf16), (rows, f32), (rows, f32), (rows, f32)], paired, single, *others
+        )
         from_core.append(others)
-        give, own = mapped("chip_sums", chip_sums, [(rows, bf16), (rows, f32)], paired, single, *others)
         chip.append(own)
         arriving.append(swapped(give, 2))
     score(0.375)

time: 54.4 us -> 52.4 us (0.963)
  waiting for transfers between devices: 9.02 us -> 5.7 us
  starting transfers between devices: 20.4 us -> 22 us
    ppermute x17 -> x18, waiting for transfers between devices: 9.02 us -> 5.69 us  [swapped(): lax.ppermute(block, 'seq', [(i, i ^ distance) for i in range(lax.axis_siz...]
    ppermute x17 -> x18, starting transfers between devices: 19.9 us -> 21.5 us  [swapped(): lax.ppermute(block, 'seq', [(i, i ^ distance) for i in range(lax.axis_siz...]
    pallas_call x31 -> x30, Pallas kernels: 24.3 us -> 24.1 us  [call(): pl.pallas_call(ordered, in_specs=[*in_specs, *[IN_PLACE] * len(before)],...]
  transfers between devices with their start and end apart: 18 -> 19, of which waited for: 9 -> 9; matrix products, arithmetic and copies ran while one was open for 0% -> 0% of each run, Pallas kernels for 39% -> 40%
where the time goes in v7:
time: 52.4 us; the launch traced here: 52.3 us
  Pallas kernels  24.1 us (46%)
  starting transfers between devices  22 us (42%)
  waiting for transfers between devices  5.7 us (11%)
    pallas_call x30, Pallas kernels, call(): pl.pallas_call(ordered, in_specs=[*in_specs, *[IN_PLACE] * len(before)],...  24.1 us
    ppermute x18, starting transfers between devices, swapped(): lax.ppermute(block, 'seq', [(i, i ^ distance) for i in range(lax.axis_siz...  21.5 us
    ppermute x18, waiting for transfers between devices, swapped(): lax.ppermute(block, 'seq', [(i, i ^ distance) for i in range(lax.axis_siz...  5.69 us
  transfers between devices with their start and end apart: 19, of which 9 were waited for; matrix products, arithmetic and copies ran while one was open for 0% of the time, Pallas kernels for 40%

profile of v7, /device:TPU:0, one launch (start us, length us, event | category | flops | bytes accessed | tf_op | source)
XLA Modules:
  0.0 52.3 jit_solution(2052682995856150689)
XLA Ops:
  0.0 1.3 %pack_rims.1.refs_4_ = bf16[16,4608]{1,0:T(8,128)(2,1)S(1)} custom-call(bf16[256,6144]{1,0:T(8,128)(2,1)} %refs_0_.23, bf16[256,6144]{1,0:T(8,128)(2,1)} %refs_0_.15, bf16[256,6144]{1,0:T(8,128)(2,1)} %refs_1_.15), custom_call_target="tpu_custom_call" | custom-call | flops 1024 | bytes 1024 | tf_op jit(solution)/shard_map/pack_rims/pallas_call | solution.py:39
  1.4 0.5 collective-permute-start.1
  1.9 2.6 %collective-permute-start = (bf16[16,4608]{1,0:T(8,128)(2,1)S(1)}, bf16[16,4608]{1,0:T(8,128)(2,1)S(1)}, u32[]{:S(2)}, u32[]{:S(2)}) collective-permute-start(bf16[16,4608]{1,0:T(8,128)(2,1)S(1)} %pack_rims.1.refs_4_), channel_id=1, source_target_pairs={{0,1},{1,0},{2,3},{3,2},{4,5},{5,4},{6,7},{7,6},{8,9},{9,8},{10,11... | collective-permute-start | bytes 442376 | tf_op jit(solution)/shard_map/ppermute | solution.py:404
  4.5 3.6 %near_states.1 = (bf16[256,3072]{1,0:T(8,128)(2,1)S(1)}, bf16[256,3072]{1,0:T(8,128)(2,1)S(1)}, bf16[768,128]{1,0:T(8,128)(2,1)S(1)}, bf16[768,128]{1,0:T(8,128)...) custom-call(bf16[256,6144]{1,0:T(8,128)(2,1)S(1)} %copy-done.1, ...), custom_call_target="tpu_custom_call" | custom-call | flops 1024 | bytes 1024 | tf_op jit(solution)/shard_map/near_states/pallas_call | solution.py:39
  8.2 0.5 collective-permute-start.3
  8.7 0.3 first_rows.2
  9.0 0.1 collective-permute-start.4
  9.2 0.7 %first_rows.3 = (bf16[16,1536]{1,0:T(8,128)(2,1)S(1)}, bf16[16,1536]{1,0:T(8,128)(2,1)S(1)}, f32[768,128]{1,0:T(8,128)S(1)}, f32[768,128]{1,0:T(8,128)S(1)}) custom-call(bf16[16,3072]{1,0:T(8,128)(2,1)S(1)} %get-tuple-element.76.refs_0_, bf16[16,3072]{1,0:T(8,128)(2,1)S(1)} %get-tuple-element.77.refs_1_.refs_6_, bf16[3,4,6144]{2,1,0:T(4,128)(2,1)S(1)} %copy-done.3, ...), custom_call_target="tpu_custom_call" | custom-call | flops 1024 | bytes 1024 | tf_op jit(solution)/shard_map/first_rows/pallas_call | solution.py:39
  9.9 0.5 collective-permute-done.4.refs_4_
  10.4 0.3 chip_sums.2
  10.7 1.9 %collective-permute-start.7 = (bf16[768,128]{1,0:T(8,128)(2,1)S(1)}, bf16[768,128]{1,0:T(8,128)(2,1)S(1)}, u32[]{:S(2)}, u32[]{:S(2)}) collective-permute-start(bf16[768,128]{1,0:T(8,128)(2,1)S(1)} %get-tuple-element.91), channel_id=1, source_target_pairs={{0,2},{1,3},{2,0},{3,1},{4,6},{5,7},{6,4},{7,5},{8,10},{9,11},{10,... | collective-permute-start | bytes 589832 | tf_op jit(solution)/shard_map/ppermute | solution.py:404
  12.6 1.9 %whole_states.2 = (bf16[256,1536]{1,0:T(8,128)(2,1)S(1)}, bf16[256,1536]{1,0:T(8,128)(2,1)S(1)}, bf16[768,128]{1,0:T(8,128)(2,1)S(1)}, bf16[768,128]{1,0:T(8,128)(2,1)S(1)}) custom-call(bf16[256,6144]{1,0:T(8,128)(2,1)S(1)} %copy-done.1, bf16[256,6144]{1,0:T(8,128)(2,1)S(1)} %copy-done.2, bf16[3,4,6144]{2,1,0:T(4,128)(2,1)S(1)} %copy-done.3, ...), custom_call_target="tpu_custom_call" | custom-call | flops 1024 | bytes 1024 | tf_op jit(solution)/shard_map/whole_states/pallas_call | solution.py:39
  14.6 0.5 collective-permute-start.6
  15.1 1.9 %whole_states.3 = (bf16[256,1536]{1,0:T(8,128)(2,1)S(1)}, bf16[256,1536]{1,0:T(8,128)(2,1)S(1)}, f32[768,128]{1,0:T(8,128)S(1)}, f32[768,128]{1,0:T(8,128)S(1)}) custom-call(bf16[256,6144]{1,0:T(8,128)(2,1)S(1)} %copy-done.1, bf16[256,6144]{1,0:T(8,128)(2,1)S(1)} %copy-done.2, bf16[3,4,6144]{2,1,0:T(4,128)(2,1)S(1)} %copy-done.3, ...), custom_call_target="tpu_custom_call" | custom-call | flops 1024 | bytes 1024 | tf_op jit(solution)/shard_map/whole_states/pallas_call | solution.py:39
  17.0 0.9 %collective-permute-done.7.refs_1_ = bf16[768,128]{1,0:T(8,128)(2,1)S(1)} collective-permute-done((bf16[768,128]{1,0:T(8,128)(2,1)S(1)}, bf16[768,128]{1,0:T(8,128)(2,1)S(1)}, u32[]{:S(2)}, u32[]{:S(2)}) %collective-permute-start.7) | collective-permute-done | bytes 196640 | tf_op jit(solution)/shard_map/ppermute | solution.py:404
  18.0 1.8 %collective-permute-start.8 = (bf16[768,128]{1,0:T(8,128)(2,1)S(1)}, bf16[768,128]{1,0:T(8,128)(2,1)S(1)}, u32[]{:S(2)}, u32[]{:S(2)}) collective-permute-start(bf16[768,128]{1,0:T(8,128)(2,1)S(1)} %get-tuple-element.94), channel_id=1, source_target_pairs={{0,2},{1,3},{2,0},{3,1},{4,6},{5,7},{6,4},{7,5},{8,10},{9,11},{10,... | collective-permute-start | bytes 589832 | tf_op jit(solution)/shard_map/ppermute | solution.py:404
  19.8 1.6 %collective-permute-start.10 = (bf16[768,128]{1,0:T(8,128)(2,1)S(1)}, bf16[768,128]{1,0:T(8,128)(2,1)S(1)}, u32[]{:S(2)}, u32[]{:S(2)}) collective-permute-start(bf16[768,128]{1,0:T(8,128)(2,1)S(1)} %get-tuple-element.92.refs_4_), channel_id=1, source_target_pairs={{0,4},{1,5},{2,6},{3,7},{4,0},{5,1},{6,2},{7,3},{8,12},{9,13},{10,... | collective-permute-start | bytes 589832 | tf_op jit(solution)/shard_map/ppermute | solution.py:404
  21.4 0.9 %within_block.8 = (bf16[256,768]{1,0:T(8,128)(2,1)S(1)}, f32[256,768]{1,0:T(8,128)S(1)}) custom-call(bf16[256,6144]{1,0:T(8,128)(2,1)S(1)} %copy-done, bf16[3,4,6144]{2,1,0:T(4,128)(2,1)S(1)} %copy-done.3, bf16[128,128]{1,0:T(8,128)(2,1)S(1)} %copy-done.4, bf16[16,4608]{1,0:T(8,128)(2,1)S(1)} %collective-permute-done.refs_4_.refs_3_, ...), custom_call_target="tpu_custom_call" | custom-call | flops 1024 | bytes 1024 | tf_op jit(solution)/shard_map/within_block/pallas_call | solution.py:39
  22.3 0.9 %within_block.9 = (bf16[256,768]{1,0:T(8,128)(2,1)S(1)}, f32[256,768]{1,0:T(8,128)S(1)}) custom-call(bf16[256,6144]{1,0:T(8,128)(2,1)S(1)} %copy-done, bf16[3,4,6144]{2,1,0:T(4,128)(2,1)S(1)} %copy-done.3, bf16[128,128]{1,0:T(8,128)(2,1)S(1)} %copy-done.4, bf16[16,4608]{1,0:T(8,128)(2,1)S(1)} %collective-permute-done.refs_4_.refs_3_, ...), custom_call_target="tpu_custom_call" | custom-call | flops 1024 | bytes 1024 | tf_op jit(solution)/shard_map/within_block/pallas_call | solution.py:39
  23.2 0.9 %within_block.10 = (bf16[256,768]{1,0:T(8,128)(2,1)S(1)}, f32[256,768]{1,0:T(8,128)S(1)}) custom-call(bf16[256,6144]{1,0:T(8,128)(2,1)S(1)} %copy-done, bf16[3,4,6144]{2,1,0:T(4,128)(2,1)S(1)} %copy-done.3, bf16[128,128]{1,0:T(8,128)(2,1)S(1)} %copy-done.4, bf16[16,4608]{1,0:T(8,128)(2,1)S(1)} %collective-permute-done.refs_4_.refs_3_, ...), custom_call_target="tpu_custom_call" | custom-call | flops 1024 | bytes 1024 | tf_op jit(solution)/shard_map/within_block/pallas_call | solution.py:39
  24.2 0.2 collective-permute-done.8.refs_1_
  24.4 1.6 %collective-permute-start.9 = (bf16[768,128]{1,0:T(8,128)(2,1)S(1)}, bf16[768,128]{1,0:T(8,128)(2,1)S(1)}, u32[]{:S(2)}, u32[]{:S(2)}) collective-permute-start(bf16[768,128]{1,0:T(8,128)(2,1)S(1)} %get-tuple-element.106.refs_2_), channel_id=1, source_target_pairs={{0,4},{1,5},{2,6},{3,7},{4,0},{5,1},{6,2},{7,3},{8,12},{9,13},{10,... | collective-permute-start | bytes 589832 | tf_op jit(solution)/shard_map/ppermute | solution.py:404
  26.0 0.1 plane_sums.2
  26.1 2.6 %collective-permute-start.12 = (bf16[384,128]{1,0:T(8,128)(2,1)S(1)}, bf16[384,128]{1,0:T(8,128)(2,1)S(1)}, u32[]{:S(2)}, u32[]{:S(2)}) collective-permute-start(bf16[384,128]{1,0:T(8,128)(2,1)S(1)} %get-tuple-element.108.refs_7_), channel_id=1, source_target_pairs={{0,8},{1,9},{2,10},{3,11},{4,12},{5,13},{6,14},{7,15},{8,0},{9,1},... | collective-permute-start | bytes 294920 | tf_op jit(solution)/shard_map/ppermute | solution.py:404
  28.6 0.9 %within_block.11 = (bf16[256,768]{1,0:T(8,128)(2,1)S(1)}, f32[256,768]{1,0:T(8,128)S(1)}) custom-call(bf16[256,6144]{1,0:T(8,128)(2,1)S(1)} %copy-done, bf16[3,4,6144]{2,1,0:T(4,128)(2,1)S(1)} %copy-done.3, bf16[128,128]{1,0:T(8,128)(2,1)S(1)} %copy-done.4, bf16[16,4608]{1,0:T(8,128)(2,1)S(1)} %collective-permute-done.refs_4_.refs_3_, ...), custom_call_target="tpu_custom_call" | custom-call | flops 1024 | bytes 1024 | tf_op jit(solution)/shard_map/within_block/pallas_call | solution.py:39
  29.5 1.8 %collective-permute-done.9.refs_1_ = bf16[768,128]{1,0:T(8,128)(2,1)S(1)} collective-permute-done((bf16[768,128]{1,0:T(8,128)(2,1)S(1)}, bf16[768,128]{1,0:T(8,128)(2,1)S(1)}, u32[]{:S(2)}, u32[]{:S(2)}) %collective-permute-start.9) | collective-permute-done | bytes 196640 | tf_op jit(solution)/shard_map/ppermute | solution.py:404
  31.3 0.1 plane_sums.3
  31.4 2.4 %collective-permute-start.11 = (bf16[384,128]{1,0:T(8,128)(2,1)S(1)}, bf16[384,128]{1,0:T(8,128)(2,1)S(1)}, u32[]{:S(2)}, u32[]{:S(2)}) collective-permute-start(bf16[384,128]{1,0:T(8,128)(2,1)S(1)} %get-tuple-element.112.refs_1_), channel_id=1, source_target_pairs={{0,8},{1,9},{2,10},{3,11},{4,12},{5,13},{6,14},{7,15},{8,0},{9,1},... | collective-permute-start | bytes 294920 | tf_op jit(solution)/shard_map/ppermute | solution.py:404
  33.8 2.0 %collective-permute-start.14 = (bf16[384,128]{1,0:T(8,128)(2,1)S(1)}, bf16[384,128]{1,0:T(8,128)(2,1)S(1)}, u32[]{:S(2)}, u32[]{:S(2)}) collective-permute-start(bf16[384,128]{1,0:T(8,128)(2,1)S(1)} %halves.2.refs_9_.refs_6_), channel_id=1, source_target_pairs={{0,4},{1,5},{2,6},{3,7},{4,0},{5,1},{6,2},{7,3},{8,12},{9,13},{10,... | collective-permute-start | bytes 294920 | tf_op jit(solution)/shard_map/ppermute | solution.py:404
  35.8 1.1 %within_block.12 = (bf16[256,768]{1,0:T(8,128)(2,1)S(1)}, f32[256,768]{1,0:T(8,128)S(1)}) custom-call(bf16[256,6144]{1,0:T(8,128)(2,1)S(1)} %copy-done, bf16[3,4,6144]{2,1,0:T(4,128)(2,1)S(1)} %copy-done.3, bf16[128,128]{1,0:T(8,128)(2,1)S(1)} %copy-done.4, bf16[16,4608]{1,0:T(8,128)(2,1)S(1)} %collective-permute-done.refs_4_.refs_3_, ...), custom_call_target="tpu_custom_call" | custom-call | flops 1024 | bytes 1024 | tf_op jit(solution)/shard_map/within_block/pallas_call | solution.py:39
  36.9 0.9 %within_block.13 = (bf16[256,768]{1,0:T(8,128)(2,1)S(1)}, f32[256,768]{1,0:T(8,128)S(1)}) custom-call(bf16[256,6144]{1,0:T(8,128)(2,1)S(1)} %copy-done, bf16[3,4,6144]{2,1,0:T(4,128)(2,1)S(1)} %copy-done.3, bf16[128,128]{1,0:T(8,128)(2,1)S(1)} %copy-done.4, bf16[16,4608]{1,0:T(8,128)(2,1)S(1)} %collective-permute-done.refs_4_.refs_3_, ...), custom_call_target="tpu_custom_call" | custom-call | flops 1024 | bytes 1024 | tf_op jit(solution)/shard_map/within_block/pallas_call | solution.py:39
  37.8 0.3 collective-permute-done.11.refs_0_
  38.2 0.3 collective-permute-start.13
  38.5 0.9 %collective-permute-done.14.refs_7_ = bf16[384,128]{1,0:T(8,128)(2,1)S(1)} collective-permute-done((bf16[384,128]{1,0:T(8,128)(2,1)S(1)}, bf16[384,128]{1,0:T(8,128)(2,1)S(1)}, u32[]{:S(2)}, u32[]{:S(2)}) %collective-permute-start.14) | collective-permute-done | bytes 98336 | tf_op jit(solution)/shard_map/ppermute | solution.py:404
  39.4 0.2 own_prefixes.2
  39.6 1.8 %collective-permute-start.16 = (bf16[768,128]{1,0:T(8,128)(2,1)S(1)}, bf16[768,128]{1,0:T(8,128)(2,1)S(1)}, u32[]{:S(2)}, u32[]{:S(2)}) collective-permute-start(bf16[768,128]{1,0:T(8,128)(2,1)S(1)} %get-tuple-element.124), channel_id=1, source_target_pairs={{0,2},{1,3},{2,0},{3,1},{4,6},{5,7},{6,4},{7,5},{8,10},{9,11},{10,... | collective-permute-start | bytes 589832 | tf_op jit(solution)/shard_map/ppermute | solution.py:404
  41.3 0.9 %within_block.14 = (bf16[256,768]{1,0:T(8,128)(2,1)S(1)}, f32[256,768]{1,0:T(8,128)S(1)}) custom-call(bf16[256,6144]{1,0:T(8,128)(2,1)S(1)} %copy-done, bf16[3,4,6144]{2,1,0:T(4,128)(2,1)S(1)} %copy-done.3, bf16[128,128]{1,0:T(8,128)(2,1)S(1)} %copy-done.4, bf16[16,4608]{1,0:T(8,128)(2,1)S(1)} %collective-permute-done.refs_4_.refs_3_, ...), custom_call_target="tpu_custom_call" | custom-call | flops 1024 | bytes 1024 | tf_op jit(solution)/shard_map/within_block/pallas_call | solution.py:39
  42.3 0.6 %collective-permute-done.13.refs_7_ = bf16[384,128]{1,0:T(8,128)(2,1)S(1)} collective-permute-done((bf16[384,128]{1,0:T(8,128)(2,1)S(1)}, bf16[384,128]{1,0:T(8,128)(2,1)S(1)}, u32[]{:S(2)}, u32[]{:S(2)}) %collective-permute-start.13) | collective-permute-done | bytes 98336 | tf_op jit(solution)/shard_map/ppermute | solution.py:404
  42.8 0.2 own_prefixes.3
  43.0 1.5 %collective-permute-start.15 = (bf16[768,128]{1,0:T(8,128)(2,1)S(1)}, bf16[768,128]{1,0:T(8,128)(2,1)S(1)}, u32[]{:S(2)}, u32[]{:S(2)}) collective-permute-start(bf16[768,128]{1,0:T(8,128)(2,1)S(1)} %get-tuple-element.121), channel_id=1, source_target_pairs={{0,2},{1,3},{2,0},{3,1},{4,6},{5,7},{6,4},{7,5},{8,10},{9,11},{10,... | collective-permute-start | bytes 589832 | tf_op jit(solution)/shard_map/ppermute | solution.py:404
  44.5 0.9 %within_block.15 = (bf16[256,768]{1,0:T(8,128)(2,1)S(1)}, f32[256,768]{1,0:T(8,128)S(1)}) custom-call(bf16[256,6144]{1,0:T(8,128)(2,1)S(1)} %copy-done, bf16[3,4,6144]{2,1,0:T(4,128)(2,1)S(1)} %copy-done.3, bf16[128,128]{1,0:T(8,128)(2,1)S(1)} %copy-done.4, bf16[16,4608]{1,0:T(8,128)(2,1)S(1)} %collective-permute-done.refs_4_.refs_3_, ...), custom_call_target="tpu_custom_call" | custom-call | flops 1024 | bytes 1024 | tf_op jit(solution)/shard_map/within_block/pallas_call | solution.py:39
  45.4 1.4 %finish.4 = (bf16[256,6144]{1,0:T(8,128)(2,1)}, f32[8,128]{1,0:T(8,128)S(1)}) custom-call(f32[1,6144]{1,0:T(1,128)S(1)} %bitcast.1, bf16[768,128]{1,0:T(8,128)(2,1)S(1)} %get-tuple-element.126.refs_1_, bf16[768,128]{1,0:T(8,128)(2,1)S(1)} %get-tuple-element.127.refs_2_, bf16[256,768]{1,0:T(8,128)(2,1)S(1)} %get-tuple-element.128.refs_3_, ...), custom_call_target="tpu_custom_call" | custom-call | flops 1024 | bytes 1024 | tf_op jit(solution)/shard_map/finish/pallas_call | solution.py:39
  46.8 0.1 paired_prefixes.2
  47.0 1.2 %finish.5 = (bf16[256,6144]{1,0:T(8,128)(2,1)}, f32[8,128]{1,0:T(8,128)S(1)}) custom-call(f32[1,6144]{1,0:T(1,128)S(1)} %bitcast.2, bf16[768,128]{1,0:T(8,128)(2,1)S(1)} %get-tuple-element.132.refs_1_, bf16[256,768]{1,0:T(8,128)(2,1)S(1)} %get-tuple-element.133.refs_2_, ...), custom_call_target="tpu_custom_call", output_to_operand_aliasing={{0}: (4, {})} | custom-call | flops 1024 | bytes 1024 | tf_op jit(solution)/shard_map/finish/pallas_call | solution.py:39
  48.3 0.5 collective-permute-done.15.refs_0_
  48.8 0.1 paired_prefixes.3
  49.0 1.6 %finish.6 = (bf16[256,6144]{1,0:T(8,128)(2,1)}, f32[8,128]{1,0:T(8,128)S(1)}) custom-call(f32[1,6144]{1,0:T(1,128)S(1)} %bitcast.3, bf16[768,128]{1,0:T(8,128)(2,1)S(1)} %get-tuple-element.140.refs_1_, bf16[1536,128]{1,0:T(8,128)(2,1)S(1)} %collective-permute-done.18.refs_2_, ...), custom_call_target="tpu_custom_call", output_to_operand_aliasing={{0}: (9, {})} | custom-call | flops 1024 | bytes 1024 | tf_op jit(solution)/shard_map/finish/pallas_call | solution.py:39
  50.7 1.4 %finish.7 = bf16[256,6144]{1,0:T(8,128)(2,1)} custom-call(f32[1,6144]{1,0:T(1,128)S(1)} %bitcast.4, bf16[1536,128]{1,0:T(8,128)(2,1)S(1)} %collective-permute-done.17.refs_1_, bf16[256,768]{1,0:T(8,128)(2,1)S(1)} %get-tuple-element.138.refs_2_, bf16[256,768]{1,0:T(8,128)(2,1)S(1)} %get-tuple-element.139.refs_3_, ...), custom_call_target="tpu_custom_call", output_to_operand_aliasing={{}: (6, {})} | custom-call | flops 1024 | bytes 1024 | tf_op jit(solution)/shard_map/finish/pallas_call | solution.py:39
  (33 shorter events, 0.7 us)
Async XLA Ops:
  0.0 4.5 %copy-start.2 = (bf16[256,6144]{1,0:T(8,128)(2,1)S(1)}, bf16[256,6144]{1,0:T(8,128)(2,1)}, u32[]{:S(2)}) copy-start(bf16[256,6144]{1,0:T(8,128)(2,1)} %refs_1_.15) | copy-start | bytes 9437188
  0.0 4.5 %copy-start.1 = (bf16[256,6144]{1,0:T(8,128)(2,1)S(1)}, bf16[256,6144]{1,0:T(8,128)(2,1)}, u32[]{:S(2)}) copy-start(bf16[256,6144]{1,0:T(8,128)(2,1)} %refs_0_.15) | copy-start | bytes 9437188
  0.0 4.5 %copy-start.4 = (bf16[128,128]{1,0:T(8,128)(2,1)S(1)}, bf16[128,128]{1,0:T(8,128)(2,1)}, u32[]{:S(2)}) copy-start(bf16[128,128]{1,0:T(8,128)(2,1)} %refs_2_.27) | copy-start | bytes 98308
  0.0 4.5 %copy-start.3 = (bf16[3,4,6144]{2,1,0:T(4,128)(2,1)S(1)}, bf16[3,4,6144]{2,1,0:T(4,128)(2,1)}, u32[]{:S(2)}) copy-start(bf16[3,4,6144]{2,1,0:T(4,128)(2,1)} %refs_1_.23) | copy-start | bytes 442372
  1.4 7.4 %collective-permute-start.1 = (bf16[16,4608]{1,0:T(8,128)(2,1)S(1)}, bf16[16,4608]{1,0:T(8,128)(2,1)S(1)}, u32[]{:S(2)}, u32[]{:S(2)}) collective-permute-start(bf16[16,4608]{1,0:T(8,128)(2,1)S(1)} %pack_rims.1.refs_4_), channel_id=1, source_target_pairs={{0,1},{1,2},{2,0},{3,4},{4,3},{5,6},{6,5},{7,8},{8,7},{9,10},{10,9... | collective-permute-start | bytes 442376 | tf_op jit(solution)/shard_map/ppermute | solution.py:412
  1.9 6.8 %collective-permute-start = (bf16[16,4608]{1,0:T(8,128)(2,1)S(1)}, bf16[16,4608]{1,0:T(8,128)(2,1)S(1)}, u32[]{:S(2)}, u32[]{:S(2)}) collective-permute-start(bf16[16,4608]{1,0:T(8,128)(2,1)S(1)} %pack_rims.1.refs_4_), channel_id=1, source_target_pairs={{0,1},{1,0},{2,3},{3,2},{4,5},{5,4},{6,7},{7,6},{8,9},{9,8},{10,11... | collective-permute-start | bytes 442376 | tf_op jit(solution)/shard_map/ppermute | solution.py:404
  8.1 1.7 %collective-permute-start.2 = (bf16[768,128]{1,0:T(8,128)(2,1)S(1)}, bf16[768,128]{1,0:T(8,128)(2,1)S(1)}, u32[]{:S(2)}, u32[]{:S(2)}) collective-permute-start(bf16[768,128]{1,0:T(8,128)(2,1)S(1)} %get-tuple-element.82), channel_id=1, source_target_pairs={{0,1},{1,0},{2,3},{3,2},{4,5},{5,4},{6,7},{7,6},{8,9},{9,8},{10,11... | collective-permute-start | bytes 589832 | tf_op jit(solution)/shard_map/ppermute | solution.py:404
  8.2 1.7 %collective-permute-start.3 = (bf16[768,128]{1,0:T(8,128)(2,1)S(1)}, bf16[768,128]{1,0:T(8,128)(2,1)S(1)}, u32[]{:S(2)}, u32[]{:S(2)}) collective-permute-start(bf16[768,128]{1,0:T(8,128)(2,1)S(1)} %get-tuple-element.83), channel_id=1, source_target_pairs={{0,1},{1,0},{2,3},{3,2},{4,5},{5,4},{6,7},{7,6},{8,9},{9,8},{10,11... | collective-permute-start | bytes 589832 | tf_op jit(solution)/shard_map/ppermute | solution.py:404
  9.0 1.4 %collective-permute-start.4 = (bf16[32,1536]{1,0:T(8,128)(2,1)S(1)}, bf16[32,1536]{1,0:T(8,128)(2,1)S(1)}, u32[]{:S(2)}, u32[]{:S(2)}) collective-permute-start(bf16[32,1536]{1,0:T(8,128)(2,1)S(1)} %pad_maximum_fusion), channel_id=1, source_target_pairs={{0,1},{1,0},{2,3},{3,2},{4,5},{5,4},{6,7},{7,6},{8,9},{9,8},{10,11... | collective-permute-start | bytes 294920 | tf_op jit(solution)/shard_map/ppermute | solution.py:404
  10.7 7.1 %collective-permute-start.7 = (bf16[768,128]{1,0:T(8,128)(2,1)S(1)}, bf16[768,128]{1,0:T(8,128)(2,1)S(1)}, u32[]{:S(2)}, u32[]{:S(2)}) collective-permute-start(bf16[768,128]{1,0:T(8,128)(2,1)S(1)} %get-tuple-element.91), channel_id=1, source_target_pairs={{0,2},{1,3},{2,0},{3,1},{4,6},{5,7},{6,4},{7,5},{8,10},{9,11},{10,... | collective-permute-start | bytes 589832 | tf_op jit(solution)/shard_map/ppermute | solution.py:404
  14.5 3.4 %collective-permute-start.5 = (bf16[768,128]{1,0:T(8,128)(2,1)S(1)}, bf16[768,128]{1,0:T(8,128)(2,1)S(1)}, u32[]{:S(2)}, u32[]{:S(2)}) collective-permute-start(bf16[768,128]{1,0:T(8,128)(2,1)S(1)} %get-tuple-element.89), channel_id=1, source_target_pairs={{0,1},{1,0},{2,3},{3,2},{4,5},{5,4},{6,7},{7,6},{8,9},{9,8},{10,11... | collective-permute-start | bytes 589832 | tf_op jit(solution)/shard_map/ppermute | solution.py:404
  14.6 6.8 %copy-start = (bf16[256,6144]{1,0:T(8,128)(2,1)S(1)}, bf16[256,6144]{1,0:T(8,128)(2,1)}, u32[]{:S(2)}) copy-start(bf16[256,6144]{1,0:T(8,128)(2,1)} %refs_0_.23) | copy-start | bytes 9437188
  14.6 3.3 %collective-permute-start.6 = (bf16[768,128]{1,0:T(8,128)(2,1)S(1)}, bf16[768,128]{1,0:T(8,128)(2,1)S(1)}, u32[]{:S(2)}, u32[]{:S(2)}) collective-permute-start(bf16[768,128]{1,0:T(8,128)(2,1)S(1)} %get-tuple-element.86.refs_6_), channel_id=1, source_target_pairs={{0,1},{1,0},{2,3},{3,2},{4,5},{5,4},{6,7},{7,6},{8,9},{9,8},{10,11... | collective-permute-start | bytes 589832 | tf_op jit(solution)/shard_map/ppermute | solution.py:404
  18.0 6.3 %collective-permute-start.8 = (bf16[768,128]{1,0:T(8,128)(2,1)S(1)}, bf16[768,128]{1,0:T(8,128)(2,1)S(1)}, u32[]{:S(2)}, u32[]{:S(2)}) collective-permute-start(bf16[768,128]{1,0:T(8,128)(2,1)S(1)} %get-tuple-element.94), channel_id=1, source_target_pairs={{0,2},{1,3},{2,0},{3,1},{4,6},{5,7},{6,4},{7,5},{8,10},{9,11},{10,... | collective-permute-start | bytes 589832 | tf_op jit(solution)/shard_map/ppermute | solution.py:404
  19.8 6.1 %collective-permute-start.10 = (bf16[768,128]{1,0:T(8,128)(2,1)S(1)}, bf16[768,128]{1,0:T(8,128)(2,1)S(1)}, u32[]{:S(2)}, u32[]{:S(2)}) collective-permute-start(bf16[768,128]{1,0:T(8,128)(2,1)S(1)} %get-tuple-element.92.refs_4_), channel_id=1, source_target_pairs={{0,4},{1,5},{2,6},{3,7},{4,0},{5,1},{6,2},{7,3},{8,12},{9,13},{10,... | collective-permute-start | bytes 589832 | tf_op jit(solution)/shard_map/ppermute | solution.py:404
  24.4 6.9 %collective-permute-start.9 = (bf16[768,128]{1,0:T(8,128)(2,1)S(1)}, bf16[768,128]{1,0:T(8,128)(2,1)S(1)}, u32[]{:S(2)}, u32[]{:S(2)}) collective-permute-start(bf16[768,128]{1,0:T(8,128)(2,1)S(1)} %get-tuple-element.106.refs_2_), channel_id=1, source_target_pairs={{0,4},{1,5},{2,6},{3,7},{4,0},{5,1},{6,2},{7,3},{8,12},{9,13},{10,... | collective-permute-start | bytes 589832 | tf_op jit(solution)/shard_map/ppermute | solution.py:404
  26.1 7.7 %collective-permute-start.12 = (bf16[384,128]{1,0:T(8,128)(2,1)S(1)}, bf16[384,128]{1,0:T(8,128)(2,1)S(1)}, u32[]{:S(2)}, u32[]{:S(2)}) collective-permute-start(bf16[384,128]{1,0:T(8,128)(2,1)S(1)} %get-tuple-element.108.refs_7_), channel_id=1, source_target_pairs={{0,8},{1,9},{2,10},{3,11},{4,12},{5,13},{6,14},{7,15},{8,0},{9,1},... | collective-permute-start | bytes 294920 | tf_op jit(solution)/shard_map/ppermute | solution.py:404
  31.4 6.7 %collective-permute-start.11 = (bf16[384,128]{1,0:T(8,128)(2,1)S(1)}, bf16[384,128]{1,0:T(8,128)(2,1)S(1)}, u32[]{:S(2)}, u32[]{:S(2)}) collective-permute-start(bf16[384,128]{1,0:T(8,128)(2,1)S(1)} %get-tuple-element.112.refs_1_), channel_id=1, source_target_pairs={{0,8},{1,9},{2,10},{3,11},{4,12},{5,13},{6,14},{7,15},{8,0},{9,1},... | collective-permute-start | bytes 294920 | tf_op jit(solution)/shard_map/ppermute | solution.py:404
  33.8 5.6 %collective-permute-start.14 = (bf16[384,128]{1,0:T(8,128)(2,1)S(1)}, bf16[384,128]{1,0:T(8,128)(2,1)S(1)}, u32[]{:S(2)}, u32[]{:S(2)}) collective-permute-start(bf16[384,128]{1,0:T(8,128)(2,1)S(1)} %halves.2.refs_9_.refs_6_), channel_id=1, source_target_pairs={{0,4},{1,5},{2,6},{3,7},{4,0},{5,1},{6,2},{7,3},{8,12},{9,13},{10,... | collective-permute-start | bytes 294920 | tf_op jit(solution)/shard_map/ppermute | solution.py:404
  38.2 4.7 %collective-permute-start.13 = (bf16[384,128]{1,0:T(8,128)(2,1)S(1)}, bf16[384,128]{1,0:T(8,128)(2,1)S(1)}, u32[]{:S(2)}, u32[]{:S(2)}) collective-permute-start(bf16[384,128]{1,0:T(8,128)(2,1)S(1)} %halves.3.refs_8_.refs_6_), channel_id=1, source_target_pairs={{0,4},{1,5},{2,6},{3,7},{4,0},{5,1},{6,2},{7,3},{8,12},{9,13},{10,... | collective-permute-start | bytes 294920 | tf_op jit(solution)/shard_map/ppermute | solution.py:404
  39.6 7.3 %collective-permute-start.16 = (bf16[768,128]{1,0:T(8,128)(2,1)S(1)}, bf16[768,128]{1,0:T(8,128)(2,1)S(1)}, u32[]{:S(2)}, u32[]{:S(2)}) collective-permute-start(bf16[768,128]{1,0:T(8,128)(2,1)S(1)} %get-tuple-element.124), channel_id=1, source_target_pairs={{0,2},{1,3},{2,0},{3,1},{4,6},{5,7},{6,4},{7,5},{8,10},{9,11},{10,... | collective-permute-start | bytes 589832 | tf_op jit(solution)/shard_map/ppermute | solution.py:404
  43.0 2.4 %copy-start.5 = (f32[6144]{0:T(1024)S(1)}, f32[6144]{0:T(1024)}, u32[]{:S(2)}) copy-start(f32[6144]{0:T(1024)} %param.11) | copy-start | bytes 73732
  43.0 5.7 %collective-permute-start.15 = (bf16[768,128]{1,0:T(8,128)(2,1)S(1)}, bf16[768,128]{1,0:T(8,128)(2,1)S(1)}, u32[]{:S(2)}, u32[]{:S(2)}) collective-permute-start(bf16[768,128]{1,0:T(8,128)(2,1)S(1)} %get-tuple-element.121), channel_id=1, source_target_pairs={{0,2},{1,3},{2,0},{3,1},{4,6},{5,7},{6,4},{7,5},{8,10},{9,11},{10,... | collective-permute-start | bytes 589832 | tf_op jit(solution)/shard_map/ppermute | solution.py:404
  47.0 2.0 %collective-permute-start.18 = (bf16[1536,128]{1,0:T(8,128)(2,1)S(1)}, bf16[1536,128]{1,0:T(8,128)(2,1)S(1)}, u32[]{:S(2)}, u32[]{:S(2)}) collective-permute-start(bf16[1536,128]{1,0:T(8,128)(2,1)S(1)} %get-tuple-element.135.refs_5_), channel_id=1, source_target_pairs={{0,1},{1,0},{2,3},{3,2},{4,5},{5,4},{6,7},{7,6},{8,9},{9,8},{10,11... | collective-permute-start | bytes 1179656 | tf_op jit(solution)/shard_map/ppermute | solution.py:404
  48.9 1.8 %collective-permute-start.17 = (bf16[1536,128]{1,0:T(8,128)(2,1)S(1)}, bf16[1536,128]{1,0:T(8,128)(2,1)S(1)}, u32[]{:S(2)}, u32[]{:S(2)}) collective-permute-start(bf16[1536,128]{1,0:T(8,128)(2,1)S(1)} %get-tuple-element.137.refs_10_), channel_id=1, source_target_pairs={{0,1},{1,0},{2,3},{3,2},{4,5},{5,4},{6,7},{7,6},{8,9},{9,8},{10,11... | collective-permute-start | bytes 1179656 | tf_op jit(solution)/shard_map/ppermute | solution.py:404

commit v8 on v7

--- a/solution.py
+++ b/solution.py
@@ -158,18 +158,18 @@
 
 
 def near_states_kernel(
-    group, key_ref, value_ref, taps_ref, map_ref,
-    feat_ref, conv_ref, other_ref, other_next, state_ref, key_first, value_first, scratch,
+    group, quarters, key_ref, value_ref, taps_ref, map_ref, feat_ref, conv_ref, key_first, value_first, *rest
 ):
+    (*states, scratch) = rest
     head_dim = map_ref.shape[0]
     width = key_ref.shape[1]
     size = width // (4 * GROUPS)
     back = taps_ref.shape[1] - 1
     row = lax.broadcasted_iota(jnp.int32, (RIM, head_dim), 0)
-    for quarter in range(4):
+    for i, quarter in enumerate(quarters):
         for start in range(0, size, head_dim):
             natural = columns(quarter_start(quarter, width) + group * size + start, head_dim)
-            at = quarter * size + start
+            at = i * size + start
             local = slice(at, at + head_dim)
             buffers = scratch.at[at // head_dim % scratch.shape[0]]
             key, value = key_ref[:, natural], value_ref[:, natural]
@@ -183,24 +183,21 @@
             later = jnp.where(row < back, 0.0, key_feat[:RIM].astype(f32)).astype(bf16)
             key_feat = jnp.concatenate([later, key_feat[RIM:]], axis=0)
             state = state_of(key_feat, value_conv)
-            if quarter < 2:
-                (other_ref, other_next)[quarter][start : start + head_dim] = state.astype(bf16)
-            else:
-                state_ref[at - 2 * size : at - 2 * size + head_dim] = state
-
-
-def near_states(group, key_seq, value_seq, conv_kernel, feature_map):
+            states[i][start : start + head_dim] = state.astype(states[i].dtype)
+
+
+def near_states(group, quarters, state_type, key_seq, value_seq, conv_kernel, feature_map):
     tok_count, width = key_seq.shape
     head_dim = feature_map.shape[0]
-    size = width // GROUPS
-    rows, firsts = shape((tok_count, size), bf16), shape((RIM, size), bf16)
-    other = shape((size // 4, head_dim), bf16)
+    size = width // (4 * GROUPS)
+    count = len(quarters)
+    rows, firsts = shape((tok_count, count * size), bf16), shape((RIM, count * size), bf16)
     return kernel_call(
-        functools.partial(near_states_kernel, group),
+        functools.partial(near_states_kernel, group, quarters),
         "near_states",
         [IN_VMEM] * 4,
-        [IN_VMEM] * 7,
-        [rows, rows, other, other, shape((size // 2, head_dim), f32), firsts, firsts],
+        [IN_VMEM] * (4 + count),
+        [rows, rows, firsts, firsts, *[shape((size, head_dim), state_type)] * count],
         [pltpu.VMEM((BLOCK_HEADS, 2, TILE + tok_count, head_dim), f32)],
     )(key_seq, value_seq, conv_kernel, feature_map)
 
@@ -253,7 +250,7 @@
     back = taps_ref.shape[1] - 1
     size = width // (4 * GROUPS)
     for i, quarter in enumerate(quarters):
-        here, there = slice(i * size, (i + 1) * size), slice(quarter * size, (quarter + 1) * size)
+        here = there = slice(i * size, (i + 1) * size)
         natural = columns(quarter_start(quarter, width) + group * size, size)
         rim = state_rim(core_rim, chip_rim, quarter, width, group * size, size)
         conv = convolved(
@@ -266,8 +263,8 @@
         feat = jnp.concatenate(feats, axis=1)
         feat_ref[:, here], conv_ref[:, here] = feat, value_conv
         if state_refs:
-            old_ref, *new_refs = state_refs
-            new_refs[i][...] = old_ref[here] + first_states(feat, value_conv, head_dim, back)
+            old_refs, new_refs = state_refs[: len(quarters)], state_refs[len(quarters) :]
+            new_refs[i][...] = old_refs[i][...] + first_states(feat, value_conv, head_dim, back)
 
 
 def first_states(feat, value_conv, head_dim, back):
@@ -279,25 +276,30 @@
     return jnp.concatenate(states, axis=0)
 
 
-def first_rows(group, quarters, key_first, value_first, conv_kernel, feature_map, rims, state=None):
+def first_rows(group, quarters, key_first, value_first, conv_kernel, feature_map, rims, before=()):
     width = conv_kernel.shape[2]
     head_dim = feature_map.shape[0]
     size = width // (4 * GROUPS)
     rows = shape((RIM, len(quarters) * size), bf16)
-    states = [] if state is None else [shape((size, head_dim), f32)] * len(quarters)
-    operands = [key_first, value_first, conv_kernel, feature_map, *rims, *([] if state is None else [state])]
+    more = [shape((size, head_dim), f32)] * len(before) if before else [rows]
+    operands = [key_first, value_first, conv_kernel, feature_map, *rims, *before]
     body = functools.partial(first_rows_kernel, group, quarters)
 
     def reordered(*refs):
-        sources, (feat_ref, conv_ref, *sums, scratch) = refs[:6], refs[len(operands) :]
-        body(*sources, *refs[6 : len(operands)], *sums, feat_ref, conv_ref, scratch)
+        sources, (feat_ref, conv_ref, *more, scratch) = refs[:6], refs[len(operands) :]
+        if before:
+            body(*sources, *refs[6 : len(operands)], *more, feat_ref, conv_ref, scratch)
+        else:
+            body(*sources, feat_ref, conv_ref, scratch)
+            tiles = [ref[...].astype(f32)[:TILE] for ref in (feat_ref, conv_ref)]
+            more[0][...] = jnp.concatenate(tiles, axis=0).astype(bf16)
 
     return kernel_call(
         reordered,
         "first_rows",
         [IN_VMEM] * len(operands),
-        [IN_VMEM] * (2 + len(states)),
-        [rows, rows, *states],
+        [IN_VMEM] * (2 + len(more)),
+        [rows, rows, *more],
         [pltpu.VMEM((len(quarters), 2, TILE + RIM, size), f32)],
     )(*operands)
 
@@ -463,7 +465,10 @@
     def chip_sums(device, paired, own, *arrived):
         states, firsts = [part.astype(f32) for part in arrived[:2]], arrived[2:]
         for first in firsts:
-            more = first_states(first[:RIM], first[RIM:], head_dim, tap_count - 1)
+            first = first.astype(f32)
+            blank = jnp.zeros((TILE, first.shape[1]), f32)
+            first = [jnp.concatenate([part, blank], axis=0).astype(bf16) for part in (first[:TILE], first[TILE:])]
+            more = first_states(*first, head_dim, tap_count - 1)
             states = [states[0] + more[:rows], states[1] + more[rows:]]
         return paired + states[0], own + states[1], *states
 
@@ -484,14 +489,15 @@
         give = total.astype(bf16)
         return total, before, jnp.where(upper, give[rows // 2 :], give[: rows // 2])
 
-    def own_prefixes(distance, device, own, paired, cored, state, *step):
+    def back_prefixes(distance, device, own, *step):
         before = plane_sums(distance, device, *step)[1] if step else jnp.zeros((rows, head_dim), f32)
-        own_part = before + jnp.where(of_pair(device), paired.astype(f32), 0.0)
-        others = before + jnp.where(of_pair(device), 0.0, own)
+        return before, before + jnp.where(of_pair(device), 0.0, own)
+
+    def own_prefixes(device, before, paired, cored, state):
+        before = before + jnp.where(of_pair(device), paired.astype(f32), 0.0)
         return (
-            others,
-            own_part + jnp.where(of_core(device), cored.astype(f32), 0.0),
-            own_part + jnp.where(of_core(device), 0.0, state),
+            before + jnp.where(of_core(device), cored.astype(f32), 0.0),
+            before + jnp.where(of_core(device), 0.0, state),
         )
 
     def paired_prefixes(device, arrived, cored, state, own):
@@ -514,15 +520,20 @@
 
     for g in groups:
         if g == 0:
-            *kept, other, other_next, partial, key_first, value_first = near_states(
-                g, key_seq, value_seq, conv_kernel, feature_map
+            near.append([])
+            *kept, key_first, value_first, other, other_next = near_states(
+                g, (0, 1), bf16, key_seq, value_seq, conv_kernel, feature_map
             )
-            near.append([(*kept, q * rows) for q in range(4)])
+            near[g] += [(*kept, q * rows) for q in range(2)]
             others = [swapped(other, 1), swapped(other_next, 1)]
-            first_a = first_rows(g, (0, 1), key_first, value_first, conv_kernel, feature_map, rims)
-            others.append(swapped(jnp.concatenate(first_a, axis=0), 1))
+            *kept, key_next, value_next, paired, single = near_states(
+                g, (2, 3), f32, key_seq, value_seq, conv_kernel, feature_map
+            )
+            near[g] += [(*kept, q * rows) for q in range(2)]
+            *first_a, first_tiles = first_rows(g, (0, 1), key_first, value_first, conv_kernel, feature_map, rims)
+            others.append(swapped(first_tiles, 1))
             *first_b, paired, single = first_rows(
-                g, (2, 3), key_first, value_first, conv_kernel, feature_map, rims, partial
+                g, (2, 3), key_next, value_next, conv_kernel, feature_map, rims, (paired, single)
             )
             firsts.append((first_a, first_b))
         else:
@@ -573,17 +584,23 @@
         step = ()
         if distance < device_count:
             step = (running[g], *([] if distance == 4 else [earlier[g]]), *arriving[g])
-        others, own, own_give[g] = mapped(
+        before, give = mapped(
+            "back_prefixes",
+            functools.partial(back_prefixes, distance),
+            [(rows, f32), (rows, bf16)],
+            chip[g],
+            *step,
+        )
+        back[g] = swapped(give, 2)
+        own, own_give[g] = mapped(
             "own_prefixes",
-            functools.partial(own_prefixes, distance),
-            [(rows, bf16)] * 3,
-            chip[g],
+            own_prefixes,
+            [(rows, bf16)] * 2,
+            before,
             from_pair[g],
             from_core[g][1],
             state_b[g][1],
-            *step,
-        )
-        back[g] = swapped(others, 2)
+        )
         owns.append(own)
         score(0.75 + (1 - 0.75) * (g + 1) / GROUPS)
     out = finish([[(3, g)] for g in groups], mixed, owns, gain, None)

time: 52.4 us -> 52.4 us (level)
  starting transfers between devices: 22 us -> 22.8 us
  waiting for transfers between devices: 5.7 us -> 4.96 us
    ppermute x18, starting transfers between devices: 21.5 us -> 22.3 us  [swapped(): lax.ppermute(block, 'seq', [(i, i ^ distance) for i in range(lax.axis_siz...]
    ppermute x18, waiting for transfers between devices: 5.69 us -> 4.95 us  [swapped(): lax.ppermute(block, 'seq', [(i, i ^ distance) for i in range(lax.axis_siz...]
    pallas_call x30 -> x33, Pallas kernels: 24.1 us -> 24 us  [call(): pl.pallas_call(ordered, in_specs=[*in_specs, *[IN_PLACE] * len(before)],...]
  transfers between devices with their start and end apart: 19 -> 19, of which waited for: 9 -> 8; matrix products, arithmetic and copies ran while one was open for 0% -> 0% of each run, Pallas kernels for 40% -> 40%
where the time goes in v8:
time: 52.4 us; the launch traced here: 52.2 us
  Pallas kernels  24 us (46%)
  starting transfers between devices  22.8 us (44%)
  waiting for transfers between devices  4.96 us (9%)
    pallas_call x33, Pallas kernels, call(): pl.pallas_call(ordered, in_specs=[*in_specs, *[IN_PLACE] * len(before)],...  24 us
    ppermute x18, starting transfers between devices, swapped(): lax.ppermute(block, 'seq', [(i, i ^ distance) for i in range(lax.axis_siz...  22.3 us
    ppermute x18, waiting for transfers between devices, swapped(): lax.ppermute(block, 'seq', [(i, i ^ distance) for i in range(lax.axis_siz...  4.95 us
  transfers between devices with their start and end apart: 19, of which 8 were waited for; matrix products, arithmetic and copies ran while one was open for 0% of the time, Pallas kernels for 40%

profile of v8, /device:TPU:0, one launch (start us, length us, event | category | flops | bytes accessed | tf_op | source)
XLA Modules:
  0.0 52.2 jit_solution(13269686397147609079)
XLA Ops:
  0.0 1.3 %pack_rims.1.refs_4_ = bf16[16,4608]{1,0:T(8,128)(2,1)S(1)} custom-call(bf16[256,6144]{1,0:T(8,128)(2,1)} %refs_0_.25, bf16[256,6144]{1,0:T(8,128)(2,1)} %refs_0_.17, bf16[256,6144]{1,0:T(8,128)(2,1)} %refs_1_.17), custom_call_target="tpu_custom_call" | custom-call | flops 1024 | bytes 1024 | tf_op jit(solution)/shard_map/pack_rims/pallas_call | solution.py:39
  1.4 0.5 collective-permute-start.1
  1.9 2.6 %collective-permute-start = (bf16[16,4608]{1,0:T(8,128)(2,1)S(1)}, bf16[16,4608]{1,0:T(8,128)(2,1)S(1)}, u32[]{:S(2)}, u32[]{:S(2)}) collective-permute-start(bf16[16,4608]{1,0:T(8,128)(2,1)S(1)} %pack_rims.1.refs_4_), channel_id=1, source_target_pairs={{0,1},{1,0},{2,3},{3,2},{4,5},{5,4},{6,7},{7,6},{8,9},{9,8},{10,11... | collective-permute-start | bytes 442376 | tf_op jit(solution)/shard_map/ppermute | solution.py:406
  4.5 1.9 %near_states.2 = (bf16[256,1536]{1,0:T(8,128)(2,1)S(1)}, bf16[256,1536]{1,0:T(8,128)(2,1)S(1)}, bf16[16,1536]{1,0:T(8,128)(2,1)S(1)}, bf16[16,1536]{1,0:T(8,128)...) custom-call(bf16[256,6144]{1,0:T(8,128)(2,1)S(1)} %copy-done.1, bf16[256,6144]{1,0:T(8,128)(2,1)S(1)} %copy-done.2, ...), custom_call_target="tpu_custom_call" | custom-call | flops 1024 | bytes 1024 | tf_op jit(solution)/shard_map/near_states/pallas_call | solution.py:39
  6.5 0.5 collective-permute-start.3
  7.0 1.8 %near_states.3 = (bf16[256,1536]{1,0:T(8,128)(2,1)S(1)}, bf16[256,1536]{1,0:T(8,128)(2,1)S(1)}, bf16[16,1536]{1,0:T(8,128)(2,1)S(1)}, bf16[16,1536]{1,0:T(8,128)...) custom-call(bf16[256,6144]{1,0:T(8,128)(2,1)S(1)} %copy-done.1, bf16[256,6144]{1,0:T(8,128)(2,1)S(1)} %copy-done.2, ...), custom_call_target="tpu_custom_call" | custom-call | flops 1024 | bytes 1024 | tf_op jit(solution)/shard_map/near_states/pallas_call | solution.py:39
  8.9 0.3 first_rows.2
  9.2 0.1 collective-permute-start.4
  9.3 0.7 %first_rows.3 = (bf16[16,1536]{1,0:T(8,128)(2,1)S(1)}, bf16[16,1536]{1,0:T(8,128)(2,1)S(1)}, f32[768,128]{1,0:T(8,128)S(1)}, f32[768,128]{1,0:T(8,128)S(1)}) custom-call(bf16[16,1536]{1,0:T(8,128)(2,1)S(1)} %get-tuple-element.85.refs_0_, bf16[16,1536]{1,0:T(8,128)(2,1)S(1)} %get-tuple-element.86.refs_1_, bf16[3,4,6144]{2,1,0:T(4,128)(2,1)S(1)} %copy-done.3, ...), custom_call_target="tpu_custom_call" | custom-call | flops 1024 | bytes 1024 | tf_op jit(solution)/shard_map/first_rows/pallas_call | solution.py:39
  10.0 0.5 collective-permute-done.4.refs_4_
  10.5 0.3 chip_sums.2
  10.8 1.8 %collective-permute-start.7 = (bf16[768,128]{1,0:T(8,128)(2,1)S(1)}, bf16[768,128]{1,0:T(8,128)(2,1)S(1)}, u32[]{:S(2)}, u32[]{:S(2)}) collective-permute-start(bf16[768,128]{1,0:T(8,128)(2,1)S(1)} %get-tuple-element.101), channel_id=1, source_target_pairs={{0,2},{1,3},{2,0},{3,1},{4,6},{5,7},{6,4},{7,5},{8,10},{9,11},{10,... | collective-permute-start | bytes 589832 | tf_op jit(solution)/shard_map/ppermute | solution.py:406
  12.5 1.9 %whole_states.2 = (bf16[256,1536]{1,0:T(8,128)(2,1)S(1)}, bf16[256,1536]{1,0:T(8,128)(2,1)S(1)}, bf16[768,128]{1,0:T(8,128)(2,1)S(1)}, bf16[768,128]{1,0:T(8,128)(2,1)S(1)}) custom-call(bf16[256,6144]{1,0:T(8,128)(2,1)S(1)} %copy-done.1, bf16[256,6144]{1,0:T(8,128)(2,1)S(1)} %copy-done.2, bf16[3,4,6144]{2,1,0:T(4,128)(2,1)S(1)} %copy-done.3, ...), custom_call_target="tpu_custom_call" | custom-call | flops 1024 | bytes 1024 | tf_op jit(solution)/shard_map/whole_states/pallas_call | solution.py:39
  14.5 0.5 collective-permute-start.6
  15.0 1.9 %whole_states.3 = (bf16[256,1536]{1,0:T(8,128)(2,1)S(1)}, bf16[256,1536]{1,0:T(8,128)(2,1)S(1)}, f32[768,128]{1,0:T(8,128)S(1)}, f32[768,128]{1,0:T(8,128)S(1)}) custom-call(bf16[256,6144]{1,0:T(8,128)(2,1)S(1)} %copy-done.1, bf16[256,6144]{1,0:T(8,128)(2,1)S(1)} %copy-done.2, bf16[3,4,6144]{2,1,0:T(4,128)(2,1)S(1)} %copy-done.3, ...), custom_call_target="tpu_custom_call" | custom-call | flops 1024 | bytes 1024 | tf_op jit(solution)/shard_map/whole_states/pallas_call | solution.py:39
  16.9 0.9 %collective-permute-done.7.refs_1_ = bf16[768,128]{1,0:T(8,128)(2,1)S(1)} collective-permute-done((bf16[768,128]{1,0:T(8,128)(2,1)S(1)}, bf16[768,128]{1,0:T(8,128)(2,1)S(1)}, u32[]{:S(2)}, u32[]{:S(2)}) %collective-permute-start.7) | collective-permute-done | bytes 196640 | tf_op jit(solution)/shard_map/ppermute | solution.py:406
  18.0 1.8 %collective-permute-start.8 = (bf16[768,128]{1,0:T(8,128)(2,1)S(1)}, bf16[768,128]{1,0:T(8,128)(2,1)S(1)}, u32[]{:S(2)}, u32[]{:S(2)}) collective-permute-start(bf16[768,128]{1,0:T(8,128)(2,1)S(1)} %get-tuple-element.104), channel_id=1, source_target_pairs={{0,2},{1,3},{2,0},{3,1},{4,6},{5,7},{6,4},{7,5},{8,10},{9,11},{10,... | collective-permute-start | bytes 589832 | tf_op jit(solution)/shard_map/ppermute | solution.py:406
  19.7 1.6 %collective-permute-start.10 = (bf16[768,128]{1,0:T(8,128)(2,1)S(1)}, bf16[768,128]{1,0:T(8,128)(2,1)S(1)}, u32[]{:S(2)}, u32[]{:S(2)}) collective-permute-start(bf16[768,128]{1,0:T(8,128)(2,1)S(1)} %get-tuple-element.102.refs_4_), channel_id=1, source_target_pairs={{0,4},{1,5},{2,6},{3,7},{4,0},{5,1},{6,2},{7,3},{8,12},{9,13},{10,... | collective-permute-start | bytes 589832 | tf_op jit(solution)/shard_map/ppermute | solution.py:406
  21.3 0.9 %within_block.8 = (bf16[256,768]{1,0:T(8,128)(2,1)S(1)}, f32[256,768]{1,0:T(8,128)S(1)}) custom-call(bf16[256,6144]{1,0:T(8,128)(2,1)S(1)} %copy-done, bf16[3,4,6144]{2,1,0:T(4,128)(2,1)S(1)} %copy-done.3, bf16[128,128]{1,0:T(8,128)(2,1)S(1)} %copy-done.4, bf16[16,4608]{1,0:T(8,128)(2,1)S(1)} %collective-permute-done.refs_4_.refs_3_, ...), custom_call_target="tpu_custom_call" | custom-call | flops 1024 | bytes 1024 | tf_op jit(solution)/shard_map/within_block/pallas_call | solution.py:39
  22.2 0.9 %within_block.9 = (bf16[256,768]{1,0:T(8,128)(2,1)S(1)}, f32[256,768]{1,0:T(8,128)S(1)}) custom-call(bf16[256,6144]{1,0:T(8,128)(2,1)S(1)} %copy-done, bf16[3,4,6144]{2,1,0:T(4,128)(2,1)S(1)} %copy-done.3, bf16[128,128]{1,0:T(8,128)(2,1)S(1)} %copy-done.4, bf16[16,4608]{1,0:T(8,128)(2,1)S(1)} %collective-permute-done.refs_4_.refs_3_, ...), custom_call_target="tpu_custom_call" | custom-call | flops 1024 | bytes 1024 | tf_op jit(solution)/shard_map/within_block/pallas_call | solution.py:39
  23.1 0.9 %within_block.10 = (bf16[256,768]{1,0:T(8,128)(2,1)S(1)}, f32[256,768]{1,0:T(8,128)S(1)}) custom-call(bf16[256,6144]{1,0:T(8,128)(2,1)S(1)} %copy-done, bf16[3,4,6144]{2,1,0:T(4,128)(2,1)S(1)} %copy-done.3, bf16[128,128]{1,0:T(8,128)(2,1)S(1)} %copy-done.4, bf16[16,4608]{1,0:T(8,128)(2,1)S(1)} %collective-permute-done.refs_4_.refs_3_, ...), custom_call_target="tpu_custom_call" | custom-call | flops 1024 | bytes 1024 | tf_op jit(solution)/shard_map/within_block/pallas_call | solution.py:39
  23.9 0.3 collective-permute-done.8.refs_1_
  24.2 1.7 %collective-permute-start.9 = (bf16[768,128]{1,0:T(8,128)(2,1)S(1)}, bf16[768,128]{1,0:T(8,128)(2,1)S(1)}, u32[]{:S(2)}, u32[]{:S(2)}) collective-permute-start(bf16[768,128]{1,0:T(8,128)(2,1)S(1)} %get-tuple-element.116.refs_2_), channel_id=1, source_target_pairs={{0,4},{1,5},{2,6},{3,7},{4,0},{5,1},{6,2},{7,3},{8,12},{9,13},{10,... | collective-permute-start | bytes 589832 | tf_op jit(solution)/shard_map/ppermute | solution.py:406
  26.1 2.7 %collective-permute-start.12 = (bf16[384,128]{1,0:T(8,128)(2,1)S(1)}, bf16[384,128]{1,0:T(8,128)(2,1)S(1)}, u32[]{:S(2)}, u32[]{:S(2)}) collective-permute-start(bf16[384,128]{1,0:T(8,128)(2,1)S(1)} %get-tuple-element.118.refs_7_), channel_id=1, source_target_pairs={{0,8},{1,9},{2,10},{3,11},{4,12},{5,13},{6,14},{7,15},{8,0},{9,1},... | collective-permute-start | bytes 294920 | tf_op jit(solution)/shard_map/ppermute | solution.py:406
  28.7 0.9 %within_block.11 = (bf16[256,768]{1,0:T(8,128)(2,1)S(1)}, f32[256,768]{1,0:T(8,128)S(1)}) custom-call(bf16[256,6144]{1,0:T(8,128)(2,1)S(1)} %copy-done, bf16[3,4,6144]{2,1,0:T(4,128)(2,1)S(1)} %copy-done.3, bf16[128,128]{1,0:T(8,128)(2,1)S(1)} %copy-done.4, bf16[16,4608]{1,0:T(8,128)(2,1)S(1)} %collective-permute-done.refs_4_.refs_3_, ...), custom_call_target="tpu_custom_call" | custom-call | flops 1024 | bytes 1024 | tf_op jit(solution)/shard_map/within_block/pallas_call | solution.py:39
  29.6 1.6 %collective-permute-done.9.refs_1_ = bf16[768,128]{1,0:T(8,128)(2,1)S(1)} collective-permute-done((bf16[768,128]{1,0:T(8,128)(2,1)S(1)}, bf16[768,128]{1,0:T(8,128)(2,1)S(1)}, u32[]{:S(2)}, u32[]{:S(2)}) %collective-permute-start.9) | collective-permute-done | bytes 196640 | tf_op jit(solution)/shard_map/ppermute | solution.py:406
  31.3 2.3 %collective-permute-start.11 = (bf16[384,128]{1,0:T(8,128)(2,1)S(1)}, bf16[384,128]{1,0:T(8,128)(2,1)S(1)}, u32[]{:S(2)}, u32[]{:S(2)}) collective-permute-start(bf16[384,128]{1,0:T(8,128)(2,1)S(1)} %get-tuple-element.122.refs_1_), channel_id=1, source_target_pairs={{0,8},{1,9},{2,10},{3,11},{4,12},{5,13},{6,14},{7,15},{8,0},{9,1},... | collective-permute-start | bytes 294920 | tf_op jit(solution)/shard_map/ppermute | solution.py:406
  33.6 2.2 %collective-permute-start.14 = (bf16[384,128]{1,0:T(8,128)(2,1)S(1)}, bf16[384,128]{1,0:T(8,128)(2,1)S(1)}, u32[]{:S(2)}, u32[]{:S(2)}) collective-permute-start(bf16[384,128]{1,0:T(8,128)(2,1)S(1)} %halves.2.refs_9_.refs_3_), channel_id=1, source_target_pairs={{0,4},{1,5},{2,6},{3,7},{4,0},{5,1},{6,2},{7,3},{8,12},{9,13},{10,... | collective-permute-start | bytes 294920 | tf_op jit(solution)/shard_map/ppermute | solution.py:406
  35.9 1.0 %within_block.12 = (bf16[256,768]{1,0:T(8,128)(2,1)S(1)}, f32[256,768]{1,0:T(8,128)S(1)}) custom-call(bf16[256,6144]{1,0:T(8,128)(2,1)S(1)} %copy-done, bf16[3,4,6144]{2,1,0:T(4,128)(2,1)S(1)} %copy-done.3, bf16[128,128]{1,0:T(8,128)(2,1)S(1)} %copy-done.4, bf16[16,4608]{1,0:T(8,128)(2,1)S(1)} %collective-permute-done.refs_4_.refs_3_, ...), custom_call_target="tpu_custom_call" | custom-call | flops 1024 | bytes 1024 | tf_op jit(solution)/shard_map/within_block/pallas_call | solution.py:39
  36.9 0.9 %within_block.13 = (bf16[256,768]{1,0:T(8,128)(2,1)S(1)}, f32[256,768]{1,0:T(8,128)S(1)}) custom-call(bf16[256,6144]{1,0:T(8,128)(2,1)S(1)} %copy-done, bf16[3,4,6144]{2,1,0:T(4,128)(2,1)S(1)} %copy-done.3, bf16[128,128]{1,0:T(8,128)(2,1)S(1)} %copy-done.4, bf16[16,4608]{1,0:T(8,128)(2,1)S(1)} %collective-permute-done.refs_4_.refs_3_, ...), custom_call_target="tpu_custom_call" | custom-call | flops 1024 | bytes 1024 | tf_op jit(solution)/shard_map/within_block/pallas_call | solution.py:39
  37.8 0.3 collective-permute-done.11.refs_0_
  38.1 0.5 collective-permute-start.13
  38.6 0.6 %collective-permute-done.14.refs_4_ = bf16[384,128]{1,0:T(8,128)(2,1)S(1)} collective-permute-done((bf16[384,128]{1,0:T(8,128)(2,1)S(1)}, bf16[384,128]{1,0:T(8,128)(2,1)S(1)}, u32[]{:S(2)}, u32[]{:S(2)}) %collective-permute-start.14) | collective-permute-done | bytes 98336 | tf_op jit(solution)/shard_map/ppermute | solution.py:406
  39.2 0.1 back_prefixes.2
  39.3 2.0 %collective-permute-start.16 = (bf16[768,128]{1,0:T(8,128)(2,1)S(1)}, bf16[768,128]{1,0:T(8,128)(2,1)S(1)}, u32[]{:S(2)}, u32[]{:S(2)}) collective-permute-start(bf16[768,128]{1,0:T(8,128)(2,1)S(1)} %get-tuple-element.134.refs_4_), channel_id=1, source_target_pairs={{0,2},{1,3},{2,0},{3,1},{4,6},{5,7},{6,4},{7,5},{8,10},{9,11},{10,... | collective-permute-start | bytes 589832 | tf_op jit(solution)/shard_map/ppermute | solution.py:406
  41.5 0.9 %within_block.14 = (bf16[256,768]{1,0:T(8,128)(2,1)S(1)}, f32[256,768]{1,0:T(8,128)S(1)}) custom-call(bf16[256,6144]{1,0:T(8,128)(2,1)S(1)} %copy-done, bf16[3,4,6144]{2,1,0:T(4,128)(2,1)S(1)} %copy-done.3, bf16[128,128]{1,0:T(8,128)(2,1)S(1)} %copy-done.4, bf16[16,4608]{1,0:T(8,128)(2,1)S(1)} %collective-permute-done.refs_4_.refs_3_, ...), custom_call_target="tpu_custom_call" | custom-call | flops 1024 | bytes 1024 | tf_op jit(solution)/shard_map/within_block/pallas_call | solution.py:39
  42.3 0.4 collective-permute-done.13.refs_4_
  42.7 0.1 back_prefixes.3
  42.9 1.6 %collective-permute-start.15 = (bf16[768,128]{1,0:T(8,128)(2,1)S(1)}, bf16[768,128]{1,0:T(8,128)(2,1)S(1)}, u32[]{:S(2)}, u32[]{:S(2)}) collective-permute-start(bf16[768,128]{1,0:T(8,128)(2,1)S(1)} %get-tuple-element.137.refs_4_), channel_id=1, source_target_pairs={{0,2},{1,3},{2,0},{3,1},{4,6},{5,7},{6,4},{7,5},{8,10},{9,11},{10,... | collective-permute-start | bytes 589832 | tf_op jit(solution)/shard_map/ppermute | solution.py:406
  44.5 0.9 %within_block.15 = (bf16[256,768]{1,0:T(8,128)(2,1)S(1)}, f32[256,768]{1,0:T(8,128)S(1)}) custom-call(bf16[256,6144]{1,0:T(8,128)(2,1)S(1)} %copy-done, bf16[3,4,6144]{2,1,0:T(4,128)(2,1)S(1)} %copy-done.3, bf16[128,128]{1,0:T(8,128)(2,1)S(1)} %copy-done.4, bf16[16,4608]{1,0:T(8,128)(2,1)S(1)} %collective-permute-done.refs_4_.refs_3_, ...), custom_call_target="tpu_custom_call" | custom-call | flops 1024 | bytes 1024 | tf_op jit(solution)/shard_map/within_block/pallas_call | solution.py:39
  45.4 1.4 %finish.4 = (bf16[256,6144]{1,0:T(8,128)(2,1)}, f32[8,128]{1,0:T(8,128)S(1)}) custom-call(f32[1,6144]{1,0:T(1,128)S(1)} %bitcast.1, bf16[768,128]{1,0:T(8,128)(2,1)S(1)} %get-tuple-element.142.refs_1_, bf16[768,128]{1,0:T(8,128)(2,1)S(1)} %get-tuple-element.143.refs_2_, bf16[256,768]{1,0:T(8,128)(2,1)S(1)} %get-tuple-element.144.refs_3_, ...), custom_call_target="tpu_custom_call" | custom-call | flops 1024 | bytes 1024 | tf_op jit(solution)/shard_map/finish/pallas_call | solution.py:39
  46.9 0.1 paired_prefixes.2
  47.1 1.2 %finish.5 = (bf16[256,6144]{1,0:T(8,128)(2,1)}, f32[8,128]{1,0:T(8,128)S(1)}) custom-call(f32[1,6144]{1,0:T(1,128)S(1)} %bitcast.2, bf16[768,128]{1,0:T(8,128)(2,1)S(1)} %get-tuple-element.148.refs_1_, bf16[256,768]{1,0:T(8,128)(2,1)S(1)} %get-tuple-element.149.refs_2_, ...), custom_call_target="tpu_custom_call", output_to_operand_aliasing={{0}: (4, {})} | custom-call | flops 1024 | bytes 1024 | tf_op jit(solution)/shard_map/finish/pallas_call | solution.py:39
  48.3 0.3 collective-permute-done.15.refs_0_
  48.6 0.1 paired_prefixes.3
  48.7 0.2 collective-permute-start.17
  49.0 1.6 %finish.6 = (bf16[256,6144]{1,0:T(8,128)(2,1)}, f32[8,128]{1,0:T(8,128)S(1)}) custom-call(f32[1,6144]{1,0:T(1,128)S(1)} %bitcast.3, bf16[768,128]{1,0:T(8,128)(2,1)S(1)} %get-tuple-element.156.refs_1_, bf16[1536,128]{1,0:T(8,128)(2,1)S(1)} %collective-permute-done.18.refs_2_, ...), custom_call_target="tpu_custom_call", output_to_operand_aliasing={{0}: (9, {})} | custom-call | flops 1024 | bytes 1024 | tf_op jit(solution)/shard_map/finish/pallas_call | solution.py:39
  50.6 1.4 %finish.7 = bf16[256,6144]{1,0:T(8,128)(2,1)} custom-call(f32[1,6144]{1,0:T(1,128)S(1)} %bitcast.4, bf16[1536,128]{1,0:T(8,128)(2,1)S(1)} %collective-permute-done.17.refs_1_, bf16[256,768]{1,0:T(8,128)(2,1)S(1)} %get-tuple-element.154.refs_2_, bf16[256,768]{1,0:T(8,128)(2,1)S(1)} %get-tuple-element.155.refs_3_, ...), custom_call_target="tpu_custom_call", output_to_operand_aliasing={{}: (6, {})} | custom-call | flops 1024 | bytes 1024 | tf_op jit(solution)/shard_map/finish/pallas_call | solution.py:39
  (35 shorter events, 0.9 us)
Async XLA Ops:
  0.0 4.5 %copy-start.2 = (bf16[256,6144]{1,0:T(8,128)(2,1)S(1)}, bf16[256,6144]{1,0:T(8,128)(2,1)}, u32[]{:S(2)}) copy-start(bf16[256,6144]{1,0:T(8,128)(2,1)} %refs_1_.17) | copy-start | bytes 9437188
  0.0 4.5 %copy-start.1 = (bf16[256,6144]{1,0:T(8,128)(2,1)S(1)}, bf16[256,6144]{1,0:T(8,128)(2,1)}, u32[]{:S(2)}) copy-start(bf16[256,6144]{1,0:T(8,128)(2,1)} %refs_0_.17) | copy-start | bytes 9437188
  0.0 4.5 %copy-start.4 = (bf16[128,128]{1,0:T(8,128)(2,1)S(1)}, bf16[128,128]{1,0:T(8,128)(2,1)}, u32[]{:S(2)}) copy-start(bf16[128,128]{1,0:T(8,128)(2,1)} %refs_2_.29) | copy-start | bytes 98308
  0.0 4.5 %copy-start.3 = (bf16[3,4,6144]{2,1,0:T(4,128)(2,1)S(1)}, bf16[3,4,6144]{2,1,0:T(4,128)(2,1)}, u32[]{:S(2)}) copy-start(bf16[3,4,6144]{2,1,0:T(4,128)(2,1)} %refs_1_.25) | copy-start | bytes 442372
  1.4 7.5 %collective-permute-start.1 = (bf16[16,4608]{1,0:T(8,128)(2,1)S(1)}, bf16[16,4608]{1,0:T(8,128)(2,1)S(1)}, u32[]{:S(2)}, u32[]{:S(2)}) collective-permute-start(bf16[16,4608]{1,0:T(8,128)(2,1)S(1)} %pack_rims.1.refs_4_), channel_id=1, source_target_pairs={{0,1},{1,2},{2,0},{3,4},{4,3},{5,6},{6,5},{7,8},{8,7},{9,10},{10,9... | collective-permute-start | bytes 442376 | tf_op jit(solution)/shard_map/ppermute | solution.py:414
  1.9 7.0 %collective-permute-start = (bf16[16,4608]{1,0:T(8,128)(2,1)S(1)}, bf16[16,4608]{1,0:T(8,128)(2,1)S(1)}, u32[]{:S(2)}, u32[]{:S(2)}) collective-permute-start(bf16[16,4608]{1,0:T(8,128)(2,1)S(1)} %pack_rims.1.refs_4_), channel_id=1, source_target_pairs={{0,1},{1,0},{2,3},{3,2},{4,5},{5,4},{6,7},{7,6},{8,9},{9,8},{10,11... | collective-permute-start | bytes 442376 | tf_op jit(solution)/shard_map/ppermute | solution.py:406
  6.4 3.6 %collective-permute-start.2 = (bf16[768,128]{1,0:T(8,128)(2,1)S(1)}, bf16[768,128]{1,0:T(8,128)(2,1)S(1)}, u32[]{:S(2)}, u32[]{:S(2)}) collective-permute-start(bf16[768,128]{1,0:T(8,128)(2,1)S(1)} %get-tuple-element.94), channel_id=1, source_target_pairs={{0,1},{1,0},{2,3},{3,2},{4,5},{5,4},{6,7},{7,6},{8,9},{9,8},{10,11... | collective-permute-start | bytes 589832 | tf_op jit(solution)/shard_map/ppermute | solution.py:406
  6.5 3.5 %collective-permute-start.3 = (bf16[768,128]{1,0:T(8,128)(2,1)S(1)}, bf16[768,128]{1,0:T(8,128)(2,1)S(1)}, u32[]{:S(2)}, u32[]{:S(2)}) collective-permute-start(bf16[768,128]{1,0:T(8,128)(2,1)S(1)} %get-tuple-element.84.refs_4_), channel_id=1, source_target_pairs={{0,1},{1,0},{2,3},{3,2},{4,5},{5,4},{6,7},{7,6},{8,9},{9,8},{10,11... | collective-permute-start | bytes 589832 | tf_op jit(solution)/shard_map/ppermute | solution.py:406
  9.2 1.3 %collective-permute-start.4 = (bf16[16,1536]{1,0:T(8,128)(2,1)S(1)}, bf16[16,1536]{1,0:T(8,128)(2,1)S(1)}, u32[]{:S(2)}, u32[]{:S(2)}) collective-permute-start(bf16[16,1536]{1,0:T(8,128)(2,1)S(1)} %get-tuple-element.91.refs_8_), channel_id=1, source_target_pairs={{0,1},{1,0},{2,3},{3,2},{4,5},{5,4},{6,7},{7,6},{8,9},{9,8},{10,11... | collective-permute-start | bytes 147464 | tf_op jit(solution)/shard_map/ppermute | solution.py:406
  10.8 7.0 %collective-permute-start.7 = (bf16[768,128]{1,0:T(8,128)(2,1)S(1)}, bf16[768,128]{1,0:T(8,128)(2,1)S(1)}, u32[]{:S(2)}, u32[]{:S(2)}) collective-permute-start(bf16[768,128]{1,0:T(8,128)(2,1)S(1)} %get-tuple-element.101), channel_id=1, source_target_pairs={{0,2},{1,3},{2,0},{3,1},{4,6},{5,7},{6,4},{7,5},{8,10},{9,11},{10,... | collective-permute-start | bytes 589832 | tf_op jit(solution)/shard_map/ppermute | solution.py:406
  14.4 3.4 %collective-permute-start.5 = (bf16[768,128]{1,0:T(8,128)(2,1)S(1)}, bf16[768,128]{1,0:T(8,128)(2,1)S(1)}, u32[]{:S(2)}, u32[]{:S(2)}) collective-permute-start(bf16[768,128]{1,0:T(8,128)(2,1)S(1)} %get-tuple-element.99), channel_id=1, source_target_pairs={{0,1},{1,0},{2,3},{3,2},{4,5},{5,4},{6,7},{7,6},{8,9},{9,8},{10,11... | collective-permute-start | bytes 589832 | tf_op jit(solution)/shard_map/ppermute | solution.py:406
  14.5 6.8 %copy-start = (bf16[256,6144]{1,0:T(8,128)(2,1)S(1)}, bf16[256,6144]{1,0:T(8,128)(2,1)}, u32[]{:S(2)}) copy-start(bf16[256,6144]{1,0:T(8,128)(2,1)} %refs_0_.25) | copy-start | bytes 9437188
  14.5 3.3 %collective-permute-start.6 = (bf16[768,128]{1,0:T(8,128)(2,1)S(1)}, bf16[768,128]{1,0:T(8,128)(2,1)S(1)}, u32[]{:S(2)}, u32[]{:S(2)}) collective-permute-start(bf16[768,128]{1,0:T(8,128)(2,1)S(1)} %get-tuple-element.96.refs_6_), channel_id=1, source_target_pairs={{0,1},{1,0},{2,3},{3,2},{4,5},{5,4},{6,7},{7,6},{8,9},{9,8},{10,11... | collective-permute-start | bytes 589832 | tf_op jit(solution)/shard_map/ppermute | solution.py:406
  18.0 6.2 %collective-permute-start.8 = (bf16[768,128]{1,0:T(8,128)(2,1)S(1)}, bf16[768,128]{1,0:T(8,128)(2,1)S(1)}, u32[]{:S(2)}, u32[]{:S(2)}) collective-permute-start(bf16[768,128]{1,0:T(8,128)(2,1)S(1)} %get-tuple-element.104), channel_id=1, source_target_pairs={{0,2},{1,3},{2,0},{3,1},{4,6},{5,7},{6,4},{7,5},{8,10},{9,11},{10,... | collective-permute-start | bytes 589832 | tf_op jit(solution)/shard_map/ppermute | solution.py:406
  19.7 6.2 %collective-permute-start.10 = (bf16[768,128]{1,0:T(8,128)(2,1)S(1)}, bf16[768,128]{1,0:T(8,128)(2,1)S(1)}, u32[]{:S(2)}, u32[]{:S(2)}) collective-permute-start(bf16[768,128]{1,0:T(8,128)(2,1)S(1)} %get-tuple-element.102.refs_4_), channel_id=1, source_target_pairs={{0,4},{1,5},{2,6},{3,7},{4,0},{5,1},{6,2},{7,3},{8,12},{9,13},{10,... | collective-permute-start | bytes 589832 | tf_op jit(solution)/shard_map/ppermute | solution.py:406
  24.2 7.0 %collective-permute-start.9 = (bf16[768,128]{1,0:T(8,128)(2,1)S(1)}, bf16[768,128]{1,0:T(8,128)(2,1)S(1)}, u32[]{:S(2)}, u32[]{:S(2)}) collective-permute-start(bf16[768,128]{1,0:T(8,128)(2,1)S(1)} %get-tuple-element.116.refs_2_), channel_id=1, source_target_pairs={{0,4},{1,5},{2,6},{3,7},{4,0},{5,1},{6,2},{7,3},{8,12},{9,13},{10,... | collective-permute-start | bytes 589832 | tf_op jit(solution)/shard_map/ppermute | solution.py:406
  26.1 7.6 %collective-permute-start.12 = (bf16[384,128]{1,0:T(8,128)(2,1)S(1)}, bf16[384,128]{1,0:T(8,128)(2,1)S(1)}, u32[]{:S(2)}, u32[]{:S(2)}) collective-permute-start(bf16[384,128]{1,0:T(8,128)(2,1)S(1)} %get-tuple-element.118.refs_7_), channel_id=1, source_target_pairs={{0,8},{1,9},{2,10},{3,11},{4,12},{5,13},{6,14},{7,15},{8,0},{9,1},... | collective-permute-start | bytes 294920 | tf_op jit(solution)/shard_map/ppermute | solution.py:406
  31.3 6.7 %collective-permute-start.11 = (bf16[384,128]{1,0:T(8,128)(2,1)S(1)}, bf16[384,128]{1,0:T(8,128)(2,1)S(1)}, u32[]{:S(2)}, u32[]{:S(2)}) collective-permute-start(bf16[384,128]{1,0:T(8,128)(2,1)S(1)} %get-tuple-element.122.refs_1_), channel_id=1, source_target_pairs={{0,8},{1,9},{2,10},{3,11},{4,12},{5,13},{6,14},{7,15},{8,0},{9,1},... | collective-permute-start | bytes 294920 | tf_op jit(solution)/shard_map/ppermute | solution.py:406
  33.6 5.6 %collective-permute-start.14 = (bf16[384,128]{1,0:T(8,128)(2,1)S(1)}, bf16[384,128]{1,0:T(8,128)(2,1)S(1)}, u32[]{:S(2)}, u32[]{:S(2)}) collective-permute-start(bf16[384,128]{1,0:T(8,128)(2,1)S(1)} %halves.2.refs_9_.refs_3_), channel_id=1, source_target_pairs={{0,4},{1,5},{2,6},{3,7},{4,0},{5,1},{6,2},{7,3},{8,12},{9,13},{10,... | collective-permute-start | bytes 294920 | tf_op jit(solution)/shard_map/ppermute | solution.py:406
  38.1 4.7 %collective-permute-start.13 = (bf16[384,128]{1,0:T(8,128)(2,1)S(1)}, bf16[384,128]{1,0:T(8,128)(2,1)S(1)}, u32[]{:S(2)}, u32[]{:S(2)}) collective-permute-start(bf16[384,128]{1,0:T(8,128)(2,1)S(1)} %halves.3.refs_5_.refs_3_), channel_id=1, source_target_pairs={{0,4},{1,5},{2,6},{3,7},{4,0},{5,1},{6,2},{7,3},{8,12},{9,13},{10,... | collective-permute-start | bytes 294920 | tf_op jit(solution)/shard_map/ppermute | solution.py:406
  39.3 7.5 %collective-permute-start.16 = (bf16[768,128]{1,0:T(8,128)(2,1)S(1)}, bf16[768,128]{1,0:T(8,128)(2,1)S(1)}, u32[]{:S(2)}, u32[]{:S(2)}) collective-permute-start(bf16[768,128]{1,0:T(8,128)(2,1)S(1)} %get-tuple-element.134.refs_4_), channel_id=1, source_target_pairs={{0,2},{1,3},{2,0},{3,1},{4,6},{5,7},{6,4},{7,5},{8,10},{9,11},{10,... | collective-permute-start | bytes 589832 | tf_op jit(solution)/shard_map/ppermute | solution.py:406
  42.9 5.8 %collective-permute-start.15 = (bf16[768,128]{1,0:T(8,128)(2,1)S(1)}, bf16[768,128]{1,0:T(8,128)(2,1)S(1)}, u32[]{:S(2)}, u32[]{:S(2)}) collective-permute-start(bf16[768,128]{1,0:T(8,128)(2,1)S(1)} %get-tuple-element.137.refs_4_), channel_id=1, source_target_pairs={{0,2},{1,3},{2,0},{3,1},{4,6},{5,7},{6,4},{7,5},{8,10},{9,11},{10,... | collective-permute-start | bytes 589832 | tf_op jit(solution)/shard_map/ppermute | solution.py:406
  44.4 1.0 %copy-start.5 = (f32[6144]{0:T(1024)S(1)}, f32[6144]{0:T(1024)}, u32[]{:S(2)}) copy-start(f32[6144]{0:T(1024)} %param.11) | copy-start | bytes 73732
  47.0 2.0 %collective-permute-start.18 = (bf16[1536,128]{1,0:T(8,128)(2,1)S(1)}, bf16[1536,128]{1,0:T(8,128)(2,1)S(1)}, u32[]{:S(2)}, u32[]{:S(2)}) collective-permute-start(bf16[1536,128]{1,0:T(8,128)(2,1)S(1)} %get-tuple-element.151.refs_5_), channel_id=1, source_target_pairs={{0,1},{1,0},{2,3},{3,2},{4,5},{5,4},{6,7},{7,6},{8,9},{9,8},{10,11... | collective-permute-start | bytes 1179656 | tf_op jit(solution)/shard_map/ppermute | solution.py:406
  48.7 1.9 %collective-permute-start.17 = (bf16[1536,128]{1,0:T(8,128)(2,1)S(1)}, bf16[1536,128]{1,0:T(8,128)(2,1)S(1)}, u32[]{:S(2)}, u32[]{:S(2)}) collective-permute-start(bf16[1536,128]{1,0:T(8,128)(2,1)S(1)} %get-tuple-element.153.refs_10_), channel_id=1, source_target_pairs={{0,1},{1,0},{2,3},{3,2},{4,5},{5,4},{6,7},{7,6},{8,9},{9,8},{10,11... | collective-permute-start | bytes 1179656 | tf_op jit(solution)/shard_map/ppermute | solution.py:406

commit v9 on v8

--- a/solution.py
+++ b/solution.py
@@ -361,10 +361,10 @@
         ref[...] = jnp.zeros(ref.shape, f32)
     head_dim = prefixes[0].shape[1]
     tok_count, size = feats[0].shape
-    copies = []
+    step = size // 2 if size % (2 * head_dim) == 0 else size
+    i, copies = 0, []
     for prefix_ref, part in zip(prefixes, pieces):
         for at, (quarter, group) in enumerate(part):
-            i = len(copies)
             natural = quarter_start(quarter, out_ref.shape[1]) + group * size
             for start in range(0, size, head_dim):
                 cols = slice(start, start + head_dim)
@@ -373,8 +373,14 @@
                 inverse_rms = lax.rsqrt(jnp.mean(mixed * mixed, axis=-1, keepdims=True) + 1e-06)
                 gain = gain_ref[:, columns(natural + start, head_dim)]
                 rows[i, :, cols] = (mixed * inverse_rms * gain).astype(bf16)
-            copies.append(pltpu.make_async_copy(rows.at[i], out_ref.at[:, columns(natural, size)], sems.at[i]))
-            copies[-1].start()
+                if (start + head_dim) % step == 0:
+                    part_cols = pl.ds(start + head_dim - step, step)
+                    there = columns(natural + start + head_dim - step, step)
+                    copies.append(
+                        pltpu.make_async_copy(rows.at[i, :, part_cols], out_ref.at[:, there], sems.at[len(copies)])
+                    )
+                    copies[-1].start()
+            i += 1
     for copy in copies:
         copy.wait()
 
@@ -397,7 +403,7 @@
         in_specs,
         [IN_PLACE, IN_VMEM][: 1 if last else 2],
         [pltpu.HBM((tok_count, width), bf16), shape((TILE, 128), f32)][: 1 if last else 2],
-        [pltpu.VMEM((count, tok_count, size), bf16), pltpu.SemaphoreType.DMA((count,))],
+        [pltpu.VMEM((count, tok_count, size), bf16), pltpu.SemaphoreType.DMA((2 * count,))],
         aliases,
     )(*operands)[0]
 

time: 52.4 us -> 52.2 us (level)
  no operation moved by 1% of the time
where the time goes in v9:
time: 52.2 us; the launch traced here: 52.1 us
  Pallas kernels  23.8 us (46%)
  starting transfers between devices  22.7 us (43%)
  waiting for transfers between devices  5.09 us (10%)
    pallas_call x33, Pallas kernels, call(): pl.pallas_call(ordered, in_specs=[*in_specs, *[IN_PLACE] * len(before)],...  23.8 us
    ppermute x18, starting transfers between devices, swapped(): lax.ppermute(block, 'seq', [(i, i ^ distance) for i in range(lax.axis_siz...  22.2 us
    ppermute x18, waiting for transfers between devices, swapped(): lax.ppermute(block, 'seq', [(i, i ^ distance) for i in range(lax.axis_siz...  5.08 us
  transfers between devices with their start and end apart: 19, of which 8 were waited for; matrix products, arithmetic and copies ran while one was open for 0% of the time, Pallas kernels for 40%

profile of v9, /device:TPU:0, one launch (start us, length us, event | category | flops | bytes accessed | tf_op | source)
XLA Modules:
  0.0 52.1 jit_solution(3765325327612256850)
XLA Ops:
  0.0 1.3 %pack_rims.1.refs_4_ = bf16[16,4608]{1,0:T(8,128)(2,1)S(1)} custom-call(bf16[256,6144]{1,0:T(8,128)(2,1)} %refs_0_.25, bf16[256,6144]{1,0:T(8,128)(2,1)} %refs_0_.17, bf16[256,6144]{1,0:T(8,128)(2,1)} %refs_1_.17), custom_call_target="tpu_custom_call" | custom-call | flops 1024 | bytes 1024 | tf_op jit(solution)/shard_map/pack_rims/pallas_call | solution.py:39
  1.4 0.5 collective-permute-start.1
  1.9 2.6 %collective-permute-start = (bf16[16,4608]{1,0:T(8,128)(2,1)S(1)}, bf16[16,4608]{1,0:T(8,128)(2,1)S(1)}, u32[]{:S(2)}, u32[]{:S(2)}) collective-permute-start(bf16[16,4608]{1,0:T(8,128)(2,1)S(1)} %pack_rims.1.refs_4_), channel_id=1, source_target_pairs={{0,1},{1,0},{2,3},{3,2},{4,5},{5,4},{6,7},{7,6},{8,9},{9,8},{10,11... | collective-permute-start | bytes 442376 | tf_op jit(solution)/shard_map/ppermute | solution.py:412
  4.5 1.9 %near_states.2 = (bf16[256,1536]{1,0:T(8,128)(2,1)S(1)}, bf16[256,1536]{1,0:T(8,128)(2,1)S(1)}, bf16[16,1536]{1,0:T(8,128)(2,1)S(1)}, bf16[16,1536]{1,0:T(8,128)...) custom-call(bf16[256,6144]{1,0:T(8,128)(2,1)S(1)} %copy-done.1, bf16[256,6144]{1,0:T(8,128)(2,1)S(1)} %copy-done.2, ...), custom_call_target="tpu_custom_call" | custom-call | flops 1024 | bytes 1024 | tf_op jit(solution)/shard_map/near_states/pallas_call | solution.py:39
  6.5 0.5 collective-permute-start.3
  7.0 1.8 %near_states.3 = (bf16[256,1536]{1,0:T(8,128)(2,1)S(1)}, bf16[256,1536]{1,0:T(8,128)(2,1)S(1)}, bf16[16,1536]{1,0:T(8,128)(2,1)S(1)}, bf16[16,1536]{1,0:T(8,128)...) custom-call(bf16[256,6144]{1,0:T(8,128)(2,1)S(1)} %copy-done.1, bf16[256,6144]{1,0:T(8,128)(2,1)S(1)} %copy-done.2, ...), custom_call_target="tpu_custom_call" | custom-call | flops 1024 | bytes 1024 | tf_op jit(solution)/shard_map/near_states/pallas_call | solution.py:39
  8.9 0.3 first_rows.2
  9.2 0.1 collective-permute-start.4
  9.3 0.7 %first_rows.3 = (bf16[16,1536]{1,0:T(8,128)(2,1)S(1)}, bf16[16,1536]{1,0:T(8,128)(2,1)S(1)}, f32[768,128]{1,0:T(8,128)S(1)}, f32[768,128]{1,0:T(8,128)S(1)}) custom-call(bf16[16,1536]{1,0:T(8,128)(2,1)S(1)} %get-tuple-element.85.refs_0_, bf16[16,1536]{1,0:T(8,128)(2,1)S(1)} %get-tuple-element.86.refs_1_, bf16[3,4,6144]{2,1,0:T(4,128)(2,1)S(1)} %copy-done.3, ...), custom_call_target="tpu_custom_call" | custom-call | flops 1024 | bytes 1024 | tf_op jit(solution)/shard_map/first_rows/pallas_call | solution.py:39
  10.0 0.5 collective-permute-done.4.refs_4_
  10.5 0.3 chip_sums.2
  10.8 1.8 %collective-permute-start.7 = (bf16[768,128]{1,0:T(8,128)(2,1)S(1)}, bf16[768,128]{1,0:T(8,128)(2,1)S(1)}, u32[]{:S(2)}, u32[]{:S(2)}) collective-permute-start(bf16[768,128]{1,0:T(8,128)(2,1)S(1)} %get-tuple-element.101), channel_id=1, source_target_pairs={{0,2},{1,3},{2,0},{3,1},{4,6},{5,7},{6,4},{7,5},{8,10},{9,11},{10,... | collective-permute-start | bytes 589832 | tf_op jit(solution)/shard_map/ppermute | solution.py:412
  12.5 1.9 %whole_states.2 = (bf16[256,1536]{1,0:T(8,128)(2,1)S(1)}, bf16[256,1536]{1,0:T(8,128)(2,1)S(1)}, bf16[768,128]{1,0:T(8,128)(2,1)S(1)}, bf16[768,128]{1,0:T(8,128)(2,1)S(1)}) custom-call(bf16[256,6144]{1,0:T(8,128)(2,1)S(1)} %copy-done.1, bf16[256,6144]{1,0:T(8,128)(2,1)S(1)} %copy-done.2, bf16[3,4,6144]{2,1,0:T(4,128)(2,1)S(1)} %copy-done.3, ...), custom_call_target="tpu_custom_call" | custom-call | flops 1024 | bytes 1024 | tf_op jit(solution)/shard_map/whole_states/pallas_call | solution.py:39
  14.5 0.5 collective-permute-start.6
  15.0 1.9 %whole_states.3 = (bf16[256,1536]{1,0:T(8,128)(2,1)S(1)}, bf16[256,1536]{1,0:T(8,128)(2,1)S(1)}, f32[768,128]{1,0:T(8,128)S(1)}, f32[768,128]{1,0:T(8,128)S(1)}) custom-call(bf16[256,6144]{1,0:T(8,128)(2,1)S(1)} %copy-done.1, bf16[256,6144]{1,0:T(8,128)(2,1)S(1)} %copy-done.2, bf16[3,4,6144]{2,1,0:T(4,128)(2,1)S(1)} %copy-done.3, ...), custom_call_target="tpu_custom_call" | custom-call | flops 1024 | bytes 1024 | tf_op jit(solution)/shard_map/whole_states/pallas_call | solution.py:39
  16.9 0.9 %collective-permute-done.7.refs_1_ = bf16[768,128]{1,0:T(8,128)(2,1)S(1)} collective-permute-done((bf16[768,128]{1,0:T(8,128)(2,1)S(1)}, bf16[768,128]{1,0:T(8,128)(2,1)S(1)}, u32[]{:S(2)}, u32[]{:S(2)}) %collective-permute-start.7) | collective-permute-done | bytes 196640 | tf_op jit(solution)/shard_map/ppermute | solution.py:412
  18.0 1.8 %collective-permute-start.8 = (bf16[768,128]{1,0:T(8,128)(2,1)S(1)}, bf16[768,128]{1,0:T(8,128)(2,1)S(1)}, u32[]{:S(2)}, u32[]{:S(2)}) collective-permute-start(bf16[768,128]{1,0:T(8,128)(2,1)S(1)} %get-tuple-element.104), channel_id=1, source_target_pairs={{0,2},{1,3},{2,0},{3,1},{4,6},{5,7},{6,4},{7,5},{8,10},{9,11},{10,... | collective-permute-start | bytes 589832 | tf_op jit(solution)/shard_map/ppermute | solution.py:412
  19.7 1.6 %collective-permute-start.10 = (bf16[768,128]{1,0:T(8,128)(2,1)S(1)}, bf16[768,128]{1,0:T(8,128)(2,1)S(1)}, u32[]{:S(2)}, u32[]{:S(2)}) collective-permute-start(bf16[768,128]{1,0:T(8,128)(2,1)S(1)} %get-tuple-element.102.refs_4_), channel_id=1, source_target_pairs={{0,4},{1,5},{2,6},{3,7},{4,0},{5,1},{6,2},{7,3},{8,12},{9,13},{10,... | collective-permute-start | bytes 589832 | tf_op jit(solution)/shard_map/ppermute | solution.py:412
  21.3 0.9 %within_block.8 = (bf16[256,768]{1,0:T(8,128)(2,1)S(1)}, f32[256,768]{1,0:T(8,128)S(1)}) custom-call(bf16[256,6144]{1,0:T(8,128)(2,1)S(1)} %copy-done, bf16[3,4,6144]{2,1,0:T(4,128)(2,1)S(1)} %copy-done.3, bf16[128,128]{1,0:T(8,128)(2,1)S(1)} %copy-done.4, bf16[16,4608]{1,0:T(8,128)(2,1)S(1)} %collective-permute-done.refs_4_.refs_3_, ...), custom_call_target="tpu_custom_call" | custom-call | flops 1024 | bytes 1024 | tf_op jit(solution)/shard_map/within_block/pallas_call | solution.py:39
  22.2 0.9 %within_block.9 = (bf16[256,768]{1,0:T(8,128)(2,1)S(1)}, f32[256,768]{1,0:T(8,128)S(1)}) custom-call(bf16[256,6144]{1,0:T(8,128)(2,1)S(1)} %copy-done, bf16[3,4,6144]{2,1,0:T(4,128)(2,1)S(1)} %copy-done.3, bf16[128,128]{1,0:T(8,128)(2,1)S(1)} %copy-done.4, bf16[16,4608]{1,0:T(8,128)(2,1)S(1)} %collective-permute-done.refs_4_.refs_3_, ...), custom_call_target="tpu_custom_call" | custom-call | flops 1024 | bytes 1024 | tf_op jit(solution)/shard_map/within_block/pallas_call | solution.py:39
  23.1 0.9 %within_block.10 = (bf16[256,768]{1,0:T(8,128)(2,1)S(1)}, f32[256,768]{1,0:T(8,128)S(1)}) custom-call(bf16[256,6144]{1,0:T(8,128)(2,1)S(1)} %copy-done, bf16[3,4,6144]{2,1,0:T(4,128)(2,1)S(1)} %copy-done.3, bf16[128,128]{1,0:T(8,128)(2,1)S(1)} %copy-done.4, bf16[16,4608]{1,0:T(8,128)(2,1)S(1)} %collective-permute-done.refs_4_.refs_3_, ...), custom_call_target="tpu_custom_call" | custom-call | flops 1024 | bytes 1024 | tf_op jit(solution)/shard_map/within_block/pallas_call | solution.py:39
  23.9 0.3 collective-permute-done.8.refs_1_
  24.2 1.7 %collective-permute-start.9 = (bf16[768,128]{1,0:T(8,128)(2,1)S(1)}, bf16[768,128]{1,0:T(8,128)(2,1)S(1)}, u32[]{:S(2)}, u32[]{:S(2)}) collective-permute-start(bf16[768,128]{1,0:T(8,128)(2,1)S(1)} %get-tuple-element.116.refs_2_), channel_id=1, source_target_pairs={{0,4},{1,5},{2,6},{3,7},{4,0},{5,1},{6,2},{7,3},{8,12},{9,13},{10,... | collective-permute-start | bytes 589832 | tf_op jit(solution)/shard_map/ppermute | solution.py:412
  26.1 2.7 %collective-permute-start.12 = (bf16[384,128]{1,0:T(8,128)(2,1)S(1)}, bf16[384,128]{1,0:T(8,128)(2,1)S(1)}, u32[]{:S(2)}, u32[]{:S(2)}) collective-permute-start(bf16[384,128]{1,0:T(8,128)(2,1)S(1)} %get-tuple-element.118.refs_7_), channel_id=1, source_target_pairs={{0,8},{1,9},{2,10},{3,11},{4,12},{5,13},{6,14},{7,15},{8,0},{9,1},... | collective-permute-start | bytes 294920 | tf_op jit(solution)/shard_map/ppermute | solution.py:412
  28.7 0.9 %within_block.11 = (bf16[256,768]{1,0:T(8,128)(2,1)S(1)}, f32[256,768]{1,0:T(8,128)S(1)}) custom-call(bf16[256,6144]{1,0:T(8,128)(2,1)S(1)} %copy-done, bf16[3,4,6144]{2,1,0:T(4,128)(2,1)S(1)} %copy-done.3, bf16[128,128]{1,0:T(8,128)(2,1)S(1)} %copy-done.4, bf16[16,4608]{1,0:T(8,128)(2,1)S(1)} %collective-permute-done.refs_4_.refs_3_, ...), custom_call_target="tpu_custom_call" | custom-call | flops 1024 | bytes 1024 | tf_op jit(solution)/shard_map/within_block/pallas_call | solution.py:39
  29.6 1.6 %collective-permute-done.9.refs_1_ = bf16[768,128]{1,0:T(8,128)(2,1)S(1)} collective-permute-done((bf16[768,128]{1,0:T(8,128)(2,1)S(1)}, bf16[768,128]{1,0:T(8,128)(2,1)S(1)}, u32[]{:S(2)}, u32[]{:S(2)}) %collective-permute-start.9) | collective-permute-done | bytes 196640 | tf_op jit(solution)/shard_map/ppermute | solution.py:412
  31.3 2.3 %collective-permute-start.11 = (bf16[384,128]{1,0:T(8,128)(2,1)S(1)}, bf16[384,128]{1,0:T(8,128)(2,1)S(1)}, u32[]{:S(2)}, u32[]{:S(2)}) collective-permute-start(bf16[384,128]{1,0:T(8,128)(2,1)S(1)} %get-tuple-element.122.refs_1_), channel_id=1, source_target_pairs={{0,8},{1,9},{2,10},{3,11},{4,12},{5,13},{6,14},{7,15},{8,0},{9,1},... | collective-permute-start | bytes 294920 | tf_op jit(solution)/shard_map/ppermute | solution.py:412
  33.6 2.2 %collective-permute-start.14 = (bf16[384,128]{1,0:T(8,128)(2,1)S(1)}, bf16[384,128]{1,0:T(8,128)(2,1)S(1)}, u32[]{:S(2)}, u32[]{:S(2)}) collective-permute-start(bf16[384,128]{1,0:T(8,128)(2,1)S(1)} %halves.2.refs_9_.refs_3_), channel_id=1, source_target_pairs={{0,4},{1,5},{2,6},{3,7},{4,0},{5,1},{6,2},{7,3},{8,12},{9,13},{10,... | collective-permute-start | bytes 294920 | tf_op jit(solution)/shard_map/ppermute | solution.py:412
  35.9 1.0 %within_block.12 = (bf16[256,768]{1,0:T(8,128)(2,1)S(1)}, f32[256,768]{1,0:T(8,128)S(1)}) custom-call(bf16[256,6144]{1,0:T(8,128)(2,1)S(1)} %copy-done, bf16[3,4,6144]{2,1,0:T(4,128)(2,1)S(1)} %copy-done.3, bf16[128,128]{1,0:T(8,128)(2,1)S(1)} %copy-done.4, bf16[16,4608]{1,0:T(8,128)(2,1)S(1)} %collective-permute-done.refs_4_.refs_3_, ...), custom_call_target="tpu_custom_call" | custom-call | flops 1024 | bytes 1024 | tf_op jit(solution)/shard_map/within_block/pallas_call | solution.py:39
  36.9 0.9 %within_block.13 = (bf16[256,768]{1,0:T(8,128)(2,1)S(1)}, f32[256,768]{1,0:T(8,128)S(1)}) custom-call(bf16[256,6144]{1,0:T(8,128)(2,1)S(1)} %copy-done, bf16[3,4,6144]{2,1,0:T(4,128)(2,1)S(1)} %copy-done.3, bf16[128,128]{1,0:T(8,128)(2,1)S(1)} %copy-done.4, bf16[16,4608]{1,0:T(8,128)(2,1)S(1)} %collective-permute-done.refs_4_.refs_3_, ...), custom_call_target="tpu_custom_call" | custom-call | flops 1024 | bytes 1024 | tf_op jit(solution)/shard_map/within_block/pallas_call | solution.py:39
  37.8 0.3 collective-permute-done.11.refs_0_
  38.1 0.5 collective-permute-start.13
  38.6 0.6 %collective-permute-done.14.refs_4_ = bf16[384,128]{1,0:T(8,128)(2,1)S(1)} collective-permute-done((bf16[384,128]{1,0:T(8,128)(2,1)S(1)}, bf16[384,128]{1,0:T(8,128)(2,1)S(1)}, u32[]{:S(2)}, u32[]{:S(2)}) %collective-permute-start.14) | collective-permute-done | bytes 98336 | tf_op jit(solution)/shard_map/ppermute | solution.py:412
  39.2 0.1 back_prefixes.2
  39.3 2.0 %collective-permute-start.16 = (bf16[768,128]{1,0:T(8,128)(2,1)S(1)}, bf16[768,128]{1,0:T(8,128)(2,1)S(1)}, u32[]{:S(2)}, u32[]{:S(2)}) collective-permute-start(bf16[768,128]{1,0:T(8,128)(2,1)S(1)} %get-tuple-element.134.refs_4_), channel_id=1, source_target_pairs={{0,2},{1,3},{2,0},{3,1},{4,6},{5,7},{6,4},{7,5},{8,10},{9,11},{10,... | collective-permute-start | bytes 589832 | tf_op jit(solution)/shard_map/ppermute | solution.py:412
  41.5 0.9 %within_block.14 = (bf16[256,768]{1,0:T(8,128)(2,1)S(1)}, f32[256,768]{1,0:T(8,128)S(1)}) custom-call(bf16[256,6144]{1,0:T(8,128)(2,1)S(1)} %copy-done, bf16[3,4,6144]{2,1,0:T(4,128)(2,1)S(1)} %copy-done.3, bf16[128,128]{1,0:T(8,128)(2,1)S(1)} %copy-done.4, bf16[16,4608]{1,0:T(8,128)(2,1)S(1)} %collective-permute-done.refs_4_.refs_3_, ...), custom_call_target="tpu_custom_call" | custom-call | flops 1024 | bytes 1024 | tf_op jit(solution)/shard_map/within_block/pallas_call | solution.py:39
  42.3 0.4 collective-permute-done.13.refs_4_
  42.7 0.1 back_prefixes.3
  42.9 1.6 %collective-permute-start.15 = (bf16[768,128]{1,0:T(8,128)(2,1)S(1)}, bf16[768,128]{1,0:T(8,128)(2,1)S(1)}, u32[]{:S(2)}, u32[]{:S(2)}) collective-permute-start(bf16[768,128]{1,0:T(8,128)(2,1)S(1)} %get-tuple-element.137.refs_4_), channel_id=1, source_target_pairs={{0,2},{1,3},{2,0},{3,1},{4,6},{5,7},{6,4},{7,5},{8,10},{9,11},{10,... | collective-permute-start | bytes 589832 | tf_op jit(solution)/shard_map/ppermute | solution.py:412
  44.5 0.9 %within_block.15 = (bf16[256,768]{1,0:T(8,128)(2,1)S(1)}, f32[256,768]{1,0:T(8,128)S(1)}) custom-call(bf16[256,6144]{1,0:T(8,128)(2,1)S(1)} %copy-done, bf16[3,4,6144]{2,1,0:T(4,128)(2,1)S(1)} %copy-done.3, bf16[128,128]{1,0:T(8,128)(2,1)S(1)} %copy-done.4, bf16[16,4608]{1,0:T(8,128)(2,1)S(1)} %collective-permute-done.refs_4_.refs_3_, ...), custom_call_target="tpu_custom_call" | custom-call | flops 1024 | bytes 1024 | tf_op jit(solution)/shard_map/within_block/pallas_call | solution.py:39
  45.4 1.4 %finish.4 = (bf16[256,6144]{1,0:T(8,128)(2,1)}, f32[8,128]{1,0:T(8,128)S(1)}) custom-call(f32[1,6144]{1,0:T(1,128)S(1)} %bitcast.1, bf16[768,128]{1,0:T(8,128)(2,1)S(1)} %get-tuple-element.142.refs_1_, bf16[768,128]{1,0:T(8,128)(2,1)S(1)} %get-tuple-element.143.refs_2_, bf16[256,768]{1,0:T(8,128)(2,1)S(1)} %get-tuple-element.144.refs_3_, ...), custom_call_target="tpu_custom_call" | custom-call | flops 1024 | bytes 1024 | tf_op jit(solution)/shard_map/finish/pallas_call | solution.py:39
  46.8 0.1 paired_prefixes.2
  47.0 1.1 %finish.5 = (bf16[256,6144]{1,0:T(8,128)(2,1)}, f32[8,128]{1,0:T(8,128)S(1)}) custom-call(f32[1,6144]{1,0:T(1,128)S(1)} %bitcast.2, bf16[768,128]{1,0:T(8,128)(2,1)S(1)} %get-tuple-element.148.refs_1_, bf16[256,768]{1,0:T(8,128)(2,1)S(1)} %get-tuple-element.149.refs_2_, ...), custom_call_target="tpu_custom_call", output_to_operand_aliasing={{0}: (4, {})} | custom-call | flops 1024 | bytes 1024 | tf_op jit(solution)/shard_map/finish/pallas_call | solution.py:39
  48.2 0.4 collective-permute-done.15.refs_0_
  48.6 0.1 paired_prefixes.3
  48.7 0.1 collective-permute-start.17
  48.9 1.6 %finish.6 = (bf16[256,6144]{1,0:T(8,128)(2,1)}, f32[8,128]{1,0:T(8,128)S(1)}) custom-call(f32[1,6144]{1,0:T(1,128)S(1)} %bitcast.3, bf16[768,128]{1,0:T(8,128)(2,1)S(1)} %get-tuple-element.156.refs_1_, bf16[1536,128]{1,0:T(8,128)(2,1)S(1)} %collective-permute-done.18.refs_2_, ...), custom_call_target="tpu_custom_call", output_to_operand_aliasing={{0}: (9, {})} | custom-call | flops 1024 | bytes 1024 | tf_op jit(solution)/shard_map/finish/pallas_call | solution.py:39
  50.5 1.4 %finish.7 = bf16[256,6144]{1,0:T(8,128)(2,1)} custom-call(f32[1,6144]{1,0:T(1,128)S(1)} %bitcast.4, bf16[1536,128]{1,0:T(8,128)(2,1)S(1)} %collective-permute-done.17.refs_1_, bf16[256,768]{1,0:T(8,128)(2,1)S(1)} %get-tuple-element.154.refs_2_, bf16[256,768]{1,0:T(8,128)(2,1)S(1)} %get-tuple-element.155.refs_3_, ...), custom_call_target="tpu_custom_call", output_to_operand_aliasing={{}: (6, {})} | custom-call | flops 1024 | bytes 1024 | tf_op jit(solution)/shard_map/finish/pallas_call | solution.py:39
  (35 shorter events, 0.9 us)
Async XLA Ops:
  0.0 4.5 %copy-start.2 = (bf16[256,6144]{1,0:T(8,128)(2,1)S(1)}, bf16[256,6144]{1,0:T(8,128)(2,1)}, u32[]{:S(2)}) copy-start(bf16[256,6144]{1,0:T(8,128)(2,1)} %refs_1_.17) | copy-start | bytes 9437188
  0.0 4.5 %copy-start.1 = (bf16[256,6144]{1,0:T(8,128)(2,1)S(1)}, bf16[256,6144]{1,0:T(8,128)(2,1)}, u32[]{:S(2)}) copy-start(bf16[256,6144]{1,0:T(8,128)(2,1)} %refs_0_.17) | copy-start | bytes 9437188
  0.0 4.5 %copy-start.4 = (bf16[128,128]{1,0:T(8,128)(2,1)S(1)}, bf16[128,128]{1,0:T(8,128)(2,1)}, u32[]{:S(2)}) copy-start(bf16[128,128]{1,0:T(8,128)(2,1)} %refs_2_.29) | copy-start | bytes 98308
  0.0 4.5 %copy-start.3 = (bf16[3,4,6144]{2,1,0:T(4,128)(2,1)S(1)}, bf16[3,4,6144]{2,1,0:T(4,128)(2,1)}, u32[]{:S(2)}) copy-start(bf16[3,4,6144]{2,1,0:T(4,128)(2,1)} %refs_1_.25) | copy-start | bytes 442372
  1.4 7.5 %collective-permute-start.1 = (bf16[16,4608]{1,0:T(8,128)(2,1)S(1)}, bf16[16,4608]{1,0:T(8,128)(2,1)S(1)}, u32[]{:S(2)}, u32[]{:S(2)}) collective-permute-start(bf16[16,4608]{1,0:T(8,128)(2,1)S(1)} %pack_rims.1.refs_4_), channel_id=1, source_target_pairs={{0,1},{1,2},{2,0},{3,4},{4,3},{5,6},{6,5},{7,8},{8,7},{9,10},{10,9... | collective-permute-start | bytes 442376 | tf_op jit(solution)/shard_map/ppermute | solution.py:420
  1.9 7.0 %collective-permute-start = (bf16[16,4608]{1,0:T(8,128)(2,1)S(1)}, bf16[16,4608]{1,0:T(8,128)(2,1)S(1)}, u32[]{:S(2)}, u32[]{:S(2)}) collective-permute-start(bf16[16,4608]{1,0:T(8,128)(2,1)S(1)} %pack_rims.1.refs_4_), channel_id=1, source_target_pairs={{0,1},{1,0},{2,3},{3,2},{4,5},{5,4},{6,7},{7,6},{8,9},{9,8},{10,11... | collective-permute-start | bytes 442376 | tf_op jit(solution)/shard_map/ppermute | solution.py:412
  6.4 3.6 %collective-permute-start.2 = (bf16[768,128]{1,0:T(8,128)(2,1)S(1)}, bf16[768,128]{1,0:T(8,128)(2,1)S(1)}, u32[]{:S(2)}, u32[]{:S(2)}) collective-permute-start(bf16[768,128]{1,0:T(8,128)(2,1)S(1)} %get-tuple-element.94), channel_id=1, source_target_pairs={{0,1},{1,0},{2,3},{3,2},{4,5},{5,4},{6,7},{7,6},{8,9},{9,8},{10,11... | collective-permute-start | bytes 589832 | tf_op jit(solution)/shard_map/ppermute | solution.py:412
  6.5 3.5 %collective-permute-start.3 = (bf16[768,128]{1,0:T(8,128)(2,1)S(1)}, bf16[768,128]{1,0:T(8,128)(2,1)S(1)}, u32[]{:S(2)}, u32[]{:S(2)}) collective-permute-start(bf16[768,128]{1,0:T(8,128)(2,1)S(1)} %get-tuple-element.84.refs_4_), channel_id=1, source_target_pairs={{0,1},{1,0},{2,3},{3,2},{4,5},{5,4},{6,7},{7,6},{8,9},{9,8},{10,11... | collective-permute-start | bytes 589832 | tf_op jit(solution)/shard_map/ppermute | solution.py:412
  9.2 1.3 %collective-permute-start.4 = (bf16[16,1536]{1,0:T(8,128)(2,1)S(1)}, bf16[16,1536]{1,0:T(8,128)(2,1)S(1)}, u32[]{:S(2)}, u32[]{:S(2)}) collective-permute-start(bf16[16,1536]{1,0:T(8,128)(2,1)S(1)} %get-tuple-element.91.refs_8_), channel_id=1, source_target_pairs={{0,1},{1,0},{2,3},{3,2},{4,5},{5,4},{6,7},{7,6},{8,9},{9,8},{10,11... | collective-permute-start | bytes 147464 | tf_op jit(solution)/shard_map/ppermute | solution.py:412
  10.8 7.0 %collective-permute-start.7 = (bf16[768,128]{1,0:T(8,128)(2,1)S(1)}, bf16[768,128]{1,0:T(8,128)(2,1)S(1)}, u32[]{:S(2)}, u32[]{:S(2)}) collective-permute-start(bf16[768,128]{1,0:T(8,128)(2,1)S(1)} %get-tuple-element.101), channel_id=1, source_target_pairs={{0,2},{1,3},{2,0},{3,1},{4,6},{5,7},{6,4},{7,5},{8,10},{9,11},{10,... | collective-permute-start | bytes 589832 | tf_op jit(solution)/shard_map/ppermute | solution.py:412
  14.4 3.4 %collective-permute-start.5 = (bf16[768,128]{1,0:T(8,128)(2,1)S(1)}, bf16[768,128]{1,0:T(8,128)(2,1)S(1)}, u32[]{:S(2)}, u32[]{:S(2)}) collective-permute-start(bf16[768,128]{1,0:T(8,128)(2,1)S(1)} %get-tuple-element.99), channel_id=1, source_target_pairs={{0,1},{1,0},{2,3},{3,2},{4,5},{5,4},{6,7},{7,6},{8,9},{9,8},{10,11... | collective-permute-start | bytes 589832 | tf_op jit(solution)/shard_map/ppermute | solution.py:412
  14.5 6.8 %copy-start = (bf16[256,6144]{1,0:T(8,128)(2,1)S(1)}, bf16[256,6144]{1,0:T(8,128)(2,1)}, u32[]{:S(2)}) copy-start(bf16[256,6144]{1,0:T(8,128)(2,1)} %refs_0_.25) | copy-start | bytes 9437188
  14.5 3.3 %collective-permute-start.6 = (bf16[768,128]{1,0:T(8,128)(2,1)S(1)}, bf16[768,128]{1,0:T(8,128)(2,1)S(1)}, u32[]{:S(2)}, u32[]{:S(2)}) collective-permute-start(bf16[768,128]{1,0:T(8,128)(2,1)S(1)} %get-tuple-element.96.refs_6_), channel_id=1, source_target_pairs={{0,1},{1,0},{2,3},{3,2},{4,5},{5,4},{6,7},{7,6},{8,9},{9,8},{10,11... | collective-permute-start | bytes 589832 | tf_op jit(solution)/shard_map/ppermute | solution.py:412
  18.0 6.2 %collective-permute-start.8 = (bf16[768,128]{1,0:T(8,128)(2,1)S(1)}, bf16[768,128]{1,0:T(8,128)(2,1)S(1)}, u32[]{:S(2)}, u32[]{:S(2)}) collective-permute-start(bf16[768,128]{1,0:T(8,128)(2,1)S(1)} %get-tuple-element.104), channel_id=1, source_target_pairs={{0,2},{1,3},{2,0},{3,1},{4,6},{5,7},{6,4},{7,5},{8,10},{9,11},{10,... | collective-permute-start | bytes 589832 | tf_op jit(solution)/shard_map/ppermute | solution.py:412
  19.7 6.2 %collective-permute-start.10 = (bf16[768,128]{1,0:T(8,128)(2,1)S(1)}, bf16[768,128]{1,0:T(8,128)(2,1)S(1)}, u32[]{:S(2)}, u32[]{:S(2)}) collective-permute-start(bf16[768,128]{1,0:T(8,128)(2,1)S(1)} %get-tuple-element.102.refs_4_), channel_id=1, source_target_pairs={{0,4},{1,5},{2,6},{3,7},{4,0},{5,1},{6,2},{7,3},{8,12},{9,13},{10,... | collective-permute-start | bytes 589832 | tf_op jit(solution)/shard_map/ppermute | solution.py:412
  24.2 7.0 %collective-permute-start.9 = (bf16[768,128]{1,0:T(8,128)(2,1)S(1)}, bf16[768,128]{1,0:T(8,128)(2,1)S(1)}, u32[]{:S(2)}, u32[]{:S(2)}) collective-permute-start(bf16[768,128]{1,0:T(8,128)(2,1)S(1)} %get-tuple-element.116.refs_2_), channel_id=1, source_target_pairs={{0,4},{1,5},{2,6},{3,7},{4,0},{5,1},{6,2},{7,3},{8,12},{9,13},{10,... | collective-permute-start | bytes 589832 | tf_op jit(solution)/shard_map/ppermute | solution.py:412
  26.1 7.6 %collective-permute-start.12 = (bf16[384,128]{1,0:T(8,128)(2,1)S(1)}, bf16[384,128]{1,0:T(8,128)(2,1)S(1)}, u32[]{:S(2)}, u32[]{:S(2)}) collective-permute-start(bf16[384,128]{1,0:T(8,128)(2,1)S(1)} %get-tuple-element.118.refs_7_), channel_id=1, source_target_pairs={{0,8},{1,9},{2,10},{3,11},{4,12},{5,13},{6,14},{7,15},{8,0},{9,1},... | collective-permute-start | bytes 294920 | tf_op jit(solution)/shard_map/ppermute | solution.py:412
  31.3 6.7 %collective-permute-start.11 = (bf16[384,128]{1,0:T(8,128)(2,1)S(1)}, bf16[384,128]{1,0:T(8,128)(2,1)S(1)}, u32[]{:S(2)}, u32[]{:S(2)}) collective-permute-start(bf16[384,128]{1,0:T(8,128)(2,1)S(1)} %get-tuple-element.122.refs_1_), channel_id=1, source_target_pairs={{0,8},{1,9},{2,10},{3,11},{4,12},{5,13},{6,14},{7,15},{8,0},{9,1},... | collective-permute-start | bytes 294920 | tf_op jit(solution)/shard_map/ppermute | solution.py:412
  33.6 5.6 %collective-permute-start.14 = (bf16[384,128]{1,0:T(8,128)(2,1)S(1)}, bf16[384,128]{1,0:T(8,128)(2,1)S(1)}, u32[]{:S(2)}, u32[]{:S(2)}) collective-permute-start(bf16[384,128]{1,0:T(8,128)(2,1)S(1)} %halves.2.refs_9_.refs_3_), channel_id=1, source_target_pairs={{0,4},{1,5},{2,6},{3,7},{4,0},{5,1},{6,2},{7,3},{8,12},{9,13},{10,... | collective-permute-start | bytes 294920 | tf_op jit(solution)/shard_map/ppermute | solution.py:412
  38.1 4.7 %collective-permute-start.13 = (bf16[384,128]{1,0:T(8,128)(2,1)S(1)}, bf16[384,128]{1,0:T(8,128)(2,1)S(1)}, u32[]{:S(2)}, u32[]{:S(2)}) collective-permute-start(bf16[384,128]{1,0:T(8,128)(2,1)S(1)} %halves.3.refs_5_.refs_3_), channel_id=1, source_target_pairs={{0,4},{1,5},{2,6},{3,7},{4,0},{5,1},{6,2},{7,3},{8,12},{9,13},{10,... | collective-permute-start | bytes 294920 | tf_op jit(solution)/shard_map/ppermute | solution.py:412
  39.3 7.5 %collective-permute-start.16 = (bf16[768,128]{1,0:T(8,128)(2,1)S(1)}, bf16[768,128]{1,0:T(8,128)(2,1)S(1)}, u32[]{:S(2)}, u32[]{:S(2)}) collective-permute-start(bf16[768,128]{1,0:T(8,128)(2,1)S(1)} %get-tuple-element.134.refs_4_), channel_id=1, source_target_pairs={{0,2},{1,3},{2,0},{3,1},{4,6},{5,7},{6,4},{7,5},{8,10},{9,11},{10,... | collective-permute-start | bytes 589832 | tf_op jit(solution)/shard_map/ppermute | solution.py:412
  42.9 5.8 %collective-permute-start.15 = (bf16[768,128]{1,0:T(8,128)(2,1)S(1)}, bf16[768,128]{1,0:T(8,128)(2,1)S(1)}, u32[]{:S(2)}, u32[]{:S(2)}) collective-permute-start(bf16[768,128]{1,0:T(8,128)(2,1)S(1)} %get-tuple-element.137.refs_4_), channel_id=1, source_target_pairs={{0,2},{1,3},{2,0},{3,1},{4,6},{5,7},{6,4},{7,5},{8,10},{9,11},{10,... | collective-permute-start | bytes 589832 | tf_op jit(solution)/shard_map/ppermute | solution.py:412
  44.4 1.0 %copy-start.5 = (f32[6144]{0:T(1024)S(1)}, f32[6144]{0:T(1024)}, u32[]{:S(2)}) copy-start(f32[6144]{0:T(1024)} %param.11) | copy-start | bytes 73732
  47.0 1.9 %collective-permute-start.18 = (bf16[1536,128]{1,0:T(8,128)(2,1)S(1)}, bf16[1536,128]{1,0:T(8,128)(2,1)S(1)}, u32[]{:S(2)}, u32[]{:S(2)}) collective-permute-start(bf16[1536,128]{1,0:T(8,128)(2,1)S(1)} %get-tuple-element.151.refs_5_), channel_id=1, source_target_pairs={{0,1},{1,0},{2,3},{3,2},{4,5},{5,4},{6,7},{7,6},{8,9},{9,8},{10,11... | collective-permute-start | bytes 1179656 | tf_op jit(solution)/shard_map/ppermute | solution.py:412
  48.7 1.8 %collective-permute-start.17 = (bf16[1536,128]{1,0:T(8,128)(2,1)S(1)}, bf16[1536,128]{1,0:T(8,128)(2,1)S(1)}, u32[]{:S(2)}, u32[]{:S(2)}) collective-permute-start(bf16[1536,128]{1,0:T(8,128)(2,1)S(1)} %get-tuple-element.153.refs_10_), channel_id=1, source_target_pairs={{0,1},{1,0},{2,3},{3,2},{4,5},{5,4},{6,7},{7,6},{8,9},{9,8},{10,11... | collective-permute-start | bytes 1179656 | tf_op jit(solution)/shard_map/ppermute | solution.py:412
